TPU v7x, 32 devices: a whole 2x2x4 slice. The times are simulated.
32 devices in a mesh: panel: 8 (over z, y), rhs: 4 (over x, core).
Axes of the slice: x: 2, y: 2, z: 4, core: 2. Of those that a mesh axis runs over, the one named last changes fastest.
Arguments:
- tiles: bfloat16 [192, 5, 256, 256], P(('panel', 'rhs')), as said below
- pattern: int32 [192, 5], replicated, may hold values from 0 to 191, as said below
- counts: int32 [192], replicated, may hold values from 2 to 5
- inputs: bfloat16 [16, 49152], P('rhs', 'panel'), may hold values from -6 to 6
Outputs:
- applied: bfloat16 [16, 49152], P('rhs', 'panel')
Inputs may be any that keep to these rules, and one draw needn't show every extreme that they name: pattern[b, 0] = b; pattern[b, 1] is the mate of b: mates are mutual (the mate of the mate of b is b), lie in another panel shard of 24 blocks, in the same index of rhs (block b belongs to device b // 6, that is panel index b // 24 and rhs index (b // 6) % 4); of one device's 6 block columns exactly 1 or zero have their mates in any one panel shard; for k >= 2, pattern[b, k] = (b // 6) * 6 + (b % 6 + k - 1) % 6; entries at or after counts[b] are ignored, as are the tiles there. `tiles`: every tile at slot 0 has all its singular values between 0.1 and 8.
All inputs are finite; a program needn't handle non-finite values.
Results may differ from a plain program's by a relative error of at most 0.0049.
Values may be sent and summed in bfloat16 or wider, within the bound.
No kernel may reach another device: no remote copies, remote signals or barrier semaphores. Data moves between devices by JAX's collectives and lax.ppermute only.
A program may use at most 128 MiB of HBM per device.

v0:
```python
import functools
import jax
import jax.numpy as jnp
from jax import lax
from jax.experimental import pallas as pl
from jax.experimental.pallas import tpu as pltpu
from jax.sharding import PartitionSpec as P

STEP = 32
PIVOTS = 8
NT = (((1,), (1,)), ((), ()))
NN = (((1,), (0,)), ((), ()))
TN = (((0,), (0,)), ((), ()))


def dot(a, b, dims):
    return lax.dot_general(a, b, dims, preferred_element_type=jnp.float32)


def split3(a):
    one = a.astype(jnp.bfloat16)
    rest = a - one.astype(jnp.float32)
    two = rest.astype(jnp.bfloat16)
    three = (rest - two.astype(jnp.float32)).astype(jnp.bfloat16)
    return one, two, three


def dot6(a, b, dims):
    a1, a2, a3 = split3(a)
    b1, b2, b3 = split3(b)
    small = dot(a1, b3, dims) + dot(a3, b1, dims) + dot(a2, b2, dims)
    return dot(a1, b1, dims) + ((dot(a1, b2, dims) + dot(a2, b1, dims)) + small)


def factor(ref, slab_ref, left_ref, right_ref):
    systems, width, _ = ref.shape
    halves = width // 128
    groups = STEP // 8
    lane = lax.broadcasted_iota(jnp.int32, (8, 128), 1)
    sub = lax.broadcasted_iota(jnp.int32, (8, 128), 0)
    row_in = lax.broadcasted_iota(jnp.int32, (STEP, width), 0)
    col_in = lax.broadcasted_iota(jnp.int32, (STEP, width), 1)
    row_all = lax.broadcasted_iota(jnp.int32, (width, width), 0)
    col_all = lax.broadcasted_iota(jnp.int32, (width, width), 1)

    def spread(row):
        return jnp.broadcast_to(row, (8, 128))

    def pivots(slabs):
        for first in range(0, STEP, PIVOTS):
            top = first // 8
            tall = range(top, groups)
            own = (lane >= first) & (lane < first + PIVOTS)
            one = jnp.where(lane - 8 * top == sub, 1.0, 0.0)
            columns = []
            for x in slabs:
                columns.append([{g: spread(x[g][0][:, first + q:first + q + 1]) for g in tall} for q in range(PIVOTS)])
                for g in tall:
                    x[g][0] = jnp.where(own, one if g == top else 0.0, x[g][0])
            if first % 8 == 0:
                scales = [jnp.ones((8, 128), jnp.float32) for _ in slabs]
            for q in range(PIVOTS):
                at = first % 8 + q
                for s, x in enumerate(slabs):
                    cols = columns[s]
                    scale = lax.rsqrt(spread(cols[q][top][at:at + 1, :]))
                    scales[s] = jnp.where(sub == at, scale, scales[s])
                    c = {g: cols[q][g] * scale for g in tall}
                    c[top] = jnp.where(sub > at, c[top], 0.0)
                    for later in range(q + 1, PIVOTS):
                        m = spread(c[top][first % 8 + later:first % 8 + later + 1, :])
                        for g in tall:
                            cols[later][g] = cols[later][g] - c[g] * m
                    for h in range(halves):
                        r = spread(x[top][h][at:at + 1, :]) * scale
                        for g in tall:
                            x[g][h] = x[g][h] - c[g] * r
            if (first + PIVOTS) % 8 == 0:
                for s, x in enumerate(slabs):
                    for h in range(halves):
                        x[top][h] = x[top][h] * scales[s]

    for s in range(systems):
        slab_ref[s] = ref[s, 0:STEP]
        left_ref[s] = jnp.zeros(left_ref.shape[1:], left_ref.dtype)
        right_ref[s] = jnp.zeros(right_ref.shape[1:], right_ref.dtype)

    def block(kb, carry):
        base = pl.multiple_of(kb * STEP, STEP)
        after = pl.multiple_of(jnp.minimum(base + STEP, width - STEP), STEP)
        done = (col_all >= base - STEP) & (col_all < base) & (row_all >= base + STEP)
        for s in range(systems):
            ref[s] = jnp.where(done, 0.0, ref[s]) - dot(left_ref[s], right_ref[s], TN)
        slabs = []
        for s in range(systems):
            slabs.append([[slab_ref[s, 8 * g:8 * g + 8, 128 * h:128 * h + 128] for h in range(halves)] for g in range(groups)])
        pivots(slabs)
        for s in range(systems):
            slab = jnp.concatenate([jnp.concatenate(line, axis=1) for line in slabs[s]], axis=0)
            slab = jnp.where((col_in > row_in) & (col_in < STEP), 0.0, slab)
            n1, n2, n3 = split3(slab[:, STEP:2 * STEP])
            q1, q2, q3 = split3(pltpu.roll(slab, width - STEP, 1))
            update = dot(
                jnp.concatenate([n1, n1, n2, n2, n1, n3], axis=0),
                jnp.concatenate([q1, q2, q1, q2, q3, q1], axis=0),
                TN,
            )
            coming = pltpu.roll(ref[s, pl.ds(after, STEP), :], width - after, 1)
            slab_ref[s] = jnp.where(col_in >= width - STEP, 0.0, coming) - update
            slab = pltpu.roll(slab, base, 1)
            ref[s, pl.ds(base, STEP), :] = jnp.where(col_in >= base + STEP, 0.0, slab)
            p1, p2, p3 = split3(slab)
            zero = jnp.zeros_like(p1)
            m1, m2, m3 = (jnp.where(col_in >= base + 2 * STEP, p, zero) for p in (p1, p2, p3))
            left_ref[s] = jnp.concatenate([m1, m1, m2, m2, m1, m3], axis=0)
            right_ref[s] = jnp.concatenate([p1, p2, p1, p2, p3, p1], axis=0)
        return carry

    lax.fori_loop(0, width // STEP, block, 0)


def factor_scratch(systems, width):
    return [
        pltpu.VMEM((systems, STEP, width), jnp.float32),
        pltpu.VMEM((systems, 6 * STEP, width), jnp.bfloat16),
        pltpu.VMEM((systems, 6 * STEP, width), jnp.bfloat16),
    ]


def own_kernel(counts_ref, tiles_ref, w_ref, z_ref, *scratch):
    systems, kslots, width, _ = tiles_ref.shape
    for s in range(systems):
        near = tiles_ref[s, 0:2].reshape(2 * width, width)
        w_ref[s] = dot(near, near, TN)
        for k in range(2, kslots):
            @pl.when(k < counts_ref[s])
            def _():
                tile = tiles_ref[s, k]
                w_ref[s] += dot(tile, tile, TN)
    factor(w_ref, *scratch)
    for s in range(systems):
        w1, w2, w3 = split3(w_ref[s])
        near = jnp.concatenate([tiles_ref[s, 1], tiles_ref[s, 0]], axis=0)
        z = dot(w1, near, NT) + (dot(w2, near, NT) + dot(w3, near, NT))
        z1, z2, z3 = split3(z)
        z_ref[s, 0] = z1
        z_ref[s, 1] = z2
        z_ref[s, 2] = z3


def pair_kernel(panel_ref, w_ref, z_ref, got_ref, x_ref, up_ref, low_ref, t_ref, vt_ref, r_ref, *scratch):
    systems, _, width, _ = z_ref.shape
    for s in range(systems):
        near = got_ref[panel_ref[s]].reshape(2 * width, width)
        near_t = near.T
        x = x_ref[:, s * width:(s + 1) * width]
        z1, z2, z3 = z_ref[s, 0], z_ref[s, 1], z_ref[s, 2]
        vt = dot(near_t, z1, NT) + (dot(near_t, z2, NT) + dot(near_t, z3, NT))
        first = dot(x, z1[:, width:], NT) + (dot(x, z2[:, width:], NT) + dot(x, z3[:, width:], NT))
        vt_ref[s] = vt
        up_ref[s] = first
        r_ref[s] = dot(x, near[width:], NN) - dot6(first, vt, NT)
        t_ref[s] = dot(near_t, near, NN) - dot6(vt, vt, NT)
    factor(t_ref, *scratch)
    for s in range(systems):
        y_low = dot6(dot6(r_ref[s], t_ref[s], NT), t_ref[s], NN)
        low_ref[s] = y_low
        up_ref[s] = dot6(up_ref[s] - dot6(y_low, vt_ref[s], NN), w_ref[s], NN)


def on_device(tiles, pattern, counts, inputs):
    shards = lax.axis_size("panel")
    lanes = lax.axis_size("rhs")
    systems, kslots, width, _ = tiles.shape
    nrhs_dev = inputs.shape[0]
    nrhs = nrhs_dev * lanes
    per_panel = systems * lanes
    device = lax.axis_index("panel") * lanes + lax.axis_index("rhs")
    first = device * systems
    own_cnt = lax.dynamic_slice_in_dim(counts, first, systems, 0)
    mate_panel = lax.dynamic_slice(pattern, (first, 1), (systems, 1))[:, 0] // per_panel
    hit = mate_panel[None, :] == jnp.arange(shards, dtype=jnp.int32)[:, None]
    slot_of = jnp.sum(hit * jnp.arange(systems, dtype=jnp.int32)[None, :], axis=1)

    sendbuf = tiles[:, :2][slot_of]
    received = lax.all_to_all(sendbuf, "panel", split_axis=0, concat_axis=0, tiled=True)
    x = lax.all_to_all(inputs, "rhs", split_axis=1, concat_axis=0, tiled=True)

    vmem = pl.BlockSpec(memory_space=pltpu.VMEM)
    smem = pl.BlockSpec(memory_space=pltpu.SMEM)
    params = pltpu.CompilerParams(vmem_limit_bytes=56 * 1024 * 1024)
    w, z = pl.pallas_call(
        own_kernel,
        out_shape=(
            jax.ShapeDtypeStruct((systems, width, width), jnp.float32),
            jax.ShapeDtypeStruct((systems, 3, width, 2 * width), jnp.bfloat16),
        ),
        in_specs=[smem, vmem],
        out_specs=(vmem, vmem),
        scratch_shapes=factor_scratch(systems, width),
        compiler_params=params,
        cost_estimate=pl.CostEstimate(flops=40 * 10**9, bytes_accessed=8 * 10**6, transcendentals=0),
    )(own_cnt, tiles)
    up, low = pl.pallas_call(
        pair_kernel,
        out_shape=(
            jax.ShapeDtypeStruct((systems, nrhs, width), jnp.float32),
            jax.ShapeDtypeStruct((systems, nrhs, width), jnp.float32),
        ),
        in_specs=[smem, vmem, vmem, vmem, vmem],
        out_specs=(vmem, vmem),
        scratch_shapes=[
            pltpu.VMEM((systems, width, width), jnp.float32),
            pltpu.VMEM((systems, width, width), jnp.float32),
            pltpu.VMEM((systems, nrhs, width), jnp.float32),
        ] + factor_scratch(systems, width),
        compiler_params=params,
    )(mate_panel, w, z, received, x)
    returned = lax.all_to_all(low[slot_of], "panel", split_axis=0, concat_axis=0, tiled=True)
    result = (up + returned[mate_panel]).astype(jnp.bfloat16)
    result = jnp.swapaxes(result, 0, 1).reshape(nrhs, systems * width)
    return lax.all_to_all(result, "rhs", split_axis=0, concat_axis=1, tiled=True)


def solution(mesh):
    return jax.shard_map(
        on_device,
        mesh=mesh,
        in_specs=(P(("panel", "rhs"), None, None, None), P(), P(), P("rhs", "panel")),
        out_specs=P("rhs", "panel"),
        check_vma=False,
    )
```

profile of v0, /device:TPU:0, one launch (start us, length us, event | category | flops | bytes accessed | tf_op | source)
XLA Modules:
  0.0 123.4 jit_solution(10187620893787737955)
XLA Ops:
  0.0 0.0 slice-start
  0.0 4.3 %all-to-all-start.1 = ((bf16[4,4,1536]{2,0,1:T(4,128)(2,1)}), bf16[4,4,1536]{2,0,1:T(4,128)(2,1)S(1)}, u32[]{:S(2)}, u32[]{:S(2)}) async-start(bf16[4,4,1536]{2,0,1:T(4,128)(2,1)} %bitcast.19), calls=%async_computation.1 | async-start | bytes 98304 | tf_op jit(solution)/shard_map/all_to_all | solution.py:187
  4.3 0.8 fusion.2
  5.1 0.0 copy-start.1
  5.1 0.1 select_reduce_fusion
  5.3 0.0 copy-done.2
  5.3 0.6 dynamic_slice.7.counts_ref
  5.9 0.0 slice-done
  5.9 2.1 %gather_fusion = bf16[8,2,256,256]{3,2,1,0:T(8,128)(2,1)} fusion(bf16[6,2,256,256]{3,2,1,0:T(8,128)(2,1)S(1)} %slice-done, s32[1024]{0:T(1024)S(1)} %pad_clamp_fusion.1), kind=kCustom, calls=%fused_computation | custom fusion | bytes 4194336 | tf_op jit(solution)/shard_map/gather | solution.py:185
  7.9 0.0 copy-done.1
  8.0 0.4 all-to-all-done.1
  8.4 6.3 %all-to-all-start = ((bf16[8,2,256,256]{3,2,1,0:T(8,128)(2,1)}), bf16[8,2,256,256]{3,2,1,0:T(8,128)(2,1)S(1)}, u32[]{:S(2)}, u32[]{:S(2)}) async-start(bf16[8,2,256,256]{3,2,1,0:T(8,128)(2,1)} %gather_fusion), calls=%async_computation | async-start | bytes 4194304 | tf_op jit(solution)/shard_map/all_to_all | solution.py:186
  14.7 28.9 %shard_map.46 = (f32[6,256,256]{2,1,0:T(8,128)}, bf16[6,3,256,512]{3,2,1,0:T(8,128)(2,1)}) custom-call(s32[6]{0:T(128)} %dynamic_slice.7.counts_ref, bf16[6,5,256,256]{3,2,1,0:T(8,128)(2,1)} %tiles_ref.1), custom_call_target="tpu_custom_call" | custom-call | flops 40000000000 | bytes 8000000 | tf_op jit(solution)/shard_map/pallas_call | solution.py:192
  43.6 0.6 all_to_all.38.x_ref
  44.2 19.0 %all-to-all-done.got_ref = bf16[8,2,256,256]{3,2,1,0:T(8,128)(2,1)S(1)} async-done(((bf16[8,2,256,256]{3,2,1,0:T(8,128)(2,1)}), bf16[8,2,256,256]{3,2,1,0:T(8,128)(2,1)S(1)}, u32[]{:S(2)}, u32[]{:S(2)}) %all-to-all-start) | async-done | bytes 2097184 | tf_op jit(solution)/shard_map/all_to_all | solution.py:186
  63.2 1.4 %copy-done = bf16[8,2,256,256]{3,2,1,0:T(8,128)(2,1)} copy-done((bf16[8,2,256,256]{3,2,1,0:T(8,128)(2,1)}, bf16[8,2,256,256]{3,2,1,0:T(8,128)(2,1)S(1)}, u32[]{:S(2)}) %copy-start) | copy-done | bytes 2097176
  64.6 36.8 %shard_map.47 = (f32[6,16,256]{2,1,0:T(8,128)}, f32[6,16,256]{2,1,0:T(8,128)}) custom-call(s32[6]{0:T(128)} %copy-done.1, f32[6,256,256]{2,1,0:T(8,128)} %get-tuple-element.9.w_ref, bf16[6,3,256,512]{3,2,1,0:T(8,128)(2,1)} %get-tuple-element.10.z_ref, bf16[8,2,256,256]{3,2,1,0:T(8,128)(2,1)} %copy-done, bf16[16,1536]{1,0:T(8,128)(2,1)} %all_to_all.38.x_ref), custom_call_target="tpu_custom_call" | custom-call | tf_op jit(solution)/shard_map/pallas_call | solution.py:204
  101.4 2.1 %gather_fusion.1 = f32[8,16,256]{2,1,0:T(8,128)} fusion(f32[6,16,256]{2,1,0:T(8,128)} %get-tuple-element.12, s32[1024]{0:T(1024)S(1)} %pad_clamp_fusion.1), kind=kCustom, calls=%fused_computation.1 | custom fusion | bytes 262176 | tf_op jit(solution)/shard_map/gather | solution.py:219
  103.5 3.6 %all-to-all-start.2 = ((f32[8,16,256]{2,1,0:T(8,128)}), f32[8,16,256]{2,1,0:T(8,128)S(1)}, u32[]{:S(2)}, u32[]{:S(2)}) async-start(f32[8,16,256]{2,1,0:T(8,128)} %gather_fusion.1), calls=%async_computation.2 | async-start | bytes 262144 | tf_op jit(solution)/shard_map/all_to_all | solution.py:219
  107.1 7.3 %all-to-all-done.2 = f32[8,16,256]{2,1,0:T(8,128)S(1)} async-done(((f32[8,16,256]{2,1,0:T(8,128)}), f32[8,16,256]{2,1,0:T(8,128)S(1)}, u32[]{:S(2)}, u32[]{:S(2)}) %all-to-all-start.2) | async-done | bytes 131104 | tf_op jit(solution)/shard_map/all_to_all | solution.py:219
  114.4 0.6 gather_fusion.2
  115.0 0.9 fusion
  116.0 6.8 %all_to_all.48 = bf16[4,4,1536]{2,1,0:T(4,128)(2,1)S(1)} all-to-all(bf16[4,4,1536]{2,1,0:T(4,128)(2,1)S(1)} %all_to_all.40), channel_id=1, replica_groups=mesh['panel'=8,'rhs'=4] {'rhs'}, dimensions={0} | all-to-all | bytes 98304 | tf_op jit(solution)/shard_map/all_to_all | solution.py:222
  122.8 0.6 copy.11
  (8 shorter events, 0.1 us)
Async XLA Ops:
  0.0 5.9 %slice-start = ((bf16[6,5,256,256]{3,2,1,0:T(8,128)(2,1)}), bf16[6,2,256,256]{3,2,1,0:T(8,128)(2,1)S(1)}, s32[]{:S(2)}) async-start(bf16[6,5,256,256]{3,2,1,0:T(8,128)(2,1)} %tiles_ref.1), calls=%async_computation.4 | async-start | bytes 3145728 | tf_op jit(solution)/shard_map/slice | solution.py:185
  0.0 5.3 %copy-start.2 = (s32[192]{0:T(256)S(1)}, s32[192]{0:T(256)}, u32[]{:S(2)}) copy-start(s32[192]{0:T(256)} %param.6) | copy-start | bytes 2308
  0.0 8.4 %all-to-all-start.1 = ((bf16[4,4,1536]{2,0,1:T(4,128)(2,1)}), bf16[4,4,1536]{2,0,1:T(4,128)(2,1)S(1)}, u32[]{:S(2)}, u32[]{:S(2)}) async-start(bf16[4,4,1536]{2,0,1:T(4,128)(2,1)} %bitcast.19), calls=%async_computation.1 | async-start | bytes 98304 | tf_op jit(solution)/shard_map/all_to_all | solution.py:187
  5.1 2.8 %copy-start.1 = (s32[6]{0:T(128)}, s32[6]{0:T(128)S(1)}, u32[]{:S(2)}) copy-start(s32[6]{0:T(128)S(1)} %bitcast_select_fusion.panel_ref) | copy-start | bytes 76
  8.4 54.8 %all-to-all-start = ((bf16[8,2,256,256]{3,2,1,0:T(8,128)(2,1)}), bf16[8,2,256,256]{3,2,1,0:T(8,128)(2,1)S(1)}, u32[]{:S(2)}, u32[]{:S(2)}) async-start(bf16[8,2,256,256]{3,2,1,0:T(8,128)(2,1)} %gather_fusion), calls=%async_computation | async-start | bytes 4194304 | tf_op jit(solution)/shard_map/all_to_all | solution.py:186
  63.2 1.4 %copy-start = (bf16[8,2,256,256]{3,2,1,0:T(8,128)(2,1)}, bf16[8,2,256,256]{3,2,1,0:T(8,128)(2,1)S(1)}, u32[]{:S(2)}) copy-start(bf16[8,2,256,256]{3,2,1,0:T(8,128)(2,1)S(1)} %all-to-all-done.got_ref) | copy-start | bytes 6291460
  103.5 11.0 %all-to-all-start.2 = ((f32[8,16,256]{2,1,0:T(8,128)}), f32[8,16,256]{2,1,0:T(8,128)S(1)}, u32[]{:S(2)}, u32[]{:S(2)}) async-start(f32[8,16,256]{2,1,0:T(8,128)} %gather_fusion.1), calls=%async_computation.2 | async-start | bytes 262144 | tf_op jit(solution)/shard_map/all_to_all | solution.py:219
where the time goes:
time: 124 us; the launch traced here: 123 us
  Pallas kernels  65.7 us (53%)
  waiting for transfers between devices  26.7 us (22%)
  starting transfers between devices  14.3 us (12%)
  local copies, waits for them, and re-layouts  8 us (6%)
  blocking collectives  6.78 us (5%)
  other arithmetic  1.83 us (1%)
    pallas_call x1, Pallas kernels, on_device(): pl.pallas_call(pair_kernel, out_shape=(jax.ShapeDtypeStruct((systems, nrh...  36.8 us
    pallas_call x1, Pallas kernels, on_device(): pl.pallas_call(own_kernel, out_shape=(jax.ShapeDtypeStruct((systems, widt...  28.9 us
    all_to_all x1, waiting for transfers between devices, on_device(): lax.all_to_all(sendbuf, 'panel', split_axis=0, concat_axis=0, tiled=True)  19 us
    all_to_all x1, waiting for transfers between devices, on_device(): lax.all_to_all(low[slot_of], 'panel', split_axis=0, concat_axis=0, tiled=...  7.34 us
    all_to_all x1, blocking collectives, on_device(): lax.all_to_all(result, 'rhs', split_axis=0, concat_axis=1, tiled=True)  6.78 us
    all_to_all x1, starting transfers between devices, on_device(): lax.all_to_all(sendbuf, 'panel', split_axis=0, concat_axis=0, tiled=True)  6.32 us
    all_to_all x1, starting transfers between devices, on_device(): x = lax.all_to_all(inputs, 'rhs', split_axis=1, concat_axis=0, tiled=True)  4.34 us
    all_to_all x1, starting transfers between devices, on_device(): lax.all_to_all(low[slot_of], 'panel', split_axis=0, concat_axis=0, tiled=...  3.62 us
  transfers between devices with their start and end apart: 3, of which 3 were waited for; matrix products, arithmetic and copies ran while one was open for 3% of the time, Pallas kernels for 23%

commit v1 on v0

v1 whole, which is shorter than its diff:
```python
import functools
import jax
import jax.numpy as jnp
from jax import lax
from jax.experimental import pallas as pl
from jax.experimental.pallas import tpu as pltpu
from jax.sharding import PartitionSpec as P

STEP = 32
NT = (((1,), (1,)), ((), ()))
NN = (((1,), (0,)), ((), ()))
TN = (((0,), (0,)), ((), ()))


def dot(a, b, dims):
    return lax.dot_general(a, b, dims, preferred_element_type=jnp.float32)


def split3(a):
    one = a.astype(jnp.bfloat16)
    rest = a - one.astype(jnp.float32)
    two = rest.astype(jnp.bfloat16)
    three = (rest - two.astype(jnp.float32)).astype(jnp.bfloat16)
    return one, two, three


def dot6(a, b, dims):
    a1, a2, a3 = a
    b1, b2, b3 = b
    small = dot(a1, b3, dims) + dot(a3, b1, dims) + dot(a2, b2, dims)
    return dot(a1, b1, dims) + ((dot(a1, b2, dims) + dot(a2, b1, dims)) + small)


def apply(rows, parts, dims):
    count = rows.shape[0]
    stack = jnp.concatenate(split3(rows), axis=0)
    high = dot(stack, parts[0], dims)
    low = dot(stack[:2 * count], parts[1], dims)
    return high[:count] + ((high[count:2 * count] + low[:count]) + (high[2 * count:] + low[count:]))


def factor(ref, slab_ref, left_ref, right_ref):
    systems, width, _ = ref.shape
    halves = width // 128
    groups = STEP // 8
    lane = lax.broadcasted_iota(jnp.int32, (8, 128), 1)
    sub = lax.broadcasted_iota(jnp.int32, (8, 128), 0)
    row_in = lax.broadcasted_iota(jnp.int32, (STEP, width), 0)
    col_in = lax.broadcasted_iota(jnp.int32, (STEP, width), 1)
    row_all = lax.broadcasted_iota(jnp.int32, (width, width), 0)
    col_all = lax.broadcasted_iota(jnp.int32, (width, width), 1)

    def spread(row):
        return jnp.broadcast_to(row, (8, 128))

    def pivots(slabs):
        for first in range(0, STEP, 4):
            top, at = first // 8, first % 8
            tall = range(top, groups)
            own = (lane >= first) & (lane < first + 4)
            one = jnp.where(lane - 8 * top == sub, 1.0, 0.0)
            if at == 0:
                inverses = [None] * len(slabs)
            columns, rows = [], []
            for x in slabs:
                columns.append([{g: spread(x[g][0][:, first + q:first + q + 1]) for g in tall} for q in range(4)])
                for g in tall:
                    x[g][0] = jnp.where(own, one if g == top else 0.0, x[g][0])
                rows.append([[spread(x[top][h][at + q:at + q + 1, :]) for h in range(halves)] for q in range(4)])
            for s, x in enumerate(slabs):
                u = columns[s]
                a = {(i, j): spread(u[j][top][at + i:at + i + 1, :]) for j in range(4) for i in range(j + 1)}
                low, inv = {}, []
                for i in range(4):
                    for j in range(i, 4):
                        for k in range(i):
                            a[i, j] = a[i, j] - low[i, k] * a[k, j]
                    inv.append(pl.reciprocal(a[i, i], approx=True))
                    for j in range(i + 1, 4):
                        low[j, i] = a[i, j] * inv[i]
                for i in range(4):
                    for k in range(i):
                        for g in tall:
                            u[i][g] = u[i][g] - u[k][g] * low[i, k]
                        for h in range(halves):
                            rows[s][i][h] = rows[s][i][h] - rows[s][k][h] * low[i, k]
                for i in range(4):
                    for g in tall:
                        m = u[i][g] * inv[i]
                        if g == top:
                            m = jnp.where(sub > at + i, m, 0.0)
                        for h in range(halves):
                            x[g][h] = x[g][h] - m * rows[s][i][h]
                    inverses[s] = inv[i] if at + i == 0 else jnp.where(sub >= at + i, inv[i], inverses[s])
            if at == 4:
                for s, x in enumerate(slabs):
                    scale = inverses[s] * lax.rsqrt(inverses[s])
                    for h in range(halves):
                        x[top][h] = x[top][h] * scale

    for s in range(systems):
        slab_ref[s] = ref[s, 0:STEP]
        left_ref[s] = jnp.zeros(left_ref.shape[1:], left_ref.dtype)
        right_ref[s] = jnp.zeros(right_ref.shape[1:], right_ref.dtype)

    def block(kb, carry):
        base = pl.multiple_of(kb * STEP, STEP)
        after = pl.multiple_of(jnp.minimum(base + STEP, width - STEP), STEP)
        done = (col_all >= base - STEP) & (col_all < base) & (row_all >= base + STEP)
        for s in range(systems):
            ref[s] = jnp.where(done, 0.0, ref[s]) - dot(left_ref[s], right_ref[s], TN)
        slabs = []
        for s in range(systems):
            slabs.append([[slab_ref[s, 8 * g:8 * g + 8, 128 * h:128 * h + 128] for h in range(halves)] for g in range(groups)])
        pivots(slabs)
        for s in range(systems):
            slab = jnp.concatenate([jnp.concatenate(line, axis=1) for line in slabs[s]], axis=0)
            slab = jnp.where((col_in > row_in) & (col_in < STEP), 0.0, slab)
            n1, n2, n3 = split3(slab[:, STEP:2 * STEP])
            q1, q2, q3 = split3(pltpu.roll(slab, width - STEP, 1))
            update = dot(
                jnp.concatenate([n1, n1, n2, n2, n1, n3], axis=0),
                jnp.concatenate([q1, q2, q1, q2, q3, q1], axis=0),
                TN,
            )
            coming = pltpu.roll(ref[s, pl.ds(after, STEP), :], width - after, 1)
            slab_ref[s] = jnp.where(col_in >= width - STEP, 0.0, coming) - update
            slab = pltpu.roll(slab, base, 1)
            ref[s, pl.ds(base, STEP), :] = jnp.where(col_in >= base + STEP, 0.0, slab)
            p1, p2, p3 = split3(slab)
            zero = jnp.zeros_like(p1)
            m1, m2, m3 = (jnp.where(col_in >= base + 2 * STEP, p, zero) for p in (p1, p2, p3))
            left_ref[s] = jnp.concatenate([m1, m1, m2, m2, m1, m3], axis=0)
            right_ref[s] = jnp.concatenate([p1, p2, p1, p2, p3, p1], axis=0)
        return carry

    lax.fori_loop(0, width // STEP, block, 0)


def factor_scratch(systems, width):
    return [
        pltpu.VMEM((systems, STEP, width), jnp.float32),
        pltpu.VMEM((systems, 6 * STEP, width), jnp.bfloat16),
        pltpu.VMEM((systems, 6 * STEP, width), jnp.bfloat16),
    ]


def own_kernel(counts_ref, tiles_ref, w_ref, z_ref, g_ref, *scratch):
    systems, kslots, width, _ = tiles_ref.shape
    for s in range(systems):
        near = tiles_ref[s, 0:2].reshape(2 * width, width)
        g_ref[s] = dot(near, near, TN)
        for k in range(2, kslots):
            @pl.when(k < counts_ref[s])
            def _():
                tile = tiles_ref[s, k]
                g_ref[s] += dot(tile, tile, TN)
    factor(g_ref, *scratch)
    for s in range(systems):
        w1, w2, w3 = split3(g_ref[s])
        w_ref[s, 0] = w1
        w_ref[s, 1] = w2
        near = jnp.concatenate([tiles_ref[s, 1], tiles_ref[s, 0]], axis=0)
        z = dot(w1, near, NT) + (dot(w2, near, NT) + dot(w3, near, NT))
        z1, z2, z3 = split3(z)
        z_ref[s, 0] = z1
        z_ref[s, 1] = z2
        z_ref[s, 2] = z3


def pair_kernel(lanes, place_ref, w_ref, z_ref, x_ref, got_ref, *refs):
    up_refs, refs = refs[:lanes], refs[lanes:]
    low_ref, near_ref, t_ref, v_ref, r_ref, first_ref, sems, *scratch = refs
    systems, _, width, _ = z_ref.shape
    count = x_ref.shape[0] // lanes
    copies = [pltpu.make_async_copy(got_ref.at[place_ref[s]], near_ref.at[s], sems.at[s]) for s in range(systems)]
    for copy in copies:
        copy.start()
    low_ref[...] = jnp.zeros(low_ref.shape, low_ref.dtype)
    for s in range(systems):
        copies[s].wait()
        near = near_ref[s].reshape(2 * width, width)
        near_t = near.T
        z1, z2, z3 = z_ref[s, 0], z_ref[s, 1], z_ref[s, 2]
        v = split3(dot(near_t, z1, NT) + (dot(near_t, z2, NT) + dot(near_t, z3, NT)))
        v_ref[s, 0] = v[0]
        v_ref[s, 1] = v[1]
        t_ref[s] = dot(near_t, near, NN) - dot6(v, v, NT)
    for s in range(systems):
        x = x_ref[:, s * width:(s + 1) * width]
        first_ref[s] = dot(x, z_ref[s, 0, :, width:], NT) + dot(x, z_ref[s, 1, :, width:], NT)
        r_ref[s] = dot(x, near_ref[s, 1], NN)
    for s in range(systems):
        r_ref[s] = r_ref[s] - apply(first_ref[s], (v_ref[s, 0], v_ref[s, 1]), NT)
    factor(t_ref, *scratch)
    parts = [split3(t_ref[s])[:2] for s in range(systems)]
    half = [apply(r_ref[s], parts[s], NT) for s in range(systems)]
    last = [apply(half[s], parts[s], NN) for s in range(systems)]
    mid = [first_ref[s] - apply(last[s], (v_ref[s, 0], v_ref[s, 1]), NN) for s in range(systems)]
    for s in range(systems):
        up = apply(mid[s], (w_ref[s, 0], w_ref[s, 1]), NN)
        for e in range(lanes):
            up_refs[e][s] = up[e * count:(e + 1) * count]
            owner = lax.rem(place_ref[systems] + e, lanes)
            low_ref[place_ref[s] * lanes + owner] = last[s][e * count:(e + 1) * count]


def place_kernel(lanes, place_ref, low_ref, *refs):
    up_refs, out_ref = refs[:lanes], refs[lanes]
    systems, _, width = up_refs[0].shape
    for e in range(lanes):
        owner = lax.rem(place_ref[systems * lanes] + lanes - e, lanes)
        for s in range(systems):
            at = owner * systems + s
            total = up_refs[e][s] + low_ref[place_ref[at] * lanes + owner]
            out_ref[:, pl.ds(pl.multiple_of(at * width, width), width)] = total.astype(out_ref.dtype)


def on_device(tiles, pattern, counts, inputs):
    shards = lax.axis_size("panel")
    lanes = lax.axis_size("rhs")
    systems, kslots, width, _ = tiles.shape
    nrhs_dev = inputs.shape[0]
    own_width = systems * width
    my_panel = lax.axis_index("panel")
    my_lane = lax.axis_index("rhs")
    per_panel = systems * lanes
    own_cnt = lax.dynamic_slice_in_dim(counts, my_panel * per_panel + my_lane * systems, systems, 0)
    panel_mates = lax.dynamic_slice(pattern, (my_panel * per_panel, 1), (per_panel, 1))[:, 0] // per_panel
    mate_panel = lax.dynamic_slice_in_dim(panel_mates, my_lane * systems, systems, 0)
    hit = mate_panel[None, :] == jnp.arange(shards, dtype=jnp.int32)[:, None]
    slot_of = jnp.sum(hit * jnp.arange(systems, dtype=jnp.int32)[None, :], axis=1)
    lane_word = my_lane[None].astype(jnp.int32)

    def shift(value, by):
        return lax.ppermute(value, "rhs", [(i, (i + by) % lanes) for i in range(lanes)])

    received = lax.all_to_all(tiles[:, :2][slot_of], "panel", split_axis=0, concat_axis=0, tiled=True)

    vmem = pl.BlockSpec(memory_space=pltpu.VMEM)
    smem = pl.BlockSpec(memory_space=pltpu.SMEM)
    params = pltpu.CompilerParams(vmem_limit_bytes=56 * 1024 * 1024)
    w, z = pl.pallas_call(
        own_kernel,
        out_shape=(
            jax.ShapeDtypeStruct((systems, 2, width, width), jnp.bfloat16),
            jax.ShapeDtypeStruct((systems, 3, width, 2 * width), jnp.bfloat16),
        ),
        in_specs=[smem, vmem],
        out_specs=(vmem, vmem),
        scratch_shapes=[pltpu.VMEM((systems, width, width), jnp.float32)] + factor_scratch(systems, width),
        compiler_params=params,
        cost_estimate=pl.CostEstimate(flops=40 * 10**9, bytes_accessed=8 * 10**6, transcendentals=0),
    )(own_cnt, tiles)

    inputs, w = lax.optimization_barrier((inputs, w))
    parts = [lax.dynamic_slice_in_dim(inputs, my_lane * own_width, own_width, 1)]
    for e in range(1, lanes):
        part = lax.dynamic_slice_in_dim(inputs, (my_lane + lanes - e) % lanes * own_width, own_width, 1)
        parts.append(shift(part, -e))
    x = jnp.concatenate(parts, axis=0)

    piece = jax.ShapeDtypeStruct((systems, nrhs_dev, width), jnp.float32)
    *up, low = pl.pallas_call(
        functools.partial(pair_kernel, lanes),
        out_shape=[piece] * lanes + [jax.ShapeDtypeStruct((shards * lanes, nrhs_dev, width), jnp.float32)],
        in_specs=[smem, vmem, vmem, vmem, pl.BlockSpec(memory_space=pl.ANY)],
        out_specs=[vmem] * (lanes + 1),
        scratch_shapes=[
            pltpu.VMEM((systems, 2, width, width), jnp.bfloat16),
            pltpu.VMEM((systems, width, width), jnp.float32),
            pltpu.VMEM((systems, 2, width, width), jnp.bfloat16),
            pltpu.VMEM((systems, lanes * nrhs_dev, width), jnp.float32),
            pltpu.VMEM((systems, lanes * nrhs_dev, width), jnp.float32),
            pltpu.SemaphoreType.DMA((systems,)),
        ] + factor_scratch(systems, width),
        compiler_params=params,
    )(jnp.concatenate([mate_panel, lane_word]), w, z, x, received)
    low = lax.all_to_all(low, ("panel", "rhs"), split_axis=0, concat_axis=0, tiled=True)
    up = [up[0]] + [shift(up[e], e) for e in range(1, lanes)]
    return pl.pallas_call(
        functools.partial(place_kernel, lanes),
        out_shape=jax.ShapeDtypeStruct((nrhs_dev, per_panel * width), jnp.bfloat16),
        in_specs=[smem] + [vmem] * (lanes + 1),
        out_specs=vmem,
    )(jnp.concatenate([panel_mates, lane_word]), low, *up)


def solution(mesh):
    return jax.shard_map(
        on_device,
        mesh=mesh,
        in_specs=(P(("panel", "rhs"), None, None, None), P(), P(), P("rhs", "panel")),
        out_specs=P("rhs", "panel"),
        check_vma=False,
    )
```

time: 124 us -> 114 us (0.919)
  waiting for transfers between devices: 26.7 us -> 12.2 us
  Pallas kernels: 65.7 us -> 74.2 us
  blocking collectives: 6.78 us -> 0 us
  starting transfers between devices: 14.3 us -> 19.1 us
  local copies, waits for them, and re-layouts: 8 us -> 5.07 us
    all_to_all x3 -> x2, waiting for transfers between devices: 26.7 us -> 10.2 us  [the longest x1 7.04 us: on_device(): lax.all_to_all(tiles[:, :2][slot_of], 'panel', split_axis=0, concat_axis=...]
    pallas_call x2 -> x3, Pallas kernels: 65.7 us -> 74.2 us  [the longest x1 38.8 us: on_device(): pl.pallas_call(functools.partial(pair_kernel, lanes), out_shape=[piece] *...]
    ppermute x0 -> x6, starting transfers between devices: none -> 8.05 us  [shift(): lax.ppermute(value, 'rhs', [(i, (i + by) % lanes) for i in range(lanes)])]
    all_to_all x1 -> x0, blocking collectives: 6.78 us -> none  [on_device(): lax.all_to_all(result, 'rhs', split_axis=0, concat_axis=1, tiled=True)]
    all_to_all x3 -> x2, starting transfers between devices: 14.3 us -> 11.1 us  [the longest x1 7.41 us: on_device(): lax.all_to_all(tiles[:, :2][slot_of], 'panel', split_axis=0, concat_axis=...]
    gather x3 -> x1, local copies, waits for them, and re-layouts: 4.7 us -> 2.04 us  [on_device(): tiles[:, :2][slot_of]]
    ppermute x0 -> x6, waiting for transfers between devices: none -> 1.92 us  [shift(): lax.ppermute(value, 'rhs', [(i, (i + by) % lanes) for i in range(lanes)])]
    concatenate x0 -> x3, other arithmetic: none -> 1.86 us  [the longest x1 0.65 us: on_device(): x = jnp.concatenate(parts, axis=0)]
  transfers between devices with their start and end apart: 3 -> 8, of which waited for: 3 -> 5; matrix products, arithmetic and copies ran while one was open for 3% -> 2% of each run, Pallas kernels for 23% -> 30%
where the time goes in v1:
time: 114 us
  Pallas kernels  74.2 us (65%)
  starting transfers between devices  19.1 us (17%)
  waiting for transfers between devices  12.2 us (11%)
  local copies, waits for them, and re-layouts  5.07 us (4%)
  other arithmetic  2.89 us (3%)
    pallas_call x1, Pallas kernels, on_device(): pl.pallas_call(functools.partial(pair_kernel, lanes), out_shape=[piece] *...  38.8 us
    pallas_call x1, Pallas kernels, on_device(): pl.pallas_call(own_kernel, out_shape=(jax.ShapeDtypeStruct((systems, 2, w...  33.8 us
    ppermute x6, starting transfers between devices, shift(): lax.ppermute(value, 'rhs', [(i, (i + by) % lanes) for i in range(lanes)])  8.05 us
    all_to_all x1, starting transfers between devices, on_device(): lax.all_to_all(tiles[:, :2][slot_of], 'panel', split_axis=0, concat_axis=...  7.41 us
    all_to_all x1, waiting for transfers between devices, on_device(): lax.all_to_all(tiles[:, :2][slot_of], 'panel', split_axis=0, concat_axis=...  7.04 us
    all_to_all x1, starting transfers between devices, on_device(): lax.all_to_all(low, ('panel', 'rhs'), split_axis=0, concat_axis=0, tiled=...  3.66 us
    all_to_all x1, waiting for transfers between devices, on_device(): lax.all_to_all(low, ('panel', 'rhs'), split_axis=0, concat_axis=0, tiled=...  3.19 us
  transfers between devices with their start and end apart: 8, of which 5 were waited for; matrix products, arithmetic and copies ran while one was open for 2% of the time, Pallas kernels for 30%

profile of v1, /device:TPU:0, one launch (start us, length us, event | category | flops | bytes accessed | tf_op | source)
XLA Modules:
  0.0 113.5 jit_solution(16068071777288443759)
XLA Ops:
  0.0 0.9 bitcast_select_fusion
  1.1 0.3 slice-done
  1.4 2.0 %gather_fusion = bf16[8,2,256,256]{3,2,1,0:T(8,128)(2,1)} fusion(bf16[6,2,256,256]{3,2,1,0:T(8,128)(2,1)S(1)} %slice-done, s32[1024]{0:T(1024)S(1)} %pad_clamp_fusion), kind=kCustom, calls=%fused_computation | custom fusion | bytes 4194336 | tf_op jit(solution)/shard_map/gather | solution.py:238
  3.5 7.4 %all-to-all-start = ((bf16[8,2,256,256]{3,2,1,0:T(8,128)(2,1)}), bf16[8,2,256,256]{3,2,1,0:T(8,128)(2,1)S(1)}, u32[]{:S(2)}, u32[]{:S(2)}) async-start(bf16[8,2,256,256]{3,2,1,0:T(8,128)(2,1)} %gather_fusion), calls=%async_computation | async-start | bytes 4194304 | tf_op jit(solution)/shard_map/all_to_all | solution.py:238
  10.9 0.6 dynamic_slice.23.counts_ref
  11.5 33.8 %shard_map.46 = (bf16[6,2,256,256]{3,2,1,0:T(8,128)(2,1)}, bf16[6,3,256,512]{3,2,1,0:T(8,128)(2,1)}) custom-call(s32[6]{0:T(128)} %dynamic_slice.23.counts_ref, bf16[6,5,256,256]{3,2,1,0:T(8,128)(2,1)} %tiles_ref.1), custom_call_target="tpu_custom_call" | custom-call | flops 40000000000 | bytes 8000000 | tf_op jit(solution)/shard_map/pallas_call | solution.py:243
  45.3 0.7 collective-permute-start.2
  46.0 2.7 %collective-permute-start.1 = (bf16[4,1536]{1,0:T(4,128)(2,1)S(1)}, bf16[4,1536]{1,0:T(4,128)(2,1)S(1)}, u32[]{:S(2)}, u32[]{:S(2)}) collective-permute-start(bf16[4,1536]{1,0:T(4,128)(2,1)S(1)} %get-tuple-element.25), channel_id=1, source_target_pairs={{0,2},{1,3},{2,0},{3,1},{4,6},{5,7},{6,4},{7,5},{8,10},{9,11},{10,... | collective-permute-start | bytes 36872 | tf_op jit(solution)/shard_map/ppermute | solution.py:236
  48.6 1.4 %collective-permute-start = (bf16[4,1536]{1,0:T(4,128)(2,1)S(1)}, bf16[4,1536]{1,0:T(4,128)(2,1)S(1)}, u32[]{:S(2)}, u32[]{:S(2)}) collective-permute-start(bf16[4,1536]{1,0:T(4,128)(2,1)S(1)} %get-tuple-element.26), channel_id=1, source_target_pairs={{0,3},{1,0},{2,1},{3,2},{4,7},{5,4},{6,5},{7,6},{8,11},{9,8},{10,9... | collective-permute-start | bytes 36872 | tf_op jit(solution)/shard_map/ppermute | solution.py:236
  50.0 0.6 pad_add_fusion.1.place_ref
  50.6 0.8 collective-permute-done
  51.4 0.7 pad_maximum_fusion.x_ref
  52.1 7.0 %all-to-all-done.got_ref = bf16[8,2,256,256]{3,2,1,0:T(8,128)(2,1)S(1)} async-done(((bf16[8,2,256,256]{3,2,1,0:T(8,128)(2,1)}), bf16[8,2,256,256]{3,2,1,0:T(8,128)(2,1)S(1)}, u32[]{:S(2)}, u32[]{:S(2)}) %all-to-all-start) | async-done | bytes 2097184 | tf_op jit(solution)/shard_map/all_to_all | solution.py:238
  59.1 1.4 %copy-done = bf16[8,2,256,256]{3,2,1,0:T(8,128)(2,1)} copy-done((bf16[8,2,256,256]{3,2,1,0:T(8,128)(2,1)}, bf16[8,2,256,256]{3,2,1,0:T(8,128)(2,1)S(1)}, u32[]{:S(2)}) %copy-start) | copy-done | bytes 2097176
  60.5 38.8 %shard_map.47 = (f32[6,4,256]{2,1,0:T(4,128)}, f32[6,4,256]{2,1,0:T(4,128)}, f32[6,4,256]{2,1,0:T(4,128)}, f32[6,4,256]{2,1,0:T(4,128)}, f32[32,4,256]{2,1,0:T(4,128)}) custom-call(s32[7]{0:T(128)} %pad_add_fusion.1.place_ref, bf16[6,2,256,256]{3,2,1,0:T(8,128)(2,1)} %get-tuple-element.15.w_ref, bf16[6,3,256,512]{3,2,1,0:T(8,128)(2,1)} %get-tuple-element.16.z_ref, ...), custom_call_target="tpu_custom_call" | custom-call | tf_op jit(solution)/shard_map/pallas_call | solution.py:264
  99.3 3.7 %all-to-all-start.1 = ((f32[32,4,256]{2,1,0:T(4,128)}), f32[32,4,256]{2,1,0:T(4,128)S(1)}, u32[]{:S(2)}, u32[]{:S(2)}) async-start(f32[32,4,256]{2,1,0:T(4,128)} %get-tuple-element.18), calls=%async_computation.1 | async-start | bytes 262144 | tf_op jit(solution)/shard_map/all_to_all | solution.py:279
  103.3 1.7 %collective-permute-start.4 = (f32[6,4,256]{2,1,0:T(4,128)}, f32[6,4,256]{2,1,0:T(4,128)S(1)}, u32[]{:S(2)}, u32[]{:S(2)}) collective-permute-start(f32[6,4,256]{2,1,0:T(4,128)} %get-tuple-element.21), channel_id=1, source_target_pairs={{0,2},{1,3},{2,0},{3,1},{4,6},{5,7},{6,4},{7,5},{8,10},{9,11},{10,... | collective-permute-start | bytes 73736 | tf_op jit(solution)/shard_map/ppermute | solution.py:236
  104.9 1.3 %collective-permute-start.5 = (f32[6,4,256]{2,1,0:T(4,128)}, f32[6,4,256]{2,1,0:T(4,128)S(1)}, u32[]{:S(2)}, u32[]{:S(2)}) collective-permute-start(f32[6,4,256]{2,1,0:T(4,128)} %get-tuple-element.22), channel_id=1, source_target_pairs={{0,3},{1,0},{2,1},{3,2},{4,7},{5,4},{6,5},{7,6},{8,11},{9,8},{10,9... | collective-permute-start | bytes 73736 | tf_op jit(solution)/shard_map/ppermute | solution.py:236
  106.3 0.7 pad_add_fusion.place_ref
  106.9 0.4 collective-permute-done.4.refs_2_
  107.3 0.7 collective-permute-done.5.refs_3_
  108.0 3.2 %all-to-all-done.1.low_ref = f32[32,4,256]{2,1,0:T(4,128)S(1)} async-done(((f32[32,4,256]{2,1,0:T(4,128)}), f32[32,4,256]{2,1,0:T(4,128)S(1)}, u32[]{:S(2)}, u32[]{:S(2)}) %all-to-all-start.1) | async-done | bytes 131104 | tf_op jit(solution)/shard_map/all_to_all | solution.py:279
  111.2 0.6 copy-done.1
  111.9 1.6 %shard_map.48 = bf16[4,6144]{1,0:T(4,128)(2,1)} custom-call(s32[25]{0:T(128)} %pad_add_fusion.place_ref, f32[32,4,256]{2,1,0:T(4,128)} %copy-done.1, f32[6,4,256]{2,1,0:T(4,128)} %get-tuple-element.19.refs_0_, f32[6,4,256]{2,1,0:T(4,128)} %copy-done.3, f32[6,4,256]{2,1,0:T(4,128)} %copy-done.4, f32[6,4,256]{2,1,0:T(4,128)} %copy-done.5), custom_call_target="tpu_custom_call" | custom-call | tf_op jit(solution)/shard_map/pallas_call | solution.py:281
  (22 shorter events, 0.6 us)
Async XLA Ops:
  0.0 1.4 %slice-start = ((bf16[6,5,256,256]{3,2,1,0:T(8,128)(2,1)}), bf16[6,2,256,256]{3,2,1,0:T(8,128)(2,1)S(1)}, s32[]{:S(2)}) async-start(bf16[6,5,256,256]{3,2,1,0:T(8,128)(2,1)} %tiles_ref.1), calls=%async_computation.2 | async-start | bytes 3145728 | tf_op jit(solution)/shard_map/slice | solution.py:238
  3.5 7.4 %copy-start.6 = (s32[192]{0:T(256)S(1)}, s32[192]{0:T(256)}, u32[]{:S(2)}) copy-start(s32[192]{0:T(256)} %param.6) | copy-start | bytes 2308
  3.5 55.7 %all-to-all-start = ((bf16[8,2,256,256]{3,2,1,0:T(8,128)(2,1)}), bf16[8,2,256,256]{3,2,1,0:T(8,128)(2,1)S(1)}, u32[]{:S(2)}, u32[]{:S(2)}) async-start(bf16[8,2,256,256]{3,2,1,0:T(8,128)(2,1)} %gather_fusion), calls=%async_computation | async-start | bytes 4194304 | tf_op jit(solution)/shard_map/all_to_all | solution.py:238
  11.5 33.8 %copy-start.2 = (bf16[4,6144]{1,0:T(4,128)(2,1)S(1)}, bf16[4,6144]{1,0:T(4,128)(2,1)}, u32[]{:S(2)}) copy-start(bf16[4,6144]{1,0:T(4,128)(2,1)} %param.7) | copy-start | bytes 147460
  45.3 5.3 %collective-permute-start.2 = (bf16[4,1536]{1,0:T(4,128)(2,1)S(1)}, bf16[4,1536]{1,0:T(4,128)(2,1)S(1)}, u32[]{:S(2)}, u32[]{:S(2)}) collective-permute-start(bf16[4,1536]{1,0:T(4,128)(2,1)S(1)} %get-tuple-element.24), channel_id=1, source_target_pairs={{0,1},{1,2},{2,3},{3,0},{4,5},{5,6},{6,7},{7,4},{8,9},{9,10},{10,1... | collective-permute-start | bytes 36872 | tf_op jit(solution)/shard_map/ppermute | solution.py:236
  46.0 4.6 %collective-permute-start.1 = (bf16[4,1536]{1,0:T(4,128)(2,1)S(1)}, bf16[4,1536]{1,0:T(4,128)(2,1)S(1)}, u32[]{:S(2)}, u32[]{:S(2)}) collective-permute-start(bf16[4,1536]{1,0:T(4,128)(2,1)S(1)} %get-tuple-element.25), channel_id=1, source_target_pairs={{0,2},{1,3},{2,0},{3,1},{4,6},{5,7},{6,4},{7,5},{8,10},{9,11},{10,... | collective-permute-start | bytes 36872 | tf_op jit(solution)/shard_map/ppermute | solution.py:236
  48.6 2.8 %collective-permute-start = (bf16[4,1536]{1,0:T(4,128)(2,1)S(1)}, bf16[4,1536]{1,0:T(4,128)(2,1)S(1)}, u32[]{:S(2)}, u32[]{:S(2)}) collective-permute-start(bf16[4,1536]{1,0:T(4,128)(2,1)S(1)} %get-tuple-element.26), channel_id=1, source_target_pairs={{0,3},{1,0},{2,1},{3,2},{4,7},{5,4},{6,5},{7,6},{8,11},{9,8},{10,9... | collective-permute-start | bytes 36872 | tf_op jit(solution)/shard_map/ppermute | solution.py:236
  59.1 1.4 %copy-start = (bf16[8,2,256,256]{3,2,1,0:T(8,128)(2,1)}, bf16[8,2,256,256]{3,2,1,0:T(8,128)(2,1)S(1)}, u32[]{:S(2)}) copy-start(bf16[8,2,256,256]{3,2,1,0:T(8,128)(2,1)S(1)} %all-to-all-done.got_ref) | copy-start | bytes 6291460
  99.3 11.9 %all-to-all-start.1 = ((f32[32,4,256]{2,1,0:T(4,128)}), f32[32,4,256]{2,1,0:T(4,128)S(1)}, u32[]{:S(2)}, u32[]{:S(2)}) async-start(f32[32,4,256]{2,1,0:T(4,128)} %get-tuple-element.18), calls=%async_computation.1 | async-start | bytes 262144 | tf_op jit(solution)/shard_map/all_to_all | solution.py:279
  103.0 4.0 %collective-permute-start.3 = (f32[6,4,256]{2,1,0:T(4,128)}, f32[6,4,256]{2,1,0:T(4,128)S(1)}, u32[]{:S(2)}, u32[]{:S(2)}) collective-permute-start(f32[6,4,256]{2,1,0:T(4,128)} %get-tuple-element.20), channel_id=1, source_target_pairs={{0,1},{1,2},{2,3},{3,0},{4,5},{5,6},{6,7},{7,4},{8,9},{9,10},{10,1... | collective-permute-start | bytes 73736 | tf_op jit(solution)/shard_map/ppermute | solution.py:236
  103.3 4.1 %collective-permute-start.4 = (f32[6,4,256]{2,1,0:T(4,128)}, f32[6,4,256]{2,1,0:T(4,128)S(1)}, u32[]{:S(2)}, u32[]{:S(2)}) collective-permute-start(f32[6,4,256]{2,1,0:T(4,128)} %get-tuple-element.21), channel_id=1, source_target_pairs={{0,2},{1,3},{2,0},{3,1},{4,6},{5,7},{6,4},{7,5},{8,10},{9,11},{10,... | collective-permute-start | bytes 73736 | tf_op jit(solution)/shard_map/ppermute | solution.py:236
  104.9 3.1 %collective-permute-start.5 = (f32[6,4,256]{2,1,0:T(4,128)}, f32[6,4,256]{2,1,0:T(4,128)S(1)}, u32[]{:S(2)}, u32[]{:S(2)}) collective-permute-start(f32[6,4,256]{2,1,0:T(4,128)} %get-tuple-element.22), channel_id=1, source_target_pairs={{0,3},{1,0},{2,1},{3,2},{4,7},{5,4},{6,5},{7,6},{8,11},{9,8},{10,9... | collective-permute-start | bytes 73736 | tf_op jit(solution)/shard_map/ppermute | solution.py:236
  106.9 4.3 %copy-start.3 = (f32[6,4,256]{2,1,0:T(4,128)}, f32[6,4,256]{2,1,0:T(4,128)S(1)}, u32[]{:S(2)}) copy-start(f32[6,4,256]{2,1,0:T(4,128)S(1)} %collective-permute-done.3.refs_1_) | copy-start | bytes 73732
  107.3 3.9 %copy-start.4 = (f32[6,4,256]{2,1,0:T(4,128)}, f32[6,4,256]{2,1,0:T(4,128)S(1)}, u32[]{:S(2)}) copy-start(f32[6,4,256]{2,1,0:T(4,128)S(1)} %collective-permute-done.4.refs_2_) | copy-start | bytes 73732
  108.0 3.2 %copy-start.5 = (f32[6,4,256]{2,1,0:T(4,128)}, f32[6,4,256]{2,1,0:T(4,128)S(1)}, u32[]{:S(2)}) copy-start(f32[6,4,256]{2,1,0:T(4,128)S(1)} %collective-permute-done.5.refs_3_) | copy-start | bytes 73732
  111.2 0.7 copy-start.1

commit v2 on v1

--- a/solution.py
+++ b/solution.py
@@ -7,6 +7,7 @@
 from jax.sharding import PartitionSpec as P
 
 STEP = 32
+PIVOTS = 4
 NT = (((1,), (1,)), ((), ()))
 NN = (((1,), (0,)), ((), ()))
 TN = (((0,), (0,)), ((), ()))
@@ -29,6 +30,10 @@
     b1, b2, b3 = b
     small = dot(a1, b3, dims) + dot(a3, b1, dims) + dot(a2, b2, dims)
     return dot(a1, b1, dims) + ((dot(a1, b2, dims) + dot(a2, b1, dims)) + small)
+
+
+def dot3(a, b, dims):
+    return dot(a[0], b[0], dims) + (dot(a[0], b[1], dims) + dot(a[1], b[0], dims))
 
 
 def apply(rows, parts, dims):
@@ -54,45 +59,35 @@
         return jnp.broadcast_to(row, (8, 128))
 
     def pivots(slabs):
-        for first in range(0, STEP, 4):
-            top, at = first // 8, first % 8
+        for first in range(0, STEP, PIVOTS):
+            top, start = first // 8, first % 8
             tall = range(top, groups)
-            own = (lane >= first) & (lane < first + 4)
+            own = (lane >= first) & (lane < first + PIVOTS)
             one = jnp.where(lane - 8 * top == sub, 1.0, 0.0)
-            if at == 0:
+            if start == 0:
                 inverses = [None] * len(slabs)
-            columns, rows = [], []
+            columns = []
             for x in slabs:
-                columns.append([{g: spread(x[g][0][:, first + q:first + q + 1]) for g in tall} for q in range(4)])
+                columns.append([{g: spread(x[g][0][:, first + q:first + q + 1]) for g in tall} for q in range(PIVOTS)])
                 for g in tall:
                     x[g][0] = jnp.where(own, one if g == top else 0.0, x[g][0])
-                rows.append([[spread(x[top][h][at + q:at + q + 1, :]) for h in range(halves)] for q in range(4)])
-            for s, x in enumerate(slabs):
-                u = columns[s]
-                a = {(i, j): spread(u[j][top][at + i:at + i + 1, :]) for j in range(4) for i in range(j + 1)}
-                low, inv = {}, []
-                for i in range(4):
-                    for j in range(i, 4):
-                        for k in range(i):
-                            a[i, j] = a[i, j] - low[i, k] * a[k, j]
-                    inv.append(pl.reciprocal(a[i, i], approx=True))
-                    for j in range(i + 1, 4):
-                        low[j, i] = a[i, j] * inv[i]
-                for i in range(4):
-                    for k in range(i):
+            for q in range(PIVOTS):
+                at = start + q
+                for s, x in enumerate(slabs):
+                    cols = columns[s]
+                    inverse = pl.reciprocal(spread(cols[q][top][at:at + 1, :]), approx=True)
+                    inverses[s] = inverse if at == 0 else jnp.where(sub >= at, inverse, inverses[s])
+                    c = {g: cols[q][g] * inverse for g in tall}
+                    for later in range(q + 1, PIVOTS):
+                        m = spread(cols[q][top][start + later:start + later + 1, :])
                         for g in tall:
-                            u[i][g] = u[i][g] - u[k][g] * low[i, k]
-                        for h in range(halves):
-                            rows[s][i][h] = rows[s][i][h] - rows[s][k][h] * low[i, k]
-                for i in range(4):
-                    for g in tall:
-                        m = u[i][g] * inv[i]
-                        if g == top:
-                            m = jnp.where(sub > at + i, m, 0.0)
-                        for h in range(halves):
-                            x[g][h] = x[g][h] - m * rows[s][i][h]
-                    inverses[s] = inv[i] if at + i == 0 else jnp.where(sub >= at + i, inv[i], inverses[s])
-            if at == 4:
+                            cols[later][g] = cols[later][g] - c[g] * m
+                    c[top] = jnp.where(sub > at, c[top], 0.0)
+                    for h in range(halves):
+                        r = spread(x[top][h][at:at + 1, :])
+                        for g in tall:
+                            x[g][h] = x[g][h] - c[g] * r
+            if start + PIVOTS == 8:
                 for s, x in enumerate(slabs):
                     scale = inverses[s] * lax.rsqrt(inverses[s])
                     for h in range(halves):
@@ -168,41 +163,80 @@
         z_ref[s, 2] = z3
 
 
-def pair_kernel(lanes, place_ref, w_ref, z_ref, x_ref, got_ref, *refs):
-    up_refs, refs = refs[:lanes], refs[lanes:]
-    low_ref, near_ref, t_ref, v_ref, r_ref, first_ref, sems, *scratch = refs
+def mid_kernel(place_ref, w_ref, z_ref, x_ref, got_ref, q_ref, back_ref, first_ref, near_ref, t_ref, v_ref, r_ref, sems, *scratch):
     systems, _, width, _ = z_ref.shape
-    count = x_ref.shape[0] // lanes
+    part = near_ref.shape[3]
     copies = [pltpu.make_async_copy(got_ref.at[place_ref[s]], near_ref.at[s], sems.at[s]) for s in range(systems)]
     for copy in copies:
         copy.start()
+    for s in range(systems):
+        copies[s].wait()
+        near = near_ref[s].reshape(2 * width, part)
+        v = split3(dot(z_ref[s, 0], near, NN) + (dot(z_ref[s, 1], near, NN) + dot(z_ref[s, 2], near, NN)))
+        vt = [one.T for one in v]
+        for i in range(3):
+            v_ref[s, i] = vt[i]
+        t_ref[s] = dot(near.T, near, NN) - dot6(vt, v, NN)
+        x = x_ref[:, s * width:(s + 1) * width]
+        first = dot(x, z_ref[s, 0, :, width:], NT) + dot(x, z_ref[s, 1, :, width:], NT)
+        first_ref[s, :, :width] = first
+        r_ref[s] = dot(x, near[width:], NN) - apply(first, v, NN)
+    factor(t_ref, *scratch)
+    for s in range(systems):
+        near_t = near_ref[s].reshape(2 * width, part).T
+        own = split3(t_ref[s])
+        vt = [v_ref[s, i] for i in range(3)]
+        first_ref[s, :, width:] = apply(r_ref[s], own, NT)
+        rest = near_t.astype(jnp.float32) - dot6(vt, [z_ref[s, i] for i in range(3)], NN)
+        q = split3(dot6(own, split3(rest), NN))
+        for i in range(3):
+            q_ref[s, i] = q[i]
+        left = split3(-dot3(own, split3(dot3(vt, (w_ref[s, 0], w_ref[s, 1]), NN)), NN))
+        for i in range(2):
+            back_ref[s, i, :, :width] = left[i]
+            back_ref[s, i, :, width:] = own[i]
+
+
+def last_kernel(lanes, place_ref, w_ref, back_ref, first_ref, x_ref, got_ref, z_any, q_any, *refs):
+    up_refs, refs = refs[:lanes], refs[lanes:]
+    low_ref, near_ref, z_ref, q_ref, t_ref, v_ref, r_ref, sems, *scratch = refs
+    systems, _, width, _ = z_ref.shape
+    part = near_ref.shape[3]
+    count = x_ref.shape[0] // lanes
+    copies = []
+    for s in range(systems):
+        pairs = ((got_ref.at[place_ref[s]], near_ref.at[s]), (z_any.at[s], z_ref.at[s]), (q_any.at[s], q_ref.at[s]))
+        copies.append([pltpu.make_async_copy(a, b, sems.at[s, i]) for i, (a, b) in enumerate(pairs)])
+        for copy in copies[s]:
+            copy.start()
     low_ref[...] = jnp.zeros(low_ref.shape, low_ref.dtype)
     for s in range(systems):
-        copies[s].wait()
-        near = near_ref[s].reshape(2 * width, width)
-        near_t = near.T
-        z1, z2, z3 = z_ref[s, 0], z_ref[s, 1], z_ref[s, 2]
-        v = split3(dot(near_t, z1, NT) + (dot(near_t, z2, NT) + dot(near_t, z3, NT)))
+        for copy in copies[s]:
+            copy.wait()
+        near = near_ref[s].reshape(2 * width, part)
+        upper = dot(z_ref[s, 0], near, NN) + (dot(z_ref[s, 1], near, NN) + dot(z_ref[s, 2], near, NN))
+        lower = dot(q_ref[s, 0], near, NN) + (dot(q_ref[s, 1], near, NN) + dot(q_ref[s, 2], near, NN))
+        v = split3(jnp.concatenate([upper, lower], axis=0))
+        vt = [one.T for one in v]
         v_ref[s, 0] = v[0]
         v_ref[s, 1] = v[1]
-        t_ref[s] = dot(near_t, near, NN) - dot6(v, v, NT)
+        t_ref[s] = dot(near.T, near, NN) - dot6(vt, v, NN)
     for s in range(systems):
         x = x_ref[:, s * width:(s + 1) * width]
-        first_ref[s] = dot(x, z_ref[s, 0, :, width:], NT) + dot(x, z_ref[s, 1, :, width:], NT)
-        r_ref[s] = dot(x, near_ref[s, 1], NN)
-    for s in range(systems):
-        r_ref[s] = r_ref[s] - apply(first_ref[s], (v_ref[s, 0], v_ref[s, 1]), NT)
+        r_ref[s] = dot(x, near_ref[s, 1], NN) - apply(first_ref[s], (v_ref[s, 0], v_ref[s, 1]), NN)
     factor(t_ref, *scratch)
     parts = [split3(t_ref[s])[:2] for s in range(systems)]
     half = [apply(r_ref[s], parts[s], NT) for s in range(systems)]
     last = [apply(half[s], parts[s], NN) for s in range(systems)]
-    mid = [first_ref[s] - apply(last[s], (v_ref[s, 0], v_ref[s, 1]), NN) for s in range(systems)]
-    for s in range(systems):
-        up = apply(mid[s], (w_ref[s, 0], w_ref[s, 1]), NN)
+    mid = [first_ref[s] - apply(last[s], (v_ref[s, 0], v_ref[s, 1]), NT) for s in range(systems)]
+    for s in range(systems):
+        both = apply(mid[s][:, width:], (back_ref[s, 0], back_ref[s, 1]), NN)
+        up = apply(mid[s][:, :width], (w_ref[s, 0], w_ref[s, 1]), NN) + both[:, :width]
+        low = jnp.concatenate([both[:, width:], last[s]], axis=1)
         for e in range(lanes):
             up_refs[e][s] = up[e * count:(e + 1) * count]
             owner = lax.rem(place_ref[systems] + e, lanes)
-            low_ref[place_ref[s] * lanes + owner] = last[s][e * count:(e + 1) * count]
+            low_ref[place_ref[s] * lanes + owner] = low[e * count:(e + 1) * count]
 
 
 def place_kernel(lanes, place_ref, low_ref, *refs):
@@ -235,11 +269,17 @@
     def shift(value, by):
         return lax.ppermute(value, "rhs", [(i, (i + by) % lanes) for i in range(lanes)])
 
-    received = lax.all_to_all(tiles[:, :2][slot_of], "panel", split_axis=0, concat_axis=0, tiled=True)
+    def exchange(source, at, size):
+        block = source[:, :2, :, at:at + size][slot_of]
+        return lax.all_to_all(block, "panel", split_axis=0, concat_axis=0, tiled=True)
+
+    part = width // 2
+    got_one = exchange(tiles, 0, part)
 
     vmem = pl.BlockSpec(memory_space=pltpu.VMEM)
     smem = pl.BlockSpec(memory_space=pltpu.SMEM)
-    params = pltpu.CompilerParams(vmem_limit_bytes=56 * 1024 * 1024)
+    anywhere = pl.BlockSpec(memory_space=pl.ANY)
+    params = pltpu.CompilerParams(vmem_limit_bytes=28 * 1024 * 1024)
     w, z = pl.pallas_call(
         own_kernel,
         out_shape=(
@@ -250,32 +290,57 @@
         out_specs=(vmem, vmem),
         scratch_shapes=[pltpu.VMEM((systems, width, width), jnp.float32)] + factor_scratch(systems, width),
         compiler_params=params,
-        cost_estimate=pl.CostEstimate(flops=40 * 10**9, bytes_accessed=8 * 10**6, transcendentals=0),
+        cost_estimate=pl.CostEstimate(flops=20 * 10**9, bytes_accessed=8 * 10**6, transcendentals=0),
     )(own_cnt, tiles)
 
-    inputs, w = lax.optimization_barrier((inputs, w))
+    later, inputs, w = lax.optimization_barrier((tiles, inputs, w))
+    got_two = exchange(later, part, width - part)
     parts = [lax.dynamic_slice_in_dim(inputs, my_lane * own_width, own_width, 1)]
     for e in range(1, lanes):
-        part = lax.dynamic_slice_in_dim(inputs, (my_lane + lanes - e) % lanes * own_width, own_width, 1)
-        parts.append(shift(part, -e))
+        part_e = lax.dynamic_slice_in_dim(inputs, (my_lane + lanes - e) % lanes * own_width, own_width, 1)
+        parts.append(shift(part_e, -e))
     x = jnp.concatenate(parts, axis=0)
-
+    nrhs = lanes * nrhs_dev
+    place = jnp.concatenate([mate_panel, lane_word])
+
+    q, back, first = pl.pallas_call(
+        mid_kernel,
+        out_shape=(
+            jax.ShapeDtypeStruct((systems, 3, part, 2 * width), jnp.bfloat16),
+            jax.ShapeDtypeStruct((systems, 2, part, width + part), jnp.bfloat16),
+            jax.ShapeDtypeStruct((systems, nrhs, width + part), jnp.float32),
+        ),
+        in_specs=[smem, vmem, vmem, vmem, anywhere],
+        out_specs=(vmem, vmem, vmem),
+        scratch_shapes=[
+            pltpu.VMEM((systems, 2, width, part), jnp.bfloat16),
+            pltpu.VMEM((systems, part, part), jnp.float32),
+            pltpu.VMEM((systems, 3, part, width), jnp.bfloat16),
+            pltpu.VMEM((systems, nrhs, part), jnp.float32),
+            pltpu.SemaphoreType.DMA((systems,)),
+        ] + factor_scratch(systems, part),
+        compiler_params=params,
+        cost_estimate=pl.CostEstimate(flops=15 * 10**9, bytes_accessed=8 * 10**6, transcendentals=0),
+    )(place, w, z, x, got_one)
+
+    rest = width - part
     piece = jax.ShapeDtypeStruct((systems, nrhs_dev, width), jnp.float32)
     *up, low = pl.pallas_call(
-        functools.partial(pair_kernel, lanes),
+        functools.partial(last_kernel, lanes),
         out_shape=[piece] * lanes + [jax.ShapeDtypeStruct((shards * lanes, nrhs_dev, width), jnp.float32)],
-        in_specs=[smem, vmem, vmem, vmem, pl.BlockSpec(memory_space=pl.ANY)],
+        in_specs=[smem, vmem, vmem, vmem, vmem, anywhere, anywhere, anywhere],
         out_specs=[vmem] * (lanes + 1),
         scratch_shapes=[
-            pltpu.VMEM((systems, 2, width, width), jnp.bfloat16),
-            pltpu.VMEM((systems, width, width), jnp.float32),
-            pltpu.VMEM((systems, 2, width, width), jnp.bfloat16),
-            pltpu.VMEM((systems, lanes * nrhs_dev, width), jnp.float32),
-            pltpu.VMEM((systems, lanes * nrhs_dev, width), jnp.float32),
-            pltpu.SemaphoreType.DMA((systems,)),
-        ] + factor_scratch(systems, width),
+            pltpu.VMEM((systems, 2, width, rest), jnp.bfloat16),
+            pltpu.VMEM((systems, 3, width, 2 * width), jnp.bfloat16),
+            pltpu.VMEM((systems, 3, part, 2 * width), jnp.bfloat16),
+            pltpu.VMEM((systems, rest, rest), jnp.float32),
+            pltpu.VMEM((systems, 2, width + part, rest), jnp.bfloat16),
+            pltpu.VMEM((systems, nrhs, rest), jnp.float32),
+            pltpu.SemaphoreType.DMA((systems, 3)),
+        ] + factor_scratch(systems, rest),
         compiler_params=params,
-    )(jnp.concatenate([mate_panel, lane_word]), w, z, x, received)
+    )(place, w, back, first, x, got_two, z, q)
     low = lax.all_to_all(low, ("panel", "rhs"), split_axis=0, concat_axis=0, tiled=True)
     up = [up[0]] + [shift(up[e], e) for e in range(1, lanes)]
     return pl.pallas_call(

time: 114 us -> 129 us (1.13)
  local copies, waits for them, and re-layouts: 5.07 us -> 25.8 us
  starting transfers between devices: 19.1 us -> 26.5 us
  Pallas kernels: 74.2 us -> 67.9 us
  waiting for transfers between devices: 12.2 us -> 6.2 us
    unnamed x14 -> x42, local copies, waits for them, and re-layouts: 2.03 us -> 20.9 us
    all_to_all x1 -> x2, starting transfers between devices: 7.41 us -> 15.2 us  [exchange(): lax.all_to_all(block, 'panel', split_axis=0, concat_axis=0, tiled=True)]
    pallas_call x1, Pallas kernels: 33.8 us -> 26.6 us  [on_device(): pl.pallas_call(own_kernel, out_shape=(jax.ShapeDtypeStruct((systems, 2, w...]
    all_to_all x1 -> x2, waiting for transfers between devices: 7.04 us -> 0.01 us  [exchange(): lax.all_to_all(block, 'panel', split_axis=0, concat_axis=0, tiled=True)]
    ppermute x6, starting transfers between devices: 8.05 us -> 5.11 us  [shift(): lax.ppermute(value, 'rhs', [(i, (i + by) % lanes) for i in range(lanes)])]
    all_to_all x1, starting transfers between devices: 3.66 us -> 6.18 us  [on_device(): lax.all_to_all(low, ('panel', 'rhs'), split_axis=0, concat_axis=0, tiled=...]
    gather x1 -> x2, local copies, waits for them, and re-layouts: 2.04 us -> 3.4 us  [exchange(): block = source[:, :2, :, at:at + size][slot_of]]
    pallas_call x1 -> x2, Pallas kernels: 38.8 us -> 39.7 us  [the longest x1 20.5 us: on_device(): pl.pallas_call(mid_kernel, out_shape=(jax.ShapeDtypeStruct((systems, 3, p...]
  transfers between devices with their start and end apart: 8 -> 9, of which waited for: 5 -> 5; matrix products, arithmetic and copies ran while one was open for 2% -> 2% of each run, Pallas kernels for 30% -> 37%
where the time goes in v2:
time: 129 us; the launch traced here: 128 us
  Pallas kernels  67.9 us (53%)
  starting transfers between devices  26.5 us (21%)
  local copies, waits for them, and re-layouts  25.8 us (20%)
  waiting for transfers between devices  6.2 us (5%)
  other arithmetic  1.67 us (1%)
    pallas_call x1, Pallas kernels, on_device(): pl.pallas_call(own_kernel, out_shape=(jax.ShapeDtypeStruct((systems, 2, w...  26.6 us
    unnamed x42, local copies, waits for them, and re-layouts  20.9 us
    pallas_call x1, Pallas kernels, on_device(): pl.pallas_call(mid_kernel, out_shape=(jax.ShapeDtypeStruct((systems, 3, p...  20.5 us
    pallas_call x1, Pallas kernels, on_device(): pl.pallas_call(functools.partial(last_kernel, lanes), out_shape=[piece] *...  19.2 us
    all_to_all x2, starting transfers between devices, exchange(): lax.all_to_all(block, 'panel', split_axis=0, concat_axis=0, tiled=True)  15.2 us
    all_to_all x1, starting transfers between devices, on_device(): lax.all_to_all(low, ('panel', 'rhs'), split_axis=0, concat_axis=0, tiled=...  6.18 us
    ppermute x6, starting transfers between devices, shift(): lax.ppermute(value, 'rhs', [(i, (i + by) % lanes) for i in range(lanes)])  5.11 us
    all_to_all x1, waiting for transfers between devices, on_device(): lax.all_to_all(low, ('panel', 'rhs'), split_axis=0, concat_axis=0, tiled=...  3.41 us
  transfers between devices with their start and end apart: 9, of which 5 were waited for; matrix products, arithmetic and copies ran while one was open for 2% of the time, Pallas kernels for 37%

profile of v2, /device:TPU:0, one launch (start us, length us, event | category | flops | bytes accessed | tf_op | source)
XLA Modules:
  0.0 128.2 jit_solution(11694434627900135733)
XLA Ops:
  1.0 1.2 slice.6
  2.2 1.6 %gather_fusion = bf16[8,2,256,128]{3,2,1,0:T(8,128)(2,1)} fusion(bf16[6,2,256,128]{3,2,1,0:T(8,128)(2,1)S(1)} %slice.6, s32[1024]{0:T(1024)S(1)} %pad_clamp_fusion), kind=kCustom, calls=%fused_computation | custom fusion | bytes 2097184 | tf_op jit(solution)/shard_map/gather | solution.py:273
  3.8 7.3 %all-to-all-start = ((bf16[8,2,256,128]{3,2,1,0:T(8,128)(2,1)}), bf16[8,2,256,128]{3,2,1,0:T(8,128)(2,1)S(1)}, u32[]{:S(2)}, u32[]{:S(2)}) async-start(bf16[8,2,256,128]{3,2,1,0:T(8,128)(2,1)} %gather_fusion), calls=%async_computation | async-start | bytes 2097152 | tf_op jit(solution)/shard_map/all_to_all | solution.py:274
  11.2 2.1 %copy-done.10 = bf16[6,5,256,256]{3,2,1,0:T(8,128)(2,1)S(1)} copy-done((bf16[6,5,256,256]{3,2,1,0:T(8,128)(2,1)S(1)}, bf16[6,5,256,256]{3,2,1,0:T(8,128)(2,1)}, u32[]{:S(2)}) %copy-start.10) | copy-done | bytes 3932184
  13.3 26.6 %shard_map.46 = (bf16[6,2,256,256]{3,2,1,0:T(8,128)(2,1)S(1)}, bf16[6,3,256,512]{3,2,1,0:T(8,128)(2,1)S(1)}) custom-call(s32[6]{0:T(128)S(1)} %dynamic_slice.23.counts_ref, bf16[6,5,256,256]{3,2,1,0:T(8,128)(2,1)S(1)} %copy-done.10), custom_call_target="tpu_custom_call" | custom-call | flops 20000000000 | bytes 8000000 | tf_op jit(solution)/shard_map/pallas_call | solution.py:283
  39.9 2.1 %copy-done = bf16[6,3,256,512]{3,2,1,0:T(8,128)(2,1)} copy-done((bf16[6,3,256,512]{3,2,1,0:T(8,128)(2,1)}, bf16[6,3,256,512]{3,2,1,0:T(8,128)(2,1)S(1)}, u32[]{:S(2)}) %copy-start) | copy-done | bytes 4718616
  42.0 1.2 copy-done.3
  43.4 1.8 %gather_fusion.1 = bf16[8,2,256,128]{3,2,1,0:T(8,128)(2,1)} fusion(bf16[6,2,256,128]{3,2,1,0:T(8,128)(2,1)S(1)} %slice.7, s32[1024]{0:T(1024)S(1)} %pad_clamp_fusion), kind=kCustom, calls=%fused_computation.1 | custom fusion | bytes 2097184 | tf_op jit(solution)/shard_map/gather | solution.py:273
  46.1 8.0 %all-to-all-start.1 = ((bf16[8,2,256,128]{3,2,1,0:T(8,128)(2,1)}), bf16[8,2,256,128]{3,2,1,0:T(8,128)(2,1)S(1)}, u32[]{:S(2)}, u32[]{:S(2)}) async-start(bf16[8,2,256,128]{3,2,1,0:T(8,128)(2,1)} %gather_fusion.1), calls=%async_computation.1 | async-start | bytes 2097152 | tf_op jit(solution)/shard_map/all_to_all | solution.py:274
  54.3 1.7 %collective-permute-start = (bf16[4,1536]{1,0:T(4,128)(2,1)S(1)}, bf16[4,1536]{1,0:T(4,128)(2,1)S(1)}, u32[]{:S(2)}, u32[]{:S(2)}) collective-permute-start(bf16[4,1536]{1,0:T(4,128)(2,1)S(1)} %get-tuple-element.34), channel_id=1, source_target_pairs={{0,3},{1,0},{2,1},{3,2},{4,7},{5,4},{6,5},{7,6},{8,11},{9,8},{10,9... | collective-permute-start | bytes 36872 | tf_op jit(solution)/shard_map/ppermute | solution.py:270
  56.0 1.3 collective-permute-done.2
  58.0 2.3 %copy-done.1 = bf16[6,3,256,512]{3,2,1,0:T(8,128)(2,1)S(1)} copy-done((bf16[6,3,256,512]{3,2,1,0:T(8,128)(2,1)S(1)}, bf16[6,3,256,512]{3,2,1,0:T(8,128)(2,1)}, u32[]{:S(2)}) %copy-start.1) | copy-done | bytes 4718616
  60.3 1.4 %copy-done.4 = bf16[6,2,256,256]{3,2,1,0:T(8,128)(2,1)S(1)} copy-done((bf16[6,2,256,256]{3,2,1,0:T(8,128)(2,1)S(1)}, bf16[6,2,256,256]{3,2,1,0:T(8,128)(2,1)}, u32[]{:S(2)}) %copy-start.4) | copy-done | bytes 1572888
  61.7 1.2 copy-done.9
  62.9 20.5 %shard_map.47 = (bf16[6,3,128,512]{3,2,1,0:T(8,128)(2,1)S(1)}, bf16[6,2,128,384]{3,2,1,0:T(8,128)(2,1)S(1)}, f32[6,16,384]{2,1,0:T(8,128)S(1)}) custom-call(s32[7]{0:T(128)S(1)} %pad_add_fusion.1.place_ref, bf16[6,2,256,256]{3,2,1,0:T(8,128)(2,1)S(1)} %copy-done.4, bf16[6,3,256,512]{3,2,1,0:T(8,128)(2,1)S(1)} %copy-done.1, ...), custom_call_target="tpu_custom_call" | custom-call | flops 15000000512 | bytes 8000000 | tf_op jit(solution)/shard_map/pallas_call | solution.py:306
  85.1 2.3 %copy-done.2 = bf16[6,3,256,512]{3,2,1,0:T(8,128)(2,1)S(1)} copy-done((bf16[6,3,256,512]{3,2,1,0:T(8,128)(2,1)S(1)}, bf16[6,3,256,512]{3,2,1,0:T(8,128)(2,1)}, u32[]{:S(2)}) %copy-start.2) | copy-done | bytes 4718616
  87.5 1.4 %copy-done.5 = bf16[6,2,256,256]{3,2,1,0:T(8,128)(2,1)S(1)} copy-done((bf16[6,2,256,256]{3,2,1,0:T(8,128)(2,1)S(1)}, bf16[6,2,256,256]{3,2,1,0:T(8,128)(2,1)}, u32[]{:S(2)}) %copy-start.5) | copy-done | bytes 1572888
  88.9 1.3 copy-done.7
  91.1 19.2 %shard_map.48 = (f32[6,4,256]{2,1,0:T(4,128)S(1)}, f32[6,4,256]{2,1,0:T(4,128)S(1)}, f32[6,4,256]{2,1,0:T(4,128)S(1)}, f32[6,4,256]{2,1,0:T(4,128)S(1)}, f32[32,4,256]{2,1,0:T(4,128)S(1)}) custom-call(s32[7]{0:T(128)S(1)} %pad_add_fusion.1.place_ref, bf16[6,2,256,256]{3,2,1,0:T(8,128)(2,1)S(1)} %copy-done.5, bf16[6,2,128,384]{3,2,1,0:T(8,128)(2,1)S(1)} %copy-done.7, ...), custom_call_target="tpu_custom_call" | custom-call | tf_op jit(solution)/shard_map/pallas_call | solution.py:328
  111.5 6.2 %all-to-all-start.2 = ((f32[32,4,256]{2,1,0:T(4,128)}), f32[32,4,256]{2,1,0:T(4,128)S(1)}, u32[]{:S(2)}, u32[]{:S(2)}) async-start(f32[32,4,256]{2,1,0:T(4,128)} %copy-done.13), calls=%async_computation.2 | async-start | bytes 262144 | tf_op jit(solution)/shard_map/all_to_all | solution.py:344
  118.0 1.7 %collective-permute-start.4 = (f32[6,4,256]{2,1,0:T(4,128)S(1)}, f32[6,4,256]{2,1,0:T(4,128)S(1)}, u32[]{:S(2)}, u32[]{:S(2)}) collective-permute-start(f32[6,4,256]{2,1,0:T(4,128)S(1)} %get-tuple-element.29), channel_id=1, source_target_pairs={{0,2},{1,3},{2,0},{3,1},{4,6},{5,7},{6,4},{7,5},{8,10},{9,11},{10,... | collective-permute-start | bytes 73736 | tf_op jit(solution)/shard_map/ppermute | solution.py:270
  119.6 1.3 %collective-permute-start.5 = (f32[6,4,256]{2,1,0:T(4,128)S(1)}, f32[6,4,256]{2,1,0:T(4,128)S(1)}, u32[]{:S(2)}, u32[]{:S(2)}) collective-permute-start(f32[6,4,256]{2,1,0:T(4,128)S(1)} %get-tuple-element.30), channel_id=1, source_target_pairs={{0,3},{1,0},{2,1},{3,2},{4,7},{5,4},{6,5},{7,6},{8,11},{9,8},{10,9... | collective-permute-start | bytes 73736 | tf_op jit(solution)/shard_map/ppermute | solution.py:270
  122.5 3.4 %all-to-all-done.2.low_ref = f32[32,4,256]{2,1,0:T(4,128)S(1)} async-done(((f32[32,4,256]{2,1,0:T(4,128)}), f32[32,4,256]{2,1,0:T(4,128)S(1)}, u32[]{:S(2)}, u32[]{:S(2)}) %all-to-all-start.2) | async-done | bytes 131104 | tf_op jit(solution)/shard_map/all_to_all | solution.py:344
  126.6 1.6 %shard_map.49 = bf16[4,6144]{1,0:T(4,128)(2,1)} custom-call(s32[25]{0:T(128)} %pad_add_fusion.place_ref, f32[32,4,256]{2,1,0:T(4,128)} %copy-done.15, f32[6,4,256]{2,1,0:T(4,128)} %copy-done.14, f32[6,4,256]{2,1,0:T(4,128)} %copy-done.17, f32[6,4,256]{2,1,0:T(4,128)} %copy-done.18, f32[6,4,256]{2,1,0:T(4,128)} %copy-done.19), custom_call_target="tpu_custom_call" | custom-call | tf_op jit(solution)/shard_map/pallas_call | solution.py:346
  (54 shorter events, 9.4 us)
Async XLA Ops:
  2.2 8.9 %copy-start.20 = (s32[192]{0:T(256)S(1)}, s32[192]{0:T(256)}, u32[]{:S(2)}) copy-start(s32[192]{0:T(256)} %param.6) | copy-start | bytes 2308
  3.8 41.3 %all-to-all-start = ((bf16[8,2,256,128]{3,2,1,0:T(8,128)(2,1)}), bf16[8,2,256,128]{3,2,1,0:T(8,128)(2,1)S(1)}, u32[]{:S(2)}, u32[]{:S(2)}) async-start(bf16[8,2,256,128]{3,2,1,0:T(8,128)(2,1)} %gather_fusion), calls=%async_computation | async-start | bytes 2097152 | tf_op jit(solution)/shard_map/all_to_all | solution.py:274
  11.2 2.1 %copy-start.10 = (bf16[6,5,256,256]{3,2,1,0:T(8,128)(2,1)S(1)}, bf16[6,5,256,256]{3,2,1,0:T(8,128)(2,1)}, u32[]{:S(2)}) copy-start(bf16[6,5,256,256]{3,2,1,0:T(8,128)(2,1)} %tiles_ref.1) | copy-start | bytes 11796484
  39.9 2.1 %copy-start = (bf16[6,3,256,512]{3,2,1,0:T(8,128)(2,1)}, bf16[6,3,256,512]{3,2,1,0:T(8,128)(2,1)S(1)}, u32[]{:S(2)}) copy-start(bf16[6,3,256,512]{3,2,1,0:T(8,128)(2,1)S(1)} %get-tuple-element.20.z_ref.z_any) | copy-start | bytes 14155780
  42.0 1.2 copy-start.3
  43.4 10.7 %copy-start.16 = (bf16[4,6144]{1,0:T(4,128)(2,1)S(1)}, bf16[4,6144]{1,0:T(4,128)(2,1)}, u32[]{:S(2)}) copy-start(bf16[4,6144]{1,0:T(4,128)(2,1)} %param.7) | copy-start | bytes 147460
  46.1 39.0 %all-to-all-start.1 = ((bf16[8,2,256,128]{3,2,1,0:T(8,128)(2,1)}), bf16[8,2,256,128]{3,2,1,0:T(8,128)(2,1)S(1)}, u32[]{:S(2)}, u32[]{:S(2)}) async-start(bf16[8,2,256,128]{3,2,1,0:T(8,128)(2,1)} %gather_fusion.1), calls=%async_computation.1 | async-start | bytes 2097152 | tf_op jit(solution)/shard_map/all_to_all | solution.py:274
  54.1 3.2 %collective-permute-start.2 = (bf16[4,1536]{1,0:T(4,128)(2,1)S(1)}, bf16[4,1536]{1,0:T(4,128)(2,1)S(1)}, u32[]{:S(2)}, u32[]{:S(2)}) collective-permute-start(bf16[4,1536]{1,0:T(4,128)(2,1)S(1)} %get-tuple-element.32), channel_id=1, source_target_pairs={{0,1},{1,2},{2,3},{3,0},{4,5},{5,6},{6,7},{7,4},{8,9},{9,10},{10,1... | collective-permute-start | bytes 36872 | tf_op jit(solution)/shard_map/ppermute | solution.py:270
  54.2 3.8 %collective-permute-start.1 = (bf16[4,1536]{1,0:T(4,128)(2,1)S(1)}, bf16[4,1536]{1,0:T(4,128)(2,1)S(1)}, u32[]{:S(2)}, u32[]{:S(2)}) collective-permute-start(bf16[4,1536]{1,0:T(4,128)(2,1)S(1)} %get-tuple-element.33), channel_id=1, source_target_pairs={{0,2},{1,3},{2,0},{3,1},{4,6},{5,7},{6,4},{7,5},{8,10},{9,11},{10,... | collective-permute-start | bytes 36872 | tf_op jit(solution)/shard_map/ppermute | solution.py:270
  54.3 3.7 %collective-permute-start = (bf16[4,1536]{1,0:T(4,128)(2,1)S(1)}, bf16[4,1536]{1,0:T(4,128)(2,1)S(1)}, u32[]{:S(2)}, u32[]{:S(2)}) collective-permute-start(bf16[4,1536]{1,0:T(4,128)(2,1)S(1)} %get-tuple-element.34), channel_id=1, source_target_pairs={{0,3},{1,0},{2,1},{3,2},{4,7},{5,4},{6,5},{7,6},{8,11},{9,8},{10,9... | collective-permute-start | bytes 36872 | tf_op jit(solution)/shard_map/ppermute | solution.py:270
  58.0 2.3 %copy-start.1 = (bf16[6,3,256,512]{3,2,1,0:T(8,128)(2,1)S(1)}, bf16[6,3,256,512]{3,2,1,0:T(8,128)(2,1)}, u32[]{:S(2)}) copy-start(bf16[6,3,256,512]{3,2,1,0:T(8,128)(2,1)} %copy-done) | copy-start | bytes 14155780
  60.3 1.4 %copy-start.4 = (bf16[6,2,256,256]{3,2,1,0:T(8,128)(2,1)S(1)}, bf16[6,2,256,256]{3,2,1,0:T(8,128)(2,1)}, u32[]{:S(2)}) copy-start(bf16[6,2,256,256]{3,2,1,0:T(8,128)(2,1)} %copy-done.3) | copy-start | bytes 4718596
  61.7 1.2 copy-start.9
  83.4 1.0 copy-start.6
  85.1 2.3 %copy-start.2 = (bf16[6,3,256,512]{3,2,1,0:T(8,128)(2,1)S(1)}, bf16[6,3,256,512]{3,2,1,0:T(8,128)(2,1)}, u32[]{:S(2)}) copy-start(bf16[6,3,256,512]{3,2,1,0:T(8,128)(2,1)} %copy-done) | copy-start | bytes 14155780
  87.5 1.4 %copy-start.5 = (bf16[6,2,256,256]{3,2,1,0:T(8,128)(2,1)S(1)}, bf16[6,2,256,256]{3,2,1,0:T(8,128)(2,1)}, u32[]{:S(2)}) copy-start(bf16[6,2,256,256]{3,2,1,0:T(8,128)(2,1)} %copy-done.3) | copy-start | bytes 4718596
  88.9 1.3 copy-start.7
  111.5 14.4 %all-to-all-start.2 = ((f32[32,4,256]{2,1,0:T(4,128)}), f32[32,4,256]{2,1,0:T(4,128)S(1)}, u32[]{:S(2)}, u32[]{:S(2)}) async-start(f32[32,4,256]{2,1,0:T(4,128)} %copy-done.13), calls=%async_computation.2 | async-start | bytes 262144 | tf_op jit(solution)/shard_map/all_to_all | solution.py:344
  117.7 4.0 %collective-permute-start.3 = (f32[6,4,256]{2,1,0:T(4,128)S(1)}, f32[6,4,256]{2,1,0:T(4,128)S(1)}, u32[]{:S(2)}, u32[]{:S(2)}) collective-permute-start(f32[6,4,256]{2,1,0:T(4,128)S(1)} %get-tuple-element.28), channel_id=1, source_target_pairs={{0,1},{1,2},{2,3},{3,0},{4,5},{5,6},{6,7},{7,4},{8,9},{9,10},{10,1... | collective-permute-start | bytes 73736 | tf_op jit(solution)/shard_map/ppermute | solution.py:270
  118.0 4.0 %collective-permute-start.4 = (f32[6,4,256]{2,1,0:T(4,128)S(1)}, f32[6,4,256]{2,1,0:T(4,128)S(1)}, u32[]{:S(2)}, u32[]{:S(2)}) collective-permute-start(f32[6,4,256]{2,1,0:T(4,128)S(1)} %get-tuple-element.29), channel_id=1, source_target_pairs={{0,2},{1,3},{2,0},{3,1},{4,6},{5,7},{6,4},{7,5},{8,10},{9,11},{10,... | collective-permute-start | bytes 73736 | tf_op jit(solution)/shard_map/ppermute | solution.py:270
  119.6 2.9 %collective-permute-start.5 = (f32[6,4,256]{2,1,0:T(4,128)S(1)}, f32[6,4,256]{2,1,0:T(4,128)S(1)}, u32[]{:S(2)}, u32[]{:S(2)}) collective-permute-start(f32[6,4,256]{2,1,0:T(4,128)S(1)} %get-tuple-element.30), channel_id=1, source_target_pairs={{0,3},{1,0},{2,1},{3,2},{4,7},{5,4},{6,5},{7,6},{8,11},{9,8},{10,9... | collective-permute-start | bytes 73736 | tf_op jit(solution)/shard_map/ppermute | solution.py:270
  121.6 4.3 %copy-start.17 = (f32[6,4,256]{2,1,0:T(4,128)}, f32[6,4,256]{2,1,0:T(4,128)S(1)}, u32[]{:S(2)}) copy-start(f32[6,4,256]{2,1,0:T(4,128)S(1)} %collective-permute-done.3.refs_1_) | copy-start | bytes 73732
  122.0 3.9 %copy-start.18 = (f32[6,4,256]{2,1,0:T(4,128)}, f32[6,4,256]{2,1,0:T(4,128)S(1)}, u32[]{:S(2)}) copy-start(f32[6,4,256]{2,1,0:T(4,128)S(1)} %collective-permute-done.4.refs_2_) | copy-start | bytes 73732
  122.5 3.4 %copy-start.19 = (f32[6,4,256]{2,1,0:T(4,128)}, f32[6,4,256]{2,1,0:T(4,128)S(1)}, u32[]{:S(2)}) copy-start(f32[6,4,256]{2,1,0:T(4,128)S(1)} %collective-permute-done.5.refs_3_) | copy-start | bytes 73732
  (6 other events, 4.4 us)

commit v3 on v1

--- a/solution.py
+++ b/solution.py
@@ -7,6 +7,7 @@
 from jax.sharding import PartitionSpec as P
 
 STEP = 32
+PIVOTS = 4
 NT = (((1,), (1,)), ((), ()))
 NN = (((1,), (0,)), ((), ()))
 TN = (((0,), (0,)), ((), ()))
@@ -54,45 +55,35 @@
         return jnp.broadcast_to(row, (8, 128))
 
     def pivots(slabs):
-        for first in range(0, STEP, 4):
-            top, at = first // 8, first % 8
+        for first in range(0, STEP, PIVOTS):
+            top, start = first // 8, first % 8
             tall = range(top, groups)
-            own = (lane >= first) & (lane < first + 4)
+            own = (lane >= first) & (lane < first + PIVOTS)
             one = jnp.where(lane - 8 * top == sub, 1.0, 0.0)
-            if at == 0:
+            if start == 0:
                 inverses = [None] * len(slabs)
-            columns, rows = [], []
+            columns = []
             for x in slabs:
-                columns.append([{g: spread(x[g][0][:, first + q:first + q + 1]) for g in tall} for q in range(4)])
+                columns.append([{g: spread(x[g][0][:, first + q:first + q + 1]) for g in tall} for q in range(PIVOTS)])
                 for g in tall:
                     x[g][0] = jnp.where(own, one if g == top else 0.0, x[g][0])
-                rows.append([[spread(x[top][h][at + q:at + q + 1, :]) for h in range(halves)] for q in range(4)])
-            for s, x in enumerate(slabs):
-                u = columns[s]
-                a = {(i, j): spread(u[j][top][at + i:at + i + 1, :]) for j in range(4) for i in range(j + 1)}
-                low, inv = {}, []
-                for i in range(4):
-                    for j in range(i, 4):
-                        for k in range(i):
-                            a[i, j] = a[i, j] - low[i, k] * a[k, j]
-                    inv.append(pl.reciprocal(a[i, i], approx=True))
-                    for j in range(i + 1, 4):
-                        low[j, i] = a[i, j] * inv[i]
-                for i in range(4):
-                    for k in range(i):
+            for q in range(PIVOTS):
+                at = start + q
+                for s, x in enumerate(slabs):
+                    cols = columns[s]
+                    inverse = pl.reciprocal(spread(cols[q][top][at:at + 1, :]), approx=True)
+                    inverses[s] = inverse if at == 0 else jnp.where(sub >= at, inverse, inverses[s])
+                    c = {g: cols[q][g] * inverse for g in tall}
+                    for later in range(q + 1, PIVOTS):
+                        m = spread(cols[q][top][start + later:start + later + 1, :])
                         for g in tall:
-                            u[i][g] = u[i][g] - u[k][g] * low[i, k]
-                        for h in range(halves):
-                            rows[s][i][h] = rows[s][i][h] - rows[s][k][h] * low[i, k]
-                for i in range(4):
-                    for g in tall:
-                        m = u[i][g] * inv[i]
-                        if g == top:
-                            m = jnp.where(sub > at + i, m, 0.0)
-                        for h in range(halves):
-                            x[g][h] = x[g][h] - m * rows[s][i][h]
-                    inverses[s] = inv[i] if at + i == 0 else jnp.where(sub >= at + i, inv[i], inverses[s])
-            if at == 4:
+                            cols[later][g] = cols[later][g] - c[g] * m
+                    c[top] = jnp.where(sub > at, c[top], 0.0)
+                    for h in range(halves):
+                        r = spread(x[top][h][at:at + 1, :])
+                        for g in tall:
+                            x[g][h] = x[g][h] - c[g] * r
+            if start + PIVOTS == 8:
                 for s, x in enumerate(slabs):
                     scale = inverses[s] * lax.rsqrt(inverses[s])
                     for h in range(halves):
@@ -137,11 +128,32 @@
     lax.fori_loop(0, width // STEP, block, 0)
 
 
+def factor_pair(ref, tile_ref, *scratch):
+    systems, width, _ = ref.shape
+    half = width // 2
+    for s in range(systems):
+        tile_ref[s] = ref[s, :half, :half]
+    factor(tile_ref, *scratch)
+    for s in range(systems):
+        ref[s, :half, :half] = tile_ref[s]
+        u = split3(dot6(split3(tile_ref[s]), split3(ref[s, :half, half:]), NN))
+        ref[s, :half, half:] = jnp.zeros((half, half), jnp.float32)
+        ut = [one.T for one in u]
+        tile_ref[s] = ref[s, half:, half:] - dot6(ut, u, NN)
+        ref[s, half:, :half] = dot6(ut, split3(ref[s, :half, :half]), NN)
+    factor(tile_ref, *scratch)
+    for s in range(systems):
+        ref[s, half:, half:] = tile_ref[s]
+        ref[s, half:, :half] = -dot6(split3(tile_ref[s]), split3(ref[s, half:, :half]), NN)
+
+
 def factor_scratch(systems, width):
+    half = width // 2
     return [
-        pltpu.VMEM((systems, STEP, width), jnp.float32),
-        pltpu.VMEM((systems, 6 * STEP, width), jnp.bfloat16),
-        pltpu.VMEM((systems, 6 * STEP, width), jnp.bfloat16),
+        pltpu.VMEM((systems, half, half), jnp.float32),
+        pltpu.VMEM((systems, STEP, half), jnp.float32),
+        pltpu.VMEM((systems, 6 * STEP, half), jnp.bfloat16),
+        pltpu.VMEM((systems, 6 * STEP, half), jnp.bfloat16),
     ]
 
 
@@ -155,7 +167,7 @@
             def _():
                 tile = tiles_ref[s, k]
                 g_ref[s] += dot(tile, tile, TN)
-    factor(g_ref, *scratch)
+    factor_pair(g_ref, *scratch)
     for s in range(systems):
         w1, w2, w3 = split3(g_ref[s])
         w_ref[s, 0] = w1
@@ -168,17 +180,23 @@
         z_ref[s, 2] = z3
 
 
-def pair_kernel(lanes, place_ref, w_ref, z_ref, x_ref, got_ref, *refs):
+def pair_kernel(lanes, place_ref, x_ref, w_any, z_any, got_ref, *refs):
     up_refs, refs = refs[:lanes], refs[lanes:]
-    low_ref, near_ref, t_ref, v_ref, r_ref, first_ref, sems, *scratch = refs
+    low_ref, near_ref, w_ref, z_ref, t_ref, v_ref, r_ref, first_ref, sems, *scratch = refs
     systems, _, width, _ = z_ref.shape
     count = x_ref.shape[0] // lanes
-    copies = [pltpu.make_async_copy(got_ref.at[place_ref[s]], near_ref.at[s], sems.at[s]) for s in range(systems)]
-    for copy in copies:
-        copy.start()
+    copies = []
+    for s in range(systems):
+        pairs = ((got_ref.at[place_ref[s]], near_ref.at[s]), (z_any.at[s], z_ref.at[s]))
+        copies.append([pltpu.make_async_copy(a, b, sems.at[s, i]) for i, (a, b) in enumerate(pairs)])
+        for copy in copies[s]:
+            copy.start()
+    w_copy = pltpu.make_async_copy(w_any, w_ref, sems.at[systems, 0])
+    w_copy.start()
     low_ref[...] = jnp.zeros(low_ref.shape, low_ref.dtype)
     for s in range(systems):
-        copies[s].wait()
+        for copy in copies[s]:
+            copy.wait()
         near = near_ref[s].reshape(2 * width, width)
         near_t = near.T
         z1, z2, z3 = z_ref[s, 0], z_ref[s, 1], z_ref[s, 2]
@@ -192,11 +210,12 @@
         r_ref[s] = dot(x, near_ref[s, 1], NN)
     for s in range(systems):
         r_ref[s] = r_ref[s] - apply(first_ref[s], (v_ref[s, 0], v_ref[s, 1]), NT)
-    factor(t_ref, *scratch)
+    factor_pair(t_ref, *scratch)
     parts = [split3(t_ref[s])[:2] for s in range(systems)]
     half = [apply(r_ref[s], parts[s], NT) for s in range(systems)]
     last = [apply(half[s], parts[s], NN) for s in range(systems)]
     mid = [first_ref[s] - apply(last[s], (v_ref[s, 0], v_ref[s, 1]), NN) for s in range(systems)]
+    w_copy.wait()
     for s in range(systems):
         up = apply(mid[s], (w_ref[s, 0], w_ref[s, 1]), NN)
         for e in range(lanes):
@@ -239,6 +258,7 @@
 
     vmem = pl.BlockSpec(memory_space=pltpu.VMEM)
     smem = pl.BlockSpec(memory_space=pltpu.SMEM)
+    anywhere = pl.BlockSpec(memory_space=pl.ANY)
     params = pltpu.CompilerParams(vmem_limit_bytes=56 * 1024 * 1024)
     w, z = pl.pallas_call(
         own_kernel,
@@ -264,18 +284,20 @@
     *up, low = pl.pallas_call(
         functools.partial(pair_kernel, lanes),
         out_shape=[piece] * lanes + [jax.ShapeDtypeStruct((shards * lanes, nrhs_dev, width), jnp.float32)],
-        in_specs=[smem, vmem, vmem, vmem, pl.BlockSpec(memory_space=pl.ANY)],
+        in_specs=[smem, vmem, anywhere, anywhere, anywhere],
         out_specs=[vmem] * (lanes + 1),
         scratch_shapes=[
             pltpu.VMEM((systems, 2, width, width), jnp.bfloat16),
+            pltpu.VMEM((systems, 2, width, width), jnp.bfloat16),
+            pltpu.VMEM((systems, 3, width, 2 * width), jnp.bfloat16),
             pltpu.VMEM((systems, width, width), jnp.float32),
             pltpu.VMEM((systems, 2, width, width), jnp.bfloat16),
             pltpu.VMEM((systems, lanes * nrhs_dev, width), jnp.float32),
             pltpu.VMEM((systems, lanes * nrhs_dev, width), jnp.float32),
-            pltpu.SemaphoreType.DMA((systems,)),
+            pltpu.SemaphoreType.DMA((systems + 1, 2)),
         ] + factor_scratch(systems, width),
         compiler_params=params,
-    )(jnp.concatenate([mate_panel, lane_word]), w, z, x, received)
+    )(jnp.concatenate([mate_panel, lane_word]), x, w, z, received)
     low = lax.all_to_all(low, ("panel", "rhs"), split_axis=0, concat_axis=0, tiled=True)
     up = [up[0]] + [shift(up[e], e) for e in range(1, lanes)]
     return pl.pallas_call(

time: 114 us -> 108 us (0.947)
  Pallas kernels: 74.2 us -> 65.1 us
  waiting for transfers between devices: 12.2 us -> 17.8 us
  starting transfers between devices: 19.1 us -> 16.7 us
    pallas_call x1, Pallas kernels: 38.8 us -> 32.9 us  [on_device(): pl.pallas_call(functools.partial(pair_kernel, lanes), out_shape=[piece] *...]
    all_to_all x1, waiting for transfers between devices: 7.04 us -> 12.6 us  [on_device(): lax.all_to_all(tiles[:, :2][slot_of], 'panel', split_axis=0, concat_axis=...]
    pallas_call x1, Pallas kernels: 33.8 us -> 30.5 us  [on_device(): pl.pallas_call(own_kernel, out_shape=(jax.ShapeDtypeStruct((systems, 2, w...]
    ppermute x6, starting transfers between devices: 8.05 us -> 5.67 us  [shift(): lax.ppermute(value, 'rhs', [(i, (i + by) % lanes) for i in range(lanes)])]
  transfers between devices with their start and end apart: 8 -> 8, of which waited for: 5 -> 6; matrix products, arithmetic and copies ran while one was open for 2% -> 2% of each run, Pallas kernels for 30% -> 28%
where the time goes in v3:
time: 108 us
  Pallas kernels  65.1 us (60%)
  waiting for transfers between devices  17.8 us (16%)
  starting transfers between devices  16.7 us (15%)
  local copies, waits for them, and re-layouts  5.07 us (5%)
  other arithmetic  2.89 us (3%)
    pallas_call x1, Pallas kernels, on_device(): pl.pallas_call(functools.partial(pair_kernel, lanes), out_shape=[piece] *...  32.9 us
    pallas_call x1, Pallas kernels, on_device(): pl.pallas_call(own_kernel, out_shape=(jax.ShapeDtypeStruct((systems, 2, w...  30.5 us
    all_to_all x1, waiting for transfers between devices, on_device(): lax.all_to_all(tiles[:, :2][slot_of], 'panel', split_axis=0, concat_axis=...  12.6 us
    all_to_all x1, starting transfers between devices, on_device(): lax.all_to_all(tiles[:, :2][slot_of], 'panel', split_axis=0, concat_axis=...  7.41 us
    ppermute x6, starting transfers between devices, shift(): lax.ppermute(value, 'rhs', [(i, (i + by) % lanes) for i in range(lanes)])  5.67 us
    all_to_all x1, starting transfers between devices, on_device(): lax.all_to_all(low, ('panel', 'rhs'), split_axis=0, concat_axis=0, tiled=...  3.65 us
    all_to_all x1, waiting for transfers between devices, on_device(): lax.all_to_all(low, ('panel', 'rhs'), split_axis=0, concat_axis=0, tiled=...  3.19 us
  transfers between devices with their start and end apart: 8, of which 6 were waited for; matrix products, arithmetic and copies ran while one was open for 2% of the time, Pallas kernels for 28%

profile of v3, /device:TPU:0, one launch (start us, length us, event | category | flops | bytes accessed | tf_op | source)
XLA Modules:
  0.0 107.6 jit_solution(1969637349377601618)
XLA Ops:
  0.0 0.9 bitcast_select_fusion
  1.1 0.3 slice-done
  1.4 2.0 %gather_fusion = bf16[8,2,256,256]{3,2,1,0:T(8,128)(2,1)} fusion(bf16[6,2,256,256]{3,2,1,0:T(8,128)(2,1)S(1)} %slice-done, s32[1024]{0:T(1024)S(1)} %pad_clamp_fusion), kind=kCustom, calls=%fused_computation | custom fusion | bytes 4194336 | tf_op jit(solution)/shard_map/gather | solution.py:257
  3.5 7.4 %all-to-all-start = ((bf16[8,2,256,256]{3,2,1,0:T(8,128)(2,1)}), bf16[8,2,256,256]{3,2,1,0:T(8,128)(2,1)S(1)}, u32[]{:S(2)}, u32[]{:S(2)}) async-start(bf16[8,2,256,256]{3,2,1,0:T(8,128)(2,1)} %gather_fusion), calls=%async_computation | async-start | bytes 4194304 | tf_op jit(solution)/shard_map/all_to_all | solution.py:257
  10.9 0.6 dynamic_slice.23.counts_ref
  11.5 30.5 %shard_map.46 = (bf16[6,2,256,256]{3,2,1,0:T(8,128)(2,1)}, bf16[6,3,256,512]{3,2,1,0:T(8,128)(2,1)}) custom-call(s32[6]{0:T(128)} %dynamic_slice.23.counts_ref, bf16[6,5,256,256]{3,2,1,0:T(8,128)(2,1)} %tiles_ref.1), custom_call_target="tpu_custom_call" | custom-call | flops 40000000000 | bytes 8000000 | tf_op jit(solution)/shard_map/pallas_call | solution.py:263
  42.1 0.9 collective-permute-start.1
  43.0 1.4 %collective-permute-start = (bf16[4,1536]{1,0:T(4,128)(2,1)S(1)}, bf16[4,1536]{1,0:T(4,128)(2,1)S(1)}, u32[]{:S(2)}, u32[]{:S(2)}) collective-permute-start(bf16[4,1536]{1,0:T(4,128)(2,1)S(1)} %get-tuple-element.26), channel_id=1, source_target_pairs={{0,3},{1,0},{2,1},{3,2},{4,7},{5,4},{6,5},{7,6},{8,11},{9,8},{10,9... | collective-permute-start | bytes 36872 | tf_op jit(solution)/shard_map/ppermute | solution.py:255
  44.4 0.6 pad_add_fusion.1.place_ref
  45.2 0.7 collective-permute-done.1
  45.9 0.7 pad_maximum_fusion.x_ref
  46.5 12.6 %all-to-all-done.got_ref = bf16[8,2,256,256]{3,2,1,0:T(8,128)(2,1)S(1)} async-done(((bf16[8,2,256,256]{3,2,1,0:T(8,128)(2,1)}), bf16[8,2,256,256]{3,2,1,0:T(8,128)(2,1)S(1)}, u32[]{:S(2)}, u32[]{:S(2)}) %all-to-all-start) | async-done | bytes 2097184 | tf_op jit(solution)/shard_map/all_to_all | solution.py:257
  59.1 1.4 %copy-done = bf16[8,2,256,256]{3,2,1,0:T(8,128)(2,1)} copy-done((bf16[8,2,256,256]{3,2,1,0:T(8,128)(2,1)}, bf16[8,2,256,256]{3,2,1,0:T(8,128)(2,1)S(1)}, u32[]{:S(2)}) %copy-start) | copy-done | bytes 2097176
  60.5 32.9 %shard_map.47 = (f32[6,4,256]{2,1,0:T(4,128)}, f32[6,4,256]{2,1,0:T(4,128)}, f32[6,4,256]{2,1,0:T(4,128)}, f32[6,4,256]{2,1,0:T(4,128)}, f32[32,4,256]{2,1,0:T(4,128)}) custom-call(s32[7]{0:T(128)} %pad_add_fusion.1.place_ref, bf16[16,1536]{1,0:T(8,128)(2,1)} %pad_maximum_fusion.x_ref, bf16[6,2,256,256]{3,2,1,0:T(8,128)(2,1)} %get-tuple-element.16.w_any, ...), custom_call_target="tpu_custom_call" | custom-call | tf_op jit(solution)/shard_map/pallas_call | solution.py:284
  93.4 3.6 %all-to-all-start.1 = ((f32[32,4,256]{2,1,0:T(4,128)}), f32[32,4,256]{2,1,0:T(4,128)S(1)}, u32[]{:S(2)}, u32[]{:S(2)}) async-start(f32[32,4,256]{2,1,0:T(4,128)} %get-tuple-element.18), calls=%async_computation.1 | async-start | bytes 262144 | tf_op jit(solution)/shard_map/all_to_all | solution.py:301
  97.1 0.3 collective-permute-start.3
  97.4 1.7 %collective-permute-start.4 = (f32[6,4,256]{2,1,0:T(4,128)}, f32[6,4,256]{2,1,0:T(4,128)S(1)}, u32[]{:S(2)}, u32[]{:S(2)}) collective-permute-start(f32[6,4,256]{2,1,0:T(4,128)} %get-tuple-element.21), channel_id=1, source_target_pairs={{0,2},{1,3},{2,0},{3,1},{4,6},{5,7},{6,4},{7,5},{8,10},{9,11},{10,... | collective-permute-start | bytes 73736 | tf_op jit(solution)/shard_map/ppermute | solution.py:255
  99.0 1.3 %collective-permute-start.5 = (f32[6,4,256]{2,1,0:T(4,128)}, f32[6,4,256]{2,1,0:T(4,128)S(1)}, u32[]{:S(2)}, u32[]{:S(2)}) collective-permute-start(f32[6,4,256]{2,1,0:T(4,128)} %get-tuple-element.22), channel_id=1, source_target_pairs={{0,3},{1,0},{2,1},{3,2},{4,7},{5,4},{6,5},{7,6},{8,11},{9,8},{10,9... | collective-permute-start | bytes 73736 | tf_op jit(solution)/shard_map/ppermute | solution.py:255
  100.4 0.7 pad_add_fusion.place_ref
  101.0 0.4 collective-permute-done.4.refs_2_
  101.5 0.7 collective-permute-done.5.refs_3_
  102.1 3.2 %all-to-all-done.1.low_ref = f32[32,4,256]{2,1,0:T(4,128)S(1)} async-done(((f32[32,4,256]{2,1,0:T(4,128)}), f32[32,4,256]{2,1,0:T(4,128)S(1)}, u32[]{:S(2)}, u32[]{:S(2)}) %all-to-all-start.1) | async-done | bytes 131104 | tf_op jit(solution)/shard_map/all_to_all | solution.py:301
  105.3 0.6 copy-done.1
  106.0 1.6 %shard_map.48 = bf16[4,6144]{1,0:T(4,128)(2,1)} custom-call(s32[25]{0:T(128)} %pad_add_fusion.place_ref, f32[32,4,256]{2,1,0:T(4,128)} %copy-done.1, f32[6,4,256]{2,1,0:T(4,128)} %get-tuple-element.19.refs_0_, f32[6,4,256]{2,1,0:T(4,128)} %copy-done.3, f32[6,4,256]{2,1,0:T(4,128)} %copy-done.4, f32[6,4,256]{2,1,0:T(4,128)} %copy-done.5), custom_call_target="tpu_custom_call" | custom-call | tf_op jit(solution)/shard_map/pallas_call | solution.py:303
  (22 shorter events, 0.5 us)
Async XLA Ops:
  0.0 1.4 %slice-start = ((bf16[6,5,256,256]{3,2,1,0:T(8,128)(2,1)}), bf16[6,2,256,256]{3,2,1,0:T(8,128)(2,1)S(1)}, s32[]{:S(2)}) async-start(bf16[6,5,256,256]{3,2,1,0:T(8,128)(2,1)} %tiles_ref.1), calls=%async_computation.2 | async-start | bytes 3145728 | tf_op jit(solution)/shard_map/slice | solution.py:257
  3.5 7.4 %copy-start.6 = (s32[192]{0:T(256)S(1)}, s32[192]{0:T(256)}, u32[]{:S(2)}) copy-start(s32[192]{0:T(256)} %param.6) | copy-start | bytes 2308
  3.5 55.7 %all-to-all-start = ((bf16[8,2,256,256]{3,2,1,0:T(8,128)(2,1)}), bf16[8,2,256,256]{3,2,1,0:T(8,128)(2,1)S(1)}, u32[]{:S(2)}, u32[]{:S(2)}) async-start(bf16[8,2,256,256]{3,2,1,0:T(8,128)(2,1)} %gather_fusion), calls=%async_computation | async-start | bytes 4194304 | tf_op jit(solution)/shard_map/all_to_all | solution.py:257
  11.5 30.5 %copy-start.2 = (bf16[4,6144]{1,0:T(4,128)(2,1)S(1)}, bf16[4,6144]{1,0:T(4,128)(2,1)}, u32[]{:S(2)}) copy-start(bf16[4,6144]{1,0:T(4,128)(2,1)} %param.7) | copy-start | bytes 147460
  42.0 3.2 %collective-permute-start.2 = (bf16[4,1536]{1,0:T(4,128)(2,1)S(1)}, bf16[4,1536]{1,0:T(4,128)(2,1)S(1)}, u32[]{:S(2)}, u32[]{:S(2)}) collective-permute-start(bf16[4,1536]{1,0:T(4,128)(2,1)S(1)} %get-tuple-element.24), channel_id=1, source_target_pairs={{0,1},{1,2},{2,3},{3,0},{4,5},{5,6},{6,7},{7,4},{8,9},{9,10},{10,1... | collective-permute-start | bytes 36872 | tf_op jit(solution)/shard_map/ppermute | solution.py:255
  42.1 3.8 %collective-permute-start.1 = (bf16[4,1536]{1,0:T(4,128)(2,1)S(1)}, bf16[4,1536]{1,0:T(4,128)(2,1)S(1)}, u32[]{:S(2)}, u32[]{:S(2)}) collective-permute-start(bf16[4,1536]{1,0:T(4,128)(2,1)S(1)} %get-tuple-element.25), channel_id=1, source_target_pairs={{0,2},{1,3},{2,0},{3,1},{4,6},{5,7},{6,4},{7,5},{8,10},{9,11},{10,... | collective-permute-start | bytes 36872 | tf_op jit(solution)/shard_map/ppermute | solution.py:255
  43.0 2.9 %collective-permute-start = (bf16[4,1536]{1,0:T(4,128)(2,1)S(1)}, bf16[4,1536]{1,0:T(4,128)(2,1)S(1)}, u32[]{:S(2)}, u32[]{:S(2)}) collective-permute-start(bf16[4,1536]{1,0:T(4,128)(2,1)S(1)} %get-tuple-element.26), channel_id=1, source_target_pairs={{0,3},{1,0},{2,1},{3,2},{4,7},{5,4},{6,5},{7,6},{8,11},{9,8},{10,9... | collective-permute-start | bytes 36872 | tf_op jit(solution)/shard_map/ppermute | solution.py:255
  59.1 1.4 %copy-start = (bf16[8,2,256,256]{3,2,1,0:T(8,128)(2,1)}, bf16[8,2,256,256]{3,2,1,0:T(8,128)(2,1)S(1)}, u32[]{:S(2)}) copy-start(bf16[8,2,256,256]{3,2,1,0:T(8,128)(2,1)S(1)} %all-to-all-done.got_ref) | copy-start | bytes 6291460
  93.4 11.9 %all-to-all-start.1 = ((f32[32,4,256]{2,1,0:T(4,128)}), f32[32,4,256]{2,1,0:T(4,128)S(1)}, u32[]{:S(2)}, u32[]{:S(2)}) async-start(f32[32,4,256]{2,1,0:T(4,128)} %get-tuple-element.18), calls=%async_computation.1 | async-start | bytes 262144 | tf_op jit(solution)/shard_map/all_to_all | solution.py:301
  97.1 4.0 %collective-permute-start.3 = (f32[6,4,256]{2,1,0:T(4,128)}, f32[6,4,256]{2,1,0:T(4,128)S(1)}, u32[]{:S(2)}, u32[]{:S(2)}) collective-permute-start(f32[6,4,256]{2,1,0:T(4,128)} %get-tuple-element.20), channel_id=1, source_target_pairs={{0,1},{1,2},{2,3},{3,0},{4,5},{5,6},{6,7},{7,4},{8,9},{9,10},{10,1... | collective-permute-start | bytes 73736 | tf_op jit(solution)/shard_map/ppermute | solution.py:255
  97.4 4.1 %collective-permute-start.4 = (f32[6,4,256]{2,1,0:T(4,128)}, f32[6,4,256]{2,1,0:T(4,128)S(1)}, u32[]{:S(2)}, u32[]{:S(2)}) collective-permute-start(f32[6,4,256]{2,1,0:T(4,128)} %get-tuple-element.21), channel_id=1, source_target_pairs={{0,2},{1,3},{2,0},{3,1},{4,6},{5,7},{6,4},{7,5},{8,10},{9,11},{10,... | collective-permute-start | bytes 73736 | tf_op jit(solution)/shard_map/ppermute | solution.py:255
  99.0 3.1 %collective-permute-start.5 = (f32[6,4,256]{2,1,0:T(4,128)}, f32[6,4,256]{2,1,0:T(4,128)S(1)}, u32[]{:S(2)}, u32[]{:S(2)}) collective-permute-start(f32[6,4,256]{2,1,0:T(4,128)} %get-tuple-element.22), channel_id=1, source_target_pairs={{0,3},{1,0},{2,1},{3,2},{4,7},{5,4},{6,5},{7,6},{8,11},{9,8},{10,9... | collective-permute-start | bytes 73736 | tf_op jit(solution)/shard_map/ppermute | solution.py:255
  101.0 4.3 %copy-start.3 = (f32[6,4,256]{2,1,0:T(4,128)}, f32[6,4,256]{2,1,0:T(4,128)S(1)}, u32[]{:S(2)}) copy-start(f32[6,4,256]{2,1,0:T(4,128)S(1)} %collective-permute-done.3.refs_1_) | copy-start | bytes 73732
  101.5 3.9 %copy-start.4 = (f32[6,4,256]{2,1,0:T(4,128)}, f32[6,4,256]{2,1,0:T(4,128)S(1)}, u32[]{:S(2)}) copy-start(f32[6,4,256]{2,1,0:T(4,128)S(1)} %collective-permute-done.4.refs_2_) | copy-start | bytes 73732
  102.1 3.2 %copy-start.5 = (f32[6,4,256]{2,1,0:T(4,128)}, f32[6,4,256]{2,1,0:T(4,128)S(1)}, u32[]{:S(2)}) copy-start(f32[6,4,256]{2,1,0:T(4,128)S(1)} %collective-permute-done.5.refs_3_) | copy-start | bytes 73732
  105.3 0.7 copy-start.1

commit v4 on v1

--- a/solution.py
+++ b/solution.py
@@ -54,49 +54,61 @@
         return jnp.broadcast_to(row, (8, 128))
 
     def pivots(slabs):
+        each = range(len(slabs))
         for first in range(0, STEP, 4):
             top, at = first // 8, first % 8
             tall = range(top, groups)
             own = (lane >= first) & (lane < first + 4)
             one = jnp.where(lane - 8 * top == sub, 1.0, 0.0)
             if at == 0:
-                inverses = [None] * len(slabs)
-            columns, rows = [], []
+                inverses = [None for _ in each]
+            u = [[{g: spread(x[g][0][:, first + q:first + q + 1]) for g in tall} for q in range(4)] for x in slabs]
+            a = [{(i, j): spread(u[s][j][top][at + i:at + i + 1, :]) for j in range(4) for i in range(j + 1)} for s in each]
             for x in slabs:
-                columns.append([{g: spread(x[g][0][:, first + q:first + q + 1]) for g in tall} for q in range(4)])
                 for g in tall:
                     x[g][0] = jnp.where(own, one if g == top else 0.0, x[g][0])
-                rows.append([[spread(x[top][h][at + q:at + q + 1, :]) for h in range(halves)] for q in range(4)])
-            for s, x in enumerate(slabs):
-                u = columns[s]
-                a = {(i, j): spread(u[j][top][at + i:at + i + 1, :]) for j in range(4) for i in range(j + 1)}
-                low, inv = {}, []
-                for i in range(4):
+            y = [[[spread(x[top][h][at + q:at + q + 1, :]) for h in range(halves)] for q in range(4)] for x in slabs]
+            low = [{} for _ in each]
+            inv = [[None] * 4 for _ in each]
+            for p in (0, 2):
+                n = p + 1
+                delta = [a[s][p, p] * a[s][n, n] - a[s][p, n] * a[s][p, n] for s in each]
+                for s in each:
+                    inv[s][p] = pl.reciprocal(a[s][p, p], approx=True)
+                    inv[s][n] = pl.reciprocal(delta[s], approx=True) * a[s][p, p]
+                for j in range(n, 4):
+                    for s in each:
+                        low[s][j, p] = a[s][p, j] * inv[s][p]
+                for j in range(n + 1, 4):
+                    for s in each:
+                        a[s][n, j] = a[s][n, j] - low[s][n, p] * a[s][p, j]
+                for j in range(n + 1, 4):
+                    for s in each:
+                        low[s][j, n] = a[s][n, j] * inv[s][n]
+                for i in range(n + 1, 4):
                     for j in range(i, 4):
-                        for k in range(i):
-                            a[i, j] = a[i, j] - low[i, k] * a[k, j]
-                    inv.append(pl.reciprocal(a[i, i], approx=True))
-                    for j in range(i + 1, 4):
-                        low[j, i] = a[i, j] * inv[i]
-                for i in range(4):
-                    for k in range(i):
+                        for s in each:
+                            a[s][i, j] = (a[s][i, j] - low[s][i, p] * a[s][p, j]) - low[s][i, n] * a[s][n, j]
+            for i in range(4):
+                for k in range(i):
+                    for s in each:
                         for g in tall:
-                            u[i][g] = u[i][g] - u[k][g] * low[i, k]
+                            u[s][i][g] = u[s][i][g] - u[s][k][g] * low[s][i, k]
                         for h in range(halves):
-                            rows[s][i][h] = rows[s][i][h] - rows[s][k][h] * low[i, k]
-                for i in range(4):
+                            y[s][i][h] = y[s][i][h] - y[s][k][h] * low[s][i, k]
+                for s in each:
+                    inverses[s] = inv[s][i] if at + i == 0 else jnp.where(sub >= at + i, inv[s][i], inverses[s])
                     for g in tall:
-                        m = u[i][g] * inv[i]
+                        m = u[s][i][g] * inv[s][i]
                         if g == top:
                             m = jnp.where(sub > at + i, m, 0.0)
                         for h in range(halves):
-                            x[g][h] = x[g][h] - m * rows[s][i][h]
-                    inverses[s] = inv[i] if at + i == 0 else jnp.where(sub >= at + i, inv[i], inverses[s])
+                            slabs[s][g][h] = slabs[s][g][h] - m * y[s][i][h]
             if at == 4:
-                for s, x in enumerate(slabs):
+                for s in each:
                     scale = inverses[s] * lax.rsqrt(inverses[s])
                     for h in range(halves):
-                        x[top][h] = x[top][h] * scale
+                        slabs[s][top][h] = slabs[s][top][h] * scale
 
     for s in range(systems):
         slab_ref[s] = ref[s, 0:STEP]
@@ -145,6 +157,11 @@
     ]
 
 
+def scaled(matrix):
+    factor_of = 1.0 / jnp.max(jnp.max(matrix, axis=1, keepdims=True), axis=0, keepdims=True)
+    return matrix * factor_of, jnp.sqrt(factor_of)
+
+
 def own_kernel(counts_ref, tiles_ref, w_ref, z_ref, g_ref, *scratch):
     systems, kslots, width, _ = tiles_ref.shape
     for s in range(systems):
@@ -155,9 +172,13 @@
             def _():
                 tile = tiles_ref[s, k]
                 g_ref[s] += dot(tile, tile, TN)
+    roots = []
+    for s in range(systems):
+        g_ref[s], root = scaled(g_ref[s])
+        roots.append(root)
     factor(g_ref, *scratch)
     for s in range(systems):
-        w1, w2, w3 = split3(g_ref[s])
+        w1, w2, w3 = split3(g_ref[s] * roots[s])
         w_ref[s, 0] = w1
         w_ref[s, 1] = w2
         near = jnp.concatenate([tiles_ref[s, 1], tiles_ref[s, 0]], axis=0)
@@ -168,24 +189,32 @@
         z_ref[s, 2] = z3
 
 
-def pair_kernel(lanes, place_ref, w_ref, z_ref, x_ref, got_ref, *refs):
+def pair_kernel(lanes, place_ref, x_ref, w_any, z_any, got_ref, *refs):
     up_refs, refs = refs[:lanes], refs[lanes:]
-    low_ref, near_ref, t_ref, v_ref, r_ref, first_ref, sems, *scratch = refs
+    low_ref, near_ref, w_ref, z_ref, t_ref, v_ref, r_ref, first_ref, sems, *scratch = refs
     systems, _, width, _ = z_ref.shape
     count = x_ref.shape[0] // lanes
-    copies = [pltpu.make_async_copy(got_ref.at[place_ref[s]], near_ref.at[s], sems.at[s]) for s in range(systems)]
-    for copy in copies:
-        copy.start()
+    copies = []
+    for s in range(systems):
+        pairs = ((got_ref.at[place_ref[s]], near_ref.at[s]), (z_any.at[s], z_ref.at[s]))
+        copies.append([pltpu.make_async_copy(a, b, sems.at[s, i]) for i, (a, b) in enumerate(pairs)])
+        for copy in copies[s]:
+            copy.start()
+    w_copy = pltpu.make_async_copy(w_any, w_ref, sems.at[systems, 0])
+    w_copy.start()
     low_ref[...] = jnp.zeros(low_ref.shape, low_ref.dtype)
-    for s in range(systems):
-        copies[s].wait()
+    roots = []
+    for s in range(systems):
+        for copy in copies[s]:
+            copy.wait()
         near = near_ref[s].reshape(2 * width, width)
         near_t = near.T
         z1, z2, z3 = z_ref[s, 0], z_ref[s, 1], z_ref[s, 2]
         v = split3(dot(near_t, z1, NT) + (dot(near_t, z2, NT) + dot(near_t, z3, NT)))
         v_ref[s, 0] = v[0]
         v_ref[s, 1] = v[1]
-        t_ref[s] = dot(near_t, near, NN) - dot6(v, v, NT)
+        t_ref[s], root = scaled(dot(near_t, near, NN) - dot6(v, v, NT))
+        roots.append(root)
     for s in range(systems):
         x = x_ref[:, s * width:(s + 1) * width]
         first_ref[s] = dot(x, z_ref[s, 0, :, width:], NT) + dot(x, z_ref[s, 1, :, width:], NT)
@@ -193,10 +222,11 @@
     for s in range(systems):
         r_ref[s] = r_ref[s] - apply(first_ref[s], (v_ref[s, 0], v_ref[s, 1]), NT)
     factor(t_ref, *scratch)
-    parts = [split3(t_ref[s])[:2] for s in range(systems)]
+    parts = [split3(t_ref[s] * roots[s])[:2] for s in range(systems)]
     half = [apply(r_ref[s], parts[s], NT) for s in range(systems)]
     last = [apply(half[s], parts[s], NN) for s in range(systems)]
     mid = [first_ref[s] - apply(last[s], (v_ref[s, 0], v_ref[s, 1]), NN) for s in range(systems)]
+    w_copy.wait()
     for s in range(systems):
         up = apply(mid[s], (w_ref[s, 0], w_ref[s, 1]), NN)
         for e in range(lanes):
@@ -239,6 +269,7 @@
 
     vmem = pl.BlockSpec(memory_space=pltpu.VMEM)
     smem = pl.BlockSpec(memory_space=pltpu.SMEM)
+    anywhere = pl.BlockSpec(memory_space=pl.ANY)
     params = pltpu.CompilerParams(vmem_limit_bytes=56 * 1024 * 1024)
     w, z = pl.pallas_call(
         own_kernel,
@@ -264,18 +295,20 @@
     *up, low = pl.pallas_call(
         functools.partial(pair_kernel, lanes),
         out_shape=[piece] * lanes + [jax.ShapeDtypeStruct((shards * lanes, nrhs_dev, width), jnp.float32)],
-        in_specs=[smem, vmem, vmem, vmem, pl.BlockSpec(memory_space=pl.ANY)],
+        in_specs=[smem, vmem, anywhere, anywhere, anywhere],
         out_specs=[vmem] * (lanes + 1),
         scratch_shapes=[
             pltpu.VMEM((systems, 2, width, width), jnp.bfloat16),
+            pltpu.VMEM((systems, 2, width, width), jnp.bfloat16),
+            pltpu.VMEM((systems, 3, width, 2 * width), jnp.bfloat16),
             pltpu.VMEM((systems, width, width), jnp.float32),
             pltpu.VMEM((systems, 2, width, width), jnp.bfloat16),
             pltpu.VMEM((systems, lanes * nrhs_dev, width), jnp.float32),
             pltpu.VMEM((systems, lanes * nrhs_dev, width), jnp.float32),
-            pltpu.SemaphoreType.DMA((systems,)),
+            pltpu.SemaphoreType.DMA((systems + 1, 2)),
         ] + factor_scratch(systems, width),
         compiler_params=params,
-    )(jnp.concatenate([mate_panel, lane_word]), w, z, x, received)
+    )(jnp.concatenate([mate_panel, lane_word]), x, w, z, received)
     low = lax.all_to_all(low, ("panel", "rhs"), split_axis=0, concat_axis=0, tiled=True)
     up = [up[0]] + [shift(up[e], e) for e in range(1, lanes)]
     return pl.pallas_call(

time: 114 us -> 113 us (level)
  starting transfers between devices: 19.1 us -> 17.4 us
    ppermute x6, starting transfers between devices: 8.05 us -> 6.31 us  [shift(): lax.ppermute(value, 'rhs', [(i, (i + by) % lanes) for i in range(lanes)])]
  transfers between devices with their start and end apart: 8 -> 8, of which waited for: 5 -> 6; matrix products, arithmetic and copies ran while one was open for 2% -> 2% of each run, Pallas kernels for 30% -> 31%
where the time goes in v4:
time: 113 us
  Pallas kernels  73.8 us (65%)
  starting transfers between devices  17.4 us (15%)
  waiting for transfers between devices  13.3 us (12%)
  local copies, waits for them, and re-layouts  5.07 us (4%)
  other arithmetic  2.89 us (3%)
    pallas_call x1, Pallas kernels, on_device(): pl.pallas_call(functools.partial(pair_kernel, lanes), out_shape=[piece] *...  37.8 us
    pallas_call x1, Pallas kernels, on_device(): pl.pallas_call(own_kernel, out_shape=(jax.ShapeDtypeStruct((systems, 2, w...  34.4 us
    all_to_all x1, waiting for transfers between devices, on_device(): lax.all_to_all(tiles[:, :2][slot_of], 'panel', split_axis=0, concat_axis=...  8.08 us
    all_to_all x1, starting transfers between devices, on_device(): lax.all_to_all(tiles[:, :2][slot_of], 'panel', split_axis=0, concat_axis=...  7.41 us
    ppermute x6, starting transfers between devices, shift(): lax.ppermute(value, 'rhs', [(i, (i + by) % lanes) for i in range(lanes)])  6.31 us
    all_to_all x1, starting transfers between devices, on_device(): lax.all_to_all(low, ('panel', 'rhs'), split_axis=0, concat_axis=0, tiled=...  3.66 us
    all_to_all x1, waiting for transfers between devices, on_device(): lax.all_to_all(low, ('panel', 'rhs'), split_axis=0, concat_axis=0, tiled=...  3.19 us
  transfers between devices with their start and end apart: 8, of which 6 were waited for; matrix products, arithmetic and copies ran while one was open for 2% of the time, Pallas kernels for 31%

profile of v4, /device:TPU:0, one launch (start us, length us, event | category | flops | bytes accessed | tf_op | source)
XLA Modules:
  0.0 112.5 jit_solution(13473105522005983351)
XLA Ops:
  0.0 0.9 bitcast_select_fusion
  1.1 0.3 slice-done
  1.4 2.0 %gather_fusion = bf16[8,2,256,256]{3,2,1,0:T(8,128)(2,1)} fusion(bf16[6,2,256,256]{3,2,1,0:T(8,128)(2,1)S(1)} %slice-done, s32[1024]{0:T(1024)S(1)} %pad_clamp_fusion), kind=kCustom, calls=%fused_computation | custom fusion | bytes 4194336 | tf_op jit(solution)/shard_map/gather | solution.py:268
  3.5 7.4 %all-to-all-start = ((bf16[8,2,256,256]{3,2,1,0:T(8,128)(2,1)}), bf16[8,2,256,256]{3,2,1,0:T(8,128)(2,1)S(1)}, u32[]{:S(2)}, u32[]{:S(2)}) async-start(bf16[8,2,256,256]{3,2,1,0:T(8,128)(2,1)} %gather_fusion), calls=%async_computation | async-start | bytes 4194304 | tf_op jit(solution)/shard_map/all_to_all | solution.py:268
  10.9 0.6 dynamic_slice.23.counts_ref
  11.5 34.4 %shard_map.46 = (bf16[6,2,256,256]{3,2,1,0:T(8,128)(2,1)}, bf16[6,3,256,512]{3,2,1,0:T(8,128)(2,1)}) custom-call(s32[6]{0:T(128)} %dynamic_slice.23.counts_ref, bf16[6,5,256,256]{3,2,1,0:T(8,128)(2,1)} %tiles_ref.1), custom_call_target="tpu_custom_call" | custom-call | flops 40000000000 | bytes 8000000 | tf_op jit(solution)/shard_map/pallas_call | solution.py:274
  45.9 2.8 %collective-permute-start.1 = (bf16[4,1536]{1,0:T(4,128)(2,1)S(1)}, bf16[4,1536]{1,0:T(4,128)(2,1)S(1)}, u32[]{:S(2)}, u32[]{:S(2)}) collective-permute-start(bf16[4,1536]{1,0:T(4,128)(2,1)S(1)} %get-tuple-element.25), channel_id=1, source_target_pairs={{0,2},{1,3},{2,0},{3,1},{4,6},{5,7},{6,4},{7,5},{8,10},{9,11},{10,... | collective-permute-start | bytes 36872 | tf_op jit(solution)/shard_map/ppermute | solution.py:266
  48.9 0.6 pad_add_fusion.1.place_ref
  49.4 0.2 collective-permute-done.2
  49.7 0.7 collective-permute-done.1
  50.4 0.7 pad_maximum_fusion.x_ref
  51.0 8.1 %all-to-all-done.got_ref = bf16[8,2,256,256]{3,2,1,0:T(8,128)(2,1)S(1)} async-done(((bf16[8,2,256,256]{3,2,1,0:T(8,128)(2,1)}), bf16[8,2,256,256]{3,2,1,0:T(8,128)(2,1)S(1)}, u32[]{:S(2)}, u32[]{:S(2)}) %all-to-all-start) | async-done | bytes 2097184 | tf_op jit(solution)/shard_map/all_to_all | solution.py:268
  59.1 1.4 %copy-done = bf16[8,2,256,256]{3,2,1,0:T(8,128)(2,1)} copy-done((bf16[8,2,256,256]{3,2,1,0:T(8,128)(2,1)}, bf16[8,2,256,256]{3,2,1,0:T(8,128)(2,1)S(1)}, u32[]{:S(2)}) %copy-start) | copy-done | bytes 2097176
  60.5 37.8 %shard_map.47 = (f32[6,4,256]{2,1,0:T(4,128)}, f32[6,4,256]{2,1,0:T(4,128)}, f32[6,4,256]{2,1,0:T(4,128)}, f32[6,4,256]{2,1,0:T(4,128)}, f32[32,4,256]{2,1,0:T(4,128)}) custom-call(s32[7]{0:T(128)} %pad_add_fusion.1.place_ref, bf16[16,1536]{1,0:T(8,128)(2,1)} %pad_maximum_fusion.x_ref, bf16[6,2,256,256]{3,2,1,0:T(8,128)(2,1)} %get-tuple-element.16.w_any, ...), custom_call_target="tpu_custom_call" | custom-call | tf_op jit(solution)/shard_map/pallas_call | solution.py:295
  98.3 3.7 %all-to-all-start.1 = ((f32[32,4,256]{2,1,0:T(4,128)}), f32[32,4,256]{2,1,0:T(4,128)S(1)}, u32[]{:S(2)}, u32[]{:S(2)}) async-start(f32[32,4,256]{2,1,0:T(4,128)} %get-tuple-element.18), calls=%async_computation.1 | async-start | bytes 262144 | tf_op jit(solution)/shard_map/all_to_all | solution.py:312
  102.0 0.3 collective-permute-start.3
  102.3 1.7 %collective-permute-start.4 = (f32[6,4,256]{2,1,0:T(4,128)}, f32[6,4,256]{2,1,0:T(4,128)S(1)}, u32[]{:S(2)}, u32[]{:S(2)}) collective-permute-start(f32[6,4,256]{2,1,0:T(4,128)} %get-tuple-element.21), channel_id=1, source_target_pairs={{0,2},{1,3},{2,0},{3,1},{4,6},{5,7},{6,4},{7,5},{8,10},{9,11},{10,... | collective-permute-start | bytes 73736 | tf_op jit(solution)/shard_map/ppermute | solution.py:266
  104.0 1.3 %collective-permute-start.5 = (f32[6,4,256]{2,1,0:T(4,128)}, f32[6,4,256]{2,1,0:T(4,128)S(1)}, u32[]{:S(2)}, u32[]{:S(2)}) collective-permute-start(f32[6,4,256]{2,1,0:T(4,128)} %get-tuple-element.22), channel_id=1, source_target_pairs={{0,3},{1,0},{2,1},{3,2},{4,7},{5,4},{6,5},{7,6},{8,11},{9,8},{10,9... | collective-permute-start | bytes 73736 | tf_op jit(solution)/shard_map/ppermute | solution.py:266
  105.3 0.7 pad_add_fusion.place_ref
  106.0 0.4 collective-permute-done.4.refs_2_
  106.4 0.7 collective-permute-done.5.refs_3_
  107.0 3.2 %all-to-all-done.1.low_ref = f32[32,4,256]{2,1,0:T(4,128)S(1)} async-done(((f32[32,4,256]{2,1,0:T(4,128)}), f32[32,4,256]{2,1,0:T(4,128)S(1)}, u32[]{:S(2)}, u32[]{:S(2)}) %all-to-all-start.1) | async-done | bytes 131104 | tf_op jit(solution)/shard_map/all_to_all | solution.py:312
  110.2 0.6 copy-done.1
  110.9 1.6 %shard_map.48 = bf16[4,6144]{1,0:T(4,128)(2,1)} custom-call(s32[25]{0:T(128)} %pad_add_fusion.place_ref, f32[32,4,256]{2,1,0:T(4,128)} %copy-done.1, f32[6,4,256]{2,1,0:T(4,128)} %get-tuple-element.19.refs_0_, f32[6,4,256]{2,1,0:T(4,128)} %copy-done.3, f32[6,4,256]{2,1,0:T(4,128)} %copy-done.4, f32[6,4,256]{2,1,0:T(4,128)} %copy-done.5), custom_call_target="tpu_custom_call" | custom-call | tf_op jit(solution)/shard_map/pallas_call | solution.py:314
  (22 shorter events, 0.5 us)
Async XLA Ops:
  0.0 1.4 %slice-start = ((bf16[6,5,256,256]{3,2,1,0:T(8,128)(2,1)}), bf16[6,2,256,256]{3,2,1,0:T(8,128)(2,1)S(1)}, s32[]{:S(2)}) async-start(bf16[6,5,256,256]{3,2,1,0:T(8,128)(2,1)} %tiles_ref.1), calls=%async_computation.2 | async-start | bytes 3145728 | tf_op jit(solution)/shard_map/slice | solution.py:268
  3.5 7.4 %copy-start.6 = (s32[192]{0:T(256)S(1)}, s32[192]{0:T(256)}, u32[]{:S(2)}) copy-start(s32[192]{0:T(256)} %param.6) | copy-start | bytes 2308
  3.5 55.7 %all-to-all-start = ((bf16[8,2,256,256]{3,2,1,0:T(8,128)(2,1)}), bf16[8,2,256,256]{3,2,1,0:T(8,128)(2,1)S(1)}, u32[]{:S(2)}, u32[]{:S(2)}) async-start(bf16[8,2,256,256]{3,2,1,0:T(8,128)(2,1)} %gather_fusion), calls=%async_computation | async-start | bytes 4194304 | tf_op jit(solution)/shard_map/all_to_all | solution.py:268
  11.5 34.4 %copy-start.2 = (bf16[4,6144]{1,0:T(4,128)(2,1)S(1)}, bf16[4,6144]{1,0:T(4,128)(2,1)}, u32[]{:S(2)}) copy-start(bf16[4,6144]{1,0:T(4,128)(2,1)} %param.7) | copy-start | bytes 147460
  45.9 3.8 %collective-permute-start.2 = (bf16[4,1536]{1,0:T(4,128)(2,1)S(1)}, bf16[4,1536]{1,0:T(4,128)(2,1)S(1)}, u32[]{:S(2)}, u32[]{:S(2)}) collective-permute-start(bf16[4,1536]{1,0:T(4,128)(2,1)S(1)} %get-tuple-element.24), channel_id=1, source_target_pairs={{0,1},{1,2},{2,3},{3,0},{4,5},{5,6},{6,7},{7,4},{8,9},{9,10},{10,1... | collective-permute-start | bytes 36872 | tf_op jit(solution)/shard_map/ppermute | solution.py:266
  45.9 4.5 %collective-permute-start.1 = (bf16[4,1536]{1,0:T(4,128)(2,1)S(1)}, bf16[4,1536]{1,0:T(4,128)(2,1)S(1)}, u32[]{:S(2)}, u32[]{:S(2)}) collective-permute-start(bf16[4,1536]{1,0:T(4,128)(2,1)S(1)} %get-tuple-element.25), channel_id=1, source_target_pairs={{0,2},{1,3},{2,0},{3,1},{4,6},{5,7},{6,4},{7,5},{8,10},{9,11},{10,... | collective-permute-start | bytes 36872 | tf_op jit(solution)/shard_map/ppermute | solution.py:266
  48.7 1.7 %collective-permute-start = (bf16[4,1536]{1,0:T(4,128)(2,1)S(1)}, bf16[4,1536]{1,0:T(4,128)(2,1)S(1)}, u32[]{:S(2)}, u32[]{:S(2)}) collective-permute-start(bf16[4,1536]{1,0:T(4,128)(2,1)S(1)} %get-tuple-element.26), channel_id=1, source_target_pairs={{0,3},{1,0},{2,1},{3,2},{4,7},{5,4},{6,5},{7,6},{8,11},{9,8},{10,9... | collective-permute-start | bytes 36872 | tf_op jit(solution)/shard_map/ppermute | solution.py:266
  59.1 1.4 %copy-start = (bf16[8,2,256,256]{3,2,1,0:T(8,128)(2,1)}, bf16[8,2,256,256]{3,2,1,0:T(8,128)(2,1)S(1)}, u32[]{:S(2)}) copy-start(bf16[8,2,256,256]{3,2,1,0:T(8,128)(2,1)S(1)} %all-to-all-done.got_ref) | copy-start | bytes 6291460
  98.3 11.9 %all-to-all-start.1 = ((f32[32,4,256]{2,1,0:T(4,128)}), f32[32,4,256]{2,1,0:T(4,128)S(1)}, u32[]{:S(2)}, u32[]{:S(2)}) async-start(f32[32,4,256]{2,1,0:T(4,128)} %get-tuple-element.18), calls=%async_computation.1 | async-start | bytes 262144 | tf_op jit(solution)/shard_map/all_to_all | solution.py:312
  102.0 4.0 %collective-permute-start.3 = (f32[6,4,256]{2,1,0:T(4,128)}, f32[6,4,256]{2,1,0:T(4,128)S(1)}, u32[]{:S(2)}, u32[]{:S(2)}) collective-permute-start(f32[6,4,256]{2,1,0:T(4,128)} %get-tuple-element.20), channel_id=1, source_target_pairs={{0,1},{1,2},{2,3},{3,0},{4,5},{5,6},{6,7},{7,4},{8,9},{9,10},{10,1... | collective-permute-start | bytes 73736 | tf_op jit(solution)/shard_map/ppermute | solution.py:266
  102.3 4.1 %collective-permute-start.4 = (f32[6,4,256]{2,1,0:T(4,128)}, f32[6,4,256]{2,1,0:T(4,128)S(1)}, u32[]{:S(2)}, u32[]{:S(2)}) collective-permute-start(f32[6,4,256]{2,1,0:T(4,128)} %get-tuple-element.21), channel_id=1, source_target_pairs={{0,2},{1,3},{2,0},{3,1},{4,6},{5,7},{6,4},{7,5},{8,10},{9,11},{10,... | collective-permute-start | bytes 73736 | tf_op jit(solution)/shard_map/ppermute | solution.py:266
  104.0 3.1 %collective-permute-start.5 = (f32[6,4,256]{2,1,0:T(4,128)}, f32[6,4,256]{2,1,0:T(4,128)S(1)}, u32[]{:S(2)}, u32[]{:S(2)}) collective-permute-start(f32[6,4,256]{2,1,0:T(4,128)} %get-tuple-element.22), channel_id=1, source_target_pairs={{0,3},{1,0},{2,1},{3,2},{4,7},{5,4},{6,5},{7,6},{8,11},{9,8},{10,9... | collective-permute-start | bytes 73736 | tf_op jit(solution)/shard_map/ppermute | solution.py:266
  106.0 4.3 %copy-start.3 = (f32[6,4,256]{2,1,0:T(4,128)}, f32[6,4,256]{2,1,0:T(4,128)S(1)}, u32[]{:S(2)}) copy-start(f32[6,4,256]{2,1,0:T(4,128)S(1)} %collective-permute-done.3.refs_1_) | copy-start | bytes 73732
  106.4 3.9 %copy-start.4 = (f32[6,4,256]{2,1,0:T(4,128)}, f32[6,4,256]{2,1,0:T(4,128)S(1)}, u32[]{:S(2)}) copy-start(f32[6,4,256]{2,1,0:T(4,128)S(1)} %collective-permute-done.4.refs_2_) | copy-start | bytes 73732
  107.0 3.2 %copy-start.5 = (f32[6,4,256]{2,1,0:T(4,128)}, f32[6,4,256]{2,1,0:T(4,128)S(1)}, u32[]{:S(2)}) copy-start(f32[6,4,256]{2,1,0:T(4,128)S(1)} %collective-permute-done.5.refs_3_) | copy-start | bytes 73732
  110.2 0.7 copy-start.1

commit v5 on v3

--- a/solution.py
+++ b/solution.py
@@ -8,6 +8,7 @@
 
 STEP = 32
 PIVOTS = 4
+TEAM = 3
 NT = (((1,), (1,)), ((), ()))
 NN = (((1,), (0,)), ((), ()))
 TN = (((0,), (0,)), ((), ()))
@@ -103,7 +104,8 @@
         slabs = []
         for s in range(systems):
             slabs.append([[slab_ref[s, 8 * g:8 * g + 8, 128 * h:128 * h + 128] for h in range(halves)] for g in range(groups)])
-        pivots(slabs)
+        for s in range(0, systems, TEAM):
+            pivots(slabs[s:s + TEAM])
         for s in range(systems):
             slab = jnp.concatenate([jnp.concatenate(line, axis=1) for line in slabs[s]], axis=0)
             slab = jnp.where((col_in > row_in) & (col_in < STEP), 0.0, slab)
@@ -128,32 +130,11 @@
     lax.fori_loop(0, width // STEP, block, 0)
 
 
-def factor_pair(ref, tile_ref, *scratch):
-    systems, width, _ = ref.shape
-    half = width // 2
-    for s in range(systems):
-        tile_ref[s] = ref[s, :half, :half]
-    factor(tile_ref, *scratch)
-    for s in range(systems):
-        ref[s, :half, :half] = tile_ref[s]
-        u = split3(dot6(split3(tile_ref[s]), split3(ref[s, :half, half:]), NN))
-        ref[s, :half, half:] = jnp.zeros((half, half), jnp.float32)
-        ut = [one.T for one in u]
-        tile_ref[s] = ref[s, half:, half:] - dot6(ut, u, NN)
-        ref[s, half:, :half] = dot6(ut, split3(ref[s, :half, :half]), NN)
-    factor(tile_ref, *scratch)
-    for s in range(systems):
-        ref[s, half:, half:] = tile_ref[s]
-        ref[s, half:, :half] = -dot6(split3(tile_ref[s]), split3(ref[s, half:, :half]), NN)
-
-
 def factor_scratch(systems, width):
-    half = width // 2
     return [
-        pltpu.VMEM((systems, half, half), jnp.float32),
-        pltpu.VMEM((systems, STEP, half), jnp.float32),
-        pltpu.VMEM((systems, 6 * STEP, half), jnp.bfloat16),
-        pltpu.VMEM((systems, 6 * STEP, half), jnp.bfloat16),
+        pltpu.VMEM((systems, STEP, width), jnp.float32),
+        pltpu.VMEM((systems, 6 * STEP, width), jnp.bfloat16),
+        pltpu.VMEM((systems, 6 * STEP, width), jnp.bfloat16),
     ]
 
 
@@ -167,7 +148,7 @@
             def _():
                 tile = tiles_ref[s, k]
                 g_ref[s] += dot(tile, tile, TN)
-    factor_pair(g_ref, *scratch)
+    factor(g_ref, *scratch)
     for s in range(systems):
         w1, w2, w3 = split3(g_ref[s])
         w_ref[s, 0] = w1
@@ -210,7 +191,7 @@
         r_ref[s] = dot(x, near_ref[s, 1], NN)
     for s in range(systems):
         r_ref[s] = r_ref[s] - apply(first_ref[s], (v_ref[s, 0], v_ref[s, 1]), NT)
-    factor_pair(t_ref, *scratch)
+    factor(t_ref, *scratch)
     parts = [split3(t_ref[s])[:2] for s in range(systems)]
     half = [apply(r_ref[s], parts[s], NT) for s in range(systems)]
     last = [apply(half[s], parts[s], NN) for s in range(systems)]
@@ -219,9 +200,9 @@
     for s in range(systems):
         up = apply(mid[s], (w_ref[s, 0], w_ref[s, 1]), NN)
         for e in range(lanes):
-            up_refs[e][s] = up[e * count:(e + 1) * count]
+            up_refs[e][s] = up[e * count:(e + 1) * count].astype(up_refs[e].dtype)
             owner = lax.rem(place_ref[systems] + e, lanes)
-            low_ref[place_ref[s] * lanes + owner] = last[s][e * count:(e + 1) * count]
+            low_ref[place_ref[s] * lanes + owner] = last[s][e * count:(e + 1) * count].astype(low_ref.dtype)
 
 
 def place_kernel(lanes, place_ref, low_ref, *refs):
@@ -231,7 +212,7 @@
         owner = lax.rem(place_ref[systems * lanes] + lanes - e, lanes)
         for s in range(systems):
             at = owner * systems + s
-            total = up_refs[e][s] + low_ref[place_ref[at] * lanes + owner]
+            total = up_refs[e][s].astype(jnp.float32) + low_ref[place_ref[at] * lanes + owner].astype(jnp.float32)
             out_ref[:, pl.ds(pl.multiple_of(at * width, width), width)] = total.astype(out_ref.dtype)
 
 
@@ -280,10 +261,10 @@
         parts.append(shift(part, -e))
     x = jnp.concatenate(parts, axis=0)
 
-    piece = jax.ShapeDtypeStruct((systems, nrhs_dev, width), jnp.float32)
+    piece = jax.ShapeDtypeStruct((systems, nrhs_dev, width), jnp.bfloat16)
     *up, low = pl.pallas_call(
         functools.partial(pair_kernel, lanes),
-        out_shape=[piece] * lanes + [jax.ShapeDtypeStruct((shards * lanes, nrhs_dev, width), jnp.float32)],
+        out_shape=[piece] * lanes + [jax.ShapeDtypeStruct((shards * lanes, nrhs_dev, width), jnp.bfloat16)],
         in_specs=[smem, vmem, anywhere, anywhere, anywhere],
         out_specs=[vmem] * (lanes + 1),
         scratch_shapes=[

time: 108 us -> 113 us (1.046)
  Pallas kernels: 65.1 us -> 78.1 us
  waiting for transfers between devices: 17.8 us -> 10.4 us
    pallas_call x1, Pallas kernels: 30.5 us -> 37.6 us  [on_device(): pl.pallas_call(own_kernel, out_shape=(jax.ShapeDtypeStruct((systems, 2, w...]
    all_to_all x1, waiting for transfers between devices: 12.6 us -> 5.49 us  [on_device(): lax.all_to_all(tiles[:, :2][slot_of], 'panel', split_axis=0, concat_axis=...]
    pallas_call x1, Pallas kernels: 32.9 us -> 38.9 us  [on_device(): pl.pallas_call(functools.partial(pair_kernel, lanes), out_shape=[piece] *...]
  transfers between devices with their start and end apart: 8 -> 8, of which waited for: 6 -> 6; matrix products, arithmetic and copies ran while one was open for 2% -> 2% of each run, Pallas kernels for 28% -> 33%
where the time goes in v5:
time: 113 us
  Pallas kernels  78.1 us (69%)
  starting transfers between devices  16.2 us (14%)
  waiting for transfers between devices  10.4 us (9%)
  local copies, waits for them, and re-layouts  5.04 us (4%)
  other arithmetic  2.88 us (3%)
    pallas_call x1, Pallas kernels, on_device(): pl.pallas_call(functools.partial(pair_kernel, lanes), out_shape=[piece] *...  38.9 us
    pallas_call x1, Pallas kernels, on_device(): pl.pallas_call(own_kernel, out_shape=(jax.ShapeDtypeStruct((systems, 2, w...  37.6 us
    all_to_all x1, starting transfers between devices, on_device(): lax.all_to_all(tiles[:, :2][slot_of], 'panel', split_axis=0, concat_axis=...  7.41 us
    all_to_all x1, waiting for transfers between devices, on_device(): lax.all_to_all(tiles[:, :2][slot_of], 'panel', split_axis=0, concat_axis=...  5.49 us
    ppermute x6, starting transfers between devices, shift(): lax.ppermute(value, 'rhs', [(i, (i + by) % lanes) for i in range(lanes)])  5.11 us
    all_to_all x1, starting transfers between devices, on_device(): lax.all_to_all(low, ('panel', 'rhs'), split_axis=0, concat_axis=0, tiled=...  3.67 us
    all_to_all x1, waiting for transfers between devices, on_device(): lax.all_to_all(low, ('panel', 'rhs'), split_axis=0, concat_axis=0, tiled=...  2.49 us
    ppermute x6, waiting for transfers between devices, shift(): lax.ppermute(value, 'rhs', [(i, (i + by) % lanes) for i in range(lanes)])  2.41 us
  transfers between devices with their start and end apart: 8, of which 6 were waited for; matrix products, arithmetic and copies ran while one was open for 2% of the time, Pallas kernels for 33%

profile of v5, /device:TPU:0, one launch (start us, length us, event | category | flops | bytes accessed | tf_op | source)
XLA Modules:
  0.0 112.7 jit_solution(5316355763843408382)
XLA Ops:
  0.0 0.9 bitcast_select_fusion
  1.1 0.3 slice-done
  1.4 2.0 %gather_fusion = bf16[8,2,256,256]{3,2,1,0:T(8,128)(2,1)} fusion(bf16[6,2,256,256]{3,2,1,0:T(8,128)(2,1)S(1)} %slice-done, s32[1024]{0:T(1024)S(1)} %pad_clamp_fusion), kind=kCustom, calls=%fused_computation | custom fusion | bytes 4194336 | tf_op jit(solution)/shard_map/gather | solution.py:238
  3.5 7.4 %all-to-all-start = ((bf16[8,2,256,256]{3,2,1,0:T(8,128)(2,1)}), bf16[8,2,256,256]{3,2,1,0:T(8,128)(2,1)S(1)}, u32[]{:S(2)}, u32[]{:S(2)}) async-start(bf16[8,2,256,256]{3,2,1,0:T(8,128)(2,1)} %gather_fusion), calls=%async_computation | async-start | bytes 4194304 | tf_op jit(solution)/shard_map/all_to_all | solution.py:238
  10.9 0.6 dynamic_slice.23.counts_ref
  11.5 37.6 %shard_map.46 = (bf16[6,2,256,256]{3,2,1,0:T(8,128)(2,1)}, bf16[6,3,256,512]{3,2,1,0:T(8,128)(2,1)}) custom-call(s32[6]{0:T(128)} %dynamic_slice.23.counts_ref, bf16[6,5,256,256]{3,2,1,0:T(8,128)(2,1)} %tiles_ref.1), custom_call_target="tpu_custom_call" | custom-call | flops 40000000000 | bytes 8000000 | tf_op jit(solution)/shard_map/pallas_call | solution.py:244
  49.3 1.7 %collective-permute-start = (bf16[4,1536]{1,0:T(4,128)(2,1)S(1)}, bf16[4,1536]{1,0:T(4,128)(2,1)S(1)}, u32[]{:S(2)}, u32[]{:S(2)}) collective-permute-start(bf16[4,1536]{1,0:T(4,128)(2,1)S(1)} %get-tuple-element.26), channel_id=1, source_target_pairs={{0,3},{1,0},{2,1},{3,2},{4,7},{5,4},{6,5},{7,6},{8,11},{9,8},{10,9... | collective-permute-start | bytes 36872 | tf_op jit(solution)/shard_map/ppermute | solution.py:236
  51.0 0.6 pad_add_fusion.1.place_ref
  51.6 0.7 collective-permute-done.2
  52.3 0.7 collective-permute-done.1
  53.0 0.7 pad_maximum_fusion.x_ref
  53.6 5.5 %all-to-all-done.got_ref = bf16[8,2,256,256]{3,2,1,0:T(8,128)(2,1)S(1)} async-done(((bf16[8,2,256,256]{3,2,1,0:T(8,128)(2,1)}), bf16[8,2,256,256]{3,2,1,0:T(8,128)(2,1)S(1)}, u32[]{:S(2)}, u32[]{:S(2)}) %all-to-all-start) | async-done | bytes 2097184 | tf_op jit(solution)/shard_map/all_to_all | solution.py:238
  59.1 1.4 %copy-done = bf16[8,2,256,256]{3,2,1,0:T(8,128)(2,1)} copy-done((bf16[8,2,256,256]{3,2,1,0:T(8,128)(2,1)}, bf16[8,2,256,256]{3,2,1,0:T(8,128)(2,1)S(1)}, u32[]{:S(2)}) %copy-start) | copy-done | bytes 2097176
  60.5 38.9 %shard_map.47 = (bf16[6,4,256]{2,1,0:T(4,128)(2,1)}, bf16[6,4,256]{2,1,0:T(4,128)(2,1)}, bf16[6,4,256]{2,1,0:T(4,128)(2,1)}, bf16[6,4,256]{2,1,0:T(4,128)(2,1)}, bf16[32,4,256]{2,1,0:T(4,128)(2,1)}) custom-call(s32[7]{0:T(128)} %pad_add_fusion.1.place_ref, bf16[16,1536]{1,0:T(8,128)(2,1)} %pad_maximum_fusion.x_ref, ...), custom_call_target="tpu_custom_call" | custom-call | tf_op jit(solution)/shard_map/pallas_call | solution.py:265
  99.4 3.7 %all-to-all-start.1 = ((bf16[32,4,256]{2,1,0:T(4,128)(2,1)}), bf16[32,4,256]{2,1,0:T(4,128)(2,1)S(1)}, u32[]{:S(2)}, u32[]{:S(2)}) async-start(bf16[32,4,256]{2,1,0:T(4,128)(2,1)} %get-tuple-element.18), calls=%async_computation.1 | async-start | bytes 131072 | tf_op jit(solution)/shard_map/all_to_all | solution.py:282
  103.1 0.3 collective-permute-start.3
  103.4 1.7 %collective-permute-start.4 = (bf16[6,4,256]{2,1,0:T(4,128)(2,1)}, bf16[6,4,256]{2,1,0:T(4,128)(2,1)S(1)}, u32[]{:S(2)}, u32[]{:S(2)}) collective-permute-start(bf16[6,4,256]{2,1,0:T(4,128)(2,1)} %get-tuple-element.21), channel_id=1, source_target_pairs={{0,2},{1,3},{2,0},{3,1},{4,6},{5,7},{6,4},{7,5},{8,10},{9,11},{10,... | collective-permute-start | bytes 36872 | tf_op jit(solution)/shard_map/ppermute | solution.py:236
  105.0 1.3 %collective-permute-start.5 = (bf16[6,4,256]{2,1,0:T(4,128)(2,1)}, bf16[6,4,256]{2,1,0:T(4,128)(2,1)S(1)}, u32[]{:S(2)}, u32[]{:S(2)}) collective-permute-start(bf16[6,4,256]{2,1,0:T(4,128)(2,1)} %get-tuple-element.22), channel_id=1, source_target_pairs={{0,3},{1,0},{2,1},{3,2},{4,7},{5,4},{6,5},{7,6},{8,11},{9,8},{10,9... | collective-permute-start | bytes 36872 | tf_op jit(solution)/shard_map/ppermute | solution.py:236
  106.4 0.6 pad_add_fusion.place_ref
  107.0 0.3 collective-permute-done.4.refs_2_
  107.3 0.7 collective-permute-done.5.refs_3_
  108.0 2.5 %all-to-all-done.1.low_ref = bf16[32,4,256]{2,1,0:T(4,128)(2,1)S(1)} async-done(((bf16[32,4,256]{2,1,0:T(4,128)(2,1)}), bf16[32,4,256]{2,1,0:T(4,128)(2,1)S(1)}, u32[]{:S(2)}, u32[]{:S(2)}) %all-to-all-start.1) | async-done | bytes 65568 | tf_op jit(solution)/shard_map/all_to_all | solution.py:282
  110.5 0.6 copy-done.1
  111.1 1.6 %shard_map.48 = bf16[4,6144]{1,0:T(4,128)(2,1)} custom-call(s32[25]{0:T(128)} %pad_add_fusion.place_ref, bf16[32,4,256]{2,1,0:T(4,128)(2,1)} %copy-done.1, bf16[6,4,256]{2,1,0:T(4,128)(2,1)} %get-tuple-element.19.refs_0_, bf16[6,4,256]{2,1,0:T(4,128)(2,1)} %copy-done.3, bf16[6,4,256]{2,1,0:T(4,128)(2,1)} %copy-done.4, bf16[6,4,256]{2,1,0:T(4,128)(2,1)} %copy-done.5), custom_call_target="tpu_custom_call" | custom-call | tf_op jit(solution)/shard_map/pallas_call | solution.py:284
  (22 shorter events, 0.4 us)
Async XLA Ops:
  0.0 1.4 %slice-start = ((bf16[6,5,256,256]{3,2,1,0:T(8,128)(2,1)}), bf16[6,2,256,256]{3,2,1,0:T(8,128)(2,1)S(1)}, s32[]{:S(2)}) async-start(bf16[6,5,256,256]{3,2,1,0:T(8,128)(2,1)} %tiles_ref.1), calls=%async_computation.2 | async-start | bytes 3145728 | tf_op jit(solution)/shard_map/slice | solution.py:238
  3.5 7.4 %copy-start.6 = (s32[192]{0:T(256)S(1)}, s32[192]{0:T(256)}, u32[]{:S(2)}) copy-start(s32[192]{0:T(256)} %param.6) | copy-start | bytes 2308
  3.5 55.7 %all-to-all-start = ((bf16[8,2,256,256]{3,2,1,0:T(8,128)(2,1)}), bf16[8,2,256,256]{3,2,1,0:T(8,128)(2,1)S(1)}, u32[]{:S(2)}, u32[]{:S(2)}) async-start(bf16[8,2,256,256]{3,2,1,0:T(8,128)(2,1)} %gather_fusion), calls=%async_computation | async-start | bytes 4194304 | tf_op jit(solution)/shard_map/all_to_all | solution.py:238
  11.5 37.6 %copy-start.2 = (bf16[4,6144]{1,0:T(4,128)(2,1)S(1)}, bf16[4,6144]{1,0:T(4,128)(2,1)}, u32[]{:S(2)}) copy-start(bf16[4,6144]{1,0:T(4,128)(2,1)} %param.7) | copy-start | bytes 147460
  49.1 3.2 %collective-permute-start.2 = (bf16[4,1536]{1,0:T(4,128)(2,1)S(1)}, bf16[4,1536]{1,0:T(4,128)(2,1)S(1)}, u32[]{:S(2)}, u32[]{:S(2)}) collective-permute-start(bf16[4,1536]{1,0:T(4,128)(2,1)S(1)} %get-tuple-element.24), channel_id=1, source_target_pairs={{0,1},{1,2},{2,3},{3,0},{4,5},{5,6},{6,7},{7,4},{8,9},{9,10},{10,1... | collective-permute-start | bytes 36872 | tf_op jit(solution)/shard_map/ppermute | solution.py:236
  49.2 3.8 %collective-permute-start.1 = (bf16[4,1536]{1,0:T(4,128)(2,1)S(1)}, bf16[4,1536]{1,0:T(4,128)(2,1)S(1)}, u32[]{:S(2)}, u32[]{:S(2)}) collective-permute-start(bf16[4,1536]{1,0:T(4,128)(2,1)S(1)} %get-tuple-element.25), channel_id=1, source_target_pairs={{0,2},{1,3},{2,0},{3,1},{4,6},{5,7},{6,4},{7,5},{8,10},{9,11},{10,... | collective-permute-start | bytes 36872 | tf_op jit(solution)/shard_map/ppermute | solution.py:236
  49.3 3.7 %collective-permute-start = (bf16[4,1536]{1,0:T(4,128)(2,1)S(1)}, bf16[4,1536]{1,0:T(4,128)(2,1)S(1)}, u32[]{:S(2)}, u32[]{:S(2)}) collective-permute-start(bf16[4,1536]{1,0:T(4,128)(2,1)S(1)} %get-tuple-element.26), channel_id=1, source_target_pairs={{0,3},{1,0},{2,1},{3,2},{4,7},{5,4},{6,5},{7,6},{8,11},{9,8},{10,9... | collective-permute-start | bytes 36872 | tf_op jit(solution)/shard_map/ppermute | solution.py:236
  59.1 1.4 %copy-start = (bf16[8,2,256,256]{3,2,1,0:T(8,128)(2,1)}, bf16[8,2,256,256]{3,2,1,0:T(8,128)(2,1)S(1)}, u32[]{:S(2)}) copy-start(bf16[8,2,256,256]{3,2,1,0:T(8,128)(2,1)S(1)} %all-to-all-done.got_ref) | copy-start | bytes 6291460
  99.4 11.1 %all-to-all-start.1 = ((bf16[32,4,256]{2,1,0:T(4,128)(2,1)}), bf16[32,4,256]{2,1,0:T(4,128)(2,1)S(1)}, u32[]{:S(2)}, u32[]{:S(2)}) async-start(bf16[32,4,256]{2,1,0:T(4,128)(2,1)} %get-tuple-element.18), calls=%async_computation.1 | async-start | bytes 131072 | tf_op jit(solution)/shard_map/all_to_all | solution.py:282
  103.1 3.9 %collective-permute-start.3 = (bf16[6,4,256]{2,1,0:T(4,128)(2,1)}, bf16[6,4,256]{2,1,0:T(4,128)(2,1)S(1)}, u32[]{:S(2)}, u32[]{:S(2)}) collective-permute-start(bf16[6,4,256]{2,1,0:T(4,128)(2,1)} %get-tuple-element.20), channel_id=1, source_target_pairs={{0,1},{1,2},{2,3},{3,0},{4,5},{5,6},{6,7},{7,4},{8,9},{9,10},{10,1... | collective-permute-start | bytes 36872 | tf_op jit(solution)/shard_map/ppermute | solution.py:236
  103.4 3.9 %collective-permute-start.4 = (bf16[6,4,256]{2,1,0:T(4,128)(2,1)}, bf16[6,4,256]{2,1,0:T(4,128)(2,1)S(1)}, u32[]{:S(2)}, u32[]{:S(2)}) collective-permute-start(bf16[6,4,256]{2,1,0:T(4,128)(2,1)} %get-tuple-element.21), channel_id=1, source_target_pairs={{0,2},{1,3},{2,0},{3,1},{4,6},{5,7},{6,4},{7,5},{8,10},{9,11},{10,... | collective-permute-start | bytes 36872 | tf_op jit(solution)/shard_map/ppermute | solution.py:236
  105.0 2.9 %collective-permute-start.5 = (bf16[6,4,256]{2,1,0:T(4,128)(2,1)}, bf16[6,4,256]{2,1,0:T(4,128)(2,1)S(1)}, u32[]{:S(2)}, u32[]{:S(2)}) collective-permute-start(bf16[6,4,256]{2,1,0:T(4,128)(2,1)} %get-tuple-element.22), channel_id=1, source_target_pairs={{0,3},{1,0},{2,1},{3,2},{4,7},{5,4},{6,5},{7,6},{8,11},{9,8},{10,9... | collective-permute-start | bytes 36872 | tf_op jit(solution)/shard_map/ppermute | solution.py:236
  107.0 3.5 %copy-start.3 = (bf16[6,4,256]{2,1,0:T(4,128)(2,1)}, bf16[6,4,256]{2,1,0:T(4,128)(2,1)S(1)}, u32[]{:S(2)}) copy-start(bf16[6,4,256]{2,1,0:T(4,128)(2,1)S(1)} %collective-permute-done.3.refs_1_) | copy-start | bytes 36868
  107.3 3.2 %copy-start.4 = (bf16[6,4,256]{2,1,0:T(4,128)(2,1)}, bf16[6,4,256]{2,1,0:T(4,128)(2,1)S(1)}, u32[]{:S(2)}) copy-start(bf16[6,4,256]{2,1,0:T(4,128)(2,1)S(1)} %collective-permute-done.4.refs_2_) | copy-start | bytes 36868
  108.0 2.5 %copy-start.5 = (bf16[6,4,256]{2,1,0:T(4,128)(2,1)}, bf16[6,4,256]{2,1,0:T(4,128)(2,1)S(1)}, u32[]{:S(2)}) copy-start(bf16[6,4,256]{2,1,0:T(4,128)(2,1)S(1)} %collective-permute-done.5.refs_3_) | copy-start | bytes 36868
  110.5 0.6 copy-start.1

commit v6 on v5

--- a/solution.py
+++ b/solution.py
@@ -8,7 +8,6 @@
 
 STEP = 32
 PIVOTS = 4
-TEAM = 3
 NT = (((1,), (1,)), ((), ()))
 NN = (((1,), (0,)), ((), ()))
 TN = (((0,), (0,)), ((), ()))
@@ -41,7 +40,7 @@
     return high[:count] + ((high[count:2 * count] + low[:count]) + (high[2 * count:] + low[count:]))
 
 
-def factor(ref, slab_ref, left_ref, right_ref):
+def factor(ref, slab_ref, past_ref):
     systems, width, _ = ref.shape
     halves = width // 128
     groups = STEP // 8
@@ -55,7 +54,8 @@
     def spread(row):
         return jnp.broadcast_to(row, (8, 128))
 
-    def pivots(slabs):
+    def pivots(slabs, pieces):
+        placed = 0
         for first in range(0, STEP, PIVOTS):
             top, start = first // 8, first % 8
             tall = range(top, groups)
@@ -84,6 +84,9 @@
                         r = spread(x[top][h][at:at + 1, :])
                         for g in tall:
                             x[g][h] = x[g][h] - c[g] * r
+                while placed * STEP < (first + q + 1) * len(pieces):
+                    pieces[placed]()
+                    placed += 1
             if start + PIVOTS == 8:
                 for s, x in enumerate(slabs):
                     scale = inverses[s] * lax.rsqrt(inverses[s])
@@ -92,20 +95,34 @@
 
     for s in range(systems):
         slab_ref[s] = ref[s, 0:STEP]
-        left_ref[s] = jnp.zeros(left_ref.shape[1:], left_ref.dtype)
-        right_ref[s] = jnp.zeros(right_ref.shape[1:], right_ref.dtype)
+        past_ref[s] = jnp.zeros(past_ref.shape[1:], past_ref.dtype)
 
     def block(kb, carry):
         base = pl.multiple_of(kb * STEP, STEP)
         after = pl.multiple_of(jnp.minimum(base + STEP, width - STEP), STEP)
         done = (col_all >= base - STEP) & (col_all < base) & (row_all >= base + STEP)
+        pieces = []
         for s in range(systems):
-            ref[s] = jnp.where(done, 0.0, ref[s]) - dot(left_ref[s], right_ref[s], TN)
+            held = {}
+
+            def prepare(s=s, held=held):
+                p1, p2, p3 = split3(past_ref[s])
+                zero = jnp.zeros_like(p1)
+                m1, m2, m3 = (jnp.where(col_in >= base + STEP, p, zero) for p in (p1, p2, p3))
+                held["left"] = jnp.concatenate([m1, m1, m2, m2, m1, m3], axis=0)
+                held["right"] = jnp.concatenate([p1, p2, p1, p2, p3, p1], axis=0)
+
+            def trail(at, s=s, held=held):
+                rows = slice(at, at + 128)
+                update = dot(held["left"][:, rows], held["right"], TN)
+                ref[s, rows] = jnp.where(done[rows], 0.0, ref[s, rows]) - update
+
+            pieces.append(prepare)
+            pieces.extend(functools.partial(trail, at) for at in range(0, width, 128))
         slabs = []
         for s in range(systems):
             slabs.append([[slab_ref[s, 8 * g:8 * g + 8, 128 * h:128 * h + 128] for h in range(halves)] for g in range(groups)])
-        for s in range(0, systems, TEAM):
-            pivots(slabs[s:s + TEAM])
+        pivots(slabs, pieces)
         for s in range(systems):
             slab = jnp.concatenate([jnp.concatenate(line, axis=1) for line in slabs[s]], axis=0)
             slab = jnp.where((col_in > row_in) & (col_in < STEP), 0.0, slab)
@@ -120,22 +137,14 @@
             slab_ref[s] = jnp.where(col_in >= width - STEP, 0.0, coming) - update
             slab = pltpu.roll(slab, base, 1)
             ref[s, pl.ds(base, STEP), :] = jnp.where(col_in >= base + STEP, 0.0, slab)
-            p1, p2, p3 = split3(slab)
-            zero = jnp.zeros_like(p1)
-            m1, m2, m3 = (jnp.where(col_in >= base + 2 * STEP, p, zero) for p in (p1, p2, p3))
-            left_ref[s] = jnp.concatenate([m1, m1, m2, m2, m1, m3], axis=0)
-            right_ref[s] = jnp.concatenate([p1, p2, p1, p2, p3, p1], axis=0)
+            past_ref[s] = slab
         return carry
 
     lax.fori_loop(0, width // STEP, block, 0)
 
 
 def factor_scratch(systems, width):
-    return [
-        pltpu.VMEM((systems, STEP, width), jnp.float32),
-        pltpu.VMEM((systems, 6 * STEP, width), jnp.bfloat16),
-        pltpu.VMEM((systems, 6 * STEP, width), jnp.bfloat16),
-    ]
+    return [pltpu.VMEM((systems, STEP, width), jnp.float32)] * 2
 
 
 def own_kernel(counts_ref, tiles_ref, w_ref, z_ref, g_ref, *scratch):
@@ -200,7 +209,7 @@
     for s in range(systems):
         up = apply(mid[s], (w_ref[s, 0], w_ref[s, 1]), NN)
         for e in range(lanes):
-            up_refs[e][s] = up[e * count:(e + 1) * count].astype(up_refs[e].dtype)
+            up_refs[e][s] = up[e * count:(e + 1) * count]
             owner = lax.rem(place_ref[systems] + e, lanes)
             low_ref[place_ref[s] * lanes + owner] = last[s][e * count:(e + 1) * count].astype(low_ref.dtype)
 
@@ -212,7 +221,7 @@
         owner = lax.rem(place_ref[systems * lanes] + lanes - e, lanes)
         for s in range(systems):
             at = owner * systems + s
-            total = up_refs[e][s].astype(jnp.float32) + low_ref[place_ref[at] * lanes + owner].astype(jnp.float32)
+            total = up_refs[e][s] + low_ref[place_ref[at] * lanes + owner].astype(jnp.float32)
             out_ref[:, pl.ds(pl.multiple_of(at * width, width), width)] = total.astype(out_ref.dtype)
 
 
@@ -261,7 +270,7 @@
         parts.append(shift(part, -e))
     x = jnp.concatenate(parts, axis=0)
 
-    piece = jax.ShapeDtypeStruct((systems, nrhs_dev, width), jnp.bfloat16)
+    piece = jax.ShapeDtypeStruct((systems, nrhs_dev, width), jnp.float32)
     *up, low = pl.pallas_call(
         functools.partial(pair_kernel, lanes),
         out_shape=[piece] * lanes + [jax.ShapeDtypeStruct((shards * lanes, nrhs_dev, width), jnp.bfloat16)],

time: 113 us -> 108 us (0.956)
  Pallas kernels: 78.1 us -> 67.8 us
  waiting for transfers between devices: 10.4 us -> 15.9 us
    pallas_call x1, Pallas kernels: 37.6 us -> 32.1 us  [on_device(): pl.pallas_call(own_kernel, out_shape=(jax.ShapeDtypeStruct((systems, 2, w...]
    all_to_all x1, waiting for transfers between devices: 5.49 us -> 11 us  [on_device(): lax.all_to_all(tiles[:, :2][slot_of], 'panel', split_axis=0, concat_axis=...]
    pallas_call x1, Pallas kernels: 38.9 us -> 34.1 us  [on_device(): pl.pallas_call(functools.partial(pair_kernel, lanes), out_shape=[piece] *...]
  transfers between devices with their start and end apart: 8 -> 8, of which waited for: 6 -> 6; matrix products, arithmetic and copies ran while one was open for 2% -> 2% of each run, Pallas kernels for 33% -> 30%
where the time goes in v6:
time: 108 us
  Pallas kernels  67.8 us (63%)
  starting transfers between devices  16.2 us (15%)
  waiting for transfers between devices  15.9 us (15%)
  local copies, waits for them, and re-layouts  5.04 us (5%)
  other arithmetic  2.93 us (3%)
    pallas_call x1, Pallas kernels, on_device(): pl.pallas_call(functools.partial(pair_kernel, lanes), out_shape=[piece] *...  34.1 us
    pallas_call x1, Pallas kernels, on_device(): pl.pallas_call(own_kernel, out_shape=(jax.ShapeDtypeStruct((systems, 2, w...  32.1 us
    all_to_all x1, waiting for transfers between devices, on_device(): lax.all_to_all(tiles[:, :2][slot_of], 'panel', split_axis=0, concat_axis=...  11 us
    all_to_all x1, starting transfers between devices, on_device(): lax.all_to_all(tiles[:, :2][slot_of], 'panel', split_axis=0, concat_axis=...  7.41 us
    ppermute x6, starting transfers between devices, shift(): lax.ppermute(value, 'rhs', [(i, (i + by) % lanes) for i in range(lanes)])  5.11 us
    all_to_all x1, starting transfers between devices, on_device(): lax.all_to_all(low, ('panel', 'rhs'), split_axis=0, concat_axis=0, tiled=...  3.66 us
    ppermute x6, waiting for transfers between devices, shift(): lax.ppermute(value, 'rhs', [(i, (i + by) % lanes) for i in range(lanes)])  2.48 us
    all_to_all x1, waiting for transfers between devices, on_device(): lax.all_to_all(low, ('panel', 'rhs'), split_axis=0, concat_axis=0, tiled=...  2.38 us
  transfers between devices with their start and end apart: 8, of which 6 were waited for; matrix products, arithmetic and copies ran while one was open for 2% of the time, Pallas kernels for 30%

profile of v6, /device:TPU:0, one launch (start us, length us, event | category | flops | bytes accessed | tf_op | source)
XLA Modules:
  0.0 107.9 jit_solution(6698729073430933138)
XLA Ops:
  0.0 0.9 bitcast_select_fusion
  1.1 0.3 slice-done
  1.4 2.0 %gather_fusion = bf16[8,2,256,256]{3,2,1,0:T(8,128)(2,1)} fusion(bf16[6,2,256,256]{3,2,1,0:T(8,128)(2,1)S(1)} %slice-done, s32[1024]{0:T(1024)S(1)} %pad_clamp_fusion), kind=kCustom, calls=%fused_computation | custom fusion | bytes 4194336 | tf_op jit(solution)/shard_map/gather | solution.py:247
  3.5 7.4 %all-to-all-start = ((bf16[8,2,256,256]{3,2,1,0:T(8,128)(2,1)}), bf16[8,2,256,256]{3,2,1,0:T(8,128)(2,1)S(1)}, u32[]{:S(2)}, u32[]{:S(2)}) async-start(bf16[8,2,256,256]{3,2,1,0:T(8,128)(2,1)} %gather_fusion), calls=%async_computation | async-start | bytes 4194304 | tf_op jit(solution)/shard_map/all_to_all | solution.py:247
  10.9 0.6 dynamic_slice.23.counts_ref
  11.5 32.1 %shard_map.46 = (bf16[6,2,256,256]{3,2,1,0:T(8,128)(2,1)}, bf16[6,3,256,512]{3,2,1,0:T(8,128)(2,1)}) custom-call(s32[6]{0:T(128)} %dynamic_slice.23.counts_ref, bf16[6,5,256,256]{3,2,1,0:T(8,128)(2,1)} %tiles_ref.1), custom_call_target="tpu_custom_call" | custom-call | flops 40000000000 | bytes 8000000 | tf_op jit(solution)/shard_map/pallas_call | solution.py:253
  43.8 1.7 %collective-permute-start = (bf16[4,1536]{1,0:T(4,128)(2,1)S(1)}, bf16[4,1536]{1,0:T(4,128)(2,1)S(1)}, u32[]{:S(2)}, u32[]{:S(2)}) collective-permute-start(bf16[4,1536]{1,0:T(4,128)(2,1)S(1)} %get-tuple-element.26), channel_id=1, source_target_pairs={{0,3},{1,0},{2,1},{3,2},{4,7},{5,4},{6,5},{7,6},{8,11},{9,8},{10,9... | collective-permute-start | bytes 36872 | tf_op jit(solution)/shard_map/ppermute | solution.py:245
  45.5 0.6 pad_add_fusion.1.place_ref
  46.1 0.7 collective-permute-done.2
  46.8 0.7 collective-permute-done.1
  47.4 0.7 pad_maximum_fusion.x_ref
  48.1 11.0 %all-to-all-done.got_ref = bf16[8,2,256,256]{3,2,1,0:T(8,128)(2,1)S(1)} async-done(((bf16[8,2,256,256]{3,2,1,0:T(8,128)(2,1)}), bf16[8,2,256,256]{3,2,1,0:T(8,128)(2,1)S(1)}, u32[]{:S(2)}, u32[]{:S(2)}) %all-to-all-start) | async-done | bytes 2097184 | tf_op jit(solution)/shard_map/all_to_all | solution.py:247
  59.1 1.4 %copy-done = bf16[8,2,256,256]{3,2,1,0:T(8,128)(2,1)} copy-done((bf16[8,2,256,256]{3,2,1,0:T(8,128)(2,1)}, bf16[8,2,256,256]{3,2,1,0:T(8,128)(2,1)S(1)}, u32[]{:S(2)}) %copy-start) | copy-done | bytes 2097176
  60.5 34.1 %shard_map.47 = (f32[6,4,256]{2,1,0:T(4,128)}, f32[6,4,256]{2,1,0:T(4,128)}, f32[6,4,256]{2,1,0:T(4,128)}, f32[6,4,256]{2,1,0:T(4,128)}, bf16[32,4,256]{2,1,0:T(4,128)(2,1)}) custom-call(s32[7]{0:T(128)} %pad_add_fusion.1.place_ref, bf16[16,1536]{1,0:T(8,128)(2,1)} %pad_maximum_fusion.x_ref, bf16[6,2,256,256]{3,2,1,0:T(8,128)(2,1)} %get-tuple-element.16.w_any, ...), custom_call_target="tpu_custom_call" | custom-call | tf_op jit(solution)/shard_map/pallas_call | solution.py:274
  94.6 3.7 %all-to-all-start.1 = ((bf16[32,4,256]{2,1,0:T(4,128)(2,1)}), bf16[32,4,256]{2,1,0:T(4,128)(2,1)S(1)}, u32[]{:S(2)}, u32[]{:S(2)}) async-start(bf16[32,4,256]{2,1,0:T(4,128)(2,1)} %get-tuple-element.18), calls=%async_computation.1 | async-start | bytes 131072 | tf_op jit(solution)/shard_map/all_to_all | solution.py:291
  98.2 0.3 collective-permute-start.3
  98.5 1.7 %collective-permute-start.4 = (f32[6,4,256]{2,1,0:T(4,128)}, f32[6,4,256]{2,1,0:T(4,128)S(1)}, u32[]{:S(2)}, u32[]{:S(2)}) collective-permute-start(f32[6,4,256]{2,1,0:T(4,128)} %get-tuple-element.21), channel_id=1, source_target_pairs={{0,2},{1,3},{2,0},{3,1},{4,6},{5,7},{6,4},{7,5},{8,10},{9,11},{10,... | collective-permute-start | bytes 73736 | tf_op jit(solution)/shard_map/ppermute | solution.py:245
  100.2 1.3 %collective-permute-start.5 = (f32[6,4,256]{2,1,0:T(4,128)}, f32[6,4,256]{2,1,0:T(4,128)S(1)}, u32[]{:S(2)}, u32[]{:S(2)}) collective-permute-start(f32[6,4,256]{2,1,0:T(4,128)} %get-tuple-element.22), channel_id=1, source_target_pairs={{0,3},{1,0},{2,1},{3,2},{4,7},{5,4},{6,5},{7,6},{8,11},{9,8},{10,9... | collective-permute-start | bytes 73736 | tf_op jit(solution)/shard_map/ppermute | solution.py:245
  101.5 0.6 pad_add_fusion.place_ref
  102.1 0.4 collective-permute-done.4.refs_2_
  102.6 0.7 collective-permute-done.5.refs_3_
  103.3 2.4 %all-to-all-done.1.low_ref = bf16[32,4,256]{2,1,0:T(4,128)(2,1)S(1)} async-done(((bf16[32,4,256]{2,1,0:T(4,128)(2,1)}), bf16[32,4,256]{2,1,0:T(4,128)(2,1)S(1)}, u32[]{:S(2)}, u32[]{:S(2)}) %all-to-all-start.1) | async-done | bytes 65568 | tf_op jit(solution)/shard_map/all_to_all | solution.py:291
  105.7 0.6 copy-done.1
  106.3 1.6 %shard_map.48 = bf16[4,6144]{1,0:T(4,128)(2,1)} custom-call(s32[25]{0:T(128)} %pad_add_fusion.place_ref, bf16[32,4,256]{2,1,0:T(4,128)(2,1)} %copy-done.1, f32[6,4,256]{2,1,0:T(4,128)} %get-tuple-element.19.refs_0_, f32[6,4,256]{2,1,0:T(4,128)} %copy-done.3, f32[6,4,256]{2,1,0:T(4,128)} %copy-done.4, f32[6,4,256]{2,1,0:T(4,128)} %copy-done.5), custom_call_target="tpu_custom_call" | custom-call | tf_op jit(solution)/shard_map/pallas_call | solution.py:293
  (22 shorter events, 0.4 us)
Async XLA Ops:
  0.0 1.4 %slice-start = ((bf16[6,5,256,256]{3,2,1,0:T(8,128)(2,1)}), bf16[6,2,256,256]{3,2,1,0:T(8,128)(2,1)S(1)}, s32[]{:S(2)}) async-start(bf16[6,5,256,256]{3,2,1,0:T(8,128)(2,1)} %tiles_ref.1), calls=%async_computation.2 | async-start | bytes 3145728 | tf_op jit(solution)/shard_map/slice | solution.py:247
  3.5 7.4 %copy-start.6 = (s32[192]{0:T(256)S(1)}, s32[192]{0:T(256)}, u32[]{:S(2)}) copy-start(s32[192]{0:T(256)} %param.6) | copy-start | bytes 2308
  3.5 55.7 %all-to-all-start = ((bf16[8,2,256,256]{3,2,1,0:T(8,128)(2,1)}), bf16[8,2,256,256]{3,2,1,0:T(8,128)(2,1)S(1)}, u32[]{:S(2)}, u32[]{:S(2)}) async-start(bf16[8,2,256,256]{3,2,1,0:T(8,128)(2,1)} %gather_fusion), calls=%async_computation | async-start | bytes 4194304 | tf_op jit(solution)/shard_map/all_to_all | solution.py:247
  11.5 32.1 %copy-start.2 = (bf16[4,6144]{1,0:T(4,128)(2,1)S(1)}, bf16[4,6144]{1,0:T(4,128)(2,1)}, u32[]{:S(2)}) copy-start(bf16[4,6144]{1,0:T(4,128)(2,1)} %param.7) | copy-start | bytes 147460
  43.6 3.2 %collective-permute-start.2 = (bf16[4,1536]{1,0:T(4,128)(2,1)S(1)}, bf16[4,1536]{1,0:T(4,128)(2,1)S(1)}, u32[]{:S(2)}, u32[]{:S(2)}) collective-permute-start(bf16[4,1536]{1,0:T(4,128)(2,1)S(1)} %get-tuple-element.24), channel_id=1, source_target_pairs={{0,1},{1,2},{2,3},{3,0},{4,5},{5,6},{6,7},{7,4},{8,9},{9,10},{10,1... | collective-permute-start | bytes 36872 | tf_op jit(solution)/shard_map/ppermute | solution.py:245
  43.7 3.8 %collective-permute-start.1 = (bf16[4,1536]{1,0:T(4,128)(2,1)S(1)}, bf16[4,1536]{1,0:T(4,128)(2,1)S(1)}, u32[]{:S(2)}, u32[]{:S(2)}) collective-permute-start(bf16[4,1536]{1,0:T(4,128)(2,1)S(1)} %get-tuple-element.25), channel_id=1, source_target_pairs={{0,2},{1,3},{2,0},{3,1},{4,6},{5,7},{6,4},{7,5},{8,10},{9,11},{10,... | collective-permute-start | bytes 36872 | tf_op jit(solution)/shard_map/ppermute | solution.py:245
  43.8 3.7 %collective-permute-start = (bf16[4,1536]{1,0:T(4,128)(2,1)S(1)}, bf16[4,1536]{1,0:T(4,128)(2,1)S(1)}, u32[]{:S(2)}, u32[]{:S(2)}) collective-permute-start(bf16[4,1536]{1,0:T(4,128)(2,1)S(1)} %get-tuple-element.26), channel_id=1, source_target_pairs={{0,3},{1,0},{2,1},{3,2},{4,7},{5,4},{6,5},{7,6},{8,11},{9,8},{10,9... | collective-permute-start | bytes 36872 | tf_op jit(solution)/shard_map/ppermute | solution.py:245
  59.1 1.4 %copy-start = (bf16[8,2,256,256]{3,2,1,0:T(8,128)(2,1)}, bf16[8,2,256,256]{3,2,1,0:T(8,128)(2,1)S(1)}, u32[]{:S(2)}) copy-start(bf16[8,2,256,256]{3,2,1,0:T(8,128)(2,1)S(1)} %all-to-all-done.got_ref) | copy-start | bytes 6291460
  94.6 11.1 %all-to-all-start.1 = ((bf16[32,4,256]{2,1,0:T(4,128)(2,1)}), bf16[32,4,256]{2,1,0:T(4,128)(2,1)S(1)}, u32[]{:S(2)}, u32[]{:S(2)}) async-start(bf16[32,4,256]{2,1,0:T(4,128)(2,1)} %get-tuple-element.18), calls=%async_computation.1 | async-start | bytes 131072 | tf_op jit(solution)/shard_map/all_to_all | solution.py:291
  98.2 3.9 %collective-permute-start.3 = (f32[6,4,256]{2,1,0:T(4,128)}, f32[6,4,256]{2,1,0:T(4,128)S(1)}, u32[]{:S(2)}, u32[]{:S(2)}) collective-permute-start(f32[6,4,256]{2,1,0:T(4,128)} %get-tuple-element.20), channel_id=1, source_target_pairs={{0,1},{1,2},{2,3},{3,0},{4,5},{5,6},{6,7},{7,4},{8,9},{9,10},{10,1... | collective-permute-start | bytes 73736 | tf_op jit(solution)/shard_map/ppermute | solution.py:245
  98.5 4.0 %collective-permute-start.4 = (f32[6,4,256]{2,1,0:T(4,128)}, f32[6,4,256]{2,1,0:T(4,128)S(1)}, u32[]{:S(2)}, u32[]{:S(2)}) collective-permute-start(f32[6,4,256]{2,1,0:T(4,128)} %get-tuple-element.21), channel_id=1, source_target_pairs={{0,2},{1,3},{2,0},{3,1},{4,6},{5,7},{6,4},{7,5},{8,10},{9,11},{10,... | collective-permute-start | bytes 73736 | tf_op jit(solution)/shard_map/ppermute | solution.py:245
  100.2 3.1 %collective-permute-start.5 = (f32[6,4,256]{2,1,0:T(4,128)}, f32[6,4,256]{2,1,0:T(4,128)S(1)}, u32[]{:S(2)}, u32[]{:S(2)}) collective-permute-start(f32[6,4,256]{2,1,0:T(4,128)} %get-tuple-element.22), channel_id=1, source_target_pairs={{0,3},{1,0},{2,1},{3,2},{4,7},{5,4},{6,5},{7,6},{8,11},{9,8},{10,9... | collective-permute-start | bytes 73736 | tf_op jit(solution)/shard_map/ppermute | solution.py:245
  102.1 3.5 %copy-start.3 = (f32[6,4,256]{2,1,0:T(4,128)}, f32[6,4,256]{2,1,0:T(4,128)S(1)}, u32[]{:S(2)}) copy-start(f32[6,4,256]{2,1,0:T(4,128)S(1)} %collective-permute-done.3.refs_1_) | copy-start | bytes 73732
  102.6 3.1 %copy-start.4 = (f32[6,4,256]{2,1,0:T(4,128)}, f32[6,4,256]{2,1,0:T(4,128)S(1)}, u32[]{:S(2)}) copy-start(f32[6,4,256]{2,1,0:T(4,128)S(1)} %collective-permute-done.4.refs_2_) | copy-start | bytes 73732
  103.3 2.4 %copy-start.5 = (f32[6,4,256]{2,1,0:T(4,128)}, f32[6,4,256]{2,1,0:T(4,128)S(1)}, u32[]{:S(2)}) copy-start(f32[6,4,256]{2,1,0:T(4,128)S(1)} %collective-permute-done.5.refs_3_) | copy-start | bytes 73732
  105.6 0.6 copy-start.1

commit v7 on v6

--- a/solution.py
+++ b/solution.py
@@ -42,35 +42,56 @@
 
 def factor(ref, slab_ref, past_ref):
     systems, width, _ = ref.shape
-    halves = width // 128
+    teams, height, _ = slab_ref.shape
+    team = height // STEP
     groups = STEP // 8
     lane = lax.broadcasted_iota(jnp.int32, (8, 128), 1)
     sub = lax.broadcasted_iota(jnp.int32, (8, 128), 0)
-    row_in = lax.broadcasted_iota(jnp.int32, (STEP, width), 0)
+    member = lane // STEP
+    place = lane % STEP
     col_in = lax.broadcasted_iota(jnp.int32, (STEP, width), 1)
     row_all = lax.broadcasted_iota(jnp.int32, (width, width), 0)
     col_all = lax.broadcasted_iota(jnp.int32, (width, width), 1)
+    row_team = lax.broadcasted_iota(jnp.int32, (height, width), 0)
+    col_team = lax.broadcasted_iota(jnp.int32, (height, width), 1)
+    row_diag = lax.broadcasted_iota(jnp.int32, (height, 128), 0)
+    col_diag = lax.broadcasted_iota(jnp.int32, (height, 128), 1)
+    same = row_diag // STEP == col_diag // STEP
+    lower = same & (col_diag <= row_diag)
 
     def spread(row):
         return jnp.broadcast_to(row, (8, 128))
 
-    def pivots(slabs, pieces):
+    def wide(parts):
+        one, two, three = parts
+        return jnp.concatenate([one, one, two, two, one, three], axis=1)
+
+    def deep(parts):
+        if height < 128:
+            filler = jnp.zeros((128 - height, width), jnp.bfloat16)
+            parts = [jnp.concatenate([part, filler], axis=0) for part in parts]
+        one, two, three = parts
+        return jnp.concatenate([one, two, one, two, three, one], axis=0)
+
+    def pivots(packs, pieces):
         placed = 0
         for first in range(0, STEP, PIVOTS):
             top, start = first // 8, first % 8
             tall = range(top, groups)
-            own = (lane >= first) & (lane < first + PIVOTS)
-            one = jnp.where(lane - 8 * top == sub, 1.0, 0.0)
+            own = (place >= first) & (place < first + PIVOTS)
+            one = jnp.where(place - 8 * top == sub, 1.0, 0.0)
             if start == 0:
-                inverses = [None] * len(slabs)
+                inverses = [None] * len(packs)
             columns = []
-            for x in slabs:
-                columns.append([{g: spread(x[g][0][:, first + q:first + q + 1]) for g in tall} for q in range(PIVOTS)])
+            for x in packs:
+                columns.append([
+                    {g: jnp.take_along_axis(x[g], lane - place + (first + q), axis=1) for g in tall} for q in range(PIVOTS)
+                ])
                 for g in tall:
-                    x[g][0] = jnp.where(own, one if g == top else 0.0, x[g][0])
+                    x[g] = jnp.where(own, one if g == top else 0.0, x[g])
             for q in range(PIVOTS):
                 at = start + q
-                for s, x in enumerate(slabs):
+                for s, x in enumerate(packs):
                     cols = columns[s]
                     inverse = pl.reciprocal(spread(cols[q][top][at:at + 1, :]), approx=True)
                     inverses[s] = inverse if at == 0 else jnp.where(sub >= at, inverse, inverses[s])
@@ -80,22 +101,20 @@
                         for g in tall:
                             cols[later][g] = cols[later][g] - c[g] * m
                     c[top] = jnp.where(sub > at, c[top], 0.0)
-                    for h in range(halves):
-                        r = spread(x[top][h][at:at + 1, :])
-                        for g in tall:
-                            x[g][h] = x[g][h] - c[g] * r
+                    r = spread(x[top][at:at + 1, :])
+                    for g in tall:
+                        x[g] = x[g] - c[g] * r
                 while placed * STEP < (first + q + 1) * len(pieces):
                     pieces[placed]()
                     placed += 1
             if start + PIVOTS == 8:
-                for s, x in enumerate(slabs):
-                    scale = inverses[s] * lax.rsqrt(inverses[s])
-                    for h in range(halves):
-                        x[top][h] = x[top][h] * scale
-
-    for s in range(systems):
-        slab_ref[s] = ref[s, 0:STEP]
-        past_ref[s] = jnp.zeros(past_ref.shape[1:], past_ref.dtype)
+                for s, x in enumerate(packs):
+                    x[top] = x[top] * (inverses[s] * lax.rsqrt(inverses[s]))
+
+    for t in range(teams):
+        for i in range(team):
+            slab_ref[t, i * STEP:(i + 1) * STEP] = ref[t * team + i, 0:STEP]
+        past_ref[t] = jnp.zeros(past_ref.shape[1:], past_ref.dtype)
 
     def block(kb, carry):
         base = pl.multiple_of(kb * STEP, STEP)
@@ -106,7 +125,8 @@
             held = {}
 
             def prepare(s=s, held=held):
-                p1, p2, p3 = split3(past_ref[s])
+                i = s % team
+                p1, p2, p3 = split3(past_ref[s // team, i * STEP:(i + 1) * STEP])
                 zero = jnp.zeros_like(p1)
                 m1, m2, m3 = (jnp.where(col_in >= base + STEP, p, zero) for p in (p1, p2, p3))
                 held["left"] = jnp.concatenate([m1, m1, m2, m2, m1, m3], axis=0)
@@ -119,32 +139,53 @@
 
             pieces.append(prepare)
             pieces.extend(functools.partial(trail, at) for at in range(0, width, 128))
-        slabs = []
-        for s in range(systems):
-            slabs.append([[slab_ref[s, 8 * g:8 * g + 8, 128 * h:128 * h + 128] for h in range(halves)] for g in range(groups)])
-        pivots(slabs, pieces)
-        for s in range(systems):
-            slab = jnp.concatenate([jnp.concatenate(line, axis=1) for line in slabs[s]], axis=0)
-            slab = jnp.where((col_in > row_in) & (col_in < STEP), 0.0, slab)
-            n1, n2, n3 = split3(slab[:, STEP:2 * STEP])
-            q1, q2, q3 = split3(pltpu.roll(slab, width - STEP, 1))
-            update = dot(
-                jnp.concatenate([n1, n1, n2, n2, n1, n3], axis=0),
-                jnp.concatenate([q1, q2, q1, q2, q3, q1], axis=0),
-                TN,
-            )
-            coming = pltpu.roll(ref[s, pl.ds(after, STEP), :], width - after, 1)
-            slab_ref[s] = jnp.where(col_in >= width - STEP, 0.0, coming) - update
+        packs = []
+        for t in range(teams):
+            pack = []
+            for g in range(groups):
+                x = jnp.where(place - 8 * g == sub, 1.0, 0.0)
+                for i in range(team):
+                    piece = slab_ref[t, i * STEP + 8 * g:i * STEP + 8 * g + 8, 0:128]
+                    if i > 0:
+                        piece = pltpu.roll(piece, i * STEP, 1)
+                    x = jnp.where(member == i, piece, x)
+                pack.append(x)
+            packs.append(pack)
+        sides = []
+        for t in range(teams):
+            ident = jnp.where(col_team == row_team % STEP, 1.0, 0.0)
+            sides.append(deep(split3(jnp.where(col_team < STEP, ident, slab_ref[t]))))
+        pivots(packs, pieces)
+        for t in range(teams):
+            inner = jnp.concatenate(packs[t], axis=0)
+            inner = jnp.where(lower, jnp.concatenate([inner] * team, axis=0), 0.0)
+            slab = dot(wide(split3(inner)), sides[t], NN)
+            ahead = []
+            for i in range(team):
+                piece = slab[i * STEP:(i + 1) * STEP, 0:128]
+                if i != 1:
+                    piece = pltpu.roll(piece, (i - 1) * STEP % 128, 1)
+                ahead.append(piece)
+            ahead = jnp.where(same, jnp.concatenate(ahead, axis=0), 0.0)
+            if height < 128:
+                ahead = jnp.concatenate([ahead, jnp.zeros((128 - height, 128), jnp.float32)], axis=0)
+            ahead = wide(split3(ahead.T[:height]))
+            update = dot(ahead, deep(split3(pltpu.roll(slab, width - STEP, 1))), NN)
+            coming = [pltpu.roll(ref[t * team + i, pl.ds(after, STEP), :], width - after, 1) for i in range(team)]
+            slab_ref[t] = jnp.where(col_team >= width - STEP, 0.0, jnp.concatenate(coming, axis=0)) - update
             slab = pltpu.roll(slab, base, 1)
-            ref[s, pl.ds(base, STEP), :] = jnp.where(col_in >= base + STEP, 0.0, slab)
-            past_ref[s] = slab
+            past_ref[t] = slab
+            for i in range(team):
+                own_rows = slab[i * STEP:(i + 1) * STEP]
+                ref[t * team + i, pl.ds(base, STEP), :] = jnp.where(col_in >= base + STEP, 0.0, own_rows)
         return carry
 
     lax.fori_loop(0, width // STEP, block, 0)
 
 
 def factor_scratch(systems, width):
-    return [pltpu.VMEM((systems, STEP, width), jnp.float32)] * 2
+    team = max(n for n in range(1, 128 // STEP + 1) if systems % n == 0)
+    return [pltpu.VMEM((systems // team, team * STEP, width), jnp.float32)] * 2
 
 
 def own_kernel(counts_ref, tiles_ref, w_ref, z_ref, g_ref, *scratch):

time: 108 us -> 102 us (0.944)
  Pallas kernels: 67.8 us -> 52.9 us
  waiting for transfers between devices: 15.9 us -> 20.9 us
  starting transfers between devices: 16.2 us -> 19.5 us
    pallas_call x1, Pallas kernels: 32.1 us -> 23.7 us  [on_device(): pl.pallas_call(own_kernel, out_shape=(jax.ShapeDtypeStruct((systems, 2, w...]
    pallas_call x1, Pallas kernels: 34.1 us -> 27.6 us  [on_device(): pl.pallas_call(functools.partial(pair_kernel, lanes), out_shape=[piece] *...]
    all_to_all x1, waiting for transfers between devices: 11 us -> 16.7 us  [on_device(): lax.all_to_all(tiles[:, :2][slot_of], 'panel', split_axis=0, concat_axis=...]
    ppermute x6, starting transfers between devices: 5.11 us -> 8.48 us  [shift(): lax.ppermute(value, 'rhs', [(i, (i + by) % lanes) for i in range(lanes)])]
  transfers between devices with their start and end apart: 8 -> 8, of which waited for: 6 -> 5; matrix products, arithmetic and copies ran while one was open for 2% -> 2% of each run, Pallas kernels for 30% -> 23%
where the time goes in v7:
time: 102 us; the launch traced here: 101 us
  Pallas kernels  52.9 us (52%)
  waiting for transfers between devices  20.9 us (20%)
  starting transfers between devices  19.5 us (19%)
  local copies, waits for them, and re-layouts  5.04 us (5%)
  other arithmetic  2.92 us (3%)
    pallas_call x1, Pallas kernels, on_device(): pl.pallas_call(functools.partial(pair_kernel, lanes), out_shape=[piece] *...  27.6 us
    pallas_call x1, Pallas kernels, on_device(): pl.pallas_call(own_kernel, out_shape=(jax.ShapeDtypeStruct((systems, 2, w...  23.7 us
    all_to_all x1, waiting for transfers between devices, on_device(): lax.all_to_all(tiles[:, :2][slot_of], 'panel', split_axis=0, concat_axis=...  16.7 us
    ppermute x6, starting transfers between devices, shift(): lax.ppermute(value, 'rhs', [(i, (i + by) % lanes) for i in range(lanes)])  8.48 us
    all_to_all x1, starting transfers between devices, on_device(): lax.all_to_all(tiles[:, :2][slot_of], 'panel', split_axis=0, concat_axis=...  7.41 us
    all_to_all x1, starting transfers between devices, on_device(): lax.all_to_all(low, ('panel', 'rhs'), split_axis=0, concat_axis=0, tiled=...  3.65 us
    all_to_all x1, waiting for transfers between devices, on_device(): lax.all_to_all(low, ('panel', 'rhs'), split_axis=0, concat_axis=0, tiled=...  2.38 us
    gather x1, local copies, waits for them, and re-layouts, on_device(): tiles[:, :2][slot_of]  2.04 us
  transfers between devices with their start and end apart: 8, of which 5 were waited for; matrix products, arithmetic and copies ran while one was open for 2% of the time, Pallas kernels for 23%

profile of v7, /device:TPU:0, one launch (start us, length us, event | category | flops | bytes accessed | tf_op | source)
XLA Modules:
  0.0 101.4 jit_solution(7749346625105336092)
XLA Ops:
  0.0 0.9 bitcast_select_fusion
  1.1 0.3 slice-done
  1.4 2.0 %gather_fusion = bf16[8,2,256,256]{3,2,1,0:T(8,128)(2,1)} fusion(bf16[6,2,256,256]{3,2,1,0:T(8,128)(2,1)S(1)} %slice-done, s32[1024]{0:T(1024)S(1)} %pad_clamp_fusion), kind=kCustom, calls=%fused_computation | custom fusion | bytes 4194336 | tf_op jit(solution)/shard_map/gather | solution.py:288
  3.5 7.4 %all-to-all-start = ((bf16[8,2,256,256]{3,2,1,0:T(8,128)(2,1)}), bf16[8,2,256,256]{3,2,1,0:T(8,128)(2,1)S(1)}, u32[]{:S(2)}, u32[]{:S(2)}) async-start(bf16[8,2,256,256]{3,2,1,0:T(8,128)(2,1)} %gather_fusion), calls=%async_computation | async-start | bytes 4194304 | tf_op jit(solution)/shard_map/all_to_all | solution.py:288
  10.9 0.6 dynamic_slice.23.counts_ref
  11.5 23.7 %shard_map.46 = (bf16[6,2,256,256]{3,2,1,0:T(8,128)(2,1)}, bf16[6,3,256,512]{3,2,1,0:T(8,128)(2,1)}) custom-call(s32[6]{0:T(128)} %dynamic_slice.23.counts_ref, bf16[6,5,256,256]{3,2,1,0:T(8,128)(2,1)} %tiles_ref.1), custom_call_target="tpu_custom_call" | custom-call | flops 40000000000 | bytes 8000000 | tf_op jit(solution)/shard_map/pallas_call | solution.py:294
  35.4 3.6 %collective-permute-start.1 = (bf16[4,1536]{1,0:T(4,128)(2,1)S(1)}, bf16[4,1536]{1,0:T(4,128)(2,1)S(1)}, u32[]{:S(2)}, u32[]{:S(2)}) collective-permute-start(bf16[4,1536]{1,0:T(4,128)(2,1)S(1)} %get-tuple-element.25), channel_id=1, source_target_pairs={{0,2},{1,3},{2,0},{3,1},{4,6},{5,7},{6,4},{7,5},{8,10},{9,11},{10,... | collective-permute-start | bytes 36872 | tf_op jit(solution)/shard_map/ppermute | solution.py:286
  39.0 1.4 %collective-permute-start = (bf16[4,1536]{1,0:T(4,128)(2,1)S(1)}, bf16[4,1536]{1,0:T(4,128)(2,1)S(1)}, u32[]{:S(2)}, u32[]{:S(2)}) collective-permute-start(bf16[4,1536]{1,0:T(4,128)(2,1)S(1)} %get-tuple-element.26), channel_id=1, source_target_pairs={{0,3},{1,0},{2,1},{3,2},{4,7},{5,4},{6,5},{7,6},{8,11},{9,8},{10,9... | collective-permute-start | bytes 36872 | tf_op jit(solution)/shard_map/ppermute | solution.py:286
  40.4 0.6 pad_add_fusion.1.place_ref
  41.0 0.8 collective-permute-done
  41.8 0.7 pad_maximum_fusion.x_ref
  42.4 16.7 %all-to-all-done.got_ref = bf16[8,2,256,256]{3,2,1,0:T(8,128)(2,1)S(1)} async-done(((bf16[8,2,256,256]{3,2,1,0:T(8,128)(2,1)}), bf16[8,2,256,256]{3,2,1,0:T(8,128)(2,1)S(1)}, u32[]{:S(2)}, u32[]{:S(2)}) %all-to-all-start) | async-done | bytes 2097184 | tf_op jit(solution)/shard_map/all_to_all | solution.py:288
  59.1 1.4 %copy-done = bf16[8,2,256,256]{3,2,1,0:T(8,128)(2,1)} copy-done((bf16[8,2,256,256]{3,2,1,0:T(8,128)(2,1)}, bf16[8,2,256,256]{3,2,1,0:T(8,128)(2,1)S(1)}, u32[]{:S(2)}) %copy-start) | copy-done | bytes 2097176
  60.5 27.6 %shard_map.47 = (f32[6,4,256]{2,1,0:T(4,128)}, f32[6,4,256]{2,1,0:T(4,128)}, f32[6,4,256]{2,1,0:T(4,128)}, f32[6,4,256]{2,1,0:T(4,128)}, bf16[32,4,256]{2,1,0:T(4,128)(2,1)}) custom-call(s32[7]{0:T(128)} %pad_add_fusion.1.place_ref, bf16[16,1536]{1,0:T(8,128)(2,1)} %pad_maximum_fusion.x_ref, bf16[6,2,256,256]{3,2,1,0:T(8,128)(2,1)} %get-tuple-element.16.w_any, ...), custom_call_target="tpu_custom_call" | custom-call | tf_op jit(solution)/shard_map/pallas_call | solution.py:315
  88.1 3.7 %all-to-all-start.1 = ((bf16[32,4,256]{2,1,0:T(4,128)(2,1)}), bf16[32,4,256]{2,1,0:T(4,128)(2,1)S(1)}, u32[]{:S(2)}, u32[]{:S(2)}) async-start(bf16[32,4,256]{2,1,0:T(4,128)(2,1)} %get-tuple-element.18), calls=%async_computation.1 | async-start | bytes 131072 | tf_op jit(solution)/shard_map/all_to_all | solution.py:332
  91.7 0.3 collective-permute-start.3
  92.0 1.7 %collective-permute-start.4 = (f32[6,4,256]{2,1,0:T(4,128)}, f32[6,4,256]{2,1,0:T(4,128)S(1)}, u32[]{:S(2)}, u32[]{:S(2)}) collective-permute-start(f32[6,4,256]{2,1,0:T(4,128)} %get-tuple-element.21), channel_id=1, source_target_pairs={{0,2},{1,3},{2,0},{3,1},{4,6},{5,7},{6,4},{7,5},{8,10},{9,11},{10,... | collective-permute-start | bytes 73736 | tf_op jit(solution)/shard_map/ppermute | solution.py:286
  93.7 1.3 %collective-permute-start.5 = (f32[6,4,256]{2,1,0:T(4,128)}, f32[6,4,256]{2,1,0:T(4,128)S(1)}, u32[]{:S(2)}, u32[]{:S(2)}) collective-permute-start(f32[6,4,256]{2,1,0:T(4,128)} %get-tuple-element.22), channel_id=1, source_target_pairs={{0,3},{1,0},{2,1},{3,2},{4,7},{5,4},{6,5},{7,6},{8,11},{9,8},{10,9... | collective-permute-start | bytes 73736 | tf_op jit(solution)/shard_map/ppermute | solution.py:286
  95.0 0.6 pad_add_fusion.place_ref
  95.7 0.4 collective-permute-done.4.refs_2_
  96.1 0.7 collective-permute-done.5.refs_3_
  96.8 2.4 %all-to-all-done.1.low_ref = bf16[32,4,256]{2,1,0:T(4,128)(2,1)S(1)} async-done(((bf16[32,4,256]{2,1,0:T(4,128)(2,1)}), bf16[32,4,256]{2,1,0:T(4,128)(2,1)S(1)}, u32[]{:S(2)}, u32[]{:S(2)}) %all-to-all-start.1) | async-done | bytes 65568 | tf_op jit(solution)/shard_map/all_to_all | solution.py:332
  99.2 0.6 copy-done.1
  99.8 1.6 %shard_map.48 = bf16[4,6144]{1,0:T(4,128)(2,1)} custom-call(s32[25]{0:T(128)} %pad_add_fusion.place_ref, bf16[32,4,256]{2,1,0:T(4,128)(2,1)} %copy-done.1, f32[6,4,256]{2,1,0:T(4,128)} %get-tuple-element.19.refs_0_, f32[6,4,256]{2,1,0:T(4,128)} %copy-done.3, f32[6,4,256]{2,1,0:T(4,128)} %copy-done.4, f32[6,4,256]{2,1,0:T(4,128)} %copy-done.5), custom_call_target="tpu_custom_call" | custom-call | tf_op jit(solution)/shard_map/pallas_call | solution.py:334
  (22 shorter events, 0.5 us)
Async XLA Ops:
  0.0 1.4 %slice-start = ((bf16[6,5,256,256]{3,2,1,0:T(8,128)(2,1)}), bf16[6,2,256,256]{3,2,1,0:T(8,128)(2,1)S(1)}, s32[]{:S(2)}) async-start(bf16[6,5,256,256]{3,2,1,0:T(8,128)(2,1)} %tiles_ref.1), calls=%async_computation.2 | async-start | bytes 3145728 | tf_op jit(solution)/shard_map/slice | solution.py:288
  3.5 7.4 %copy-start.6 = (s32[192]{0:T(256)S(1)}, s32[192]{0:T(256)}, u32[]{:S(2)}) copy-start(s32[192]{0:T(256)} %param.6) | copy-start | bytes 2308
  3.5 55.7 %all-to-all-start = ((bf16[8,2,256,256]{3,2,1,0:T(8,128)(2,1)}), bf16[8,2,256,256]{3,2,1,0:T(8,128)(2,1)S(1)}, u32[]{:S(2)}, u32[]{:S(2)}) async-start(bf16[8,2,256,256]{3,2,1,0:T(8,128)(2,1)} %gather_fusion), calls=%async_computation | async-start | bytes 4194304 | tf_op jit(solution)/shard_map/all_to_all | solution.py:288
  11.5 23.7 %copy-start.2 = (bf16[4,6144]{1,0:T(4,128)(2,1)S(1)}, bf16[4,6144]{1,0:T(4,128)(2,1)}, u32[]{:S(2)}) copy-start(bf16[4,6144]{1,0:T(4,128)(2,1)} %param.7) | copy-start | bytes 147460
  35.2 5.8 %collective-permute-start.2 = (bf16[4,1536]{1,0:T(4,128)(2,1)S(1)}, bf16[4,1536]{1,0:T(4,128)(2,1)S(1)}, u32[]{:S(2)}, u32[]{:S(2)}) collective-permute-start(bf16[4,1536]{1,0:T(4,128)(2,1)S(1)} %get-tuple-element.24), channel_id=1, source_target_pairs={{0,1},{1,2},{2,3},{3,0},{4,5},{5,6},{6,7},{7,4},{8,9},{9,10},{10,1... | collective-permute-start | bytes 36872 | tf_op jit(solution)/shard_map/ppermute | solution.py:286
  35.4 5.6 %collective-permute-start.1 = (bf16[4,1536]{1,0:T(4,128)(2,1)S(1)}, bf16[4,1536]{1,0:T(4,128)(2,1)S(1)}, u32[]{:S(2)}, u32[]{:S(2)}) collective-permute-start(bf16[4,1536]{1,0:T(4,128)(2,1)S(1)} %get-tuple-element.25), channel_id=1, source_target_pairs={{0,2},{1,3},{2,0},{3,1},{4,6},{5,7},{6,4},{7,5},{8,10},{9,11},{10,... | collective-permute-start | bytes 36872 | tf_op jit(solution)/shard_map/ppermute | solution.py:286
  39.0 2.8 %collective-permute-start = (bf16[4,1536]{1,0:T(4,128)(2,1)S(1)}, bf16[4,1536]{1,0:T(4,128)(2,1)S(1)}, u32[]{:S(2)}, u32[]{:S(2)}) collective-permute-start(bf16[4,1536]{1,0:T(4,128)(2,1)S(1)} %get-tuple-element.26), channel_id=1, source_target_pairs={{0,3},{1,0},{2,1},{3,2},{4,7},{5,4},{6,5},{7,6},{8,11},{9,8},{10,9... | collective-permute-start | bytes 36872 | tf_op jit(solution)/shard_map/ppermute | solution.py:286
  59.1 1.4 %copy-start = (bf16[8,2,256,256]{3,2,1,0:T(8,128)(2,1)}, bf16[8,2,256,256]{3,2,1,0:T(8,128)(2,1)S(1)}, u32[]{:S(2)}) copy-start(bf16[8,2,256,256]{3,2,1,0:T(8,128)(2,1)S(1)} %all-to-all-done.got_ref) | copy-start | bytes 6291460
  88.1 11.1 %all-to-all-start.1 = ((bf16[32,4,256]{2,1,0:T(4,128)(2,1)}), bf16[32,4,256]{2,1,0:T(4,128)(2,1)S(1)}, u32[]{:S(2)}, u32[]{:S(2)}) async-start(bf16[32,4,256]{2,1,0:T(4,128)(2,1)} %get-tuple-element.18), calls=%async_computation.1 | async-start | bytes 131072 | tf_op jit(solution)/shard_map/all_to_all | solution.py:332
  91.7 3.9 %collective-permute-start.3 = (f32[6,4,256]{2,1,0:T(4,128)}, f32[6,4,256]{2,1,0:T(4,128)S(1)}, u32[]{:S(2)}, u32[]{:S(2)}) collective-permute-start(f32[6,4,256]{2,1,0:T(4,128)} %get-tuple-element.20), channel_id=1, source_target_pairs={{0,1},{1,2},{2,3},{3,0},{4,5},{5,6},{6,7},{7,4},{8,9},{9,10},{10,1... | collective-permute-start | bytes 73736 | tf_op jit(solution)/shard_map/ppermute | solution.py:286
  92.0 4.0 %collective-permute-start.4 = (f32[6,4,256]{2,1,0:T(4,128)}, f32[6,4,256]{2,1,0:T(4,128)S(1)}, u32[]{:S(2)}, u32[]{:S(2)}) collective-permute-start(f32[6,4,256]{2,1,0:T(4,128)} %get-tuple-element.21), channel_id=1, source_target_pairs={{0,2},{1,3},{2,0},{3,1},{4,6},{5,7},{6,4},{7,5},{8,10},{9,11},{10,... | collective-permute-start | bytes 73736 | tf_op jit(solution)/shard_map/ppermute | solution.py:286
  93.7 3.1 %collective-permute-start.5 = (f32[6,4,256]{2,1,0:T(4,128)}, f32[6,4,256]{2,1,0:T(4,128)S(1)}, u32[]{:S(2)}, u32[]{:S(2)}) collective-permute-start(f32[6,4,256]{2,1,0:T(4,128)} %get-tuple-element.22), channel_id=1, source_target_pairs={{0,3},{1,0},{2,1},{3,2},{4,7},{5,4},{6,5},{7,6},{8,11},{9,8},{10,9... | collective-permute-start | bytes 73736 | tf_op jit(solution)/shard_map/ppermute | solution.py:286
  95.7 3.5 %copy-start.3 = (f32[6,4,256]{2,1,0:T(4,128)}, f32[6,4,256]{2,1,0:T(4,128)S(1)}, u32[]{:S(2)}) copy-start(f32[6,4,256]{2,1,0:T(4,128)S(1)} %collective-permute-done.3.refs_1_) | copy-start | bytes 73732
  96.1 3.1 %copy-start.4 = (f32[6,4,256]{2,1,0:T(4,128)}, f32[6,4,256]{2,1,0:T(4,128)S(1)}, u32[]{:S(2)}) copy-start(f32[6,4,256]{2,1,0:T(4,128)S(1)} %collective-permute-done.4.refs_2_) | copy-start | bytes 73732
  96.8 2.4 %copy-start.5 = (f32[6,4,256]{2,1,0:T(4,128)}, f32[6,4,256]{2,1,0:T(4,128)S(1)}, u32[]{:S(2)}) copy-start(f32[6,4,256]{2,1,0:T(4,128)S(1)} %collective-permute-done.5.refs_3_) | copy-start | bytes 73732
  99.2 0.6 copy-start.1

commit v8 on v7

--- a/solution.py
+++ b/solution.py
@@ -7,7 +7,6 @@
 from jax.sharding import PartitionSpec as P
 
 STEP = 32
-PIVOTS = 4
 NT = (((1,), (1,)), ((), ()))
 NN = (((1,), (0,)), ((), ()))
 TN = (((0,), (0,)), ((), ()))
@@ -30,6 +29,25 @@
     b1, b2, b3 = b
     small = dot(a1, b3, dims) + dot(a3, b1, dims) + dot(a2, b2, dims)
     return dot(a1, b1, dims) + ((dot(a1, b2, dims) + dot(a2, b1, dims)) + small)
+
+
+def dot3(a, b, dims):
+    return dot(a[0], b[0], dims) + (dot(a[0], b[1], dims) + dot(a[1], b[0], dims))
+
+
+def wide(parts):
+    one, two, three = parts
+    return jnp.concatenate([one, one, two, two, one, three], axis=1)
+
+
+def deep(parts):
+    one, two, three = parts
+    return jnp.concatenate([one, two, one, two, three, one], axis=0)
+
+
+def thirds(array):
+    count = array.shape[0] // 3
+    return array[:count] + (array[count:2 * count] + array[2 * count:])
 
 
 def apply(rows, parts, dims):
@@ -62,52 +80,69 @@
     def spread(row):
         return jnp.broadcast_to(row, (8, 128))
 
-    def wide(parts):
-        one, two, three = parts
-        return jnp.concatenate([one, one, two, two, one, three], axis=1)
-
-    def deep(parts):
-        if height < 128:
-            filler = jnp.zeros((128 - height, width), jnp.bfloat16)
-            parts = [jnp.concatenate([part, filler], axis=0) for part in parts]
-        one, two, three = parts
-        return jnp.concatenate([one, two, one, two, three, one], axis=0)
+    def padded(parts):
+        if height == 128:
+            return parts
+        filler = jnp.zeros((128 - height, width), jnp.bfloat16)
+        return [jnp.concatenate([part, filler], axis=0) for part in parts]
 
     def pivots(packs, pieces):
         placed = 0
-        for first in range(0, STEP, PIVOTS):
+        for first in range(0, STEP, 4):
             top, start = first // 8, first % 8
             tall = range(top, groups)
-            own = (place >= first) & (place < first + PIVOTS)
+            own = (place >= first) & (place < first + 4)
             one = jnp.where(place - 8 * top == sub, 1.0, 0.0)
+            each = range(len(packs))
             if start == 0:
-                inverses = [None] * len(packs)
-            columns = []
+                inverses = [None for _ in each]
+            u = [
+                [{g: jnp.take_along_axis(x[g], lane - place + (first + q), axis=1) for g in tall} for q in range(4)]
+                for x in packs
+            ]
+            a = [{(i, j): spread(u[s][j][top][start + i:start + i + 1, :]) for j in range(4) for i in range(j + 1)} for s in each]
             for x in packs:
-                columns.append([
-                    {g: jnp.take_along_axis(x[g], lane - place + (first + q), axis=1) for g in tall} for q in range(PIVOTS)
-                ])
                 for g in tall:
                     x[g] = jnp.where(own, one if g == top else 0.0, x[g])
-            for q in range(PIVOTS):
+            y = [[spread(x[top][start + q:start + q + 1, :]) for q in range(4)] for x in packs]
+            low = [{} for _ in each]
+            inv = [[None] * 4 for _ in each]
+            for p in (0, 2):
+                n = p + 1
+                delta = [a[s][p, p] * a[s][n, n] - a[s][p, n] * a[s][p, n] for s in each]
+                for s in each:
+                    inv[s][p] = pl.reciprocal(a[s][p, p], approx=True)
+                    inv[s][n] = pl.reciprocal(delta[s], approx=True) * a[s][p, p]
+                for j in range(n, 4):
+                    for s in each:
+                        low[s][j, p] = a[s][p, j] * inv[s][p]
+                for j in range(n + 1, 4):
+                    for s in each:
+                        a[s][n, j] = a[s][n, j] - low[s][n, p] * a[s][p, j]
+                for j in range(n + 1, 4):
+                    for s in each:
+                        low[s][j, n] = a[s][n, j] * inv[s][n]
+                for i in range(n + 1, 4):
+                    for j in range(i, 4):
+                        for s in each:
+                            a[s][i, j] = (a[s][i, j] - low[s][i, p] * a[s][p, j]) - low[s][i, n] * a[s][n, j]
+            for q in range(4):
                 at = start + q
-                for s, x in enumerate(packs):
-                    cols = columns[s]
-                    inverse = pl.reciprocal(spread(cols[q][top][at:at + 1, :]), approx=True)
-                    inverses[s] = inverse if at == 0 else jnp.where(sub >= at, inverse, inverses[s])
-                    c = {g: cols[q][g] * inverse for g in tall}
-                    for later in range(q + 1, PIVOTS):
-                        m = spread(cols[q][top][start + later:start + later + 1, :])
+                for s in each:
+                    for k in range(q):
                         for g in tall:
-                            cols[later][g] = cols[later][g] - c[g] * m
-                    c[top] = jnp.where(sub > at, c[top], 0.0)
-                    r = spread(x[top][at:at + 1, :])
+                            u[s][q][g] = u[s][q][g] - u[s][k][g] * low[s][q, k]
+                        y[s][q] = y[s][q] - y[s][k] * low[s][q, k]
+                    inverses[s] = inv[s][q] if at == 0 else jnp.where(sub >= at, inv[s][q], inverses[s])
                     for g in tall:
-                        x[g] = x[g] - c[g] * r
+                        m = u[s][q][g] * inv[s][q]
+                        if g == top:
+                            m = jnp.where(sub > at, m, 0.0)
+                        packs[s][g] = packs[s][g] - m * y[s][q]
                 while placed * STEP < (first + q + 1) * len(pieces):
                     pieces[placed]()
                     placed += 1
-            if start + PIVOTS == 8:
+            if start + 4 == 8:
                 for s, x in enumerate(packs):
                     x[top] = x[top] * (inverses[s] * lax.rsqrt(inverses[s]))
 
@@ -154,7 +189,7 @@
         sides = []
         for t in range(teams):
             ident = jnp.where(col_team == row_team % STEP, 1.0, 0.0)
-            sides.append(deep(split3(jnp.where(col_team < STEP, ident, slab_ref[t]))))
+            sides.append(deep(padded(split3(jnp.where(col_team < STEP, ident, slab_ref[t])))))
         pivots(packs, pieces)
         for t in range(teams):
             inner = jnp.concatenate(packs[t], axis=0)
@@ -170,7 +205,7 @@
             if height < 128:
                 ahead = jnp.concatenate([ahead, jnp.zeros((128 - height, 128), jnp.float32)], axis=0)
             ahead = wide(split3(ahead.T[:height]))
-            update = dot(ahead, deep(split3(pltpu.roll(slab, width - STEP, 1))), NN)
+            update = dot(ahead, deep(padded(split3(pltpu.roll(slab, width - STEP, 1)))), NN)
             coming = [pltpu.roll(ref[t * team + i, pl.ds(after, STEP), :], width - after, 1) for i in range(team)]
             slab_ref[t] = jnp.where(col_team >= width - STEP, 0.0, jnp.concatenate(coming, axis=0)) - update
             slab = pltpu.roll(slab, base, 1)
@@ -188,22 +223,39 @@
     return [pltpu.VMEM((systems // team, team * STEP, width), jnp.float32)] * 2
 
 
-def own_kernel(counts_ref, tiles_ref, w_ref, z_ref, g_ref, *scratch):
+def scaled(matrix):
+    factor_of = 1.0 / jnp.max(jnp.max(matrix, axis=1, keepdims=True), axis=0, keepdims=True)
+    return matrix * factor_of, jnp.sqrt(factor_of)
+
+
+def gram_kernel(counts_ref, tiles_ref, g_ref):
     systems, kslots, width, _ = tiles_ref.shape
     for s in range(systems):
         near = tiles_ref[s, 0:2].reshape(2 * width, width)
         g_ref[s] = dot(near, near, TN)
+    for s in range(systems):
         for k in range(2, kslots):
             @pl.when(k < counts_ref[s])
             def _():
                 tile = tiles_ref[s, k]
                 g_ref[s] += dot(tile, tile, TN)
-    factor(g_ref, *scratch)
-    for s in range(systems):
-        w1, w2, w3 = split3(g_ref[s])
+
+
+def own_kernel(g_ref, tiles_any, w_ref, z_ref, near_ref, t_ref, sem, *scratch):
+    systems, _, width, _ = near_ref.shape
+    copy = pltpu.make_async_copy(tiles_any.at[:, 0:2], near_ref, sem)
+    copy.start()
+    roots = []
+    for s in range(systems):
+        t_ref[s], root = scaled(g_ref[s])
+        roots.append(root)
+    factor(t_ref, *scratch)
+    copy.wait()
+    for s in range(systems):
+        w1, w2, w3 = split3(t_ref[s] * roots[s])
         w_ref[s, 0] = w1
         w_ref[s, 1] = w2
-        near = jnp.concatenate([tiles_ref[s, 1], tiles_ref[s, 0]], axis=0)
+        near = jnp.concatenate([near_ref[s, 1], near_ref[s, 0]], axis=0)
         z = dot(w1, near, NT) + (dot(w2, near, NT) + dot(w3, near, NT))
         z1, z2, z3 = split3(z)
         z_ref[s, 0] = z1
@@ -211,11 +263,10 @@
         z_ref[s, 2] = z3
 
 
-def pair_kernel(lanes, place_ref, x_ref, w_any, z_any, got_ref, *refs):
-    up_refs, refs = refs[:lanes], refs[lanes:]
-    low_ref, near_ref, w_ref, z_ref, t_ref, v_ref, r_ref, first_ref, sems, *scratch = refs
+def mid_kernel(place_ref, x_ref, got_ref, w_any, z_any, q_ref, back_ref, first_ref, rhs_ref,
+               near_ref, w_ref, z_ref, t_ref, v_ref, r_ref, sems, *scratch):
     systems, _, width, _ = z_ref.shape
-    count = x_ref.shape[0] // lanes
+    part = near_ref.shape[3]
     copies = []
     for s in range(systems):
         pairs = ((got_ref.at[place_ref[s]], near_ref.at[s]), (z_any.at[s], z_ref.at[s]))
@@ -224,35 +275,91 @@
             copy.start()
     w_copy = pltpu.make_async_copy(w_any, w_ref, sems.at[systems, 0])
     w_copy.start()
-    low_ref[...] = jnp.zeros(low_ref.shape, low_ref.dtype)
+    roots = []
     for s in range(systems):
         for copy in copies[s]:
             copy.wait()
-        near = near_ref[s].reshape(2 * width, width)
-        near_t = near.T
-        z1, z2, z3 = z_ref[s, 0], z_ref[s, 1], z_ref[s, 2]
-        v = split3(dot(near_t, z1, NT) + (dot(near_t, z2, NT) + dot(near_t, z3, NT)))
+        near = near_ref[s].reshape(2 * width, part)
+        v = split3(thirds(dot(z_ref[s].reshape(3 * width, 2 * width), near, NN)))
+        vt = [one.T for one in v]
+        for i in range(3):
+            v_ref[s, i] = vt[i]
+        t_ref[s], root = scaled(dot(near.T, near, NN) - dot(wide(vt), deep(v), NN))
+        roots.append(root)
+        x = x_ref[:, s * width:(s + 1) * width]
+        first = dot(x, z_ref[s, 0, :, width:], NT) + dot(x, z_ref[s, 1, :, width:], NT)
+        first_ref[s, :, :width] = first
+        r_ref[s] = dot(x, near[width:], NN) - apply(first, v, NN)
+    factor(t_ref, *scratch)
+    w_copy.wait()
+    for s in range(systems):
+        near_t = near_ref[s].reshape(2 * width, part).T
+        own = split3(t_ref[s] * roots[s])
+        vt = [v_ref[s, i] for i in range(3)]
+        more = apply(r_ref[s], own, NT)
+        first_ref[s, :, width:] = more
+        rest = near_t.astype(jnp.float32) - dot6(vt, [z_ref[s, i] for i in range(3)], NN)
+        q = split3(dot(wide(own), deep(split3(rest)), NN))
+        for i in range(3):
+            q_ref[s, i] = q[i]
+        x = x_ref[:, s * width:(s + 1) * width].astype(jnp.float32)
+        first = first_ref[s, :, :width]
+        rhs = jnp.concatenate([jnp.zeros_like(x), x], axis=1) - apply(first, (z_ref[s, 0], z_ref[s, 1]), NN)
+        rhs_ref[s] = rhs - apply(more, q, NN)
+        left = split3(-dot3(own, split3(dot3(vt, (w_ref[s, 0], w_ref[s, 1]), NN)), NN))
+        for i in range(2):
+            back_ref[s, i, :, :width] = left[i]
+            back_ref[s, i, :, width:] = own[i]
+
+
+def last_kernel(lanes, place_ref, first_ref, rhs_ref, got_ref, z_any, q_any, w_any, back_any, *refs):
+    up_refs, refs = refs[:lanes], refs[lanes:]
+    low_ref, near_ref, z_ref, q_ref, w_ref, back_ref, t_ref, v_ref, r_ref, sems, *scratch = refs
+    systems, _, width, _ = z_ref.shape
+    part = near_ref.shape[3]
+    count = first_ref.shape[1] // lanes
+    copies = []
+    for s in range(systems):
+        pairs = ((got_ref.at[place_ref[s]], near_ref.at[s]), (z_any.at[s], z_ref.at[s]), (q_any.at[s], q_ref.at[s]))
+        copies.append([pltpu.make_async_copy(a, b, sems.at[s, i]) for i, (a, b) in enumerate(pairs)])
+        for copy in copies[s]:
+            copy.start()
+    ends = [
+        pltpu.make_async_copy(w_any, w_ref, sems.at[systems, 0]),
+        pltpu.make_async_copy(back_any, back_ref, sems.at[systems, 1]),
+    ]
+    for copy in ends:
+        copy.start()
+    low_ref[...] = jnp.zeros(low_ref.shape, low_ref.dtype)
+    roots = []
+    for s in range(systems):
+        for copy in copies[s]:
+            copy.wait()
+        near = near_ref[s].reshape(2 * width, part)
+        upper = thirds(dot(z_ref[s].reshape(3 * width, 2 * width), near, NN))
+        lower = thirds(dot(q_ref[s].reshape(-1, 2 * width), near, NN))
+        v = split3(jnp.concatenate([upper, lower], axis=0))
         v_ref[s, 0] = v[0]
         v_ref[s, 1] = v[1]
-        t_ref[s] = dot(near_t, near, NN) - dot6(v, v, NT)
-    for s in range(systems):
-        x = x_ref[:, s * width:(s + 1) * width]
-        first_ref[s] = dot(x, z_ref[s, 0, :, width:], NT) + dot(x, z_ref[s, 1, :, width:], NT)
-        r_ref[s] = dot(x, near_ref[s, 1], NN)
-    for s in range(systems):
-        r_ref[s] = r_ref[s] - apply(first_ref[s], (v_ref[s, 0], v_ref[s, 1]), NT)
+        vt = [one.T for one in v]
+        t_ref[s], root = scaled(dot(near.T, near, NN) - dot(wide(vt), deep(v), NN))
+        roots.append(root)
+        r_ref[s] = thirds(dot(jnp.concatenate(split3(rhs_ref[s]), axis=0), near, NN))
     factor(t_ref, *scratch)
-    parts = [split3(t_ref[s])[:2] for s in range(systems)]
+    parts = [split3(t_ref[s] * roots[s])[:2] for s in range(systems)]
     half = [apply(r_ref[s], parts[s], NT) for s in range(systems)]
     last = [apply(half[s], parts[s], NN) for s in range(systems)]
-    mid = [first_ref[s] - apply(last[s], (v_ref[s, 0], v_ref[s, 1]), NN) for s in range(systems)]
-    w_copy.wait()
-    for s in range(systems):
-        up = apply(mid[s], (w_ref[s, 0], w_ref[s, 1]), NN)
+    mid = [first_ref[s] - apply(last[s], (v_ref[s, 0], v_ref[s, 1]), NT) for s in range(systems)]
+    for copy in ends:
+        copy.wait()
+    for s in range(systems):
+        both = apply(mid[s][:, width:], (back_ref[s, 0], back_ref[s, 1]), NN)
+        up = apply(mid[s][:, :width], (w_ref[s, 0], w_ref[s, 1]), NN) + both[:, :width]
+        low = jnp.concatenate([both[:, width:], last[s]], axis=1)
         for e in range(lanes):
             up_refs[e][s] = up[e * count:(e + 1) * count]
             owner = lax.rem(place_ref[systems] + e, lanes)
-            low_ref[place_ref[s] * lanes + owner] = last[s][e * count:(e + 1) * count].astype(low_ref.dtype)
+            low_ref[place_ref[s] * lanes + owner] = low[e * count:(e + 1) * count].astype(low_ref.dtype)
 
 
 def place_kernel(lanes, place_ref, low_ref, *refs):
@@ -285,50 +392,94 @@
     def shift(value, by):
         return lax.ppermute(value, "rhs", [(i, (i + by) % lanes) for i in range(lanes)])
 
-    received = lax.all_to_all(tiles[:, :2][slot_of], "panel", split_axis=0, concat_axis=0, tiled=True)
+    part = width // 2
+    rest = width - part
+    ordered = tiles[:, :2][slot_of]
+    half_one, half_two = ordered[..., :part], ordered[..., part:]
+    got_one = lax.all_to_all(half_one, "panel", split_axis=0, concat_axis=0, tiled=True)
 
     vmem = pl.BlockSpec(memory_space=pltpu.VMEM)
     smem = pl.BlockSpec(memory_space=pltpu.SMEM)
     anywhere = pl.BlockSpec(memory_space=pl.ANY)
     params = pltpu.CompilerParams(vmem_limit_bytes=56 * 1024 * 1024)
+    g = pl.pallas_call(
+        gram_kernel,
+        out_shape=jax.ShapeDtypeStruct((systems, width, width), jnp.float32),
+        in_specs=[smem, vmem],
+        out_specs=vmem,
+        compiler_params=params,
+        cost_estimate=pl.CostEstimate(flops=5 * 10**9, bytes_accessed=6 * 10**6, transcendentals=0),
+    )(own_cnt, tiles)
+    half_two, g = lax.optimization_barrier((half_two, g))
+    got_two = lax.all_to_all(half_two, "panel", split_axis=0, concat_axis=0, tiled=True)
     w, z = pl.pallas_call(
         own_kernel,
         out_shape=(
             jax.ShapeDtypeStruct((systems, 2, width, width), jnp.bfloat16),
             jax.ShapeDtypeStruct((systems, 3, width, 2 * width), jnp.bfloat16),
         ),
-        in_specs=[smem, vmem],
+        in_specs=[vmem, anywhere],
         out_specs=(vmem, vmem),
-        scratch_shapes=[pltpu.VMEM((systems, width, width), jnp.float32)] + factor_scratch(systems, width),
+        scratch_shapes=[
+            pltpu.VMEM((systems, 2, width, width), jnp.bfloat16),
+            pltpu.VMEM((systems, width, width), jnp.float32),
+            pltpu.SemaphoreType.DMA,
+        ] + factor_scratch(systems, width),
         compiler_params=params,
-        cost_estimate=pl.CostEstimate(flops=40 * 10**9, bytes_accessed=8 * 10**6, transcendentals=0),
-    )(own_cnt, tiles)
+        cost_estimate=pl.CostEstimate(flops=30 * 10**9, bytes_accessed=8 * 10**6, transcendentals=0),
+    )(g, tiles)
 
     inputs, w = lax.optimization_barrier((inputs, w))
     parts = [lax.dynamic_slice_in_dim(inputs, my_lane * own_width, own_width, 1)]
     for e in range(1, lanes):
-        part = lax.dynamic_slice_in_dim(inputs, (my_lane + lanes - e) % lanes * own_width, own_width, 1)
-        parts.append(shift(part, -e))
+        block = lax.dynamic_slice_in_dim(inputs, (my_lane + lanes - e) % lanes * own_width, own_width, 1)
+        parts.append(shift(block, -e))
     x = jnp.concatenate(parts, axis=0)
+
+    nrhs = lanes * nrhs_dev
+    where = jnp.concatenate([mate_panel, lane_word])
+    q, back, first, rhs = pl.pallas_call(
+        mid_kernel,
+        out_shape=(
+            jax.ShapeDtypeStruct((systems, 3, part, 2 * width), jnp.bfloat16),
+            jax.ShapeDtypeStruct((systems, 2, part, width + part), jnp.bfloat16),
+            jax.ShapeDtypeStruct((systems, nrhs, width + part), jnp.float32),
+            jax.ShapeDtypeStruct((systems, nrhs, 2 * width), jnp.float32),
+        ),
+        in_specs=[smem, vmem, anywhere, anywhere, anywhere],
+        out_specs=(vmem, vmem, vmem, vmem),
+        scratch_shapes=[
+            pltpu.VMEM((systems, 2, width, part), jnp.bfloat16),
+            pltpu.VMEM((systems, 2, width, width), jnp.bfloat16),
+            pltpu.VMEM((systems, 3, width, 2 * width), jnp.bfloat16),
+            pltpu.VMEM((systems, part, part), jnp.float32),
+            pltpu.VMEM((systems, 3, part, width), jnp.bfloat16),
+            pltpu.VMEM((systems, nrhs, part), jnp.float32),
+            pltpu.SemaphoreType.DMA((systems + 1, 2)),
+        ] + factor_scratch(systems, part),
+        compiler_params=params,
+        cost_estimate=pl.CostEstimate(flops=20 * 10**9, bytes_accessed=8 * 10**6, transcendentals=0),
+    )(where, x, got_one, w, z)
 
     piece = jax.ShapeDtypeStruct((systems, nrhs_dev, width), jnp.float32)
     *up, low = pl.pallas_call(
-        functools.partial(pair_kernel, lanes),
+        functools.partial(last_kernel, lanes),
         out_shape=[piece] * lanes + [jax.ShapeDtypeStruct((shards * lanes, nrhs_dev, width), jnp.bfloat16)],
-        in_specs=[smem, vmem, anywhere, anywhere, anywhere],
+        in_specs=[smem, vmem, vmem] + [anywhere] * 5,
         out_specs=[vmem] * (lanes + 1),
         scratch_shapes=[
+            pltpu.VMEM((systems, 2, width, rest), jnp.bfloat16),
+            pltpu.VMEM((systems, 3, width, 2 * width), jnp.bfloat16),
+            pltpu.VMEM((systems, 3, part, 2 * width), jnp.bfloat16),
             pltpu.VMEM((systems, 2, width, width), jnp.bfloat16),
-            pltpu.VMEM((systems, 2, width, width), jnp.bfloat16),
-            pltpu.VMEM((systems, 3, width, 2 * width), jnp.bfloat16),
-            pltpu.VMEM((systems, width, width), jnp.float32),
-            pltpu.VMEM((systems, 2, width, width), jnp.bfloat16),
-            pltpu.VMEM((systems, lanes * nrhs_dev, width), jnp.float32),
-            pltpu.VMEM((systems, lanes * nrhs_dev, width), jnp.float32),
-            pltpu.SemaphoreType.DMA((systems + 1, 2)),
-        ] + factor_scratch(systems, width),
+            pltpu.VMEM((systems, 2, part, width + part), jnp.bfloat16),
+            pltpu.VMEM((systems, rest, rest), jnp.float32),
+            pltpu.VMEM((systems, 2, width + part, rest), jnp.bfloat16),
+            pltpu.VMEM((systems, nrhs, rest), jnp.float32),
+            pltpu.SemaphoreType.DMA((systems + 1, 3)),
+        ] + factor_scratch(systems, rest),
         compiler_params=params,
-    )(jnp.concatenate([mate_panel, lane_word]), x, w, z, received)
+    )(where, first, rhs, got_two, z, q, w, back)
     low = lax.all_to_all(low, ("panel", "rhs"), split_axis=0, concat_axis=0, tiled=True)
     up = [up[0]] + [shift(up[e], e) for e in range(1, lanes)]
     return pl.pallas_call(

time: 102 us -> 111 us (1.088)
  Pallas kernels: 52.9 us -> 68.3 us
  waiting for transfers between devices: 20.9 us -> 7.12 us
  starting transfers between devices: 19.5 us -> 24.2 us
  local copies, waits for them, and re-layouts: 5.04 us -> 7.75 us
    pallas_call x1 -> x3, Pallas kernels: 27.6 us -> 45.6 us  [the longest x1 23.7 us: on_device(): pl.pallas_call(mid_kernel, out_shape=(jax.ShapeDtypeStruct((systems, 3, p...]
    all_to_all x1 -> x2, waiting for transfers between devices: 16.7 us -> 2.89 us  [the longest x1 2.89 us: on_device(): lax.all_to_all(half_two, 'panel', split_axis=0, concat_axis=0, tiled=True)]
    all_to_all x1 -> x2, starting transfers between devices: 7.41 us -> 13 us  [the longest x1 7.41 us: on_device(): lax.all_to_all(half_one, 'panel', split_axis=0, concat_axis=0, tiled=True)]
    slice x2 -> x3, local copies, waits for them, and re-layouts: 0.31 us -> 3.44 us  [the longest x1 3.12 us: on_device(): half_one, half_two = (ordered[..., :part], ordered[..., part:])]
    pallas_call x1, Pallas kernels: 23.7 us -> 21.1 us  [on_device(): pl.pallas_call(own_kernel, out_shape=(jax.ShapeDtypeStruct((systems, 2, w...]
  transfers between devices with their start and end apart: 8 -> 9, of which waited for: 5 -> 5; matrix products, arithmetic and copies ran while one was open for 2% -> 2% of each run, Pallas kernels for 23% -> 44%
where the time goes in v8:
time: 111 us
  Pallas kernels  68.3 us (62%)
  starting transfers between devices  24.2 us (22%)
  local copies, waits for them, and re-layouts  7.75 us (7%)
  waiting for transfers between devices  7.12 us (6%)
  other arithmetic  2.95 us (3%)
    pallas_call x1, Pallas kernels, on_device(): pl.pallas_call(mid_kernel, out_shape=(jax.ShapeDtypeStruct((systems, 3, p...  23.7 us
    pallas_call x1, Pallas kernels, on_device(): pl.pallas_call(own_kernel, out_shape=(jax.ShapeDtypeStruct((systems, 2, w...  21.1 us
    pallas_call x1, Pallas kernels, on_device(): pl.pallas_call(functools.partial(last_kernel, lanes), out_shape=[piece] *...  17.9 us
    ppermute x6, starting transfers between devices, shift(): lax.ppermute(value, 'rhs', [(i, (i + by) % lanes) for i in range(lanes)])  7.59 us
    all_to_all x1, starting transfers between devices, on_device(): lax.all_to_all(half_one, 'panel', split_axis=0, concat_axis=0, tiled=True)  7.41 us
    all_to_all x1, starting transfers between devices, on_device(): lax.all_to_all(half_two, 'panel', split_axis=0, concat_axis=0, tiled=True)  5.55 us
    pallas_call x1, Pallas kernels, on_device(): pl.pallas_call(gram_kernel, out_shape=jax.ShapeDtypeStruct((systems, widt...  4.05 us
    all_to_all x1, starting transfers between devices, on_device(): lax.all_to_all(low, ('panel', 'rhs'), split_axis=0, concat_axis=0, tiled=...  3.66 us
  transfers between devices with their start and end apart: 9, of which 5 were waited for; matrix products, arithmetic and copies ran while one was open for 2% of the time, Pallas kernels for 44%

profile of v8, /device:TPU:0, one launch (start us, length us, event | category | flops | bytes accessed | tf_op | source)
XLA Modules:
  0.0 110.5 jit_solution(791763257592912822)
XLA Ops:
  0.0 0.9 bitcast_select_fusion
  1.4 2.0 %gather_fusion = bf16[8,2,256,256]{3,2,1,0:T(8,128)(2,1)} fusion(bf16[6,2,256,256]{3,2,1,0:T(8,128)(2,1)S(1)} %slice-done, s32[1024]{0:T(1024)S(1)} %pad_clamp_fusion), kind=kCustom, calls=%fused_computation | custom fusion | bytes 4194336 | tf_op jit(solution)/shard_map/gather | solution.py:397
  3.4 3.1 %fusion.1 = (bf16[8,2,256,128]{3,2,1,0:T(8,128)(2,1)}, bf16[8,2,256,128]{3,2,1,0:T(8,128)(2,1)}) fusion(bf16[8,2,256,256]{3,2,1,0:T(8,128)(2,1)} %gather_fusion), kind=kLoop, calls=%fused_computation.14 | loop fusion | bytes 4194304 | tf_op jit(solution)/shard_map/slice | solution.py:398
  6.6 7.4 %all-to-all-start = ((bf16[8,2,256,128]{3,2,1,0:T(8,128)(2,1)}), bf16[8,2,256,128]{3,2,1,0:T(8,128)(2,1)S(1)}, u32[]{:S(2)}, u32[]{:S(2)}) async-start(bf16[8,2,256,128]{3,2,1,0:T(8,128)(2,1)} %get-tuple-element.35), calls=%async_computation | async-start | bytes 2097152 | tf_op jit(solution)/shard_map/all_to_all | solution.py:399
  14.6 4.0 %shard_map.46.g_ref = f32[6,256,256]{2,1,0:T(8,128)} custom-call(s32[6]{0:T(128)} %dynamic_slice.23.counts_ref, bf16[6,5,256,256]{3,2,1,0:T(8,128)(2,1)} %tiles_any.1), custom_call_target="tpu_custom_call" | custom-call | flops 5000000000 | bytes 6000000 | tf_op jit(solution)/shard_map/pallas_call | solution.py:405
  18.6 21.1 %shard_map.47 = (bf16[6,2,256,256]{3,2,1,0:T(8,128)(2,1)}, bf16[6,3,256,512]{3,2,1,0:T(8,128)(2,1)}) custom-call(f32[6,256,256]{2,1,0:T(8,128)} %shard_map.46.g_ref, bf16[6,5,256,256]{3,2,1,0:T(8,128)(2,1)} %tiles_any.1), custom_call_target="tpu_custom_call" | custom-call | flops 30000001024 | bytes 8000000 | tf_op jit(solution)/shard_map/pallas_call | solution.py:415
  39.9 3.0 %collective-permute-start.1 = (bf16[4,1536]{1,0:T(4,128)(2,1)S(1)}, bf16[4,1536]{1,0:T(4,128)(2,1)S(1)}, u32[]{:S(2)}, u32[]{:S(2)}) collective-permute-start(bf16[4,1536]{1,0:T(4,128)(2,1)S(1)} %get-tuple-element.39), channel_id=1, source_target_pairs={{0,2},{1,3},{2,0},{3,1},{4,6},{5,7},{6,4},{7,5},{8,10},{9,11},{10,... | collective-permute-start | bytes 36872 | tf_op jit(solution)/shard_map/ppermute | solution.py:393
  42.9 1.3 %collective-permute-start = (bf16[4,1536]{1,0:T(4,128)(2,1)S(1)}, bf16[4,1536]{1,0:T(4,128)(2,1)S(1)}, u32[]{:S(2)}, u32[]{:S(2)}) collective-permute-start(bf16[4,1536]{1,0:T(4,128)(2,1)S(1)} %get-tuple-element.40), channel_id=1, source_target_pairs={{0,3},{1,0},{2,1},{3,2},{4,7},{5,4},{6,5},{7,6},{8,11},{9,8},{10,9... | collective-permute-start | bytes 36872 | tf_op jit(solution)/shard_map/ppermute | solution.py:393
  44.1 0.7 pad_add_fusion.1.place_ref
  44.8 0.7 collective-permute-done
  45.5 0.7 pad_maximum_fusion.x_ref
  46.2 5.5 %all-to-all-start.1 = ((bf16[8,2,256,128]{3,2,1,0:T(8,128)(2,1)}), bf16[8,2,256,128]{3,2,1,0:T(8,128)(2,1)S(1)}, u32[]{:S(2)}, u32[]{:S(2)}) async-start(bf16[8,2,256,128]{3,2,1,0:T(8,128)(2,1)} %get-tuple-element.27), calls=%async_computation.1 | async-start | bytes 2097152 | tf_op jit(solution)/shard_map/all_to_all | solution.py:414
  51.8 23.7 %shard_map.48 = (bf16[6,3,128,512]{3,2,1,0:T(8,128)(2,1)}, bf16[6,2,128,384]{3,2,1,0:T(8,128)(2,1)}, f32[6,16,384]{2,1,0:T(8,128)}, f32[6,16,512]{2,1,0:T(8,128)}) custom-call(s32[7]{0:T(128)} %pad_add_fusion.1.place_ref, bf16[16,1536]{1,0:T(8,128)(2,1)} %pad_maximum_fusion.x_ref, bf16[8,2,256,128]{3,2,1,0:T(8,128)(2,1)} %copy-done.1, ...), custom_call_target="tpu_custom_call" | custom-call | flops 20000000000 | bytes 8000000 | tf_op jit(solution)/shard_map/pallas_call | solution.py:441
  75.4 2.9 %all-to-all-done.1.got_ref = bf16[8,2,256,128]{3,2,1,0:T(8,128)(2,1)S(1)} async-done(((bf16[8,2,256,128]{3,2,1,0:T(8,128)(2,1)}), bf16[8,2,256,128]{3,2,1,0:T(8,128)(2,1)S(1)}, u32[]{:S(2)}, u32[]{:S(2)}) %all-to-all-start.1) | async-done | bytes 1048608 | tf_op jit(solution)/shard_map/all_to_all | solution.py:414
  78.3 1.0 copy-done
  79.3 17.9 %shard_map.49 = (f32[6,4,256]{2,1,0:T(4,128)}, f32[6,4,256]{2,1,0:T(4,128)}, f32[6,4,256]{2,1,0:T(4,128)}, f32[6,4,256]{2,1,0:T(4,128)}, bf16[32,4,256]{2,1,0:T(4,128)(2,1)}) custom-call(s32[7]{0:T(128)} %pad_add_fusion.1.place_ref, f32[6,16,384]{2,1,0:T(8,128)} %get-tuple-element.25.first_ref, f32[6,16,512]{2,1,0:T(8,128)} %get-tuple-element.26.rhs_ref, ...), custom_call_target="tpu_custom_call" | custom-call | tf_op jit(solution)/shard_map/pallas_call | solution.py:465
  97.2 3.7 %all-to-all-start.2 = ((bf16[32,4,256]{2,1,0:T(4,128)(2,1)}), bf16[32,4,256]{2,1,0:T(4,128)(2,1)S(1)}, u32[]{:S(2)}, u32[]{:S(2)}) async-start(bf16[32,4,256]{2,1,0:T(4,128)(2,1)} %get-tuple-element.30), calls=%async_computation.2 | async-start | bytes 131072 | tf_op jit(solution)/shard_map/all_to_all | solution.py:483
  101.2 1.7 %collective-permute-start.4 = (f32[6,4,256]{2,1,0:T(4,128)}, f32[6,4,256]{2,1,0:T(4,128)S(1)}, u32[]{:S(2)}, u32[]{:S(2)}) collective-permute-start(f32[6,4,256]{2,1,0:T(4,128)} %get-tuple-element.33), channel_id=1, source_target_pairs={{0,2},{1,3},{2,0},{3,1},{4,6},{5,7},{6,4},{7,5},{8,10},{9,11},{10,... | collective-permute-start | bytes 73736 | tf_op jit(solution)/shard_map/ppermute | solution.py:393
  102.9 1.3 %collective-permute-start.5 = (f32[6,4,256]{2,1,0:T(4,128)}, f32[6,4,256]{2,1,0:T(4,128)S(1)}, u32[]{:S(2)}, u32[]{:S(2)}) collective-permute-start(f32[6,4,256]{2,1,0:T(4,128)} %get-tuple-element.34), channel_id=1, source_target_pairs={{0,3},{1,0},{2,1},{3,2},{4,7},{5,4},{6,5},{7,6},{8,11},{9,8},{10,9... | collective-permute-start | bytes 73736 | tf_op jit(solution)/shard_map/ppermute | solution.py:393
  104.2 0.6 pad_add_fusion.place_ref
  105.3 0.6 collective-permute-done.5.refs_3_
  105.9 2.4 %all-to-all-done.2.low_ref = bf16[32,4,256]{2,1,0:T(4,128)(2,1)S(1)} async-done(((bf16[32,4,256]{2,1,0:T(4,128)(2,1)}), bf16[32,4,256]{2,1,0:T(4,128)(2,1)S(1)}, u32[]{:S(2)}, u32[]{:S(2)}) %all-to-all-start.2) | async-done | bytes 65568 | tf_op jit(solution)/shard_map/all_to_all | solution.py:483
  108.3 0.6 copy-done.2
  108.9 1.6 %shard_map.50 = bf16[4,6144]{1,0:T(4,128)(2,1)} custom-call(s32[25]{0:T(128)} %pad_add_fusion.place_ref, bf16[32,4,256]{2,1,0:T(4,128)(2,1)} %copy-done.2, f32[6,4,256]{2,1,0:T(4,128)} %get-tuple-element.31.refs_0_, f32[6,4,256]{2,1,0:T(4,128)} %copy-done.4, f32[6,4,256]{2,1,0:T(4,128)} %copy-done.5, f32[6,4,256]{2,1,0:T(4,128)} %copy-done.6), custom_call_target="tpu_custom_call" | custom-call | tf_op jit(solution)/shard_map/pallas_call | solution.py:485
  (29 shorter events, 2.0 us)
Async XLA Ops:
  0.0 1.4 %slice-start = ((bf16[6,5,256,256]{3,2,1,0:T(8,128)(2,1)}), bf16[6,2,256,256]{3,2,1,0:T(8,128)(2,1)S(1)}, s32[]{:S(2)}) async-start(bf16[6,5,256,256]{3,2,1,0:T(8,128)(2,1)} %tiles_any.1), calls=%async_computation.3 | async-start | bytes 3145728 | tf_op jit(solution)/shard_map/slice | solution.py:397
  6.6 7.4 %copy-start.7 = (s32[192]{0:T(256)S(1)}, s32[192]{0:T(256)}, u32[]{:S(2)}) copy-start(s32[192]{0:T(256)} %param.6) | copy-start | bytes 2308
  6.6 39.6 %all-to-all-start = ((bf16[8,2,256,128]{3,2,1,0:T(8,128)(2,1)}), bf16[8,2,256,128]{3,2,1,0:T(8,128)(2,1)S(1)}, u32[]{:S(2)}, u32[]{:S(2)}) async-start(bf16[8,2,256,128]{3,2,1,0:T(8,128)(2,1)} %get-tuple-element.35), calls=%async_computation | async-start | bytes 2097152 | tf_op jit(solution)/shard_map/all_to_all | solution.py:399
  18.6 21.2 %copy-start.3 = (bf16[4,6144]{1,0:T(4,128)(2,1)S(1)}, bf16[4,6144]{1,0:T(4,128)(2,1)}, u32[]{:S(2)}) copy-start(bf16[4,6144]{1,0:T(4,128)(2,1)} %param.7) | copy-start | bytes 147460
  39.8 5.0 %collective-permute-start.2 = (bf16[4,1536]{1,0:T(4,128)(2,1)S(1)}, bf16[4,1536]{1,0:T(4,128)(2,1)S(1)}, u32[]{:S(2)}, u32[]{:S(2)}) collective-permute-start(bf16[4,1536]{1,0:T(4,128)(2,1)S(1)} %get-tuple-element.38), channel_id=1, source_target_pairs={{0,1},{1,2},{2,3},{3,0},{4,5},{5,6},{6,7},{7,4},{8,9},{9,10},{10,1... | collective-permute-start | bytes 36872 | tf_op jit(solution)/shard_map/ppermute | solution.py:393
  39.9 4.9 %collective-permute-start.1 = (bf16[4,1536]{1,0:T(4,128)(2,1)S(1)}, bf16[4,1536]{1,0:T(4,128)(2,1)S(1)}, u32[]{:S(2)}, u32[]{:S(2)}) collective-permute-start(bf16[4,1536]{1,0:T(4,128)(2,1)S(1)} %get-tuple-element.39), channel_id=1, source_target_pairs={{0,2},{1,3},{2,0},{3,1},{4,6},{5,7},{6,4},{7,5},{8,10},{9,11},{10,... | collective-permute-start | bytes 36872 | tf_op jit(solution)/shard_map/ppermute | solution.py:393
  42.9 2.7 %collective-permute-start = (bf16[4,1536]{1,0:T(4,128)(2,1)S(1)}, bf16[4,1536]{1,0:T(4,128)(2,1)S(1)}, u32[]{:S(2)}, u32[]{:S(2)}) collective-permute-start(bf16[4,1536]{1,0:T(4,128)(2,1)S(1)} %get-tuple-element.40), channel_id=1, source_target_pairs={{0,3},{1,0},{2,1},{3,2},{4,7},{5,4},{6,5},{7,6},{8,11},{9,8},{10,9... | collective-permute-start | bytes 36872 | tf_op jit(solution)/shard_map/ppermute | solution.py:393
  46.2 5.6 %copy-start.1 = (bf16[8,2,256,128]{3,2,1,0:T(8,128)(2,1)}, bf16[8,2,256,128]{3,2,1,0:T(8,128)(2,1)S(1)}, u32[]{:S(2)}) copy-start(bf16[8,2,256,128]{3,2,1,0:T(8,128)(2,1)S(1)} %all-to-all-done.got_ref) | copy-start | bytes 3145732
  46.2 32.1 %all-to-all-start.1 = ((bf16[8,2,256,128]{3,2,1,0:T(8,128)(2,1)}), bf16[8,2,256,128]{3,2,1,0:T(8,128)(2,1)S(1)}, u32[]{:S(2)}, u32[]{:S(2)}) async-start(bf16[8,2,256,128]{3,2,1,0:T(8,128)(2,1)} %get-tuple-element.27), calls=%async_computation.1 | async-start | bytes 2097152 | tf_op jit(solution)/shard_map/all_to_all | solution.py:414
  78.3 1.0 copy-start
  97.2 11.1 %all-to-all-start.2 = ((bf16[32,4,256]{2,1,0:T(4,128)(2,1)}), bf16[32,4,256]{2,1,0:T(4,128)(2,1)S(1)}, u32[]{:S(2)}, u32[]{:S(2)}) async-start(bf16[32,4,256]{2,1,0:T(4,128)(2,1)} %get-tuple-element.30), calls=%async_computation.2 | async-start | bytes 131072 | tf_op jit(solution)/shard_map/all_to_all | solution.py:483
  100.9 3.9 %collective-permute-start.3 = (f32[6,4,256]{2,1,0:T(4,128)}, f32[6,4,256]{2,1,0:T(4,128)S(1)}, u32[]{:S(2)}, u32[]{:S(2)}) collective-permute-start(f32[6,4,256]{2,1,0:T(4,128)} %get-tuple-element.32), channel_id=1, source_target_pairs={{0,1},{1,2},{2,3},{3,0},{4,5},{5,6},{6,7},{7,4},{8,9},{9,10},{10,1... | collective-permute-start | bytes 73736 | tf_op jit(solution)/shard_map/ppermute | solution.py:393
  101.2 4.1 %collective-permute-start.4 = (f32[6,4,256]{2,1,0:T(4,128)}, f32[6,4,256]{2,1,0:T(4,128)S(1)}, u32[]{:S(2)}, u32[]{:S(2)}) collective-permute-start(f32[6,4,256]{2,1,0:T(4,128)} %get-tuple-element.33), channel_id=1, source_target_pairs={{0,2},{1,3},{2,0},{3,1},{4,6},{5,7},{6,4},{7,5},{8,10},{9,11},{10,... | collective-permute-start | bytes 73736 | tf_op jit(solution)/shard_map/ppermute | solution.py:393
  102.9 3.1 %collective-permute-start.5 = (f32[6,4,256]{2,1,0:T(4,128)}, f32[6,4,256]{2,1,0:T(4,128)S(1)}, u32[]{:S(2)}, u32[]{:S(2)}) collective-permute-start(f32[6,4,256]{2,1,0:T(4,128)} %get-tuple-element.34), channel_id=1, source_target_pairs={{0,3},{1,0},{2,1},{3,2},{4,7},{5,4},{6,5},{7,6},{8,11},{9,8},{10,9... | collective-permute-start | bytes 73736 | tf_op jit(solution)/shard_map/ppermute | solution.py:393
  104.8 3.5 %copy-start.4 = (f32[6,4,256]{2,1,0:T(4,128)}, f32[6,4,256]{2,1,0:T(4,128)S(1)}, u32[]{:S(2)}) copy-start(f32[6,4,256]{2,1,0:T(4,128)S(1)} %collective-permute-done.3.refs_1_) | copy-start | bytes 73732
  105.3 3.0 %copy-start.5 = (f32[6,4,256]{2,1,0:T(4,128)}, f32[6,4,256]{2,1,0:T(4,128)S(1)}, u32[]{:S(2)}) copy-start(f32[6,4,256]{2,1,0:T(4,128)S(1)} %collective-permute-done.4.refs_2_) | copy-start | bytes 73732
  105.9 2.4 %copy-start.6 = (f32[6,4,256]{2,1,0:T(4,128)}, f32[6,4,256]{2,1,0:T(4,128)S(1)}, u32[]{:S(2)}) copy-start(f32[6,4,256]{2,1,0:T(4,128)S(1)} %collective-permute-done.5.refs_3_) | copy-start | bytes 73732
  108.3 0.6 copy-start.2

commit v9 on v7

--- a/solution.py
+++ b/solution.py
@@ -7,7 +7,6 @@
 from jax.sharding import PartitionSpec as P
 
 STEP = 32
-PIVOTS = 4
 NT = (((1,), (1,)), ((), ()))
 NN = (((1,), (0,)), ((), ()))
 TN = (((0,), (0,)), ((), ()))
@@ -30,6 +29,21 @@
     b1, b2, b3 = b
     small = dot(a1, b3, dims) + dot(a3, b1, dims) + dot(a2, b2, dims)
     return dot(a1, b1, dims) + ((dot(a1, b2, dims) + dot(a2, b1, dims)) + small)
+
+
+def wide(parts):
+    one, two, three = parts
+    return jnp.concatenate([one, one, two, two, one, three], axis=1)
+
+
+def deep(parts):
+    one, two, three = parts
+    return jnp.concatenate([one, two, one, two, three, one], axis=0)
+
+
+def thirds(array):
+    count = array.shape[0] // 3
+    return array[:count] + (array[count:2 * count] + array[2 * count:])
 
 
 def apply(rows, parts, dims):
@@ -62,52 +76,69 @@
     def spread(row):
         return jnp.broadcast_to(row, (8, 128))
 
-    def wide(parts):
-        one, two, three = parts
-        return jnp.concatenate([one, one, two, two, one, three], axis=1)
-
-    def deep(parts):
-        if height < 128:
-            filler = jnp.zeros((128 - height, width), jnp.bfloat16)
-            parts = [jnp.concatenate([part, filler], axis=0) for part in parts]
-        one, two, three = parts
-        return jnp.concatenate([one, two, one, two, three, one], axis=0)
+    def padded(parts):
+        if height == 128:
+            return parts
+        filler = jnp.zeros((128 - height, width), jnp.bfloat16)
+        return [jnp.concatenate([part, filler], axis=0) for part in parts]
 
     def pivots(packs, pieces):
         placed = 0
-        for first in range(0, STEP, PIVOTS):
+        for first in range(0, STEP, 4):
             top, start = first // 8, first % 8
             tall = range(top, groups)
-            own = (place >= first) & (place < first + PIVOTS)
+            own = (place >= first) & (place < first + 4)
             one = jnp.where(place - 8 * top == sub, 1.0, 0.0)
+            each = range(len(packs))
             if start == 0:
-                inverses = [None] * len(packs)
-            columns = []
+                inverses = [None for _ in each]
+            u = [
+                [{g: jnp.take_along_axis(x[g], lane - place + (first + q), axis=1) for g in tall} for q in range(4)]
+                for x in packs
+            ]
+            a = [{(i, j): spread(u[s][j][top][start + i:start + i + 1, :]) for j in range(4) for i in range(j + 1)} for s in each]
             for x in packs:
-                columns.append([
-                    {g: jnp.take_along_axis(x[g], lane - place + (first + q), axis=1) for g in tall} for q in range(PIVOTS)
-                ])
                 for g in tall:
                     x[g] = jnp.where(own, one if g == top else 0.0, x[g])
-            for q in range(PIVOTS):
+            y = [[spread(x[top][start + q:start + q + 1, :]) for q in range(4)] for x in packs]
+            low = [{} for _ in each]
+            inv = [[None] * 4 for _ in each]
+            for p in (0, 2):
+                n = p + 1
+                delta = [a[s][p, p] * a[s][n, n] - a[s][p, n] * a[s][p, n] for s in each]
+                for s in each:
+                    inv[s][p] = pl.reciprocal(a[s][p, p], approx=True)
+                    inv[s][n] = pl.reciprocal(delta[s], approx=True) * a[s][p, p]
+                for j in range(n, 4):
+                    for s in each:
+                        low[s][j, p] = a[s][p, j] * inv[s][p]
+                for j in range(n + 1, 4):
+                    for s in each:
+                        a[s][n, j] = a[s][n, j] - low[s][n, p] * a[s][p, j]
+                for j in range(n + 1, 4):
+                    for s in each:
+                        low[s][j, n] = a[s][n, j] * inv[s][n]
+                for i in range(n + 1, 4):
+                    for j in range(i, 4):
+                        for s in each:
+                            a[s][i, j] = (a[s][i, j] - low[s][i, p] * a[s][p, j]) - low[s][i, n] * a[s][n, j]
+            for q in range(4):
                 at = start + q
-                for s, x in enumerate(packs):
-                    cols = columns[s]
-                    inverse = pl.reciprocal(spread(cols[q][top][at:at + 1, :]), approx=True)
-                    inverses[s] = inverse if at == 0 else jnp.where(sub >= at, inverse, inverses[s])
-                    c = {g: cols[q][g] * inverse for g in tall}
-                    for later in range(q + 1, PIVOTS):
-                        m = spread(cols[q][top][start + later:start + later + 1, :])
+                for s in each:
+                    for k in range(q):
                         for g in tall:
-                            cols[later][g] = cols[later][g] - c[g] * m
-                    c[top] = jnp.where(sub > at, c[top], 0.0)
-                    r = spread(x[top][at:at + 1, :])
+                            u[s][q][g] = u[s][q][g] - u[s][k][g] * low[s][q, k]
+                        y[s][q] = y[s][q] - y[s][k] * low[s][q, k]
+                    inverses[s] = inv[s][q] if at == 0 else jnp.where(sub >= at, inv[s][q], inverses[s])
                     for g in tall:
-                        x[g] = x[g] - c[g] * r
+                        m = u[s][q][g] * inv[s][q]
+                        if g == top:
+                            m = jnp.where(sub > at, m, 0.0)
+                        packs[s][g] = packs[s][g] - m * y[s][q]
                 while placed * STEP < (first + q + 1) * len(pieces):
                     pieces[placed]()
                     placed += 1
-            if start + PIVOTS == 8:
+            if start + 4 == 8:
                 for s, x in enumerate(packs):
                     x[top] = x[top] * (inverses[s] * lax.rsqrt(inverses[s]))
 
@@ -154,7 +185,7 @@
         sides = []
         for t in range(teams):
             ident = jnp.where(col_team == row_team % STEP, 1.0, 0.0)
-            sides.append(deep(split3(jnp.where(col_team < STEP, ident, slab_ref[t]))))
+            sides.append(deep(padded(split3(jnp.where(col_team < STEP, ident, slab_ref[t])))))
         pivots(packs, pieces)
         for t in range(teams):
             inner = jnp.concatenate(packs[t], axis=0)
@@ -170,7 +201,7 @@
             if height < 128:
                 ahead = jnp.concatenate([ahead, jnp.zeros((128 - height, 128), jnp.float32)], axis=0)
             ahead = wide(split3(ahead.T[:height]))
-            update = dot(ahead, deep(split3(pltpu.roll(slab, width - STEP, 1))), NN)
+            update = dot(ahead, deep(padded(split3(pltpu.roll(slab, width - STEP, 1)))), NN)
             coming = [pltpu.roll(ref[t * team + i, pl.ds(after, STEP), :], width - after, 1) for i in range(team)]
             slab_ref[t] = jnp.where(col_team >= width - STEP, 0.0, jnp.concatenate(coming, axis=0)) - update
             slab = pltpu.roll(slab, base, 1)
@@ -188,65 +219,126 @@
     return [pltpu.VMEM((systems // team, team * STEP, width), jnp.float32)] * 2
 
 
-def own_kernel(counts_ref, tiles_ref, w_ref, z_ref, g_ref, *scratch):
+def scaled(matrix):
+    factor_of = 1.0 / jnp.max(jnp.max(matrix, axis=1, keepdims=True), axis=0, keepdims=True)
+    return matrix * factor_of, jnp.sqrt(factor_of)
+
+
+def pick_kernel(slot_ref, tiles_ref, *refs):
+    out_refs, sems = refs[:-1], refs[-1]
+    copies = []
+    for e, out_ref in enumerate(out_refs):
+        source = tiles_ref.at[jnp.maximum(slot_ref[e], 0), 0:2]
+        copies.append(pltpu.make_async_copy(source, out_ref, sems.at[e]))
+    for copy in copies:
+        copy.start()
+    for copy in copies:
+        copy.wait()
+
+
+def own_kernel(counts_ref, tiles_ref, w_ref, g_ref, *scratch):
     systems, kslots, width, _ = tiles_ref.shape
     for s in range(systems):
         near = tiles_ref[s, 0:2].reshape(2 * width, width)
         g_ref[s] = dot(near, near, TN)
+    for s in range(systems):
         for k in range(2, kslots):
             @pl.when(k < counts_ref[s])
             def _():
                 tile = tiles_ref[s, k]
                 g_ref[s] += dot(tile, tile, TN)
+    roots = []
+    for s in range(systems):
+        g_ref[s], root = scaled(g_ref[s])
+        roots.append(root)
     factor(g_ref, *scratch)
     for s in range(systems):
-        w1, w2, w3 = split3(g_ref[s])
-        w_ref[s, 0] = w1
-        w_ref[s, 1] = w2
-        near = jnp.concatenate([tiles_ref[s, 1], tiles_ref[s, 0]], axis=0)
-        z = dot(w1, near, NT) + (dot(w2, near, NT) + dot(w3, near, NT))
-        z1, z2, z3 = split3(z)
-        z_ref[s, 0] = z1
-        z_ref[s, 1] = z2
-        z_ref[s, 2] = z3
-
-
-def pair_kernel(lanes, place_ref, x_ref, w_any, z_any, got_ref, *refs):
-    up_refs, refs = refs[:lanes], refs[lanes:]
-    low_ref, near_ref, w_ref, z_ref, t_ref, v_ref, r_ref, first_ref, sems, *scratch = refs
-    systems, _, width, _ = z_ref.shape
-    count = x_ref.shape[0] // lanes
+        for i, part in enumerate(split3(g_ref[s] * roots[s])):
+            w_ref[s, i] = part
+
+
+def collect(slot_ref, shifts, got_refs, near_ref, sems):
+    spare = near_ref.shape[0] - len(shifts)
     copies = []
-    for s in range(systems):
-        pairs = ((got_ref.at[place_ref[s]], near_ref.at[s]), (z_any.at[s], z_ref.at[s]))
-        copies.append([pltpu.make_async_copy(a, b, sems.at[s, i]) for i, (a, b) in enumerate(pairs)])
-        for copy in copies[s]:
-            copy.start()
-    w_copy = pltpu.make_async_copy(w_any, w_ref, sems.at[systems, 0])
-    w_copy.start()
-    low_ref[...] = jnp.zeros(low_ref.shape, low_ref.dtype)
-    for s in range(systems):
-        for copy in copies[s]:
-            copy.wait()
-        near = near_ref[s].reshape(2 * width, width)
-        near_t = near.T
-        z1, z2, z3 = z_ref[s, 0], z_ref[s, 1], z_ref[s, 2]
-        v = split3(dot(near_t, z1, NT) + (dot(near_t, z2, NT) + dot(near_t, z3, NT)))
+    for i, (e, got_ref) in enumerate(zip(shifts, got_refs)):
+        slot = jnp.where(slot_ref[e - 1] >= 0, slot_ref[e - 1], spare + i)
+        copies.append(pltpu.make_async_copy(got_ref, near_ref.at[slot], sems.at[i]))
+    for copy in copies:
+        copy.start()
+    return copies
+
+
+def schur(near, z):
+    near_t = near.T
+    v = split3(dot(near_t, z[0], NT) + (dot(near_t, z[1], NT) + dot(near_t, z[2], NT)))
+    return v, dot(near_t, near, NN) - dot6(v, v, NT)
+
+
+def link_kernel(shifts, slot_ref, w_ref, tiles_any, *refs):
+    got_refs, refs = refs[:len(shifts)], refs[len(shifts):]
+    z_ref, v_ref, t_ref, own_ref, near_ref, own_sem, sems = refs
+    systems, _, width, _ = w_ref.shape
+    own_copy = pltpu.make_async_copy(tiles_any.at[:, 0:2], own_ref, own_sem)
+    own_copy.start()
+    for s in range(systems):
+        near_ref[s] = jnp.zeros(near_ref.shape[1:], near_ref.dtype)
+    copies = collect(slot_ref, shifts, got_refs, near_ref, sems)
+    own_copy.wait()
+    for s in range(systems):
+        own = jnp.concatenate([own_ref[s, 1], own_ref[s, 0]], axis=0)
+        z = split3(dot(w_ref[s, 0], own, NT) + (dot(w_ref[s, 1], own, NT) + dot(w_ref[s, 2], own, NT)))
+        for i in range(3):
+            z_ref[s, i] = z[i]
+    for copy in copies:
+        copy.wait()
+    for s in range(systems):
+        v, t_ref[s] = schur(near_ref[s].reshape(2 * width, width), [z_ref[s, i] for i in range(3)])
         v_ref[s, 0] = v[0]
         v_ref[s, 1] = v[1]
-        t_ref[s] = dot(near_t, near, NN) - dot6(v, v, NT)
+
+
+def pair_kernel(lanes, shifts, late, place_ref, slot_ref, x_ref, w_any, z_any, v_any, t_any, *refs):
+    got_refs, up_refs, refs = refs[:len(shifts)], refs[len(shifts):len(shifts) + lanes], refs[len(shifts) + lanes:]
+    low_ref, near_ref, w_ref, z_ref, zj_ref, v_ref, t_ref, r_ref, first_ref, near_sems, sems, *scratch = refs
+    _, _, width, _ = z_ref.shape
+    systems = first_ref.shape[0]
+    count = x_ref.shape[0] // lanes
+    near_copies = collect(slot_ref, shifts, got_refs, near_ref, near_sems)
+    late_slots = [slot_ref[e - 1] for e in late]
+    copies = [
+        pltpu.make_async_copy(z_any.at[jnp.maximum(slot, 0)], z_ref.at[i], sems.at[i]) for i, slot in enumerate(late_slots)
+    ] + [
+        pltpu.make_async_copy(t_any, t_ref.at[0:systems], sems.at[2]),
+        pltpu.make_async_copy(v_any, v_ref.at[0:systems], sems.at[3]),
+        pltpu.make_async_copy(z_any.at[:, 0:2, :, width:], zj_ref, sems.at[4]),
+    ]
+    w_copy = pltpu.make_async_copy(w_any.at[:, 0:2], w_ref, sems.at[5])
+    for copy in copies + [w_copy]:
+        copy.start()
+    low_ref[...] = jnp.zeros(low_ref.shape, low_ref.dtype)
+    for copy in near_copies + copies:
+        copy.wait()
+    for i, slot in enumerate(late_slots):
+        at = jnp.where(slot >= 0, slot, systems + i)
+        near = near_ref[jnp.maximum(slot, 0)].reshape(2 * width, width)
+        v, t_ref[at] = schur(near, [z_ref[i, p] for p in range(3)])
+        v_ref[at, 0] = v[0]
+        v_ref[at, 1] = v[1]
+    roots = []
     for s in range(systems):
         x = x_ref[:, s * width:(s + 1) * width]
-        first_ref[s] = dot(x, z_ref[s, 0, :, width:], NT) + dot(x, z_ref[s, 1, :, width:], NT)
+        first_ref[s] = dot(x, zj_ref[s, 0], NT) + dot(x, zj_ref[s, 1], NT)
         r_ref[s] = dot(x, near_ref[s, 1], NN)
     for s in range(systems):
         r_ref[s] = r_ref[s] - apply(first_ref[s], (v_ref[s, 0], v_ref[s, 1]), NT)
-    factor(t_ref, *scratch)
-    parts = [split3(t_ref[s])[:2] for s in range(systems)]
+        t_ref[s], root = scaled(t_ref[s])
+        roots.append(root)
+    factor(t_ref.at[0:systems], *scratch)
+    w_copy.wait()
+    parts = [split3(t_ref[s] * roots[s])[:2] for s in range(systems)]
     half = [apply(r_ref[s], parts[s], NT) for s in range(systems)]
     last = [apply(half[s], parts[s], NN) for s in range(systems)]
     mid = [first_ref[s] - apply(last[s], (v_ref[s, 0], v_ref[s, 1]), NN) for s in range(systems)]
-    w_copy.wait()
     for s in range(systems):
         up = apply(mid[s], (w_ref[s, 0], w_ref[s, 1]), NN)
         for e in range(lanes):
@@ -278,59 +370,101 @@
     own_cnt = lax.dynamic_slice_in_dim(counts, my_panel * per_panel + my_lane * systems, systems, 0)
     panel_mates = lax.dynamic_slice(pattern, (my_panel * per_panel, 1), (per_panel, 1))[:, 0] // per_panel
     mate_panel = lax.dynamic_slice_in_dim(panel_mates, my_lane * systems, systems, 0)
-    hit = mate_panel[None, :] == jnp.arange(shards, dtype=jnp.int32)[:, None]
-    slot_of = jnp.sum(hit * jnp.arange(systems, dtype=jnp.int32)[None, :], axis=1)
+    hops = jnp.arange(1, shards, dtype=jnp.int32)
+
+    def slots(panels):
+        hit = mate_panel[None, :] == panels[:, None]
+        return jnp.max(jnp.where(hit, jnp.arange(systems, dtype=jnp.int32)[None, :], -1), axis=1)
+
     lane_word = my_lane[None].astype(jnp.int32)
 
-    def shift(value, by):
-        return lax.ppermute(value, "rhs", [(i, (i + by) % lanes) for i in range(lanes)])
-
-    received = lax.all_to_all(tiles[:, :2][slot_of], "panel", split_axis=0, concat_axis=0, tiled=True)
+    def shift(value, axis, by):
+        size = lax.axis_size(axis)
+        return lax.ppermute(value, axis, [(i, (i + by) % size) for i in range(size)])
 
     vmem = pl.BlockSpec(memory_space=pltpu.VMEM)
     smem = pl.BlockSpec(memory_space=pltpu.SMEM)
     anywhere = pl.BlockSpec(memory_space=pl.ANY)
-    params = pltpu.CompilerParams(vmem_limit_bytes=56 * 1024 * 1024)
-    w, z = pl.pallas_call(
+    params = pltpu.CompilerParams(vmem_limit_bytes=48 * 1024 * 1024)
+    pairs = shards - 1
+    every = tuple(range(1, shards))
+    late = (1, shards - 1)
+    early = tuple(e for e in every if e not in late)
+    pieces = pl.pallas_call(
+        pick_kernel,
+        out_shape=[jax.ShapeDtypeStruct((2, width, width), jnp.bfloat16)] * pairs,
+        in_specs=[smem, anywhere],
+        out_specs=[anywhere] * pairs,
+        scratch_shapes=[pltpu.SemaphoreType.DMA((pairs,))],
+    )(slots((my_panel + hops) % shards), tiles)
+    received = {e: shift(pieces[e - 1], "panel", e) for e in early}
+
+    w = pl.pallas_call(
         own_kernel,
-        out_shape=(
-            jax.ShapeDtypeStruct((systems, 2, width, width), jnp.bfloat16),
-            jax.ShapeDtypeStruct((systems, 3, width, 2 * width), jnp.bfloat16),
-        ),
+        out_shape=jax.ShapeDtypeStruct((systems, 3, width, width), jnp.bfloat16),
         in_specs=[smem, vmem],
-        out_specs=(vmem, vmem),
+        out_specs=vmem,
         scratch_shapes=[pltpu.VMEM((systems, width, width), jnp.float32)] + factor_scratch(systems, width),
         compiler_params=params,
-        cost_estimate=pl.CostEstimate(flops=40 * 10**9, bytes_accessed=8 * 10**6, transcendentals=0),
+        cost_estimate=pl.CostEstimate(flops=30 * 10**9, bytes_accessed=8 * 10**6, transcendentals=0),
     )(own_cnt, tiles)
 
-    inputs, w = lax.optimization_barrier((inputs, w))
+    come = [received[e] for e in early]
+    held, inputs, w, come = lax.optimization_barrier(([pieces[e - 1] for e in late], inputs, w, come))
+    received.update(zip(early, come))
+    received.update({e: shift(piece, "panel", e) for e, piece in zip(late, held)})
     parts = [lax.dynamic_slice_in_dim(inputs, my_lane * own_width, own_width, 1)]
     for e in range(1, lanes):
-        part = lax.dynamic_slice_in_dim(inputs, (my_lane + lanes - e) % lanes * own_width, own_width, 1)
-        parts.append(shift(part, -e))
+        block = lax.dynamic_slice_in_dim(inputs, (my_lane + lanes - e) % lanes * own_width, own_width, 1)
+        parts.append(shift(block, "rhs", -e))
     x = jnp.concatenate(parts, axis=0)
 
+    from_slot = slots((my_panel - hops) % shards)
+    z, v, t = pl.pallas_call(
+        functools.partial(link_kernel, early),
+        out_shape=(
+            jax.ShapeDtypeStruct((systems, 3, width, 2 * width), jnp.bfloat16),
+            jax.ShapeDtypeStruct((systems, 2, width, width), jnp.bfloat16),
+            jax.ShapeDtypeStruct((systems, width, width), jnp.float32),
+        ),
+        in_specs=[smem, vmem, anywhere] + [anywhere] * len(early),
+        out_specs=(vmem, vmem, vmem),
+        scratch_shapes=[
+            pltpu.VMEM((systems, 2, width, width), jnp.bfloat16),
+            pltpu.VMEM((systems + len(early), 2, width, width), jnp.bfloat16),
+            pltpu.SemaphoreType.DMA,
+            pltpu.SemaphoreType.DMA((len(early),)),
+        ],
+        compiler_params=params,
+        cost_estimate=pl.CostEstimate(flops=12 * 10**9, bytes_accessed=8 * 10**6, transcendentals=0),
+    )(from_slot, w, tiles, *[received[e] for e in early])
+
+    nrhs = lanes * nrhs_dev
     piece = jax.ShapeDtypeStruct((systems, nrhs_dev, width), jnp.float32)
     *up, low = pl.pallas_call(
-        functools.partial(pair_kernel, lanes),
+        functools.partial(pair_kernel, lanes, every, late),
         out_shape=[piece] * lanes + [jax.ShapeDtypeStruct((shards * lanes, nrhs_dev, width), jnp.bfloat16)],
-        in_specs=[smem, vmem, anywhere, anywhere, anywhere],
+        in_specs=[smem, smem, vmem] + [anywhere] * (4 + pairs),
         out_specs=[vmem] * (lanes + 1),
         scratch_shapes=[
+            pltpu.VMEM((systems + pairs, 2, width, width), jnp.bfloat16),
             pltpu.VMEM((systems, 2, width, width), jnp.bfloat16),
+            pltpu.VMEM((len(late), 3, width, 2 * width), jnp.bfloat16),
             pltpu.VMEM((systems, 2, width, width), jnp.bfloat16),
-            pltpu.VMEM((systems, 3, width, 2 * width), jnp.bfloat16),
-            pltpu.VMEM((systems, width, width), jnp.float32),
-            pltpu.VMEM((systems, 2, width, width), jnp.bfloat16),
-            pltpu.VMEM((systems, lanes * nrhs_dev, width), jnp.float32),
-            pltpu.VMEM((systems, lanes * nrhs_dev, width), jnp.float32),
-            pltpu.SemaphoreType.DMA((systems + 1, 2)),
+            pltpu.VMEM((systems + len(late), 2, width, width), jnp.bfloat16),
+            pltpu.VMEM((systems + len(late), width, width), jnp.float32),
+            pltpu.VMEM((systems, nrhs, width), jnp.float32),
+            pltpu.VMEM((systems, nrhs, width), jnp.float32),
+            pltpu.SemaphoreType.DMA((pairs,)),
+            pltpu.SemaphoreType.DMA((6,)),
         ] + factor_scratch(systems, width),
         compiler_params=params,
-    )(jnp.concatenate([mate_panel, lane_word]), x, w, z, received)
+    )(
+        jnp.concatenate([mate_panel, lane_word]), from_slot, x, w, z, v, t,
+        *[received[e] for e in every],
+    )
     low = lax.all_to_all(low, ("panel", "rhs"), split_axis=0, concat_axis=0, tiled=True)
-    up = [up[0]] + [shift(up[e], e) for e in range(1, lanes)]
+    up = [up[0]] + [shift(up[e], "rhs", e) for e in range(1, lanes)]
     return pl.pallas_call(
         functools.partial(place_kernel, lanes),
         out_shape=jax.ShapeDtypeStruct((nrhs_dev, per_panel * width), jnp.bfloat16),

time: 102 us -> 157 us (1.54)
  Pallas kernels: 52.9 us -> 112 us
  waiting for transfers between devices: 20.9 us -> 4.32 us
  starting transfers between devices: 19.5 us -> 34.6 us
  local copies, waits for them, and re-layouts: 5.04 us -> 2.82 us
    pallas_call x2 -> x4, Pallas kernels: 51.3 us -> 111 us  [the longest x1 57.4 us: on_device(): pl.pallas_call(pick_kernel, out_shape=[jax.ShapeDtypeStruct((2, width, wi...]
    ppermute x6 -> x13, starting transfers between devices: 8.48 us -> 31.1 us  [shift(): lax.ppermute(value, axis, [(i, (i + by) % size) for i in range(size)])]
    all_to_all x1 -> x0, waiting for transfers between devices: 16.7 us -> none  [on_device(): lax.all_to_all(tiles[:, :2][slot_of], 'panel', split_axis=0, concat_axis=...]
    all_to_all x1 -> x0, starting transfers between devices: 7.41 us -> none  [on_device(): lax.all_to_all(tiles[:, :2][slot_of], 'panel', split_axis=0, concat_axis=...]
    gather x1 -> x0, local copies, waits for them, and re-layouts: 2.04 us -> none  [on_device(): tiles[:, :2][slot_of]]
  transfers between devices with their start and end apart: 8 -> 14, of which waited for: 5 -> 4; matrix products, arithmetic and copies ran while one was open for 2% -> 1% of each run, Pallas kernels for 23% -> 20%
where the time goes in v9:
time: 157 us
  Pallas kernels  112 us (71%)
  starting transfers between devices  34.6 us (22%)
  waiting for transfers between devices  4.32 us (3%)
  local copies, waits for them, and re-layouts  2.82 us (2%)
  other arithmetic  2.31 us (1%)
    pallas_call x1, Pallas kernels, on_device(): pl.pallas_call(pick_kernel, out_shape=[jax.ShapeDtypeStruct((2, width, wi...  57.4 us
    ppermute x13, starting transfers between devices, shift(): lax.ppermute(value, axis, [(i, (i + by) % size) for i in range(size)])  31.1 us
    pallas_call x1, Pallas kernels, on_device(): pl.pallas_call(functools.partial(pair_kernel, lanes, every, late), out_sh...  22.3 us
    pallas_call x1, Pallas kernels, on_device(): pl.pallas_call(own_kernel, out_shape=jax.ShapeDtypeStruct((systems, 3, wi...  20.9 us
    pallas_call x1, Pallas kernels, on_device(): pl.pallas_call(functools.partial(link_kernel, early), out_shape=(jax.Shap...  10.1 us
    all_to_all x1, starting transfers between devices, on_device(): lax.all_to_all(low, ('panel', 'rhs'), split_axis=0, concat_axis=0, tiled=...  3.53 us
  transfers between devices with their start and end apart: 14, of which 4 were waited for; matrix products, arithmetic and copies ran while one was open for 1% of the time, Pallas kernels for 20%

profile of v9, /device:TPU:0, one launch (start us, length us, event | category | flops | bytes accessed | tf_op | source)
XLA Modules:
  0.0 156.5 jit_solution(5629066475086056237)
XLA Ops:
  0.0 0.8 bitcast_select_fusion
  0.9 0.7 select_reduce_fusion
  1.6 57.4 %shard_map.46 = (bf16[2,256,256]{2,1,0:T(8,128)(2,1)}, bf16[2,256,256]{2,1,0:T(8,128)(2,1)}, bf16[2,256,256]{2,1,0:T(8,128)(2,1)}, bf16[2,256,256]{2,1,0:T(8,128...) custom-call(s32[7]{0:T(128)} %get-tuple-element.53.slot_ref, ...), custom_call_target="tpu_custom_call" | custom-call | tf_op jit(solution)/shard_map/pallas_call | solution.py:393
  59.1 3.1 %collective-permute-start = (bf16[2,256,256]{2,1,0:T(8,128)(2,1)}, bf16[2,256,256]{2,1,0:T(8,128)(2,1)S(1)}, u32[]{:S(2)}, u32[]{:S(2)}) collective-permute-start(bf16[2,256,256]{2,1,0:T(8,128)(2,1)} %get-tuple-element.31), channel_id=1, source_target_pairs={{0,8},{4,12},{8,16},{12,20},{16,24},{20,28},{24,0},{28,4},{1,9},{5... | collective-permute-start | bytes 786440 | tf_op jit(solution)/shard_map/ppermute | solution.py:383
  62.1 2.5 %collective-permute-start.1 = (bf16[2,256,256]{2,1,0:T(8,128)(2,1)}, bf16[2,256,256]{2,1,0:T(8,128)(2,1)S(1)}, u32[]{:S(2)}, u32[]{:S(2)}) collective-permute-start(bf16[2,256,256]{2,1,0:T(8,128)(2,1)} %get-tuple-element.32), channel_id=1, source_target_pairs={{0,12},{4,16},{8,20},{12,24},{16,28},{20,0},{24,4},{28,8},{1,13},{... | collective-permute-start | bytes 786440 | tf_op jit(solution)/shard_map/ppermute | solution.py:383
  64.7 1.2 collective-permute-start.2
  65.9 2.6 %collective-permute-start.3 = (bf16[2,256,256]{2,1,0:T(8,128)(2,1)}, bf16[2,256,256]{2,1,0:T(8,128)(2,1)S(1)}, u32[]{:S(2)}, u32[]{:S(2)}) collective-permute-start(bf16[2,256,256]{2,1,0:T(8,128)(2,1)} %get-tuple-element.34), channel_id=1, source_target_pairs={{0,20},{4,24},{8,28},{12,0},{16,4},{20,8},{24,12},{28,16},{1,21},{... | collective-permute-start | bytes 786440 | tf_op jit(solution)/shard_map/ppermute | solution.py:383
  68.5 1.4 collective-permute-start.4
  70.0 20.9 %shard_map.47.w_ref.w_any = bf16[6,3,256,256]{3,2,1,0:T(8,128)(2,1)S(1)} custom-call(s32[6]{0:T(128)S(1)} %dynamic_slice.23.counts_ref, bf16[6,5,256,256]{3,2,1,0:T(8,128)(2,1)} %tiles_any.1), custom_call_target="tpu_custom_call" | custom-call | flops 30000001024 | bytes 8000000 | tf_op jit(solution)/shard_map/pallas_call | solution.py:402
  90.9 1.4 copy-done
  92.4 0.8 collective-permute-done.2.refs_2_.refs_3_
  93.4 1.6 collective-permute-start.6
  94.9 1.4 collective-permute-start.5
  96.3 7.1 %collective-permute-start.8 = (bf16[2,256,256]{2,1,0:T(8,128)(2,1)S(1)}, bf16[2,256,256]{2,1,0:T(8,128)(2,1)S(1)}, u32[]{:S(2)}, u32[]{:S(2)}) collective-permute-start(bf16[2,256,256]{2,1,0:T(8,128)(2,1)S(1)} %copy-done.8), channel_id=1, source_target_pairs={{0,4},{4,8},{8,12},{12,16},{16,20},{20,24},{24,28},{28,0},{1,5},{5... | collective-permute-start | bytes 786440 | tf_op jit(solution)/shard_map/ppermute | solution.py:383
  103.4 6.9 %collective-permute-start.9 = (bf16[2,256,256]{2,1,0:T(8,128)(2,1)S(1)}, bf16[2,256,256]{2,1,0:T(8,128)(2,1)S(1)}, u32[]{:S(2)}, u32[]{:S(2)}) collective-permute-start(bf16[2,256,256]{2,1,0:T(8,128)(2,1)S(1)} %copy-done.7), channel_id=1, source_target_pairs={{0,28},{4,0},{8,4},{12,8},{16,12},{20,16},{24,20},{28,24},{1,29},{... | collective-permute-start | bytes 786440 | tf_op jit(solution)/shard_map/ppermute | solution.py:383
  110.3 10.1 %shard_map.48 = (bf16[6,3,256,512]{3,2,1,0:T(8,128)(2,1)}, bf16[6,2,256,256]{3,2,1,0:T(8,128)(2,1)S(1)}, f32[6,256,256]{2,1,0:T(8,128)S(1)}) custom-call(s32[7]{0:T(128)S(1)} %get-tuple-element.54.slot_ref, bf16[6,3,256,256]{3,2,1,0:T(8,128)(2,1)} %copy-done, bf16[6,5,256,256]{3,2,1,0:T(8,128)(2,1)} %tiles_any.1, ...), custom_call_target="tpu_custom_call" | custom-call | flops 12000000000 | bytes 8000000 | tf_op jit(solution)/shard_map/pallas_call | solution.py:423
  120.5 22.3 %shard_map.49 = (f32[6,4,256]{2,1,0:T(4,128)S(1)}, f32[6,4,256]{2,1,0:T(4,128)S(1)}, f32[6,4,256]{2,1,0:T(4,128)S(1)}, f32[6,4,256]{2,1,0:T(4,128)S(1)}, bf16[32,4,256]{2,1,0:T(4,128)(2,1)}) custom-call(s32[7]{0:T(128)S(1)} %pad_add_fusion.1.place_ref, s32[7]{0:T(128)S(1)} %get-tuple-element.54.slot_ref, bf16[16,1536]{1,0:T(8,128)(2,1)S(1)} %pad_maximum_fusion.x_ref, ...), custom_call_target="tpu_custom_call" | custom-call | tf_op jit(solution)/shard_map/pallas_call | solution.py:444
  143.4 3.5 %all-to-all-start = ((bf16[32,4,256]{2,1,0:T(4,128)(2,1)}), bf16[32,4,256]{2,1,0:T(4,128)(2,1)S(1)}, u32[]{:S(2)}, u32[]{:S(2)}) async-start(bf16[32,4,256]{2,1,0:T(4,128)(2,1)} %get-tuple-element.48), calls=%async_computation | async-start | bytes 131072 | tf_op jit(solution)/shard_map/all_to_all | solution.py:466
  147.2 1.7 %collective-permute-start.11 = (f32[6,4,256]{2,1,0:T(4,128)S(1)}, f32[6,4,256]{2,1,0:T(4,128)S(1)}, u32[]{:S(2)}, u32[]{:S(2)}) collective-permute-start(f32[6,4,256]{2,1,0:T(4,128)S(1)} %get-tuple-element.51), channel_id=1, source_target_pairs={{0,2},{1,3},{2,0},{3,1},{4,6},{5,7},{6,4},{7,5},{8,10},{9,11},{10,... | collective-permute-start | bytes 73736 | tf_op jit(solution)/shard_map/ppermute | solution.py:383
  148.9 1.3 collective-permute-start.12
  150.2 0.7 pad_add_fusion.place_ref
  151.1 0.6 collective-permute-done.12.refs_3_
  151.7 2.6 %all-to-all-done.low_ref = bf16[32,4,256]{2,1,0:T(4,128)(2,1)S(1)} async-done(((bf16[32,4,256]{2,1,0:T(4,128)(2,1)}), bf16[32,4,256]{2,1,0:T(4,128)(2,1)S(1)}, u32[]{:S(2)}, u32[]{:S(2)}) %all-to-all-start) | async-done | bytes 65568 | tf_op jit(solution)/shard_map/all_to_all | solution.py:466
  154.9 1.6 %shard_map.50 = bf16[4,6144]{1,0:T(4,128)(2,1)} custom-call(s32[25]{0:T(128)} %pad_add_fusion.place_ref, bf16[32,4,256]{2,1,0:T(4,128)(2,1)} %copy-done.2, f32[6,4,256]{2,1,0:T(4,128)} %copy-done.1, f32[6,4,256]{2,1,0:T(4,128)} %copy-done.4, f32[6,4,256]{2,1,0:T(4,128)} %copy-done.5, f32[6,4,256]{2,1,0:T(4,128)} %copy-done.6), custom_call_target="tpu_custom_call" | custom-call | tf_op jit(solution)/shard_map/pallas_call | solution.py:468
  (38 shorter events, 2.1 us)
Async XLA Ops:
  0.0 69.9 %copy-start.9 = (s32[192]{0:T(256)S(1)}, s32[192]{0:T(256)}, u32[]{:S(2)}) copy-start(s32[192]{0:T(256)} %param.6) | copy-start | bytes 2308
  59.1 33.4 %collective-permute-start = (bf16[2,256,256]{2,1,0:T(8,128)(2,1)}, bf16[2,256,256]{2,1,0:T(8,128)(2,1)S(1)}, u32[]{:S(2)}, u32[]{:S(2)}) collective-permute-start(bf16[2,256,256]{2,1,0:T(8,128)(2,1)} %get-tuple-element.31), channel_id=1, source_target_pairs={{0,8},{4,12},{8,16},{12,20},{16,24},{20,28},{24,0},{28,4},{1,9},{5... | collective-permute-start | bytes 786440 | tf_op jit(solution)/shard_map/ppermute | solution.py:383
  62.1 30.3 %collective-permute-start.1 = (bf16[2,256,256]{2,1,0:T(8,128)(2,1)}, bf16[2,256,256]{2,1,0:T(8,128)(2,1)S(1)}, u32[]{:S(2)}, u32[]{:S(2)}) collective-permute-start(bf16[2,256,256]{2,1,0:T(8,128)(2,1)} %get-tuple-element.32), channel_id=1, source_target_pairs={{0,12},{4,16},{8,20},{12,24},{16,28},{20,0},{24,4},{28,8},{1,13},{... | collective-permute-start | bytes 786440 | tf_op jit(solution)/shard_map/ppermute | solution.py:383
  64.7 28.6 %collective-permute-start.2 = (bf16[2,256,256]{2,1,0:T(8,128)(2,1)}, bf16[2,256,256]{2,1,0:T(8,128)(2,1)S(1)}, u32[]{:S(2)}, u32[]{:S(2)}) collective-permute-start(bf16[2,256,256]{2,1,0:T(8,128)(2,1)} %get-tuple-element.33), channel_id=1, source_target_pairs={{0,16},{4,20},{8,24},{12,28},{16,0},{20,4},{24,8},{28,12},{1,17},{... | collective-permute-start | bytes 786440 | tf_op jit(solution)/shard_map/ppermute | solution.py:383
  65.9 27.4 %collective-permute-start.3 = (bf16[2,256,256]{2,1,0:T(8,128)(2,1)}, bf16[2,256,256]{2,1,0:T(8,128)(2,1)S(1)}, u32[]{:S(2)}, u32[]{:S(2)}) collective-permute-start(bf16[2,256,256]{2,1,0:T(8,128)(2,1)} %get-tuple-element.34), channel_id=1, source_target_pairs={{0,20},{4,24},{8,28},{12,0},{16,4},{20,8},{24,12},{28,16},{1,21},{... | collective-permute-start | bytes 786440 | tf_op jit(solution)/shard_map/ppermute | solution.py:383
  68.5 24.7 %collective-permute-start.4 = (bf16[2,256,256]{2,1,0:T(8,128)(2,1)}, bf16[2,256,256]{2,1,0:T(8,128)(2,1)S(1)}, u32[]{:S(2)}, u32[]{:S(2)}) collective-permute-start(bf16[2,256,256]{2,1,0:T(8,128)(2,1)} %get-tuple-element.35), channel_id=1, source_target_pairs={{0,24},{4,28},{8,0},{12,4},{16,8},{20,12},{24,16},{28,20},{1,25},{... | collective-permute-start | bytes 786440 | tf_op jit(solution)/shard_map/ppermute | solution.py:383
  70.0 23.3 %copy-start.3 = (bf16[4,6144]{1,0:T(4,128)(2,1)S(1)}, bf16[4,6144]{1,0:T(4,128)(2,1)}, u32[]{:S(2)}) copy-start(bf16[4,6144]{1,0:T(4,128)(2,1)} %param.7) | copy-start | bytes 147460
  70.0 26.4 %copy-start.8 = (bf16[2,256,256]{2,1,0:T(8,128)(2,1)S(1)}, bf16[2,256,256]{2,1,0:T(8,128)(2,1)}, u32[]{:S(2)}) copy-start(bf16[2,256,256]{2,1,0:T(8,128)(2,1)} %get-tuple-element.46) | copy-start | bytes 786436
  70.0 33.4 %copy-start.7 = (bf16[2,256,256]{2,1,0:T(8,128)(2,1)S(1)}, bf16[2,256,256]{2,1,0:T(8,128)(2,1)}, u32[]{:S(2)}) copy-start(bf16[2,256,256]{2,1,0:T(8,128)(2,1)} %get-tuple-element.47) | copy-start | bytes 786436
  90.9 1.4 copy-start
  93.3 27.1 %collective-permute-start.7 = (bf16[4,1536]{1,0:T(4,128)(2,1)S(1)}, bf16[4,1536]{1,0:T(4,128)(2,1)S(1)}, u32[]{:S(2)}, u32[]{:S(2)}) collective-permute-start(bf16[4,1536]{1,0:T(4,128)(2,1)S(1)} %get-tuple-element.56), channel_id=1, source_target_pairs={{0,1},{1,2},{2,3},{3,0},{4,5},{5,6},{6,7},{7,4},{8,9},{9,10},{10,1... | collective-permute-start | bytes 36872 | tf_op jit(solution)/shard_map/ppermute | solution.py:383
  93.4 27.0 %collective-permute-start.6 = (bf16[4,1536]{1,0:T(4,128)(2,1)S(1)}, bf16[4,1536]{1,0:T(4,128)(2,1)S(1)}, u32[]{:S(2)}, u32[]{:S(2)}) collective-permute-start(bf16[4,1536]{1,0:T(4,128)(2,1)S(1)} %get-tuple-element.57), channel_id=1, source_target_pairs={{0,2},{1,3},{2,0},{3,1},{4,6},{5,7},{6,4},{7,5},{8,10},{9,11},{10,... | collective-permute-start | bytes 36872 | tf_op jit(solution)/shard_map/ppermute | solution.py:383
  94.9 25.5 %collective-permute-start.5 = (bf16[4,1536]{1,0:T(4,128)(2,1)S(1)}, bf16[4,1536]{1,0:T(4,128)(2,1)S(1)}, u32[]{:S(2)}, u32[]{:S(2)}) collective-permute-start(bf16[4,1536]{1,0:T(4,128)(2,1)S(1)} %get-tuple-element.58), channel_id=1, source_target_pairs={{0,3},{1,0},{2,1},{3,2},{4,7},{5,4},{6,5},{7,6},{8,11},{9,8},{10,9... | collective-permute-start | bytes 36872 | tf_op jit(solution)/shard_map/ppermute | solution.py:383
  96.3 24.2 %collective-permute-start.8 = (bf16[2,256,256]{2,1,0:T(8,128)(2,1)S(1)}, bf16[2,256,256]{2,1,0:T(8,128)(2,1)S(1)}, u32[]{:S(2)}, u32[]{:S(2)}) collective-permute-start(bf16[2,256,256]{2,1,0:T(8,128)(2,1)S(1)} %copy-done.8), channel_id=1, source_target_pairs={{0,4},{4,8},{8,12},{12,16},{16,20},{20,24},{24,28},{28,0},{1,5},{5... | collective-permute-start | bytes 786440 | tf_op jit(solution)/shard_map/ppermute | solution.py:383
  103.4 17.1 %collective-permute-start.9 = (bf16[2,256,256]{2,1,0:T(8,128)(2,1)S(1)}, bf16[2,256,256]{2,1,0:T(8,128)(2,1)S(1)}, u32[]{:S(2)}, u32[]{:S(2)}) collective-permute-start(bf16[2,256,256]{2,1,0:T(8,128)(2,1)S(1)} %copy-done.7), channel_id=1, source_target_pairs={{0,28},{4,0},{8,4},{12,8},{16,12},{20,16},{24,20},{28,24},{1,29},{... | collective-permute-start | bytes 786440 | tf_op jit(solution)/shard_map/ppermute | solution.py:383
  142.8 0.6 copy-start.1
  143.4 10.9 %all-to-all-start = ((bf16[32,4,256]{2,1,0:T(4,128)(2,1)}), bf16[32,4,256]{2,1,0:T(4,128)(2,1)S(1)}, u32[]{:S(2)}, u32[]{:S(2)}) async-start(bf16[32,4,256]{2,1,0:T(4,128)(2,1)} %get-tuple-element.48), calls=%async_computation | async-start | bytes 131072 | tf_op jit(solution)/shard_map/all_to_all | solution.py:466
  146.9 4.0 %collective-permute-start.10 = (f32[6,4,256]{2,1,0:T(4,128)S(1)}, f32[6,4,256]{2,1,0:T(4,128)S(1)}, u32[]{:S(2)}, u32[]{:S(2)}) collective-permute-start(f32[6,4,256]{2,1,0:T(4,128)S(1)} %get-tuple-element.50), channel_id=1, source_target_pairs={{0,1},{1,2},{2,3},{3,0},{4,5},{5,6},{6,7},{7,4},{8,9},{9,10},{10,1... | collective-permute-start | bytes 73736 | tf_op jit(solution)/shard_map/ppermute | solution.py:383
  147.2 3.9 %collective-permute-start.11 = (f32[6,4,256]{2,1,0:T(4,128)S(1)}, f32[6,4,256]{2,1,0:T(4,128)S(1)}, u32[]{:S(2)}, u32[]{:S(2)}) collective-permute-start(f32[6,4,256]{2,1,0:T(4,128)S(1)} %get-tuple-element.51), channel_id=1, source_target_pairs={{0,2},{1,3},{2,0},{3,1},{4,6},{5,7},{6,4},{7,5},{8,10},{9,11},{10,... | collective-permute-start | bytes 73736 | tf_op jit(solution)/shard_map/ppermute | solution.py:383
  148.9 2.9 %collective-permute-start.12 = (f32[6,4,256]{2,1,0:T(4,128)S(1)}, f32[6,4,256]{2,1,0:T(4,128)S(1)}, u32[]{:S(2)}, u32[]{:S(2)}) collective-permute-start(f32[6,4,256]{2,1,0:T(4,128)S(1)} %get-tuple-element.52), channel_id=1, source_target_pairs={{0,3},{1,0},{2,1},{3,2},{4,7},{5,4},{6,5},{7,6},{8,11},{9,8},{10,9... | collective-permute-start | bytes 73736 | tf_op jit(solution)/shard_map/ppermute | solution.py:383
  150.9 3.5 %copy-start.4 = (f32[6,4,256]{2,1,0:T(4,128)}, f32[6,4,256]{2,1,0:T(4,128)S(1)}, u32[]{:S(2)}) copy-start(f32[6,4,256]{2,1,0:T(4,128)S(1)} %collective-permute-done.10.refs_1_) | copy-start | bytes 73732
  151.1 3.2 %copy-start.5 = (f32[6,4,256]{2,1,0:T(4,128)}, f32[6,4,256]{2,1,0:T(4,128)S(1)}, u32[]{:S(2)}) copy-start(f32[6,4,256]{2,1,0:T(4,128)S(1)} %collective-permute-done.11.refs_2_) | copy-start | bytes 73732
  151.7 2.6 %copy-start.6 = (f32[6,4,256]{2,1,0:T(4,128)}, f32[6,4,256]{2,1,0:T(4,128)S(1)}, u32[]{:S(2)}) copy-start(f32[6,4,256]{2,1,0:T(4,128)S(1)} %collective-permute-done.12.refs_3_) | copy-start | bytes 73732
  154.3 0.6 copy-start.2

commit v10 on v9

--- a/solution.py
+++ b/solution.py
@@ -236,7 +236,7 @@
         copy.wait()
 
 
-def own_kernel(counts_ref, tiles_ref, w_ref, g_ref, *scratch):
+def own_kernel(counts_ref, tiles_ref, w_ref, z_ref, g_ref, *scratch):
     systems, kslots, width, _ = tiles_ref.shape
     for s in range(systems):
         near = tiles_ref[s, 0:2].reshape(2 * width, width)
@@ -253,8 +253,13 @@
         roots.append(root)
     factor(g_ref, *scratch)
     for s in range(systems):
-        for i, part in enumerate(split3(g_ref[s] * roots[s])):
-            w_ref[s, i] = part
+        w = split3(g_ref[s] * roots[s])
+        w_ref[s, 0] = w[0]
+        w_ref[s, 1] = w[1]
+        own = jnp.concatenate([tiles_ref[s, 1], tiles_ref[s, 0]], axis=0)
+        z = split3(dot(w[0], own, NT) + (dot(w[1], own, NT) + dot(w[2], own, NT)))
+        for i in range(3):
+            z_ref[s, i] = z[i]
 
 
 def collect(slot_ref, shifts, got_refs, near_ref, sems):
@@ -274,24 +279,20 @@
     return v, dot(near_t, near, NN) - dot6(v, v, NT)
 
 
-def link_kernel(shifts, slot_ref, w_ref, tiles_any, *refs):
+def link_kernel(shifts, slot_ref, z_any, *refs):
     got_refs, refs = refs[:len(shifts)], refs[len(shifts):]
-    z_ref, v_ref, t_ref, own_ref, near_ref, own_sem, sems = refs
-    systems, _, width, _ = w_ref.shape
-    own_copy = pltpu.make_async_copy(tiles_any.at[:, 0:2], own_ref, own_sem)
-    own_copy.start()
+    v_ref, t_ref, z_ref, near_ref, z_sems, sems = refs
+    systems, _, width, _ = z_ref.shape
     for s in range(systems):
         near_ref[s] = jnp.zeros(near_ref.shape[1:], near_ref.dtype)
     copies = collect(slot_ref, shifts, got_refs, near_ref, sems)
-    own_copy.wait()
-    for s in range(systems):
-        own = jnp.concatenate([own_ref[s, 1], own_ref[s, 0]], axis=0)
-        z = split3(dot(w_ref[s, 0], own, NT) + (dot(w_ref[s, 1], own, NT) + dot(w_ref[s, 2], own, NT)))
-        for i in range(3):
-            z_ref[s, i] = z[i]
+    z_copies = [pltpu.make_async_copy(z_any.at[s], z_ref.at[s], z_sems.at[s]) for s in range(systems)]
+    for copy in z_copies:
+        copy.start()
     for copy in copies:
         copy.wait()
     for s in range(systems):
+        z_copies[s].wait()
         v, t_ref[s] = schur(near_ref[s].reshape(2 * width, width), [z_ref[s, i] for i in range(3)])
         v_ref[s, 0] = v[0]
         v_ref[s, 1] = v[1]
@@ -312,11 +313,11 @@
         pltpu.make_async_copy(v_any, v_ref.at[0:systems], sems.at[3]),
         pltpu.make_async_copy(z_any.at[:, 0:2, :, width:], zj_ref, sems.at[4]),
     ]
-    w_copy = pltpu.make_async_copy(w_any.at[:, 0:2], w_ref, sems.at[5])
+    w_copy = pltpu.make_async_copy(w_any, w_ref, sems.at[5])
     for copy in copies + [w_copy]:
         copy.start()
     low_ref[...] = jnp.zeros(low_ref.shape, low_ref.dtype)
-    for copy in near_copies + copies:
+    for copy in near_copies + copies[:-1]:
         copy.wait()
     for i, slot in enumerate(late_slots):
         at = jnp.where(slot >= 0, slot, systems + i)
@@ -324,6 +325,7 @@
         v, t_ref[at] = schur(near, [z_ref[i, p] for p in range(3)])
         v_ref[at, 0] = v[0]
         v_ref[at, 1] = v[1]
+    copies[-1].wait()
     roots = []
     for s in range(systems):
         x = x_ref[:, s * width:(s + 1) * width]
@@ -394,50 +396,51 @@
         pick_kernel,
         out_shape=[jax.ShapeDtypeStruct((2, width, width), jnp.bfloat16)] * pairs,
         in_specs=[smem, anywhere],
-        out_specs=[anywhere] * pairs,
+        out_specs=[vmem] * pairs,
         scratch_shapes=[pltpu.SemaphoreType.DMA((pairs,))],
+        compiler_params=params,
     )(slots((my_panel + hops) % shards), tiles)
     received = {e: shift(pieces[e - 1], "panel", e) for e in early}
 
-    w = pl.pallas_call(
+    w, z = pl.pallas_call(
         own_kernel,
-        out_shape=jax.ShapeDtypeStruct((systems, 3, width, width), jnp.bfloat16),
+        out_shape=(
+            jax.ShapeDtypeStruct((systems, 2, width, width), jnp.bfloat16),
+            jax.ShapeDtypeStruct((systems, 3, width, 2 * width), jnp.bfloat16),
+        ),
         in_specs=[smem, vmem],
-        out_specs=vmem,
+        out_specs=(vmem, vmem),
         scratch_shapes=[pltpu.VMEM((systems, width, width), jnp.float32)] + factor_scratch(systems, width),
         compiler_params=params,
         cost_estimate=pl.CostEstimate(flops=30 * 10**9, bytes_accessed=8 * 10**6, transcendentals=0),
     )(own_cnt, tiles)
 
+    inputs, w = lax.optimization_barrier((inputs, w))
+    x = lax.all_to_all(inputs, "rhs", split_axis=1, concat_axis=0, tiled=True)
+    x = lax.dynamic_slice_in_dim(jnp.concatenate([x, x], axis=0), my_lane * nrhs_dev, lanes * nrhs_dev, 0)
+
     come = [received[e] for e in early]
-    held, inputs, w, come = lax.optimization_barrier(([pieces[e - 1] for e in late], inputs, w, come))
+    held, z, come = lax.optimization_barrier(([pieces[e - 1] for e in late], z, come))
     received.update(zip(early, come))
     received.update({e: shift(piece, "panel", e) for e, piece in zip(late, held)})
-    parts = [lax.dynamic_slice_in_dim(inputs, my_lane * own_width, own_width, 1)]
-    for e in range(1, lanes):
-        block = lax.dynamic_slice_in_dim(inputs, (my_lane + lanes - e) % lanes * own_width, own_width, 1)
-        parts.append(shift(block, "rhs", -e))
-    x = jnp.concatenate(parts, axis=0)
-
     from_slot = slots((my_panel - hops) % shards)
-    z, v, t = pl.pallas_call(
+    v, t = pl.pallas_call(
         functools.partial(link_kernel, early),
         out_shape=(
-            jax.ShapeDtypeStruct((systems, 3, width, 2 * width), jnp.bfloat16),
             jax.ShapeDtypeStruct((systems, 2, width, width), jnp.bfloat16),
             jax.ShapeDtypeStruct((systems, width, width), jnp.float32),
         ),
-        in_specs=[smem, vmem, anywhere] + [anywhere] * len(early),
-        out_specs=(vmem, vmem, vmem),
+        in_specs=[smem] + [anywhere] * (1 + len(early)),
+        out_specs=(vmem, vmem),
         scratch_shapes=[
-            pltpu.VMEM((systems, 2, width, width), jnp.bfloat16),
+            pltpu.VMEM((systems, 3, width, 2 * width), jnp.bfloat16),
             pltpu.VMEM((systems + len(early), 2, width, width), jnp.bfloat16),
-            pltpu.SemaphoreType.DMA,
+            pltpu.SemaphoreType.DMA((systems,)),
             pltpu.SemaphoreType.DMA((len(early),)),
         ],
         compiler_params=params,
         cost_estimate=pl.CostEstimate(flops=12 * 10**9, bytes_accessed=8 * 10**6, transcendentals=0),
-    )(from_slot, w, tiles, *[received[e] for e in early])
+    )(from_slot, z, *[received[e] for e in early])
 
     nrhs = lanes * nrhs_dev
     piece = jax.ShapeDtypeStruct((systems, nrhs_dev, width), jnp.float32)

time: 157 us -> 100 us (0.64)
  Pallas kernels: 112 us -> 57.4 us
  starting transfers between devices: 34.6 us -> 25.1 us
  waiting for transfers between devices: 4.32 us -> 8.73 us
  local copies, waits for them, and re-layouts: 2.82 us -> 6.78 us
    pallas_call x1, Pallas kernels: 57.4 us -> 1.84 us  [on_device(): pl.pallas_call(pick_kernel, out_shape=[jax.ShapeDtypeStruct((2, width, wi...]
    ppermute x13 -> x10, starting transfers between devices: 31.1 us -> 19.1 us  [shift(): lax.ppermute(value, axis, [(i, (i + by) % size) for i in range(size)])]
    unnamed x20 -> x18, local copies, waits for them, and re-layouts: 2.64 us -> 6.61 us
    all_to_all x0 -> x1, waiting for transfers between devices: none -> 3.92 us  [on_device(): x = lax.all_to_all(inputs, 'rhs', split_axis=1, concat_axis=0, tiled=True)]
    all_to_all x0 -> x1, starting transfers between devices: none -> 3.27 us  [on_device(): x = lax.all_to_all(inputs, 'rhs', split_axis=1, concat_axis=0, tiled=True)]
    pallas_call x1, Pallas kernels: 20.9 us -> 22.8 us  [on_device(): pl.pallas_call(own_kernel, out_shape=(jax.ShapeDtypeStruct((systems, 2, w...]
  transfers between devices with their start and end apart: 14 -> 12, of which waited for: 4 -> 5; matrix products, arithmetic and copies ran while one was open for 1% -> 1% of each run, Pallas kernels for 20% -> 31%
where the time goes in v10:
time: 100 us; the launch traced here: 99.9 us
  Pallas kernels  57.4 us (57%)
  starting transfers between devices  25.1 us (25%)
  waiting for transfers between devices  8.73 us (9%)
  local copies, waits for them, and re-layouts  6.78 us (7%)
  other arithmetic  1.72 us (2%)
    pallas_call x1, Pallas kernels, on_device(): pl.pallas_call(own_kernel, out_shape=(jax.ShapeDtypeStruct((systems, 2, w...  22.8 us
    pallas_call x1, Pallas kernels, on_device(): pl.pallas_call(functools.partial(pair_kernel, lanes, every, late), out_sh...  22.6 us
    ppermute x10, starting transfers between devices, shift(): lax.ppermute(value, axis, [(i, (i + by) % size) for i in range(size)])  19.1 us
    pallas_call x1, Pallas kernels, on_device(): pl.pallas_call(functools.partial(link_kernel, early), out_shape=(jax.Shap...  8.59 us
    unnamed x18, local copies, waits for them, and re-layouts  6.61 us
    all_to_all x1, waiting for transfers between devices, on_device(): x = lax.all_to_all(inputs, 'rhs', split_axis=1, concat_axis=0, tiled=True)  3.92 us
    all_to_all x1, starting transfers between devices, on_device(): x = lax.all_to_all(inputs, 'rhs', split_axis=1, concat_axis=0, tiled=True)  3.27 us
    all_to_all x1, starting transfers between devices, on_device(): lax.all_to_all(low, ('panel', 'rhs'), split_axis=0, concat_axis=0, tiled=...  2.81 us
  transfers between devices with their start and end apart: 12, of which 5 were waited for; matrix products, arithmetic and copies ran while one was open for 1% of the time, Pallas kernels for 31%

profile of v10, /device:TPU:0, one launch (start us, length us, event | category | flops | bytes accessed | tf_op | source)
XLA Modules:
  0.0 99.9 jit_solution(5098994021434535937)
XLA Ops:
  0.0 0.8 bitcast_select_fusion
  1.1 2.1 %copy-done = bf16[6,5,256,256]{3,2,1,0:T(8,128)(2,1)S(1)} copy-done((bf16[6,5,256,256]{3,2,1,0:T(8,128)(2,1)S(1)}, bf16[6,5,256,256]{3,2,1,0:T(8,128)(2,1)}, u32[]{:S(2)}) %copy-start) | copy-done | bytes 3932184
  3.2 1.8 %shard_map.47 = (bf16[2,256,256]{2,1,0:T(8,128)(2,1)S(1)}, bf16[2,256,256]{2,1,0:T(8,128)(2,1)}, bf16[2,256,256]{2,1,0:T(8,128)(2,1)}, bf16[2,256,256]{2,1,0:T(8...) custom-call(s32[7]{0:T(128)S(1)} %get-tuple-element.57.slot_ref, ...), custom_call_target="tpu_custom_call" | custom-call | tf_op jit(solution)/shard_map/pallas_call | solution.py:395
  5.1 3.1 %collective-permute-start = (bf16[2,256,256]{2,1,0:T(8,128)(2,1)}, bf16[2,256,256]{2,1,0:T(8,128)(2,1)S(1)}, u32[]{:S(2)}, u32[]{:S(2)}) collective-permute-start(bf16[2,256,256]{2,1,0:T(8,128)(2,1)} %get-tuple-element.37), channel_id=1, source_target_pairs={{0,8},{4,12},{8,16},{12,20},{16,24},{20,28},{24,0},{28,4},{1,9},{5... | collective-permute-start | bytes 786440 | tf_op jit(solution)/shard_map/ppermute | solution.py:385
  8.1 2.5 %collective-permute-start.1 = (bf16[2,256,256]{2,1,0:T(8,128)(2,1)}, bf16[2,256,256]{2,1,0:T(8,128)(2,1)S(1)}, u32[]{:S(2)}, u32[]{:S(2)}) collective-permute-start(bf16[2,256,256]{2,1,0:T(8,128)(2,1)} %get-tuple-element.38), channel_id=1, source_target_pairs={{0,12},{4,16},{8,20},{12,24},{16,28},{20,0},{24,4},{28,8},{1,13},{... | collective-permute-start | bytes 786440 | tf_op jit(solution)/shard_map/ppermute | solution.py:385
  10.7 1.2 %collective-permute-start.2 = (bf16[2,256,256]{2,1,0:T(8,128)(2,1)}, bf16[2,256,256]{2,1,0:T(8,128)(2,1)S(1)}, u32[]{:S(2)}, u32[]{:S(2)}) collective-permute-start(bf16[2,256,256]{2,1,0:T(8,128)(2,1)} %get-tuple-element.39), channel_id=1, source_target_pairs={{0,16},{4,20},{8,24},{12,28},{16,0},{20,4},{24,8},{28,12},{1,17},{... | collective-permute-start | bytes 786440 | tf_op jit(solution)/shard_map/ppermute | solution.py:385
  11.9 2.6 %collective-permute-start.3 = (bf16[2,256,256]{2,1,0:T(8,128)(2,1)}, bf16[2,256,256]{2,1,0:T(8,128)(2,1)S(1)}, u32[]{:S(2)}, u32[]{:S(2)}) collective-permute-start(bf16[2,256,256]{2,1,0:T(8,128)(2,1)} %get-tuple-element.40), channel_id=1, source_target_pairs={{0,20},{4,24},{8,28},{12,0},{16,4},{20,8},{24,12},{28,16},{1,21},{... | collective-permute-start | bytes 786440 | tf_op jit(solution)/shard_map/ppermute | solution.py:385
  14.5 1.4 %collective-permute-start.4 = (bf16[2,256,256]{2,1,0:T(8,128)(2,1)}, bf16[2,256,256]{2,1,0:T(8,128)(2,1)S(1)}, u32[]{:S(2)}, u32[]{:S(2)}) collective-permute-start(bf16[2,256,256]{2,1,0:T(8,128)(2,1)} %get-tuple-element.41), channel_id=1, source_target_pairs={{0,24},{4,28},{8,0},{12,4},{16,8},{20,12},{24,16},{28,20},{1,25},{... | collective-permute-start | bytes 786440 | tf_op jit(solution)/shard_map/ppermute | solution.py:385
  16.0 2.1 %copy-done.1 = bf16[6,5,256,256]{3,2,1,0:T(8,128)(2,1)S(1)} copy-done((bf16[6,5,256,256]{3,2,1,0:T(8,128)(2,1)S(1)}, bf16[6,5,256,256]{3,2,1,0:T(8,128)(2,1)}, u32[]{:S(2)}) %copy-start.1) | copy-done | bytes 3932184
  18.1 22.8 %shard_map.46 = (bf16[6,2,256,256]{3,2,1,0:T(8,128)(2,1)S(1)}, bf16[6,3,256,512]{3,2,1,0:T(8,128)(2,1)}) custom-call(s32[6]{0:T(128)S(1)} %dynamic_slice.14.counts_ref, bf16[6,5,256,256]{3,2,1,0:T(8,128)(2,1)S(1)} %copy-done.1), custom_call_target="tpu_custom_call" | custom-call | flops 30000001024 | bytes 8000000 | tf_op jit(solution)/shard_map/pallas_call | solution.py:405
  40.9 3.3 %all-to-all-start = ((bf16[4,4,1536]{2,0,1:T(4,128)(2,1)}), bf16[4,4,1536]{2,0,1:T(4,128)(2,1)S(1)}, u32[]{:S(2)}, u32[]{:S(2)}) async-start(bf16[4,4,1536]{2,0,1:T(4,128)(2,1)} %bitcast.3), calls=%async_computation | async-start | bytes 98304 | tf_op jit(solution)/shard_map/all_to_all | solution.py:419
  44.2 3.9 %all-to-all-done = bf16[4,4,1536]{2,0,1:T(4,128)(2,1)S(1)} async-done(((bf16[4,4,1536]{2,0,1:T(4,128)(2,1)}), bf16[4,4,1536]{2,0,1:T(4,128)(2,1)S(1)}, u32[]{:S(2)}, u32[]{:S(2)}) %all-to-all-start) | async-done | bytes 49184 | tf_op jit(solution)/shard_map/all_to_all | solution.py:419
  48.4 4.9 %collective-permute-start.6 = (bf16[2,256,256]{2,1,0:T(8,128)(2,1)S(1)}, bf16[2,256,256]{2,1,0:T(8,128)(2,1)S(1)}, u32[]{:S(2)}, u32[]{:S(2)}) collective-permute-start(bf16[2,256,256]{2,1,0:T(8,128)(2,1)S(1)} %get-tuple-element.51), channel_id=1, source_target_pairs={{0,28},{4,0},{8,4},{12,8},{16,12},{20,16},{24,20},{28,24},{1,29},{... | collective-permute-start | bytes 786440 | tf_op jit(solution)/shard_map/ppermute | solution.py:385
  53.2 8.6 %shard_map.48 = (bf16[6,2,256,256]{3,2,1,0:T(8,128)(2,1)S(1)}, f32[6,256,256]{2,1,0:T(8,128)S(1)}) custom-call(s32[7]{0:T(128)S(1)} %get-tuple-element.58.slot_ref, bf16[6,3,256,512]{3,2,1,0:T(8,128)(2,1)} %get-tuple-element.42.z_any, bf16[2,256,256]{2,1,0:T(8,128)(2,1)S(1)} %collective-permute-done.refs_0_.refs_1_, ...), custom_call_target="tpu_custom_call" | custom-call | flops 12000000000 | bytes 8000000 | tf_op jit(solution)/shard_map/pallas_call | solution.py:427
  61.8 1.2 %copy-done.2 = f32[6,256,256]{2,1,0:T(8,128)} copy-done((f32[6,256,256]{2,1,0:T(8,128)}, f32[6,256,256]{2,1,0:T(8,128)S(1)}, u32[]{:S(2)}) %copy-start.2) | copy-done | bytes 1572888
  63.0 1.3 %collective-permute-done.6.refs_6_ = bf16[2,256,256]{2,1,0:T(8,128)(2,1)S(1)} collective-permute-done((bf16[2,256,256]{2,1,0:T(8,128)(2,1)S(1)}, bf16[2,256,256]{2,1,0:T(8,128)(2,1)S(1)}, u32[]{:S(2)}, u32[]{:S(2)}) %collective-permute-start.6) | collective-permute-done | bytes 262176 | tf_op jit(solution)/shard_map/ppermute | solution.py:385
  64.3 22.6 %shard_map.49 = (f32[6,4,256]{2,1,0:T(4,128)S(1)}, f32[6,4,256]{2,1,0:T(4,128)S(1)}, f32[6,4,256]{2,1,0:T(4,128)S(1)}, f32[6,4,256]{2,1,0:T(4,128)S(1)}, bf16[32,4,256]{2,1,0:T(4,128)(2,1)}) custom-call(s32[7]{0:T(128)S(1)} %pad_add_fusion.1.place_ref, s32[7]{0:T(128)S(1)} %get-tuple-element.58.slot_ref, bf16[16,1536]{1,0:T(8,128)(2,1)S(1)} %fusion.x_ref, ...), custom_call_target="tpu_custom_call" | custom-call | tf_op jit(solution)/shard_map/pallas_call | solution.py:447
  87.5 2.8 %all-to-all-start.1 = ((bf16[32,4,256]{2,1,0:T(4,128)(2,1)}), bf16[32,4,256]{2,1,0:T(4,128)(2,1)S(1)}, u32[]{:S(2)}, u32[]{:S(2)}) async-start(bf16[32,4,256]{2,1,0:T(4,128)(2,1)} %get-tuple-element.52), calls=%async_computation.1 | async-start | bytes 131072 | tf_op jit(solution)/shard_map/all_to_all | solution.py:469
  90.6 1.7 %collective-permute-start.8 = (f32[6,4,256]{2,1,0:T(4,128)S(1)}, f32[6,4,256]{2,1,0:T(4,128)S(1)}, u32[]{:S(2)}, u32[]{:S(2)}) collective-permute-start(f32[6,4,256]{2,1,0:T(4,128)S(1)} %get-tuple-element.55), channel_id=1, source_target_pairs={{0,2},{1,3},{2,0},{3,1},{4,6},{5,7},{6,4},{7,5},{8,10},{9,11},{10,... | collective-permute-start | bytes 73736 | tf_op jit(solution)/shard_map/ppermute | solution.py:385
  92.2 1.3 %collective-permute-start.9 = (f32[6,4,256]{2,1,0:T(4,128)S(1)}, f32[6,4,256]{2,1,0:T(4,128)S(1)}, u32[]{:S(2)}, u32[]{:S(2)}) collective-permute-start(f32[6,4,256]{2,1,0:T(4,128)S(1)} %get-tuple-element.56), channel_id=1, source_target_pairs={{0,3},{1,0},{2,1},{3,2},{4,7},{5,4},{6,5},{7,6},{8,11},{9,8},{10,9... | collective-permute-start | bytes 73736 | tf_op jit(solution)/shard_map/ppermute | solution.py:385
  94.4 0.6 collective-permute-done.9.refs_3_
  95.1 2.6 %all-to-all-done.1.low_ref = bf16[32,4,256]{2,1,0:T(4,128)(2,1)S(1)} async-done(((bf16[32,4,256]{2,1,0:T(4,128)(2,1)}), bf16[32,4,256]{2,1,0:T(4,128)(2,1)S(1)}, u32[]{:S(2)}, u32[]{:S(2)}) %all-to-all-start.1) | async-done | bytes 65568 | tf_op jit(solution)/shard_map/all_to_all | solution.py:469
  97.7 0.6 copy-done.4
  98.3 1.6 %shard_map.50 = bf16[4,6144]{1,0:T(4,128)(2,1)} custom-call(s32[25]{0:T(128)} %pad_add_fusion.place_ref, bf16[32,4,256]{2,1,0:T(4,128)(2,1)} %copy-done.4, f32[6,4,256]{2,1,0:T(4,128)} %copy-done.3, f32[6,4,256]{2,1,0:T(4,128)} %copy-done.5, f32[6,4,256]{2,1,0:T(4,128)} %copy-done.6, f32[6,4,256]{2,1,0:T(4,128)} %copy-done.7), custom_call_target="tpu_custom_call" | custom-call | tf_op jit(solution)/shard_map/pallas_call | solution.py:471
  (32 shorter events, 2.4 us)
Async XLA Ops:
  1.1 2.1 %copy-start = (bf16[6,5,256,256]{3,2,1,0:T(8,128)(2,1)S(1)}, bf16[6,5,256,256]{3,2,1,0:T(8,128)(2,1)}, u32[]{:S(2)}) copy-start(bf16[6,5,256,256]{3,2,1,0:T(8,128)(2,1)} %tiles_ref.3) | copy-start | bytes 11796484
  3.2 12.7 %copy-start.8 = (s32[192]{0:T(256)S(1)}, s32[192]{0:T(256)}, u32[]{:S(2)}) copy-start(s32[192]{0:T(256)} %param.6) | copy-start | bytes 2308
  5.1 43.2 %collective-permute-start = (bf16[2,256,256]{2,1,0:T(8,128)(2,1)}, bf16[2,256,256]{2,1,0:T(8,128)(2,1)S(1)}, u32[]{:S(2)}, u32[]{:S(2)}) collective-permute-start(bf16[2,256,256]{2,1,0:T(8,128)(2,1)} %get-tuple-element.37), channel_id=1, source_target_pairs={{0,8},{4,12},{8,16},{12,20},{16,24},{20,28},{24,0},{28,4},{1,9},{5... | collective-permute-start | bytes 786440 | tf_op jit(solution)/shard_map/ppermute | solution.py:385
  8.1 40.1 %collective-permute-start.1 = (bf16[2,256,256]{2,1,0:T(8,128)(2,1)}, bf16[2,256,256]{2,1,0:T(8,128)(2,1)S(1)}, u32[]{:S(2)}, u32[]{:S(2)}) collective-permute-start(bf16[2,256,256]{2,1,0:T(8,128)(2,1)} %get-tuple-element.38), channel_id=1, source_target_pairs={{0,12},{4,16},{8,20},{12,24},{16,28},{20,0},{24,4},{28,8},{1,13},{... | collective-permute-start | bytes 786440 | tf_op jit(solution)/shard_map/ppermute | solution.py:385
  10.7 37.6 %collective-permute-start.2 = (bf16[2,256,256]{2,1,0:T(8,128)(2,1)}, bf16[2,256,256]{2,1,0:T(8,128)(2,1)S(1)}, u32[]{:S(2)}, u32[]{:S(2)}) collective-permute-start(bf16[2,256,256]{2,1,0:T(8,128)(2,1)} %get-tuple-element.39), channel_id=1, source_target_pairs={{0,16},{4,20},{8,24},{12,28},{16,0},{20,4},{24,8},{28,12},{1,17},{... | collective-permute-start | bytes 786440 | tf_op jit(solution)/shard_map/ppermute | solution.py:385
  11.9 36.4 %collective-permute-start.3 = (bf16[2,256,256]{2,1,0:T(8,128)(2,1)}, bf16[2,256,256]{2,1,0:T(8,128)(2,1)S(1)}, u32[]{:S(2)}, u32[]{:S(2)}) collective-permute-start(bf16[2,256,256]{2,1,0:T(8,128)(2,1)} %get-tuple-element.40), channel_id=1, source_target_pairs={{0,20},{4,24},{8,28},{12,0},{16,4},{20,8},{24,12},{28,16},{1,21},{... | collective-permute-start | bytes 786440 | tf_op jit(solution)/shard_map/ppermute | solution.py:385
  14.5 33.7 %collective-permute-start.4 = (bf16[2,256,256]{2,1,0:T(8,128)(2,1)}, bf16[2,256,256]{2,1,0:T(8,128)(2,1)S(1)}, u32[]{:S(2)}, u32[]{:S(2)}) collective-permute-start(bf16[2,256,256]{2,1,0:T(8,128)(2,1)} %get-tuple-element.41), channel_id=1, source_target_pairs={{0,24},{4,28},{8,0},{12,4},{16,8},{20,12},{24,16},{28,20},{1,25},{... | collective-permute-start | bytes 786440 | tf_op jit(solution)/shard_map/ppermute | solution.py:385
  16.0 2.1 %copy-start.1 = (bf16[6,5,256,256]{3,2,1,0:T(8,128)(2,1)S(1)}, bf16[6,5,256,256]{3,2,1,0:T(8,128)(2,1)}, u32[]{:S(2)}) copy-start(bf16[6,5,256,256]{3,2,1,0:T(8,128)(2,1)} %tiles_ref.3) | copy-start | bytes 11796484
  40.9 7.3 %all-to-all-start = ((bf16[4,4,1536]{2,0,1:T(4,128)(2,1)}), bf16[4,4,1536]{2,0,1:T(4,128)(2,1)S(1)}, u32[]{:S(2)}, u32[]{:S(2)}) async-start(bf16[4,4,1536]{2,0,1:T(4,128)(2,1)} %bitcast.3), calls=%async_computation | async-start | bytes 98304 | tf_op jit(solution)/shard_map/all_to_all | solution.py:419
  48.3 14.7 %collective-permute-start.5 = (bf16[2,256,256]{2,1,0:T(8,128)(2,1)S(1)}, bf16[2,256,256]{2,1,0:T(8,128)(2,1)S(1)}, u32[]{:S(2)}, u32[]{:S(2)}) collective-permute-start(bf16[2,256,256]{2,1,0:T(8,128)(2,1)S(1)} %get-tuple-element.50), channel_id=1, source_target_pairs={{0,4},{4,8},{8,12},{12,16},{16,20},{20,24},{24,28},{28,0},{1,5},{5... | collective-permute-start | bytes 786440 | tf_op jit(solution)/shard_map/ppermute | solution.py:385
  48.4 15.9 %collective-permute-start.6 = (bf16[2,256,256]{2,1,0:T(8,128)(2,1)S(1)}, bf16[2,256,256]{2,1,0:T(8,128)(2,1)S(1)}, u32[]{:S(2)}, u32[]{:S(2)}) collective-permute-start(bf16[2,256,256]{2,1,0:T(8,128)(2,1)S(1)} %get-tuple-element.51), channel_id=1, source_target_pairs={{0,28},{4,0},{8,4},{12,8},{16,12},{20,16},{24,20},{28,24},{1,29},{... | collective-permute-start | bytes 786440 | tf_op jit(solution)/shard_map/ppermute | solution.py:385
  61.8 1.2 %copy-start.2 = (f32[6,256,256]{2,1,0:T(8,128)}, f32[6,256,256]{2,1,0:T(8,128)S(1)}, u32[]{:S(2)}) copy-start(f32[6,256,256]{2,1,0:T(8,128)S(1)} %get-tuple-element.49.t_any) | copy-start | bytes 4718596
  86.8 0.6 copy-start.3
  87.5 10.2 %all-to-all-start.1 = ((bf16[32,4,256]{2,1,0:T(4,128)(2,1)}), bf16[32,4,256]{2,1,0:T(4,128)(2,1)S(1)}, u32[]{:S(2)}, u32[]{:S(2)}) async-start(bf16[32,4,256]{2,1,0:T(4,128)(2,1)} %get-tuple-element.52), calls=%async_computation.1 | async-start | bytes 131072 | tf_op jit(solution)/shard_map/all_to_all | solution.py:469
  90.3 3.9 %collective-permute-start.7 = (f32[6,4,256]{2,1,0:T(4,128)S(1)}, f32[6,4,256]{2,1,0:T(4,128)S(1)}, u32[]{:S(2)}, u32[]{:S(2)}) collective-permute-start(f32[6,4,256]{2,1,0:T(4,128)S(1)} %get-tuple-element.54), channel_id=1, source_target_pairs={{0,1},{1,2},{2,3},{3,0},{4,5},{5,6},{6,7},{7,4},{8,9},{9,10},{10,1... | collective-permute-start | bytes 73736 | tf_op jit(solution)/shard_map/ppermute | solution.py:385
  90.6 3.9 %collective-permute-start.8 = (f32[6,4,256]{2,1,0:T(4,128)S(1)}, f32[6,4,256]{2,1,0:T(4,128)S(1)}, u32[]{:S(2)}, u32[]{:S(2)}) collective-permute-start(f32[6,4,256]{2,1,0:T(4,128)S(1)} %get-tuple-element.55), channel_id=1, source_target_pairs={{0,2},{1,3},{2,0},{3,1},{4,6},{5,7},{6,4},{7,5},{8,10},{9,11},{10,... | collective-permute-start | bytes 73736 | tf_op jit(solution)/shard_map/ppermute | solution.py:385
  92.2 2.9 %collective-permute-start.9 = (f32[6,4,256]{2,1,0:T(4,128)S(1)}, f32[6,4,256]{2,1,0:T(4,128)S(1)}, u32[]{:S(2)}, u32[]{:S(2)}) collective-permute-start(f32[6,4,256]{2,1,0:T(4,128)S(1)} %get-tuple-element.56), channel_id=1, source_target_pairs={{0,3},{1,0},{2,1},{3,2},{4,7},{5,4},{6,5},{7,6},{8,11},{9,8},{10,9... | collective-permute-start | bytes 73736 | tf_op jit(solution)/shard_map/ppermute | solution.py:385
  94.2 3.5 %copy-start.5 = (f32[6,4,256]{2,1,0:T(4,128)}, f32[6,4,256]{2,1,0:T(4,128)S(1)}, u32[]{:S(2)}) copy-start(f32[6,4,256]{2,1,0:T(4,128)S(1)} %collective-permute-done.7.refs_1_) | copy-start | bytes 73732
  94.4 3.2 %copy-start.6 = (f32[6,4,256]{2,1,0:T(4,128)}, f32[6,4,256]{2,1,0:T(4,128)S(1)}, u32[]{:S(2)}) copy-start(f32[6,4,256]{2,1,0:T(4,128)S(1)} %collective-permute-done.8.refs_2_) | copy-start | bytes 73732
  95.1 2.6 %copy-start.7 = (f32[6,4,256]{2,1,0:T(4,128)}, f32[6,4,256]{2,1,0:T(4,128)S(1)}, u32[]{:S(2)}) copy-start(f32[6,4,256]{2,1,0:T(4,128)S(1)} %collective-permute-done.9.refs_3_) | copy-start | bytes 73732
  97.7 0.6 copy-start.4

commit v11 on v10

--- a/solution.py
+++ b/solution.py
@@ -236,7 +236,7 @@
         copy.wait()
 
 
-def own_kernel(counts_ref, tiles_ref, w_ref, z_ref, g_ref, *scratch):
+def own_kernel(counts_ref, tiles_ref, x_ref, w_ref, z_ref, first_ref, rhs_ref, g_ref, *scratch):
     systems, kslots, width, _ = tiles_ref.shape
     for s in range(systems):
         near = tiles_ref[s, 0:2].reshape(2 * width, width)
@@ -260,6 +260,11 @@
         z = split3(dot(w[0], own, NT) + (dot(w[1], own, NT) + dot(w[2], own, NT)))
         for i in range(3):
             z_ref[s, i] = z[i]
+        x = x_ref[:, s * width:(s + 1) * width]
+        first = dot(x, z[0][:, width:], NT) + (dot(x, z[1][:, width:], NT) + dot(x, z[2][:, width:], NT))
+        first_ref[s] = first
+        x = x.astype(jnp.float32)
+        rhs_ref[s] = jnp.concatenate([jnp.zeros_like(x), x], axis=1) - apply(first, z, NN)
 
 
 def collect(slot_ref, shifts, got_refs, near_ref, sems):
@@ -298,12 +303,11 @@
         v_ref[s, 1] = v[1]
 
 
-def pair_kernel(lanes, shifts, late, place_ref, slot_ref, x_ref, w_any, z_any, v_any, t_any, *refs):
+def pair_kernel(lanes, shifts, late, place_ref, slot_ref, first_ref, rhs_ref, w_any, z_any, v_any, t_any, *refs):
     got_refs, up_refs, refs = refs[:len(shifts)], refs[len(shifts):len(shifts) + lanes], refs[len(shifts) + lanes:]
-    low_ref, near_ref, w_ref, z_ref, zj_ref, v_ref, t_ref, r_ref, first_ref, near_sems, sems, *scratch = refs
-    _, _, width, _ = z_ref.shape
-    systems = first_ref.shape[0]
-    count = x_ref.shape[0] // lanes
+    low_ref, near_ref, w_ref, z_ref, v_ref, t_ref, r_ref, near_sems, sems, *scratch = refs
+    systems, nrhs, width = first_ref.shape
+    count = nrhs // lanes
     near_copies = collect(slot_ref, shifts, got_refs, near_ref, near_sems)
     late_slots = [slot_ref[e - 1] for e in late]
     copies = [
@@ -311,13 +315,12 @@
     ] + [
         pltpu.make_async_copy(t_any, t_ref.at[0:systems], sems.at[2]),
         pltpu.make_async_copy(v_any, v_ref.at[0:systems], sems.at[3]),
-        pltpu.make_async_copy(z_any.at[:, 0:2, :, width:], zj_ref, sems.at[4]),
     ]
-    w_copy = pltpu.make_async_copy(w_any, w_ref, sems.at[5])
+    w_copy = pltpu.make_async_copy(w_any, w_ref, sems.at[4])
     for copy in copies + [w_copy]:
         copy.start()
     low_ref[...] = jnp.zeros(low_ref.shape, low_ref.dtype)
-    for copy in near_copies + copies[:-1]:
+    for copy in near_copies + copies:
         copy.wait()
     for i, slot in enumerate(late_slots):
         at = jnp.where(slot >= 0, slot, systems + i)
@@ -325,14 +328,10 @@
         v, t_ref[at] = schur(near, [z_ref[i, p] for p in range(3)])
         v_ref[at, 0] = v[0]
         v_ref[at, 1] = v[1]
-    copies[-1].wait()
     roots = []
     for s in range(systems):
-        x = x_ref[:, s * width:(s + 1) * width]
-        first_ref[s] = dot(x, zj_ref[s, 0], NT) + dot(x, zj_ref[s, 1], NT)
-        r_ref[s] = dot(x, near_ref[s, 1], NN)
-    for s in range(systems):
-        r_ref[s] = r_ref[s] - apply(first_ref[s], (v_ref[s, 0], v_ref[s, 1]), NT)
+        near = near_ref[s].reshape(2 * width, width)
+        r_ref[s] = thirds(dot(jnp.concatenate(split3(rhs_ref[s]), axis=0), near, NN))
         t_ref[s], root = scaled(t_ref[s])
         roots.append(root)
     factor(t_ref.at[0:systems], *scratch)
@@ -391,33 +390,37 @@
     pairs = shards - 1
     every = tuple(range(1, shards))
     late = (1, shards - 1)
-    early = tuple(e for e in every if e not in late)
+    early = tuple(sorted((e for e in every if e not in late), key=lambda e: abs(2 * e - shards)))
+    most = pltpu.CompilerParams(vmem_limit_bytes=60 * 1024 * 1024)
     pieces = pl.pallas_call(
         pick_kernel,
         out_shape=[jax.ShapeDtypeStruct((2, width, width), jnp.bfloat16)] * pairs,
         in_specs=[smem, anywhere],
         out_specs=[vmem] * pairs,
         scratch_shapes=[pltpu.SemaphoreType.DMA((pairs,))],
-        compiler_params=params,
+        compiler_params=most,
     )(slots((my_panel + hops) % shards), tiles)
     received = {e: shift(pieces[e - 1], "panel", e) for e in early}
 
-    w, z = pl.pallas_call(
+    inputs, pieces = lax.optimization_barrier((inputs, pieces))
+    x = lax.all_to_all(inputs, "rhs", split_axis=1, concat_axis=0, tiled=True)
+    x = lax.dynamic_slice_in_dim(jnp.concatenate([x, x], axis=0), my_lane * nrhs_dev, lanes * nrhs_dev, 0)
+    nrhs = lanes * nrhs_dev
+
+    w, z, first, rhs = pl.pallas_call(
         own_kernel,
         out_shape=(
             jax.ShapeDtypeStruct((systems, 2, width, width), jnp.bfloat16),
             jax.ShapeDtypeStruct((systems, 3, width, 2 * width), jnp.bfloat16),
+            jax.ShapeDtypeStruct((systems, nrhs, width), jnp.float32),
+            jax.ShapeDtypeStruct((systems, nrhs, 2 * width), jnp.float32),
         ),
-        in_specs=[smem, vmem],
-        out_specs=(vmem, vmem),
+        in_specs=[smem, vmem, vmem],
+        out_specs=(vmem,) * 4,
         scratch_shapes=[pltpu.VMEM((systems, width, width), jnp.float32)] + factor_scratch(systems, width),
-        compiler_params=params,
+        compiler_params=most,
         cost_estimate=pl.CostEstimate(flops=30 * 10**9, bytes_accessed=8 * 10**6, transcendentals=0),
-    )(own_cnt, tiles)
-
-    inputs, w = lax.optimization_barrier((inputs, w))
-    x = lax.all_to_all(inputs, "rhs", split_axis=1, concat_axis=0, tiled=True)
-    x = lax.dynamic_slice_in_dim(jnp.concatenate([x, x], axis=0), my_lane * nrhs_dev, lanes * nrhs_dev, 0)
+    )(own_cnt, tiles, x)
 
     come = [received[e] for e in early]
     held, z, come = lax.optimization_barrier(([pieces[e - 1] for e in late], z, come))
@@ -438,32 +441,29 @@
             pltpu.SemaphoreType.DMA((systems,)),
             pltpu.SemaphoreType.DMA((len(early),)),
         ],
-        compiler_params=params,
+        compiler_params=most,
         cost_estimate=pl.CostEstimate(flops=12 * 10**9, bytes_accessed=8 * 10**6, transcendentals=0),
     )(from_slot, z, *[received[e] for e in early])
 
-    nrhs = lanes * nrhs_dev
     piece = jax.ShapeDtypeStruct((systems, nrhs_dev, width), jnp.float32)
     *up, low = pl.pallas_call(
         functools.partial(pair_kernel, lanes, every, late),
         out_shape=[piece] * lanes + [jax.ShapeDtypeStruct((shards * lanes, nrhs_dev, width), jnp.bfloat16)],
-        in_specs=[smem, smem, vmem] + [anywhere] * (4 + pairs),
+        in_specs=[smem, smem, vmem, vmem] + [anywhere] * (4 + pairs),
         out_specs=[vmem] * (lanes + 1),
         scratch_shapes=[
             pltpu.VMEM((systems + pairs, 2, width, width), jnp.bfloat16),
             pltpu.VMEM((systems, 2, width, width), jnp.bfloat16),
             pltpu.VMEM((len(late), 3, width, 2 * width), jnp.bfloat16),
-            pltpu.VMEM((systems, 2, width, width), jnp.bfloat16),
             pltpu.VMEM((systems + len(late), 2, width, width), jnp.bfloat16),
             pltpu.VMEM((systems + len(late), width, width), jnp.float32),
             pltpu.VMEM((systems, nrhs, width), jnp.float32),
-            pltpu.VMEM((systems, nrhs, width), jnp.float32),
             pltpu.SemaphoreType.DMA((pairs,)),
-            pltpu.SemaphoreType.DMA((6,)),
+            pltpu.SemaphoreType.DMA((5,)),
         ] + factor_scratch(systems, width),
         compiler_params=params,
     )(
-        jnp.concatenate([mate_panel, lane_word]), from_slot, x, w, z, v, t,
+        jnp.concatenate([mate_panel, lane_word]), from_slot, first, rhs, w, z, v, t,
         *[received[e] for e in every],
     )
     low = lax.all_to_all(low, ("panel", "rhs"), split_axis=0, concat_axis=0, tiled=True)

time: 100 us -> 108 us (1.080)
  Pallas kernels: 57.4 us -> 64.6 us
  waiting for transfers between devices: 8.73 us -> 7.03 us
  local copies, waits for them, and re-layouts: 6.78 us -> 8.1 us
  other arithmetic: 1.72 us -> 2.9 us
    pallas_call x1, Pallas kernels: 22.8 us -> 26.4 us  [on_device(): pl.pallas_call(own_kernel, out_shape=(jax.ShapeDtypeStruct((systems, 2, w...]
    pallas_call x1, Pallas kernels: 8.59 us -> 11.4 us  [on_device(): pl.pallas_call(functools.partial(link_kernel, early), out_shape=(jax.Shap...]
    pallas_call x1, Pallas kernels: 1.84 us -> 3.54 us  [on_device(): pl.pallas_call(pick_kernel, out_shape=[jax.ShapeDtypeStruct((2, width, wi...]
    ppermute x10, waiting for transfers between devices: 2.22 us -> 0.98 us  [shift(): lax.ppermute(value, axis, [(i, (i + by) % size) for i in range(size)])]
    unnamed x18 -> x44, local copies, waits for them, and re-layouts: 6.61 us -> 7.41 us
  transfers between devices with their start and end apart: 12 -> 12, of which waited for: 5 -> 4; matrix products, arithmetic and copies ran while one was open for 1% -> 2% of each run, Pallas kernels for 31% -> 35%
where the time goes in v11:
time: 108 us
  Pallas kernels  64.6 us (60%)
  starting transfers between devices  24.6 us (23%)
  local copies, waits for them, and re-layouts  8.1 us (8%)
  waiting for transfers between devices  7.03 us (7%)
  other arithmetic  2.9 us (3%)
    pallas_call x1, Pallas kernels, on_device(): pl.pallas_call(own_kernel, out_shape=(jax.ShapeDtypeStruct((systems, 2, w...  26.4 us
    pallas_call x1, Pallas kernels, on_device(): pl.pallas_call(functools.partial(pair_kernel, lanes, every, late), out_sh...  21.7 us
    ppermute x10, starting transfers between devices, shift(): lax.ppermute(value, axis, [(i, (i + by) % size) for i in range(size)])  18.8 us
    pallas_call x1, Pallas kernels, on_device(): pl.pallas_call(functools.partial(link_kernel, early), out_shape=(jax.Shap...  11.4 us
    unnamed x44, local copies, waits for them, and re-layouts  7.41 us
    pallas_call x1, Pallas kernels, on_device(): pl.pallas_call(pick_kernel, out_shape=[jax.ShapeDtypeStruct((2, width, wi...  3.54 us
    all_to_all x1, waiting for transfers between devices, on_device(): x = lax.all_to_all(inputs, 'rhs', split_axis=1, concat_axis=0, tiled=True)  3.33 us
    all_to_all x1, starting transfers between devices, on_device(): x = lax.all_to_all(inputs, 'rhs', split_axis=1, concat_axis=0, tiled=True)  3.27 us
  transfers between devices with their start and end apart: 12, of which 4 were waited for; matrix products, arithmetic and copies ran while one was open for 2% of the time, Pallas kernels for 35%

profile of v11, /device:TPU:0, one launch (start us, length us, event | category | flops | bytes accessed | tf_op | source)
XLA Modules:
  0.0 107.5 jit_solution(18372476909828345154)
XLA Ops:
  0.9 0.8 select_reduce_fusion
  1.7 3.5 %shard_map.46 = (bf16[2,256,256]{2,1,0:T(8,128)(2,1)}, bf16[2,256,256]{2,1,0:T(8,128)(2,1)}, bf16[2,256,256]{2,1,0:T(8,128)(2,1)}, bf16[2,256,256]{2,1,0:T(8,128...) custom-call(s32[7]{0:T(128)} %get-tuple-element.63.slot_ref, ...), custom_call_target="tpu_custom_call" | custom-call | tf_op jit(solution)/shard_map/pallas_call | solution.py:395
  5.2 3.1 %collective-permute-start.3 = (bf16[2,256,256]{2,1,0:T(8,128)(2,1)}, bf16[2,256,256]{2,1,0:T(8,128)(2,1)S(1)}, u32[]{:S(2)}, u32[]{:S(2)}) collective-permute-start(bf16[2,256,256]{2,1,0:T(8,128)(2,1)} %get-tuple-element.35), channel_id=1, source_target_pairs={{0,8},{4,12},{8,16},{12,20},{16,24},{20,28},{24,0},{28,4},{1,9},{5... | collective-permute-start | bytes 786440 | tf_op jit(solution)/shard_map/ppermute | solution.py:384
  8.3 2.5 %collective-permute-start.1 = (bf16[2,256,256]{2,1,0:T(8,128)(2,1)}, bf16[2,256,256]{2,1,0:T(8,128)(2,1)S(1)}, u32[]{:S(2)}, u32[]{:S(2)}) collective-permute-start(bf16[2,256,256]{2,1,0:T(8,128)(2,1)} %get-tuple-element.36), channel_id=1, source_target_pairs={{0,12},{4,16},{8,20},{12,24},{16,28},{20,0},{24,4},{28,8},{1,13},{... | collective-permute-start | bytes 786440 | tf_op jit(solution)/shard_map/ppermute | solution.py:384
  10.8 1.2 %collective-permute-start = (bf16[2,256,256]{2,1,0:T(8,128)(2,1)}, bf16[2,256,256]{2,1,0:T(8,128)(2,1)S(1)}, u32[]{:S(2)}, u32[]{:S(2)}) collective-permute-start(bf16[2,256,256]{2,1,0:T(8,128)(2,1)} %get-tuple-element.37), channel_id=1, source_target_pairs={{0,16},{4,20},{8,24},{12,28},{16,0},{20,4},{24,8},{28,12},{1,17},{... | collective-permute-start | bytes 786440 | tf_op jit(solution)/shard_map/ppermute | solution.py:384
  12.1 2.6 %collective-permute-start.2 = (bf16[2,256,256]{2,1,0:T(8,128)(2,1)}, bf16[2,256,256]{2,1,0:T(8,128)(2,1)S(1)}, u32[]{:S(2)}, u32[]{:S(2)}) collective-permute-start(bf16[2,256,256]{2,1,0:T(8,128)(2,1)} %get-tuple-element.38), channel_id=1, source_target_pairs={{0,20},{4,24},{8,28},{12,0},{16,4},{20,8},{24,12},{28,16},{1,21},{... | collective-permute-start | bytes 786440 | tf_op jit(solution)/shard_map/ppermute | solution.py:384
  14.7 1.4 %collective-permute-start.4 = (bf16[2,256,256]{2,1,0:T(8,128)(2,1)}, bf16[2,256,256]{2,1,0:T(8,128)(2,1)S(1)}, u32[]{:S(2)}, u32[]{:S(2)}) collective-permute-start(bf16[2,256,256]{2,1,0:T(8,128)(2,1)} %get-tuple-element.39), channel_id=1, source_target_pairs={{0,24},{4,28},{8,0},{12,4},{16,8},{20,12},{24,16},{28,20},{1,25},{... | collective-permute-start | bytes 786440 | tf_op jit(solution)/shard_map/ppermute | solution.py:384
  16.1 3.3 %all-to-all-start = ((bf16[4,4,1536]{2,0,1:T(4,128)(2,1)}), bf16[4,4,1536]{2,0,1:T(4,128)(2,1)S(1)}, u32[]{:S(2)}, u32[]{:S(2)}) async-start(bf16[4,4,1536]{2,0,1:T(4,128)(2,1)} %bitcast.3), calls=%async_computation | async-start | bytes 98304 | tf_op jit(solution)/shard_map/all_to_all | solution.py:406
  20.0 3.3 %all-to-all-done = bf16[4,4,1536]{2,0,1:T(4,128)(2,1)S(1)} async-done(((bf16[4,4,1536]{2,0,1:T(4,128)(2,1)}), bf16[4,4,1536]{2,0,1:T(4,128)(2,1)S(1)}, u32[]{:S(2)}, u32[]{:S(2)}) %all-to-all-start) | async-done | bytes 49184 | tf_op jit(solution)/shard_map/all_to_all | solution.py:406
  24.0 26.4 %shard_map.47 = (bf16[6,2,256,256]{3,2,1,0:T(8,128)(2,1)}, bf16[6,3,256,512]{3,2,1,0:T(8,128)(2,1)}, f32[6,16,256]{2,1,0:T(8,128)}, f32[6,16,512]{2,1,0:T(8,128)}) custom-call(s32[6]{0:T(128)} %dynamic_slice.14.counts_ref, bf16[6,5,256,256]{3,2,1,0:T(8,128)(2,1)} %tiles_ref.3, bf16[16,1536]{1,0:T(8,128)(2,1)} %fusion.x_ref), custom_call_target="tpu_custom_call" | custom-call | flops 30000001024 | bytes 8000000 | tf_op jit(solution)/shard_map/pallas_call | solution.py:410
  50.6 4.7 %collective-permute-start.6 = (bf16[2,256,256]{2,1,0:T(8,128)(2,1)S(1)}, bf16[2,256,256]{2,1,0:T(8,128)(2,1)S(1)}, u32[]{:S(2)}, u32[]{:S(2)}) collective-permute-start(bf16[2,256,256]{2,1,0:T(8,128)(2,1)S(1)} %copy-done.20), channel_id=1, source_target_pairs={{0,28},{4,0},{8,4},{12,8},{16,12},{20,16},{24,20},{28,24},{1,29},{... | collective-permute-start | bytes 786440 | tf_op jit(solution)/shard_map/ppermute | solution.py:384
  55.4 11.4 %shard_map.48 = (bf16[6,2,256,256]{3,2,1,0:T(8,128)(2,1)}, f32[6,256,256]{2,1,0:T(8,128)}) custom-call(s32[7]{0:T(128)} %get-tuple-element.64.slot_ref, bf16[6,3,256,512]{3,2,1,0:T(8,128)(2,1)} %get-tuple-element.48.z_any, bf16[2,256,256]{2,1,0:T(8,128)(2,1)} %copy-done.6, bf16[2,256,256]{2,1,0:T(8,128)(2,1)} %copy-done.4, bf16[2,256,256]{2,1,0:T(8,128)(2,1)} %copy-done.8, ...), custom_call_target="tpu_custom_call" | custom-call | flops 12000000000 | bytes 8000000 | tf_op jit(solution)/shard_map/pallas_call | solution.py:430
  66.8 1.4 %copy-done.1 = bf16[6,2,256,256]{3,2,1,0:T(8,128)(2,1)S(1)} copy-done((bf16[6,2,256,256]{3,2,1,0:T(8,128)(2,1)S(1)}, bf16[6,2,256,256]{3,2,1,0:T(8,128)(2,1)}, u32[]{:S(2)}) %copy-start.1) | copy-done | bytes 1572888
  68.3 0.9 copy-done.3
  69.2 0.9 copy-done.5
  70.2 0.9 copy-done.7
  71.1 0.9 copy-done.9
  72.1 0.9 copy-done.11
  73.0 21.7 %shard_map.49 = (f32[6,4,256]{2,1,0:T(4,128)S(1)}, f32[6,4,256]{2,1,0:T(4,128)S(1)}, f32[6,4,256]{2,1,0:T(4,128)S(1)}, f32[6,4,256]{2,1,0:T(4,128)S(1)}, bf16[32,4,256]{2,1,0:T(4,128)(2,1)}) custom-call(s32[7]{0:T(128)S(1)} %pad_add_fusion.1.place_ref, s32[7]{0:T(128)S(1)} %copy-done.15, f32[6,16,256]{2,1,0:T(8,128)S(1)} %copy-done.13, ...), custom_call_target="tpu_custom_call" | custom-call | tf_op jit(solution)/shard_map/pallas_call | solution.py:449
  95.3 2.6 %all-to-all-start.1 = ((bf16[32,4,256]{2,1,0:T(4,128)(2,1)}), bf16[32,4,256]{2,1,0:T(4,128)(2,1)S(1)}, u32[]{:S(2)}, u32[]{:S(2)}) async-start(bf16[32,4,256]{2,1,0:T(4,128)(2,1)} %get-tuple-element.58), calls=%async_computation.1 | async-start | bytes 131072 | tf_op jit(solution)/shard_map/all_to_all | solution.py:469
  98.0 1.7 %collective-permute-start.8 = (f32[6,4,256]{2,1,0:T(4,128)S(1)}, f32[6,4,256]{2,1,0:T(4,128)S(1)}, u32[]{:S(2)}, u32[]{:S(2)}) collective-permute-start(f32[6,4,256]{2,1,0:T(4,128)S(1)} %get-tuple-element.61), channel_id=1, source_target_pairs={{0,2},{1,3},{2,0},{3,1},{4,6},{5,7},{6,4},{7,5},{8,10},{9,11},{10,... | collective-permute-start | bytes 73736 | tf_op jit(solution)/shard_map/ppermute | solution.py:384
  99.7 1.3 %collective-permute-start.9 = (f32[6,4,256]{2,1,0:T(4,128)S(1)}, f32[6,4,256]{2,1,0:T(4,128)S(1)}, u32[]{:S(2)}, u32[]{:S(2)}) collective-permute-start(f32[6,4,256]{2,1,0:T(4,128)S(1)} %get-tuple-element.62), channel_id=1, source_target_pairs={{0,3},{1,0},{2,1},{3,2},{4,7},{5,4},{6,5},{7,6},{8,11},{9,8},{10,9... | collective-permute-start | bytes 73736 | tf_op jit(solution)/shard_map/ppermute | solution.py:384
  102.6 2.7 %all-to-all-done.1.low_ref = bf16[32,4,256]{2,1,0:T(4,128)(2,1)S(1)} async-done(((bf16[32,4,256]{2,1,0:T(4,128)(2,1)}), bf16[32,4,256]{2,1,0:T(4,128)(2,1)S(1)}, u32[]{:S(2)}, u32[]{:S(2)}) %all-to-all-start.1) | async-done | bytes 65568 | tf_op jit(solution)/shard_map/all_to_all | solution.py:469
  105.9 1.6 %shard_map.50 = bf16[4,6144]{1,0:T(4,128)(2,1)} custom-call(s32[25]{0:T(128)} %pad_add_fusion.place_ref, bf16[32,4,256]{2,1,0:T(4,128)(2,1)} %copy-done.16, f32[6,4,256]{2,1,0:T(4,128)} %copy-done.14, f32[6,4,256]{2,1,0:T(4,128)} %copy-done.17, f32[6,4,256]{2,1,0:T(4,128)} %copy-done.18, f32[6,4,256]{2,1,0:T(4,128)} %copy-done.19), custom_call_target="tpu_custom_call" | custom-call | tf_op jit(solution)/shard_map/pallas_call | solution.py:471
  (58 shorter events, 5.3 us)
Async XLA Ops:
  1.7 17.7 %copy-start.21 = (s32[192]{0:T(256)S(1)}, s32[192]{0:T(256)}, u32[]{:S(2)}) copy-start(s32[192]{0:T(256)} %param.6) | copy-start | bytes 2308
  5.2 45.3 %collective-permute-start.3 = (bf16[2,256,256]{2,1,0:T(8,128)(2,1)}, bf16[2,256,256]{2,1,0:T(8,128)(2,1)S(1)}, u32[]{:S(2)}, u32[]{:S(2)}) collective-permute-start(bf16[2,256,256]{2,1,0:T(8,128)(2,1)} %get-tuple-element.35), channel_id=1, source_target_pairs={{0,8},{4,12},{8,16},{12,20},{16,24},{20,28},{24,0},{28,4},{1,9},{5... | collective-permute-start | bytes 786440 | tf_op jit(solution)/shard_map/ppermute | solution.py:384
  8.3 42.2 %collective-permute-start.1 = (bf16[2,256,256]{2,1,0:T(8,128)(2,1)}, bf16[2,256,256]{2,1,0:T(8,128)(2,1)S(1)}, u32[]{:S(2)}, u32[]{:S(2)}) collective-permute-start(bf16[2,256,256]{2,1,0:T(8,128)(2,1)} %get-tuple-element.36), channel_id=1, source_target_pairs={{0,12},{4,16},{8,20},{12,24},{16,28},{20,0},{24,4},{28,8},{1,13},{... | collective-permute-start | bytes 786440 | tf_op jit(solution)/shard_map/ppermute | solution.py:384
  10.8 39.7 %collective-permute-start = (bf16[2,256,256]{2,1,0:T(8,128)(2,1)}, bf16[2,256,256]{2,1,0:T(8,128)(2,1)S(1)}, u32[]{:S(2)}, u32[]{:S(2)}) collective-permute-start(bf16[2,256,256]{2,1,0:T(8,128)(2,1)} %get-tuple-element.37), channel_id=1, source_target_pairs={{0,16},{4,20},{8,24},{12,28},{16,0},{20,4},{24,8},{28,12},{1,17},{... | collective-permute-start | bytes 786440 | tf_op jit(solution)/shard_map/ppermute | solution.py:384
  12.1 38.5 %collective-permute-start.2 = (bf16[2,256,256]{2,1,0:T(8,128)(2,1)}, bf16[2,256,256]{2,1,0:T(8,128)(2,1)S(1)}, u32[]{:S(2)}, u32[]{:S(2)}) collective-permute-start(bf16[2,256,256]{2,1,0:T(8,128)(2,1)} %get-tuple-element.38), channel_id=1, source_target_pairs={{0,20},{4,24},{8,28},{12,0},{16,4},{20,8},{24,12},{28,16},{1,21},{... | collective-permute-start | bytes 786440 | tf_op jit(solution)/shard_map/ppermute | solution.py:384
  14.7 35.8 %collective-permute-start.4 = (bf16[2,256,256]{2,1,0:T(8,128)(2,1)}, bf16[2,256,256]{2,1,0:T(8,128)(2,1)S(1)}, u32[]{:S(2)}, u32[]{:S(2)}) collective-permute-start(bf16[2,256,256]{2,1,0:T(8,128)(2,1)} %get-tuple-element.39), channel_id=1, source_target_pairs={{0,24},{4,28},{8,0},{12,4},{16,8},{20,12},{24,16},{28,20},{1,25},{... | collective-permute-start | bytes 786440 | tf_op jit(solution)/shard_map/ppermute | solution.py:384
  16.1 7.3 %all-to-all-start = ((bf16[4,4,1536]{2,0,1:T(4,128)(2,1)}), bf16[4,4,1536]{2,0,1:T(4,128)(2,1)S(1)}, u32[]{:S(2)}, u32[]{:S(2)}) async-start(bf16[4,4,1536]{2,0,1:T(4,128)(2,1)} %bitcast.3), calls=%async_computation | async-start | bytes 98304 | tf_op jit(solution)/shard_map/all_to_all | solution.py:406
  24.0 26.6 %copy-start.20 = (bf16[2,256,256]{2,1,0:T(8,128)(2,1)S(1)}, bf16[2,256,256]{2,1,0:T(8,128)(2,1)}, u32[]{:S(2)}) copy-start(bf16[2,256,256]{2,1,0:T(8,128)(2,1)} %get-tuple-element.57) | copy-start | bytes 786436
  50.5 4.9 %copy-start.2 = (bf16[2,256,256]{2,1,0:T(8,128)(2,1)}, bf16[2,256,256]{2,1,0:T(8,128)(2,1)S(1)}, u32[]{:S(2)}) copy-start(bf16[2,256,256]{2,1,0:T(8,128)(2,1)S(1)} %collective-permute-done.3.refs_3_.refs_1_) | copy-start | bytes 786436
  50.5 4.9 %copy-start.4 = (bf16[2,256,256]{2,1,0:T(8,128)(2,1)}, bf16[2,256,256]{2,1,0:T(8,128)(2,1)S(1)}, u32[]{:S(2)}) copy-start(bf16[2,256,256]{2,1,0:T(8,128)(2,1)S(1)} %collective-permute-done.1.refs_1_.refs_2_) | copy-start | bytes 786436
  50.5 4.8 %copy-start.6 = (bf16[2,256,256]{2,1,0:T(8,128)(2,1)}, bf16[2,256,256]{2,1,0:T(8,128)(2,1)S(1)}, u32[]{:S(2)}) copy-start(bf16[2,256,256]{2,1,0:T(8,128)(2,1)S(1)} %collective-permute-done.refs_0_.refs_3_) | copy-start | bytes 786436
  50.5 4.8 %copy-start.8 = (bf16[2,256,256]{2,1,0:T(8,128)(2,1)}, bf16[2,256,256]{2,1,0:T(8,128)(2,1)S(1)}, u32[]{:S(2)}) copy-start(bf16[2,256,256]{2,1,0:T(8,128)(2,1)S(1)} %collective-permute-done.2.refs_2_.refs_4_) | copy-start | bytes 786436
  50.5 4.8 %copy-start.10 = (bf16[2,256,256]{2,1,0:T(8,128)(2,1)}, bf16[2,256,256]{2,1,0:T(8,128)(2,1)S(1)}, u32[]{:S(2)}) copy-start(bf16[2,256,256]{2,1,0:T(8,128)(2,1)S(1)} %collective-permute-done.4.refs_4_.refs_5_) | copy-start | bytes 786436
  50.6 16.2 %collective-permute-start.5 = (bf16[2,256,256]{2,1,0:T(8,128)(2,1)}, bf16[2,256,256]{2,1,0:T(8,128)(2,1)S(1)}, u32[]{:S(2)}, u32[]{:S(2)}) collective-permute-start(bf16[2,256,256]{2,1,0:T(8,128)(2,1)} %get-tuple-element.56), channel_id=1, source_target_pairs={{0,4},{4,8},{8,12},{12,16},{16,20},{20,24},{24,28},{28,0},{1,5},{5... | collective-permute-start | bytes 786440 | tf_op jit(solution)/shard_map/ppermute | solution.py:384
  50.6 16.2 %collective-permute-start.6 = (bf16[2,256,256]{2,1,0:T(8,128)(2,1)S(1)}, bf16[2,256,256]{2,1,0:T(8,128)(2,1)S(1)}, u32[]{:S(2)}, u32[]{:S(2)}) collective-permute-start(bf16[2,256,256]{2,1,0:T(8,128)(2,1)S(1)} %copy-done.20), channel_id=1, source_target_pairs={{0,28},{4,0},{8,4},{12,8},{16,12},{20,16},{24,20},{28,24},{1,29},{... | collective-permute-start | bytes 786440 | tf_op jit(solution)/shard_map/ppermute | solution.py:384
  55.4 11.4 %copy-start = (bf16[6,2,256,256]{3,2,1,0:T(8,128)(2,1)S(1)}, bf16[6,2,256,256]{3,2,1,0:T(8,128)(2,1)}, u32[]{:S(2)}) copy-start(bf16[6,2,256,256]{3,2,1,0:T(8,128)(2,1)} %get-tuple-element.44.w_any) | copy-start | bytes 4718596
  55.4 11.4 %copy-start.12 = (f32[6,16,512]{2,1,0:T(8,128)S(1)}, f32[6,16,512]{2,1,0:T(8,128)}, u32[]{:S(2)}) copy-start(f32[6,16,512]{2,1,0:T(8,128)} %get-tuple-element.43.rhs_ref) | copy-start | bytes 589828
  55.4 11.4 %copy-start.13 = (f32[6,16,256]{2,1,0:T(8,128)S(1)}, f32[6,16,256]{2,1,0:T(8,128)}, u32[]{:S(2)}) copy-start(f32[6,16,256]{2,1,0:T(8,128)} %get-tuple-element.42.first_ref) | copy-start | bytes 294916
  55.4 11.4 %copy-start.15 = (s32[7]{0:T(128)S(1)}, s32[7]{0:T(128)}, u32[]{:S(2)}) copy-start(s32[7]{0:T(128)} %get-tuple-element.64.slot_ref) | copy-start | bytes 88
  95.3 10.0 %all-to-all-start.1 = ((bf16[32,4,256]{2,1,0:T(4,128)(2,1)}), bf16[32,4,256]{2,1,0:T(4,128)(2,1)S(1)}, u32[]{:S(2)}, u32[]{:S(2)}) async-start(bf16[32,4,256]{2,1,0:T(4,128)(2,1)} %get-tuple-element.58), calls=%async_computation.1 | async-start | bytes 131072 | tf_op jit(solution)/shard_map/all_to_all | solution.py:469
  97.9 3.7 %collective-permute-start.7 = (f32[6,4,256]{2,1,0:T(4,128)S(1)}, f32[6,4,256]{2,1,0:T(4,128)S(1)}, u32[]{:S(2)}, u32[]{:S(2)}) collective-permute-start(f32[6,4,256]{2,1,0:T(4,128)S(1)} %get-tuple-element.60), channel_id=1, source_target_pairs={{0,1},{1,2},{2,3},{3,0},{4,5},{5,6},{6,7},{7,4},{8,9},{9,10},{10,1... | collective-permute-start | bytes 73736 | tf_op jit(solution)/shard_map/ppermute | solution.py:384
  98.0 3.9 %collective-permute-start.8 = (f32[6,4,256]{2,1,0:T(4,128)S(1)}, f32[6,4,256]{2,1,0:T(4,128)S(1)}, u32[]{:S(2)}, u32[]{:S(2)}) collective-permute-start(f32[6,4,256]{2,1,0:T(4,128)S(1)} %get-tuple-element.61), channel_id=1, source_target_pairs={{0,2},{1,3},{2,0},{3,1},{4,6},{5,7},{6,4},{7,5},{8,10},{9,11},{10,... | collective-permute-start | bytes 73736 | tf_op jit(solution)/shard_map/ppermute | solution.py:384
  99.7 2.8 %collective-permute-start.9 = (f32[6,4,256]{2,1,0:T(4,128)S(1)}, f32[6,4,256]{2,1,0:T(4,128)S(1)}, u32[]{:S(2)}, u32[]{:S(2)}) collective-permute-start(f32[6,4,256]{2,1,0:T(4,128)S(1)} %get-tuple-element.62), channel_id=1, source_target_pairs={{0,3},{1,0},{2,1},{3,2},{4,7},{5,4},{6,5},{7,6},{8,11},{9,8},{10,9... | collective-permute-start | bytes 73736 | tf_op jit(solution)/shard_map/ppermute | solution.py:384
  101.6 3.7 %copy-start.17 = (f32[6,4,256]{2,1,0:T(4,128)}, f32[6,4,256]{2,1,0:T(4,128)S(1)}, u32[]{:S(2)}) copy-start(f32[6,4,256]{2,1,0:T(4,128)S(1)} %collective-permute-done.7.refs_1_) | copy-start | bytes 73732
  (10 other events, 13.5 us)

commit v12 on v7

--- a/solution.py
+++ b/solution.py
@@ -7,7 +7,6 @@
 from jax.sharding import PartitionSpec as P
 
 STEP = 32
-PIVOTS = 4
 NT = (((1,), (1,)), ((), ()))
 NN = (((1,), (0,)), ((), ()))
 TN = (((0,), (0,)), ((), ()))
@@ -30,6 +29,25 @@
     b1, b2, b3 = b
     small = dot(a1, b3, dims) + dot(a3, b1, dims) + dot(a2, b2, dims)
     return dot(a1, b1, dims) + ((dot(a1, b2, dims) + dot(a2, b1, dims)) + small)
+
+
+def dot3(a, b, dims):
+    return dot(a[0], b[0], dims) + (dot(a[0], b[1], dims) + dot(a[1], b[0], dims))
+
+
+def wide(parts):
+    one, two, three = parts
+    return jnp.concatenate([one, one, two, two, one, three], axis=1)
+
+
+def deep(parts):
+    one, two, three = parts
+    return jnp.concatenate([one, two, one, two, three, one], axis=0)
+
+
+def thirds(array):
+    count = array.shape[0] // 3
+    return array[:count] + (array[count:2 * count] + array[2 * count:])
 
 
 def apply(rows, parts, dims):
@@ -62,52 +80,69 @@
     def spread(row):
         return jnp.broadcast_to(row, (8, 128))
 
-    def wide(parts):
-        one, two, three = parts
-        return jnp.concatenate([one, one, two, two, one, three], axis=1)
-
-    def deep(parts):
-        if height < 128:
-            filler = jnp.zeros((128 - height, width), jnp.bfloat16)
-            parts = [jnp.concatenate([part, filler], axis=0) for part in parts]
-        one, two, three = parts
-        return jnp.concatenate([one, two, one, two, three, one], axis=0)
+    def padded(parts):
+        if height == 128:
+            return parts
+        filler = jnp.zeros((128 - height, width), jnp.bfloat16)
+        return [jnp.concatenate([part, filler], axis=0) for part in parts]
 
     def pivots(packs, pieces):
         placed = 0
-        for first in range(0, STEP, PIVOTS):
+        for first in range(0, STEP, 4):
             top, start = first // 8, first % 8
             tall = range(top, groups)
-            own = (place >= first) & (place < first + PIVOTS)
+            own = (place >= first) & (place < first + 4)
             one = jnp.where(place - 8 * top == sub, 1.0, 0.0)
+            each = range(len(packs))
             if start == 0:
-                inverses = [None] * len(packs)
-            columns = []
+                inverses = [None for _ in each]
+            u = [
+                [{g: jnp.take_along_axis(x[g], lane - place + (first + q), axis=1) for g in tall} for q in range(4)]
+                for x in packs
+            ]
+            a = [{(i, j): spread(u[s][j][top][start + i:start + i + 1, :]) for j in range(4) for i in range(j + 1)} for s in each]
             for x in packs:
-                columns.append([
-                    {g: jnp.take_along_axis(x[g], lane - place + (first + q), axis=1) for g in tall} for q in range(PIVOTS)
-                ])
                 for g in tall:
                     x[g] = jnp.where(own, one if g == top else 0.0, x[g])
-            for q in range(PIVOTS):
+            y = [[spread(x[top][start + q:start + q + 1, :]) for q in range(4)] for x in packs]
+            low = [{} for _ in each]
+            inv = [[None] * 4 for _ in each]
+            for p in (0, 2):
+                n = p + 1
+                delta = [a[s][p, p] * a[s][n, n] - a[s][p, n] * a[s][p, n] for s in each]
+                for s in each:
+                    inv[s][p] = pl.reciprocal(a[s][p, p], approx=True)
+                    inv[s][n] = pl.reciprocal(delta[s], approx=True) * a[s][p, p]
+                for j in range(n, 4):
+                    for s in each:
+                        low[s][j, p] = a[s][p, j] * inv[s][p]
+                for j in range(n + 1, 4):
+                    for s in each:
+                        a[s][n, j] = a[s][n, j] - low[s][n, p] * a[s][p, j]
+                for j in range(n + 1, 4):
+                    for s in each:
+                        low[s][j, n] = a[s][n, j] * inv[s][n]
+                for i in range(n + 1, 4):
+                    for j in range(i, 4):
+                        for s in each:
+                            a[s][i, j] = (a[s][i, j] - low[s][i, p] * a[s][p, j]) - low[s][i, n] * a[s][n, j]
+            for q in range(4):
                 at = start + q
-                for s, x in enumerate(packs):
-                    cols = columns[s]
-                    inverse = pl.reciprocal(spread(cols[q][top][at:at + 1, :]), approx=True)
-                    inverses[s] = inverse if at == 0 else jnp.where(sub >= at, inverse, inverses[s])
-                    c = {g: cols[q][g] * inverse for g in tall}
-                    for later in range(q + 1, PIVOTS):
-                        m = spread(cols[q][top][start + later:start + later + 1, :])
+                for s in each:
+                    for k in range(q):
                         for g in tall:
-                            cols[later][g] = cols[later][g] - c[g] * m
-                    c[top] = jnp.where(sub > at, c[top], 0.0)
-                    r = spread(x[top][at:at + 1, :])
+                            u[s][q][g] = u[s][q][g] - u[s][k][g] * low[s][q, k]
+                        y[s][q] = y[s][q] - y[s][k] * low[s][q, k]
+                    inverses[s] = inv[s][q] if at == 0 else jnp.where(sub >= at, inv[s][q], inverses[s])
                     for g in tall:
-                        x[g] = x[g] - c[g] * r
+                        m = u[s][q][g] * inv[s][q]
+                        if g == top:
+                            m = jnp.where(sub > at, m, 0.0)
+                        packs[s][g] = packs[s][g] - m * y[s][q]
                 while placed * STEP < (first + q + 1) * len(pieces):
                     pieces[placed]()
                     placed += 1
-            if start + PIVOTS == 8:
+            if start + 4 == 8:
                 for s, x in enumerate(packs):
                     x[top] = x[top] * (inverses[s] * lax.rsqrt(inverses[s]))
 
@@ -154,7 +189,7 @@
         sides = []
         for t in range(teams):
             ident = jnp.where(col_team == row_team % STEP, 1.0, 0.0)
-            sides.append(deep(split3(jnp.where(col_team < STEP, ident, slab_ref[t]))))
+            sides.append(deep(padded(split3(jnp.where(col_team < STEP, ident, slab_ref[t])))))
         pivots(packs, pieces)
         for t in range(teams):
             inner = jnp.concatenate(packs[t], axis=0)
@@ -170,7 +205,7 @@
             if height < 128:
                 ahead = jnp.concatenate([ahead, jnp.zeros((128 - height, 128), jnp.float32)], axis=0)
             ahead = wide(split3(ahead.T[:height]))
-            update = dot(ahead, deep(split3(pltpu.roll(slab, width - STEP, 1))), NN)
+            update = dot(ahead, deep(padded(split3(pltpu.roll(slab, width - STEP, 1)))), NN)
             coming = [pltpu.roll(ref[t * team + i, pl.ds(after, STEP), :], width - after, 1) for i in range(team)]
             slab_ref[t] = jnp.where(col_team >= width - STEP, 0.0, jnp.concatenate(coming, axis=0)) - update
             slab = pltpu.roll(slab, base, 1)
@@ -188,6 +223,11 @@
     return [pltpu.VMEM((systems // team, team * STEP, width), jnp.float32)] * 2
 
 
+def scaled(matrix):
+    factor_of = 1.0 / jnp.max(jnp.max(matrix, axis=1, keepdims=True), axis=0, keepdims=True)
+    return matrix * factor_of, jnp.sqrt(factor_of)
+
+
 def own_kernel(counts_ref, tiles_ref, w_ref, z_ref, g_ref, *scratch):
     systems, kslots, width, _ = tiles_ref.shape
     for s in range(systems):
@@ -198,9 +238,13 @@
             def _():
                 tile = tiles_ref[s, k]
                 g_ref[s] += dot(tile, tile, TN)
+    roots = []
+    for s in range(systems):
+        g_ref[s], root = scaled(g_ref[s])
+        roots.append(root)
     factor(g_ref, *scratch)
     for s in range(systems):
-        w1, w2, w3 = split3(g_ref[s])
+        w1, w2, w3 = split3(g_ref[s] * roots[s])
         w_ref[s, 0] = w1
         w_ref[s, 1] = w2
         near = jnp.concatenate([tiles_ref[s, 1], tiles_ref[s, 0]], axis=0)
@@ -211,48 +255,82 @@
         z_ref[s, 2] = z3
 
 
-def pair_kernel(lanes, place_ref, x_ref, w_any, z_any, got_ref, *refs):
-    up_refs, refs = refs[:lanes], refs[lanes:]
-    low_ref, near_ref, w_ref, z_ref, t_ref, v_ref, r_ref, first_ref, sems, *scratch = refs
+def ready_kernel(x_ref, w_any, z_any, base_ref, rhs_ref, m_ref, w_ref, z_ref, sems):
     systems, _, width, _ = z_ref.shape
-    count = x_ref.shape[0] // lanes
+    w_copy = pltpu.make_async_copy(w_any, w_ref, sems.at[systems])
+    w_copy.start()
+    copies = [pltpu.make_async_copy(z_any.at[s], z_ref.at[s], sems.at[s]) for s in range(systems)]
+    for copy in copies:
+        copy.start()
+    w_copy.wait()
+    for s in range(systems):
+        copies[s].wait()
+        z = [z_ref[s, i] for i in range(3)]
+        w = [w_ref[s, i] for i in range(2)]
+        x = x_ref[:, s * width:(s + 1) * width]
+        first = dot(x, z[0][:, width:], NT) + (dot(x, z[1][:, width:], NT) + dot(x, z[2][:, width:], NT))
+        base_ref[s] = apply(first, w, NN)
+        x = x.astype(jnp.float32)
+        rhs = jnp.concatenate([jnp.zeros_like(x), x], axis=1) - apply(first, z, NN)
+        rhs_ref[s] = jnp.concatenate(split3(rhs), axis=0)
+        m = split3(dot3(z, w, TN))
+        m_ref[s, 0] = m[0]
+        m_ref[s, 1] = m[1]
+
+
+def pair_kernel(lanes, place_ref, rhs_ref, z_any, got_ref, low_ref, y_ref, near_ref, z_ref, t_ref, r_ref, sems, *scratch):
+    systems, _, width, _ = z_ref.shape
+    count = y_ref.shape[1] // lanes
     copies = []
     for s in range(systems):
         pairs = ((got_ref.at[place_ref[s]], near_ref.at[s]), (z_any.at[s], z_ref.at[s]))
         copies.append([pltpu.make_async_copy(a, b, sems.at[s, i]) for i, (a, b) in enumerate(pairs)])
         for copy in copies[s]:
             copy.start()
-    w_copy = pltpu.make_async_copy(w_any, w_ref, sems.at[systems, 0])
-    w_copy.start()
     low_ref[...] = jnp.zeros(low_ref.shape, low_ref.dtype)
+    roots = []
     for s in range(systems):
         for copy in copies[s]:
             copy.wait()
         near = near_ref[s].reshape(2 * width, width)
         near_t = near.T
-        z1, z2, z3 = z_ref[s, 0], z_ref[s, 1], z_ref[s, 2]
-        v = split3(dot(near_t, z1, NT) + (dot(near_t, z2, NT) + dot(near_t, z3, NT)))
-        v_ref[s, 0] = v[0]
-        v_ref[s, 1] = v[1]
-        t_ref[s] = dot(near_t, near, NN) - dot6(v, v, NT)
-    for s in range(systems):
-        x = x_ref[:, s * width:(s + 1) * width]
-        first_ref[s] = dot(x, z_ref[s, 0, :, width:], NT) + dot(x, z_ref[s, 1, :, width:], NT)
-        r_ref[s] = dot(x, near_ref[s, 1], NN)
-    for s in range(systems):
-        r_ref[s] = r_ref[s] - apply(first_ref[s], (v_ref[s, 0], v_ref[s, 1]), NT)
+        v = split3(thirds(dot(z_ref[s].reshape(3 * width, 2 * width), near, NN)))
+        vt = [one.T for one in v]
+        once = dot(jnp.concatenate(vt, axis=0), v[0], NN)
+        twice = dot(jnp.concatenate(vt[:2], axis=0), v[1], NN)
+        small = once[2 * width:] + twice[width:] + dot(vt[0], v[2], NN)
+        square = once[:width] + ((once[width:2 * width] + twice[:width]) + small)
+        t_ref[s], root = scaled(dot(near_t, near, NN) - square)
+        roots.append(root)
+        r_ref[s] = thirds(dot(rhs_ref[s], near, NN))
     factor(t_ref, *scratch)
-    parts = [split3(t_ref[s])[:2] for s in range(systems)]
+    parts = [split3(t_ref[s] * roots[s])[:2] for s in range(systems)]
     half = [apply(r_ref[s], parts[s], NT) for s in range(systems)]
-    last = [apply(half[s], parts[s], NN) for s in range(systems)]
-    mid = [first_ref[s] - apply(last[s], (v_ref[s, 0], v_ref[s, 1]), NN) for s in range(systems)]
-    w_copy.wait()
-    for s in range(systems):
-        up = apply(mid[s], (w_ref[s, 0], w_ref[s, 1]), NN)
+    for s in range(systems):
+        y = apply(half[s], parts[s], NN)
+        y_ref[s] = y
+        for e in range(lanes):
+            owner = lax.rem(place_ref[systems] + e, lanes)
+            low_ref[place_ref[s] * lanes + owner] = y[e * count:(e + 1) * count].astype(low_ref.dtype)
+
+
+def own_part_kernel(lanes, place_ref, y_ref, base_ref, m_any, got_ref, *refs):
+    up_refs, (near_ref, m_ref, sems) = refs[:lanes], refs[lanes:]
+    systems, nrhs, width = y_ref.shape
+    count = nrhs // lanes
+    copies = []
+    for s in range(systems):
+        pairs = ((got_ref.at[place_ref[s]], near_ref.at[s]), (m_any.at[s], m_ref.at[s]))
+        copies.append([pltpu.make_async_copy(a, b, sems.at[s, i]) for i, (a, b) in enumerate(pairs)])
+        for copy in copies[s]:
+            copy.start()
+    for s in range(systems):
+        for copy in copies[s]:
+            copy.wait()
+        back = thirds(dot(jnp.concatenate(split3(y_ref[s]), axis=0), near_ref[s].reshape(2 * width, width), NT))
+        up = base_ref[s] - apply(back, (m_ref[s, 0], m_ref[s, 1]), NN)
         for e in range(lanes):
             up_refs[e][s] = up[e * count:(e + 1) * count]
-            owner = lax.rem(place_ref[systems] + e, lanes)
-            low_ref[place_ref[s] * lanes + owner] = last[s][e * count:(e + 1) * count].astype(low_ref.dtype)
 
 
 def place_kernel(lanes, place_ref, low_ref, *refs):
@@ -311,24 +389,56 @@
         parts.append(shift(part, -e))
     x = jnp.concatenate(parts, axis=0)
 
-    piece = jax.ShapeDtypeStruct((systems, nrhs_dev, width), jnp.float32)
-    *up, low = pl.pallas_call(
-        functools.partial(pair_kernel, lanes),
-        out_shape=[piece] * lanes + [jax.ShapeDtypeStruct((shards * lanes, nrhs_dev, width), jnp.bfloat16)],
-        in_specs=[smem, vmem, anywhere, anywhere, anywhere],
-        out_specs=[vmem] * (lanes + 1),
+    nrhs = lanes * nrhs_dev
+    rows = jax.ShapeDtypeStruct((systems, nrhs, width), jnp.float32)
+    base, rhs, m = pl.pallas_call(
+        ready_kernel,
+        out_shape=(
+            rows,
+            jax.ShapeDtypeStruct((systems, 3 * nrhs, 2 * width), jnp.bfloat16),
+            jax.ShapeDtypeStruct((systems, 2, 2 * width, width), jnp.bfloat16),
+        ),
+        in_specs=[vmem, anywhere, anywhere],
+        out_specs=(vmem,) * 3,
         scratch_shapes=[
             pltpu.VMEM((systems, 2, width, width), jnp.bfloat16),
+            pltpu.VMEM((systems, 3, width, 2 * width), jnp.bfloat16),
+            pltpu.SemaphoreType.DMA((systems + 1,)),
+        ],
+        compiler_params=params,
+        cost_estimate=pl.CostEstimate(flops=5 * 10**9, bytes_accessed=8 * 10**6, transcendentals=0),
+    )(x, w, z)
+
+    where = jnp.concatenate([mate_panel, lane_word])
+    piece = jax.ShapeDtypeStruct((systems, nrhs_dev, width), jnp.float32)
+    less = pltpu.CompilerParams(vmem_limit_bytes=40 * 1024 * 1024)
+    low, y = pl.pallas_call(
+        functools.partial(pair_kernel, lanes),
+        out_shape=(jax.ShapeDtypeStruct((shards * lanes, nrhs_dev, width), jnp.bfloat16), rows),
+        in_specs=[smem, vmem, anywhere, anywhere],
+        out_specs=(vmem, vmem),
+        scratch_shapes=[
             pltpu.VMEM((systems, 2, width, width), jnp.bfloat16),
             pltpu.VMEM((systems, 3, width, 2 * width), jnp.bfloat16),
             pltpu.VMEM((systems, width, width), jnp.float32),
+            pltpu.VMEM((systems, nrhs, width), jnp.float32),
+            pltpu.SemaphoreType.DMA((systems, 2)),
+        ] + factor_scratch(systems, width),
+        compiler_params=less,
+    )(where, rhs, z, received)
+    up = pl.pallas_call(
+        functools.partial(own_part_kernel, lanes),
+        out_shape=[piece] * lanes,
+        in_specs=[smem, vmem, vmem, anywhere, anywhere],
+        out_specs=[vmem] * lanes,
+        scratch_shapes=[
             pltpu.VMEM((systems, 2, width, width), jnp.bfloat16),
-            pltpu.VMEM((systems, lanes * nrhs_dev, width), jnp.float32),
-            pltpu.VMEM((systems, lanes * nrhs_dev, width), jnp.float32),
-            pltpu.SemaphoreType.DMA((systems + 1, 2)),
-        ] + factor_scratch(systems, width),
-        compiler_params=params,
-    )(jnp.concatenate([mate_panel, lane_word]), x, w, z, received)
+            pltpu.VMEM((systems, 2, 2 * width, width), jnp.bfloat16),
+            pltpu.SemaphoreType.DMA((systems, 2)),
+        ],
+        compiler_params=less,
+        cost_estimate=pl.CostEstimate(flops=10**9, bytes_accessed=6 * 10**6, transcendentals=0),
+    )(where, y, base, m, received)
     low = lax.all_to_all(low, ("panel", "rhs"), split_axis=0, concat_axis=0, tiled=True)
     up = [up[0]] + [shift(up[e], e) for e in range(1, lanes)]
     return pl.pallas_call(

time: 102 us -> 105 us (1.029)
  Pallas kernels: 52.9 us -> 62.7 us
  waiting for transfers between devices: 20.9 us -> 11.1 us
  local copies, waits for them, and re-layouts: 5.04 us -> 9.45 us
    pallas_call x1 -> x3, Pallas kernels: 27.6 us -> 37.5 us  [the longest x1 25.4 us: on_device(): pl.pallas_call(functools.partial(pair_kernel, lanes), out_shape=(jax.Shap...]
    all_to_all x1, waiting for transfers between devices: 16.7 us -> 8.88 us  [on_device(): lax.all_to_all(tiles[:, :2][slot_of], 'panel', split_axis=0, concat_axis=...]
    unnamed x14 -> x22, local copies, waits for them, and re-layouts: 2 us -> 6.4 us
    all_to_all x1, waiting for transfers between devices: 2.38 us -> 0.01 us  [on_device(): lax.all_to_all(low, ('panel', 'rhs'), split_axis=0, concat_axis=0, tiled=...]
  transfers between devices with their start and end apart: 8 -> 8, of which waited for: 5 -> 5; matrix products, arithmetic and copies ran while one was open for 2% -> 2% of each run, Pallas kernels for 23% -> 34%
where the time goes in v12:
time: 105 us
  Pallas kernels  62.7 us (60%)
  starting transfers between devices  19 us (18%)
  waiting for transfers between devices  11.1 us (11%)
  local copies, waits for them, and re-layouts  9.45 us (9%)
  other arithmetic  2.41 us (2%)
    pallas_call x1, Pallas kernels, on_device(): pl.pallas_call(functools.partial(pair_kernel, lanes), out_shape=(jax.Shap...  25.4 us
    pallas_call x1, Pallas kernels, on_device(): pl.pallas_call(own_kernel, out_shape=(jax.ShapeDtypeStruct((systems, 2, w...  23.7 us
    all_to_all x1, waiting for transfers between devices, on_device(): lax.all_to_all(tiles[:, :2][slot_of], 'panel', split_axis=0, concat_axis=...  8.88 us
    pallas_call x1, Pallas kernels, on_device(): pl.pallas_call(ready_kernel, out_shape=(rows, jax.ShapeDtypeStruct((syste...  8.28 us
    ppermute x6, starting transfers between devices, shift(): lax.ppermute(value, 'rhs', [(i, (i + by) % lanes) for i in range(lanes)])  7.96 us
    all_to_all x1, starting transfers between devices, on_device(): lax.all_to_all(tiles[:, :2][slot_of], 'panel', split_axis=0, concat_axis=...  7.41 us
    unnamed x22, local copies, waits for them, and re-layouts  6.4 us
    pallas_call x1, Pallas kernels, on_device(): pl.pallas_call(functools.partial(own_part_kernel, lanes), out_shape=[piec...  3.75 us
  transfers between devices with their start and end apart: 8, of which 5 were waited for; matrix products, arithmetic and copies ran while one was open for 2% of the time, Pallas kernels for 34%

profile of v12, /device:TPU:0, one launch (start us, length us, event | category | flops | bytes accessed | tf_op | source)
XLA Modules:
  0.0 104.8 jit_solution(6340799004481628642)
XLA Ops:
  0.0 0.9 bitcast_select_fusion
  1.4 2.1 %gather_fusion = bf16[8,2,256,256]{3,2,1,0:T(8,128)(2,1)} fusion(bf16[6,2,256,256]{3,2,1,0:T(8,128)(2,1)S(1)} %slice-done, s32[1024]{0:T(1024)S(1)} %pad_clamp_fusion), kind=kCustom, calls=%fused_computation | custom fusion | bytes 4194336 | tf_op jit(solution)/shard_map/gather | solution.py:366
  3.5 7.4 %all-to-all-start = ((bf16[8,2,256,256]{3,2,1,0:T(8,128)(2,1)}), bf16[8,2,256,256]{3,2,1,0:T(8,128)(2,1)S(1)}, u32[]{:S(2)}, u32[]{:S(2)}) async-start(bf16[8,2,256,256]{3,2,1,0:T(8,128)(2,1)} %gather_fusion), calls=%async_computation | async-start | bytes 4194304 | tf_op jit(solution)/shard_map/all_to_all | solution.py:366
  10.9 0.6 dynamic_slice.23.counts_ref
  11.5 23.7 %shard_map.46 = (bf16[6,2,256,256]{3,2,1,0:T(8,128)(2,1)}, bf16[6,3,256,512]{3,2,1,0:T(8,128)(2,1)}) custom-call(s32[6]{0:T(128)} %dynamic_slice.23.counts_ref, bf16[6,5,256,256]{3,2,1,0:T(8,128)(2,1)} %tiles_ref.1), custom_call_target="tpu_custom_call" | custom-call | flops 40000000000 | bytes 8000000 | tf_op jit(solution)/shard_map/pallas_call | solution.py:372
  35.3 3.3 %collective-permute-start.1 = (bf16[4,1536]{1,0:T(4,128)(2,1)S(1)}, bf16[4,1536]{1,0:T(4,128)(2,1)S(1)}, u32[]{:S(2)}, u32[]{:S(2)}) collective-permute-start(bf16[4,1536]{1,0:T(4,128)(2,1)S(1)} %get-tuple-element.33), channel_id=1, source_target_pairs={{0,2},{1,3},{2,0},{3,1},{4,6},{5,7},{6,4},{7,5},{8,10},{9,11},{10,... | collective-permute-start | bytes 36872 | tf_op jit(solution)/shard_map/ppermute | solution.py:364
  38.5 1.4 %collective-permute-start = (bf16[4,1536]{1,0:T(4,128)(2,1)S(1)}, bf16[4,1536]{1,0:T(4,128)(2,1)S(1)}, u32[]{:S(2)}, u32[]{:S(2)}) collective-permute-start(bf16[4,1536]{1,0:T(4,128)(2,1)S(1)} %get-tuple-element.34), channel_id=1, source_target_pairs={{0,3},{1,0},{2,1},{3,2},{4,7},{5,4},{6,5},{7,6},{8,11},{9,8},{10,9... | collective-permute-start | bytes 36872 | tf_op jit(solution)/shard_map/ppermute | solution.py:364
  40.2 1.1 %collective-permute-done = bf16[4,1536]{1,0:T(4,128)(2,1)S(1)} collective-permute-done((bf16[4,1536]{1,0:T(4,128)(2,1)S(1)}, bf16[4,1536]{1,0:T(4,128)(2,1)S(1)}, u32[]{:S(2)}, u32[]{:S(2)}) %collective-permute-start) | collective-permute-done | bytes 12320 | tf_op jit(solution)/shard_map/ppermute | solution.py:364
  41.3 0.7 pad_maximum_fusion.x_ref
  42.0 8.3 %shard_map.47 = (f32[6,16,256]{2,1,0:T(8,128)}, bf16[6,48,512]{2,1,0:T(8,128)(2,1)}, bf16[6,2,512,256]{3,2,1,0:T(8,128)(2,1)}) custom-call(bf16[16,1536]{1,0:T(8,128)(2,1)} %pad_maximum_fusion.x_ref, bf16[6,2,256,256]{3,2,1,0:T(8,128)(2,1)} %get-tuple-element.20.w_any, bf16[6,3,256,512]{3,2,1,0:T(8,128)(2,1)} %get-tuple-element.21.z_any), custom_call_target="tpu_custom_call" | custom-call | flops 5000000000 | bytes 8000000 | tf_op jit(solution)/shard_map/pallas_call | solution.py:394
  50.3 8.9 %all-to-all-done.got_ref = bf16[8,2,256,256]{3,2,1,0:T(8,128)(2,1)S(1)} async-done(((bf16[8,2,256,256]{3,2,1,0:T(8,128)(2,1)}), bf16[8,2,256,256]{3,2,1,0:T(8,128)(2,1)S(1)}, u32[]{:S(2)}, u32[]{:S(2)}) %all-to-all-start) | async-done | bytes 2097184 | tf_op jit(solution)/shard_map/all_to_all | solution.py:366
  59.1 2.3 %copy-done = bf16[6,3,256,512]{3,2,1,0:T(8,128)(2,1)S(1)} copy-done((bf16[6,3,256,512]{3,2,1,0:T(8,128)(2,1)S(1)}, bf16[6,3,256,512]{3,2,1,0:T(8,128)(2,1)}, u32[]{:S(2)}) %copy-start) | copy-done | bytes 4718616
  61.5 1.0 copy-done.2
  62.4 25.4 %shard_map.48 = (bf16[32,4,256]{2,1,0:T(4,128)(2,1)}, f32[6,16,256]{2,1,0:T(8,128)S(1)}) custom-call(s32[7]{0:T(128)S(1)} %pad_add_fusion.1.place_ref, bf16[6,48,512]{2,1,0:T(8,128)(2,1)S(1)} %copy-done.2, bf16[6,3,256,512]{3,2,1,0:T(8,128)(2,1)S(1)} %copy-done, bf16[8,2,256,256]{3,2,1,0:T(8,128)(2,1)S(1)} %all-to-all-done.got_ref), custom_call_target="tpu_custom_call" | custom-call | tf_op jit(solution)/shard_map/pallas_call | solution.py:415
  87.9 3.7 %all-to-all-start.1 = ((bf16[32,4,256]{2,1,0:T(4,128)(2,1)}), bf16[32,4,256]{2,1,0:T(4,128)(2,1)S(1)}, u32[]{:S(2)}, u32[]{:S(2)}) async-start(bf16[32,4,256]{2,1,0:T(4,128)(2,1)} %get-tuple-element.23), calls=%async_computation.1 | async-start | bytes 131072 | tf_op jit(solution)/shard_map/all_to_all | solution.py:442
  91.6 1.9 %copy-done.1 = bf16[6,2,512,256]{3,2,1,0:T(8,128)(2,1)S(1)} copy-done((bf16[6,2,512,256]{3,2,1,0:T(8,128)(2,1)S(1)}, bf16[6,2,512,256]{3,2,1,0:T(8,128)(2,1)}, u32[]{:S(2)}) %copy-start.1) | copy-done | bytes 3145752
  93.4 3.8 %shard_map.49 = (f32[6,4,256]{2,1,0:T(4,128)S(1)}, f32[6,4,256]{2,1,0:T(4,128)S(1)}, f32[6,4,256]{2,1,0:T(4,128)S(1)}, f32[6,4,256]{2,1,0:T(4,128)S(1)}) custom-call(s32[7]{0:T(128)S(1)} %pad_add_fusion.1.place_ref, f32[6,16,256]{2,1,0:T(8,128)S(1)} %get-tuple-element.24.y_ref, f32[6,16,256]{2,1,0:T(8,128)S(1)} %copy-done.3, ...), custom_call_target="tpu_custom_call" | custom-call | flops 1000000000 | bytes 6000000 | tf_op jit(solution)/shard_map/pallas_call | solution.py:429
  97.2 0.6 copy-done.4
  98.1 1.7 %collective-permute-start.4 = (f32[6,4,256]{2,1,0:T(4,128)S(1)}, f32[6,4,256]{2,1,0:T(4,128)S(1)}, u32[]{:S(2)}, u32[]{:S(2)}) collective-permute-start(f32[6,4,256]{2,1,0:T(4,128)S(1)} %get-tuple-element.29), channel_id=1, source_target_pairs={{0,2},{1,3},{2,0},{3,1},{4,6},{5,7},{6,4},{7,5},{8,10},{9,11},{10,... | collective-permute-start | bytes 73736 | tf_op jit(solution)/shard_map/ppermute | solution.py:364
  99.7 1.3 %collective-permute-start.5 = (f32[6,4,256]{2,1,0:T(4,128)S(1)}, f32[6,4,256]{2,1,0:T(4,128)S(1)}, u32[]{:S(2)}, u32[]{:S(2)}) collective-permute-start(f32[6,4,256]{2,1,0:T(4,128)S(1)} %get-tuple-element.30), channel_id=1, source_target_pairs={{0,3},{1,0},{2,1},{3,2},{4,7},{5,4},{6,5},{7,6},{8,11},{9,8},{10,9... | collective-permute-start | bytes 73736 | tf_op jit(solution)/shard_map/ppermute | solution.py:364
  101.1 0.7 pad_add_fusion.place_ref
  101.9 0.7 collective-permute-done.5.refs_3_
  102.6 0.6 copy-done.9
  103.2 1.6 %shard_map.50 = bf16[4,6144]{1,0:T(4,128)(2,1)} custom-call(s32[25]{0:T(128)} %pad_add_fusion.place_ref, bf16[32,4,256]{2,1,0:T(4,128)(2,1)} %copy-done.5, f32[6,4,256]{2,1,0:T(4,128)} %copy-done.4, f32[6,4,256]{2,1,0:T(4,128)} %copy-done.7, f32[6,4,256]{2,1,0:T(4,128)} %copy-done.8, f32[6,4,256]{2,1,0:T(4,128)} %copy-done.9), custom_call_target="tpu_custom_call" | custom-call | tf_op jit(solution)/shard_map/pallas_call | solution.py:444
  (32 shorter events, 1.4 us)
Async XLA Ops:
  0.0 1.4 %slice-start = ((bf16[6,5,256,256]{3,2,1,0:T(8,128)(2,1)}), bf16[6,2,256,256]{3,2,1,0:T(8,128)(2,1)S(1)}, s32[]{:S(2)}) async-start(bf16[6,5,256,256]{3,2,1,0:T(8,128)(2,1)} %tiles_ref.1), calls=%async_computation.2 | async-start | bytes 3145728 | tf_op jit(solution)/shard_map/slice | solution.py:366
  3.5 7.4 %copy-start.10 = (s32[192]{0:T(256)S(1)}, s32[192]{0:T(256)}, u32[]{:S(2)}) copy-start(s32[192]{0:T(256)} %param.6) | copy-start | bytes 2308
  3.5 55.7 %all-to-all-start = ((bf16[8,2,256,256]{3,2,1,0:T(8,128)(2,1)}), bf16[8,2,256,256]{3,2,1,0:T(8,128)(2,1)S(1)}, u32[]{:S(2)}, u32[]{:S(2)}) async-start(bf16[8,2,256,256]{3,2,1,0:T(8,128)(2,1)} %gather_fusion), calls=%async_computation | async-start | bytes 4194304 | tf_op jit(solution)/shard_map/all_to_all | solution.py:366
  11.5 23.7 %copy-start.6 = (bf16[4,6144]{1,0:T(4,128)(2,1)S(1)}, bf16[4,6144]{1,0:T(4,128)(2,1)}, u32[]{:S(2)}) copy-start(bf16[4,6144]{1,0:T(4,128)(2,1)} %param.7) | copy-start | bytes 147460
  35.2 4.8 %collective-permute-start.2 = (bf16[4,1536]{1,0:T(4,128)(2,1)S(1)}, bf16[4,1536]{1,0:T(4,128)(2,1)S(1)}, u32[]{:S(2)}, u32[]{:S(2)}) collective-permute-start(bf16[4,1536]{1,0:T(4,128)(2,1)S(1)} %get-tuple-element.32), channel_id=1, source_target_pairs={{0,1},{1,2},{2,3},{3,0},{4,5},{5,6},{6,7},{7,4},{8,9},{9,10},{10,1... | collective-permute-start | bytes 36872 | tf_op jit(solution)/shard_map/ppermute | solution.py:364
  35.3 4.9 %collective-permute-start.1 = (bf16[4,1536]{1,0:T(4,128)(2,1)S(1)}, bf16[4,1536]{1,0:T(4,128)(2,1)S(1)}, u32[]{:S(2)}, u32[]{:S(2)}) collective-permute-start(bf16[4,1536]{1,0:T(4,128)(2,1)S(1)} %get-tuple-element.33), channel_id=1, source_target_pairs={{0,2},{1,3},{2,0},{3,1},{4,6},{5,7},{6,4},{7,5},{8,10},{9,11},{10,... | collective-permute-start | bytes 36872 | tf_op jit(solution)/shard_map/ppermute | solution.py:364
  38.5 2.8 %collective-permute-start = (bf16[4,1536]{1,0:T(4,128)(2,1)S(1)}, bf16[4,1536]{1,0:T(4,128)(2,1)S(1)}, u32[]{:S(2)}, u32[]{:S(2)}) collective-permute-start(bf16[4,1536]{1,0:T(4,128)(2,1)S(1)} %get-tuple-element.34), channel_id=1, source_target_pairs={{0,3},{1,0},{2,1},{3,2},{4,7},{5,4},{6,5},{7,6},{8,11},{9,8},{10,9... | collective-permute-start | bytes 36872 | tf_op jit(solution)/shard_map/ppermute | solution.py:364
  59.1 2.3 %copy-start = (bf16[6,3,256,512]{3,2,1,0:T(8,128)(2,1)S(1)}, bf16[6,3,256,512]{3,2,1,0:T(8,128)(2,1)}, u32[]{:S(2)}) copy-start(bf16[6,3,256,512]{3,2,1,0:T(8,128)(2,1)} %get-tuple-element.21.z_any) | copy-start | bytes 14155780
  61.5 1.0 copy-start.2
  62.4 29.1 %copy-start.3 = (f32[6,16,256]{2,1,0:T(8,128)S(1)}, f32[6,16,256]{2,1,0:T(8,128)}, u32[]{:S(2)}) copy-start(f32[6,16,256]{2,1,0:T(8,128)} %get-tuple-element.25.base_ref) | copy-start | bytes 294916
  87.9 14.7 %all-to-all-start.1 = ((bf16[32,4,256]{2,1,0:T(4,128)(2,1)}), bf16[32,4,256]{2,1,0:T(4,128)(2,1)S(1)}, u32[]{:S(2)}, u32[]{:S(2)}) async-start(bf16[32,4,256]{2,1,0:T(4,128)(2,1)} %get-tuple-element.23), calls=%async_computation.1 | async-start | bytes 131072 | tf_op jit(solution)/shard_map/all_to_all | solution.py:442
  91.6 1.9 %copy-start.1 = (bf16[6,2,512,256]{3,2,1,0:T(8,128)(2,1)S(1)}, bf16[6,2,512,256]{3,2,1,0:T(8,128)(2,1)}, u32[]{:S(2)}) copy-start(bf16[6,2,512,256]{3,2,1,0:T(8,128)(2,1)} %get-tuple-element.26.m_any) | copy-start | bytes 9437188
  97.2 0.6 copy-start.4
  97.8 3.9 %collective-permute-start.3 = (f32[6,4,256]{2,1,0:T(4,128)S(1)}, f32[6,4,256]{2,1,0:T(4,128)S(1)}, u32[]{:S(2)}, u32[]{:S(2)}) collective-permute-start(f32[6,4,256]{2,1,0:T(4,128)S(1)} %get-tuple-element.28), channel_id=1, source_target_pairs={{0,1},{1,2},{2,3},{3,0},{4,5},{5,6},{6,7},{7,4},{8,9},{9,10},{10,1... | collective-permute-start | bytes 73736 | tf_op jit(solution)/shard_map/ppermute | solution.py:364
  98.1 3.8 %collective-permute-start.4 = (f32[6,4,256]{2,1,0:T(4,128)S(1)}, f32[6,4,256]{2,1,0:T(4,128)S(1)}, u32[]{:S(2)}, u32[]{:S(2)}) collective-permute-start(f32[6,4,256]{2,1,0:T(4,128)S(1)} %get-tuple-element.29), channel_id=1, source_target_pairs={{0,2},{1,3},{2,0},{3,1},{4,6},{5,7},{6,4},{7,5},{8,10},{9,11},{10,... | collective-permute-start | bytes 73736 | tf_op jit(solution)/shard_map/ppermute | solution.py:364
  99.7 2.9 %collective-permute-start.5 = (f32[6,4,256]{2,1,0:T(4,128)S(1)}, f32[6,4,256]{2,1,0:T(4,128)S(1)}, u32[]{:S(2)}, u32[]{:S(2)}) collective-permute-start(f32[6,4,256]{2,1,0:T(4,128)S(1)} %get-tuple-element.30), channel_id=1, source_target_pairs={{0,3},{1,0},{2,1},{3,2},{4,7},{5,4},{6,5},{7,6},{8,11},{9,8},{10,9... | collective-permute-start | bytes 73736 | tf_op jit(solution)/shard_map/ppermute | solution.py:364
  101.7 0.9 copy-start.7
  101.9 0.7 copy-start.8
  102.6 0.6 copy-start.9
  102.6 0.6 copy-start.5

commit v13 on v12

--- a/solution.py
+++ b/solution.py
@@ -29,10 +29,6 @@
     b1, b2, b3 = b
     small = dot(a1, b3, dims) + dot(a3, b1, dims) + dot(a2, b2, dims)
     return dot(a1, b1, dims) + ((dot(a1, b2, dims) + dot(a2, b1, dims)) + small)
-
-
-def dot3(a, b, dims):
-    return dot(a[0], b[0], dims) + (dot(a[0], b[1], dims) + dot(a[1], b[0], dims))
 
 
 def wide(parts):
@@ -248,89 +244,70 @@
         w_ref[s, 0] = w1
         w_ref[s, 1] = w2
         near = jnp.concatenate([tiles_ref[s, 1], tiles_ref[s, 0]], axis=0)
-        z = dot(w1, near, NT) + (dot(w2, near, NT) + dot(w3, near, NT))
-        z1, z2, z3 = split3(z)
-        z_ref[s, 0] = z1
-        z_ref[s, 1] = z2
-        z_ref[s, 2] = z3
-
-
-def ready_kernel(x_ref, w_any, z_any, base_ref, rhs_ref, m_ref, w_ref, z_ref, sems):
-    systems, _, width, _ = z_ref.shape
-    w_copy = pltpu.make_async_copy(w_any, w_ref, sems.at[systems])
-    w_copy.start()
+        z = dot(jnp.concatenate([w1, w2, w3], axis=1), jnp.concatenate([near] * 3, axis=1), NT)
+        for i, part in enumerate(split3(z)):
+            z_ref[s, :, i * 2 * width:(i + 1) * 2 * width] = part
+
+
+def ready_kernel(x_ref, z_any, first_ref, rhs_ref, z_ref, sems):
+    systems, _, width = first_ref.shape
     copies = [pltpu.make_async_copy(z_any.at[s], z_ref.at[s], sems.at[s]) for s in range(systems)]
     for copy in copies:
         copy.start()
-    w_copy.wait()
     for s in range(systems):
         copies[s].wait()
-        z = [z_ref[s, i] for i in range(3)]
-        w = [w_ref[s, i] for i in range(2)]
+        z = [z_ref[s, :, i * 2 * width:(i + 1) * 2 * width] for i in range(3)]
         x = x_ref[:, s * width:(s + 1) * width]
         first = dot(x, z[0][:, width:], NT) + (dot(x, z[1][:, width:], NT) + dot(x, z[2][:, width:], NT))
-        base_ref[s] = apply(first, w, NN)
+        first_ref[s] = first
         x = x.astype(jnp.float32)
         rhs = jnp.concatenate([jnp.zeros_like(x), x], axis=1) - apply(first, z, NN)
         rhs_ref[s] = jnp.concatenate(split3(rhs), axis=0)
-        m = split3(dot3(z, w, TN))
-        m_ref[s, 0] = m[0]
-        m_ref[s, 1] = m[1]
-
-
-def pair_kernel(lanes, place_ref, rhs_ref, z_any, got_ref, low_ref, y_ref, near_ref, z_ref, t_ref, r_ref, sems, *scratch):
-    systems, _, width, _ = z_ref.shape
-    count = y_ref.shape[1] // lanes
+
+
+def pair_kernel(lanes, place_ref, first_ref, rhs_ref, w_any, z_any, got_ref, *refs):
+    up_refs, refs = refs[:lanes], refs[lanes:]
+    low_ref, near_ref, w_ref, z_ref, t_ref, v_ref, r_ref, sems, *scratch = refs
+    systems, nrhs, width = first_ref.shape
+    count = nrhs // lanes
     copies = []
     for s in range(systems):
         pairs = ((got_ref.at[place_ref[s]], near_ref.at[s]), (z_any.at[s], z_ref.at[s]))
         copies.append([pltpu.make_async_copy(a, b, sems.at[s, i]) for i, (a, b) in enumerate(pairs)])
         for copy in copies[s]:
             copy.start()
+    w_copy = pltpu.make_async_copy(w_any, w_ref, sems.at[systems, 0])
+    w_copy.start()
     low_ref[...] = jnp.zeros(low_ref.shape, low_ref.dtype)
     roots = []
     for s in range(systems):
         for copy in copies[s]:
             copy.wait()
         near = near_ref[s].reshape(2 * width, width)
-        near_t = near.T
-        v = split3(thirds(dot(z_ref[s].reshape(3 * width, 2 * width), near, NN)))
-        vt = [one.T for one in v]
-        once = dot(jnp.concatenate(vt, axis=0), v[0], NN)
-        twice = dot(jnp.concatenate(vt[:2], axis=0), v[1], NN)
-        small = once[2 * width:] + twice[width:] + dot(vt[0], v[2], NN)
-        square = once[:width] + ((once[width:2 * width] + twice[:width]) + small)
-        t_ref[s], root = scaled(dot(near_t, near, NN) - square)
+        v = dot(z_ref[s], jnp.concatenate([near] * 3, axis=0), NN)
+        v1, v2, v3 = split3(v)
+        n1, n2, n3 = split3(-v.T)
+        v_ref[s, 0] = n1
+        v_ref[s, 1] = n2
+        t_ref[s], root = scaled(dot(
+            jnp.concatenate([near.T, n1, n1, n2, n2, n1, n3], axis=1),
+            jnp.concatenate([near, v1, v2, v1, v2, v3, v1], axis=0),
+            NN,
+        ))
         roots.append(root)
         r_ref[s] = thirds(dot(rhs_ref[s], near, NN))
     factor(t_ref, *scratch)
+    w_copy.wait()
     parts = [split3(t_ref[s] * roots[s])[:2] for s in range(systems)]
     half = [apply(r_ref[s], parts[s], NT) for s in range(systems)]
-    for s in range(systems):
-        y = apply(half[s], parts[s], NN)
-        y_ref[s] = y
-        for e in range(lanes):
-            owner = lax.rem(place_ref[systems] + e, lanes)
-            low_ref[place_ref[s] * lanes + owner] = y[e * count:(e + 1) * count].astype(low_ref.dtype)
-
-
-def own_part_kernel(lanes, place_ref, y_ref, base_ref, m_any, got_ref, *refs):
-    up_refs, (near_ref, m_ref, sems) = refs[:lanes], refs[lanes:]
-    systems, nrhs, width = y_ref.shape
-    count = nrhs // lanes
-    copies = []
-    for s in range(systems):
-        pairs = ((got_ref.at[place_ref[s]], near_ref.at[s]), (m_any.at[s], m_ref.at[s]))
-        copies.append([pltpu.make_async_copy(a, b, sems.at[s, i]) for i, (a, b) in enumerate(pairs)])
-        for copy in copies[s]:
-            copy.start()
-    for s in range(systems):
-        for copy in copies[s]:
-            copy.wait()
-        back = thirds(dot(jnp.concatenate(split3(y_ref[s]), axis=0), near_ref[s].reshape(2 * width, width), NT))
-        up = base_ref[s] - apply(back, (m_ref[s, 0], m_ref[s, 1]), NN)
+    last = [apply(half[s], parts[s], NN) for s in range(systems)]
+    mid = [first_ref[s] + apply(last[s], (v_ref[s, 0], v_ref[s, 1]), NN) for s in range(systems)]
+    for s in range(systems):
+        up = apply(mid[s], (w_ref[s, 0], w_ref[s, 1]), NN)
         for e in range(lanes):
             up_refs[e][s] = up[e * count:(e + 1) * count]
+            owner = lax.rem(place_ref[systems] + e, lanes)
+            low_ref[place_ref[s] * lanes + owner] = last[s][e * count:(e + 1) * count].astype(low_ref.dtype)
 
 
 def place_kernel(lanes, place_ref, low_ref, *refs):
@@ -373,7 +350,7 @@
         own_kernel,
         out_shape=(
             jax.ShapeDtypeStruct((systems, 2, width, width), jnp.bfloat16),
-            jax.ShapeDtypeStruct((systems, 3, width, 2 * width), jnp.bfloat16),
+            jax.ShapeDtypeStruct((systems, width, 6 * width), jnp.bfloat16),
         ),
         in_specs=[smem, vmem],
         out_specs=(vmem, vmem),
@@ -391,54 +368,36 @@
 
     nrhs = lanes * nrhs_dev
     rows = jax.ShapeDtypeStruct((systems, nrhs, width), jnp.float32)
-    base, rhs, m = pl.pallas_call(
+    first, rhs = pl.pallas_call(
         ready_kernel,
-        out_shape=(
-            rows,
-            jax.ShapeDtypeStruct((systems, 3 * nrhs, 2 * width), jnp.bfloat16),
-            jax.ShapeDtypeStruct((systems, 2, 2 * width, width), jnp.bfloat16),
-        ),
-        in_specs=[vmem, anywhere, anywhere],
-        out_specs=(vmem,) * 3,
+        out_shape=(rows, jax.ShapeDtypeStruct((systems, 3 * nrhs, 2 * width), jnp.bfloat16)),
+        in_specs=[vmem, anywhere],
+        out_specs=(vmem, vmem),
         scratch_shapes=[
-            pltpu.VMEM((systems, 2, width, width), jnp.bfloat16),
-            pltpu.VMEM((systems, 3, width, 2 * width), jnp.bfloat16),
-            pltpu.SemaphoreType.DMA((systems + 1,)),
+            pltpu.VMEM((systems, width, 6 * width), jnp.bfloat16),
+            pltpu.SemaphoreType.DMA((systems,)),
         ],
         compiler_params=params,
         cost_estimate=pl.CostEstimate(flops=5 * 10**9, bytes_accessed=8 * 10**6, transcendentals=0),
-    )(x, w, z)
-
-    where = jnp.concatenate([mate_panel, lane_word])
+    )(x, z)
+
     piece = jax.ShapeDtypeStruct((systems, nrhs_dev, width), jnp.float32)
-    less = pltpu.CompilerParams(vmem_limit_bytes=40 * 1024 * 1024)
-    low, y = pl.pallas_call(
+    *up, low = pl.pallas_call(
         functools.partial(pair_kernel, lanes),
-        out_shape=(jax.ShapeDtypeStruct((shards * lanes, nrhs_dev, width), jnp.bfloat16), rows),
-        in_specs=[smem, vmem, anywhere, anywhere],
-        out_specs=(vmem, vmem),
+        out_shape=[piece] * lanes + [jax.ShapeDtypeStruct((shards * lanes, nrhs_dev, width), jnp.bfloat16)],
+        in_specs=[smem, vmem, vmem, anywhere, anywhere, anywhere],
+        out_specs=[vmem] * (lanes + 1),
         scratch_shapes=[
             pltpu.VMEM((systems, 2, width, width), jnp.bfloat16),
-            pltpu.VMEM((systems, 3, width, 2 * width), jnp.bfloat16),
+            pltpu.VMEM((systems, 2, width, width), jnp.bfloat16),
+            pltpu.VMEM((systems, width, 6 * width), jnp.bfloat16),
             pltpu.VMEM((systems, width, width), jnp.float32),
+            pltpu.VMEM((systems, 2, width, width), jnp.bfloat16),
             pltpu.VMEM((systems, nrhs, width), jnp.float32),
-            pltpu.SemaphoreType.DMA((systems, 2)),
+            pltpu.SemaphoreType.DMA((systems + 1, 2)),
         ] + factor_scratch(systems, width),
-        compiler_params=less,
-    )(where, rhs, z, received)
-    up = pl.pallas_call(
-        functools.partial(own_part_kernel, lanes),
-        out_shape=[piece] * lanes,
-        in_specs=[smem, vmem, vmem, anywhere, anywhere],
-        out_specs=[vmem] * lanes,
-        scratch_shapes=[
-            pltpu.VMEM((systems, 2, width, width), jnp.bfloat16),
-            pltpu.VMEM((systems, 2, 2 * width, width), jnp.bfloat16),
-            pltpu.SemaphoreType.DMA((systems, 2)),
-        ],
-        compiler_params=less,
-        cost_estimate=pl.CostEstimate(flops=10**9, bytes_accessed=6 * 10**6, transcendentals=0),
-    )(where, y, base, m, received)
+        compiler_params=params,
+    )(jnp.concatenate([mate_panel, lane_word]), first, rhs, w, z, received)
     low = lax.all_to_all(low, ("panel", "rhs"), split_axis=0, concat_axis=0, tiled=True)
     up = [up[0]] + [shift(up[e], e) for e in range(1, lanes)]
     return pl.pallas_call(

time: 105 us -> 101 us (0.962)
  local copies, waits for them, and re-layouts: 9.45 us -> 5.01 us
  waiting for transfers between devices: 11.1 us -> 15.3 us
  Pallas kernels: 62.7 us -> 59.9 us
  starting transfers between devices: 19 us -> 17.6 us
    unnamed x22 -> x14, local copies, waits for them, and re-layouts: 6.4 us -> 1.98 us
    all_to_all x1, waiting for transfers between devices: 0.01 us -> 2.36 us  [on_device(): lax.all_to_all(low, ('panel', 'rhs'), split_axis=0, concat_axis=0, tiled=...]
    pallas_call x1, Pallas kernels: 8.28 us -> 6.04 us  [on_device(): pl.pallas_call(ready_kernel, out_shape=(rows, jax.ShapeDtypeStruct((syste...]
    all_to_all x1, waiting for transfers between devices: 8.88 us -> 11.1 us  [on_device(): lax.all_to_all(tiles[:, :2][slot_of], 'panel', split_axis=0, concat_axis=...]
    pallas_call x2 -> x1, Pallas kernels: 29.2 us -> 27.2 us  [on_device(): pl.pallas_call(functools.partial(pair_kernel, lanes), out_shape=[piece] *...]
    pallas_call x1, Pallas kernels: 23.7 us -> 25.2 us  [on_device(): pl.pallas_call(own_kernel, out_shape=(jax.ShapeDtypeStruct((systems, 2, w...]
    ppermute x6, starting transfers between devices: 7.96 us -> 6.5 us  [shift(): lax.ppermute(value, 'rhs', [(i, (i + by) % lanes) for i in range(lanes)])]
  transfers between devices with their start and end apart: 8 -> 8, of which waited for: 5 -> 5; matrix products, arithmetic and copies ran while one was open for 2% -> 3% of each run, Pallas kernels for 34% -> 31%
where the time goes in v13:
time: 101 us
  Pallas kernels  59.9 us (59%)
  starting transfers between devices  17.6 us (17%)
  waiting for transfers between devices  15.3 us (15%)
  local copies, waits for them, and re-layouts  5.01 us (5%)
  other arithmetic  2.95 us (3%)
    pallas_call x1, Pallas kernels, on_device(): pl.pallas_call(functools.partial(pair_kernel, lanes), out_shape=[piece] *...  27.2 us
    pallas_call x1, Pallas kernels, on_device(): pl.pallas_call(own_kernel, out_shape=(jax.ShapeDtypeStruct((systems, 2, w...  25.2 us
    all_to_all x1, waiting for transfers between devices, on_device(): lax.all_to_all(tiles[:, :2][slot_of], 'panel', split_axis=0, concat_axis=...  11.1 us
    all_to_all x1, starting transfers between devices, on_device(): lax.all_to_all(tiles[:, :2][slot_of], 'panel', split_axis=0, concat_axis=...  7.41 us
    ppermute x6, starting transfers between devices, shift(): lax.ppermute(value, 'rhs', [(i, (i + by) % lanes) for i in range(lanes)])  6.5 us
    pallas_call x1, Pallas kernels, on_device(): pl.pallas_call(ready_kernel, out_shape=(rows, jax.ShapeDtypeStruct((syste...  6.04 us
    all_to_all x1, starting transfers between devices, on_device(): lax.all_to_all(low, ('panel', 'rhs'), split_axis=0, concat_axis=0, tiled=...  3.66 us
    all_to_all x1, waiting for transfers between devices, on_device(): lax.all_to_all(low, ('panel', 'rhs'), split_axis=0, concat_axis=0, tiled=...  2.36 us
  transfers between devices with their start and end apart: 8, of which 5 were waited for; matrix products, arithmetic and copies ran while one was open for 3% of the time, Pallas kernels for 31%

profile of v13, /device:TPU:0, one launch (start us, length us, event | category | flops | bytes accessed | tf_op | source)
XLA Modules:
  0.0 100.9 jit_solution(15446235139506976590)
XLA Ops:
  0.0 0.9 bitcast_select_fusion
  1.1 0.3 slice-done
  1.4 2.0 %gather_fusion = bf16[8,2,256,256]{3,2,1,0:T(8,128)(2,1)} fusion(bf16[6,2,256,256]{3,2,1,0:T(8,128)(2,1)S(1)} %slice-done, s32[1024]{0:T(1024)S(1)} %pad_clamp_fusion), kind=kCustom, calls=%fused_computation | custom fusion | bytes 4194336 | tf_op jit(solution)/shard_map/gather | solution.py:343
  3.5 7.4 %all-to-all-start = ((bf16[8,2,256,256]{3,2,1,0:T(8,128)(2,1)}), bf16[8,2,256,256]{3,2,1,0:T(8,128)(2,1)S(1)}, u32[]{:S(2)}, u32[]{:S(2)}) async-start(bf16[8,2,256,256]{3,2,1,0:T(8,128)(2,1)} %gather_fusion), calls=%async_computation | async-start | bytes 4194304 | tf_op jit(solution)/shard_map/all_to_all | solution.py:343
  10.9 0.6 dynamic_slice.23.counts_ref
  11.5 25.2 %shard_map.46 = (bf16[6,2,256,256]{3,2,1,0:T(8,128)(2,1)}, bf16[6,256,1536]{2,1,0:T(8,128)(2,1)}) custom-call(s32[6]{0:T(128)} %dynamic_slice.23.counts_ref, bf16[6,5,256,256]{3,2,1,0:T(8,128)(2,1)} %tiles_ref.1), custom_call_target="tpu_custom_call" | custom-call | flops 40000000000 | bytes 8000000 | tf_op jit(solution)/shard_map/pallas_call | solution.py:349
  36.7 1.8 %collective-permute-start.1 = (bf16[4,1536]{1,0:T(4,128)(2,1)S(1)}, bf16[4,1536]{1,0:T(4,128)(2,1)S(1)}, u32[]{:S(2)}, u32[]{:S(2)}) collective-permute-start(bf16[4,1536]{1,0:T(4,128)(2,1)S(1)} %get-tuple-element.29), channel_id=1, source_target_pairs={{0,2},{1,3},{2,0},{3,1},{4,6},{5,7},{6,4},{7,5},{8,10},{9,11},{10,... | collective-permute-start | bytes 36872 | tf_op jit(solution)/shard_map/ppermute | solution.py:341
  38.5 1.4 %collective-permute-start = (bf16[4,1536]{1,0:T(4,128)(2,1)S(1)}, bf16[4,1536]{1,0:T(4,128)(2,1)S(1)}, u32[]{:S(2)}, u32[]{:S(2)}) collective-permute-start(bf16[4,1536]{1,0:T(4,128)(2,1)S(1)} %get-tuple-element.30), channel_id=1, source_target_pairs={{0,3},{1,0},{2,1},{3,2},{4,7},{5,4},{6,5},{7,6},{8,11},{9,8},{10,9... | collective-permute-start | bytes 36872 | tf_op jit(solution)/shard_map/ppermute | solution.py:341
  39.9 0.7 pad_add_fusion.1.place_ref
  40.5 0.7 collective-permute-done
  41.3 0.7 pad_maximum_fusion.x_ref
  42.0 6.0 %shard_map.47 = (f32[6,16,256]{2,1,0:T(8,128)}, bf16[6,48,512]{2,1,0:T(8,128)(2,1)}) custom-call(bf16[16,1536]{1,0:T(8,128)(2,1)} %pad_maximum_fusion.x_ref, bf16[6,256,1536]{2,1,0:T(8,128)(2,1)} %get-tuple-element.18.z_any), custom_call_target="tpu_custom_call" | custom-call | flops 5000000000 | bytes 8000000 | tf_op jit(solution)/shard_map/pallas_call | solution.py:371
  48.0 11.1 %all-to-all-done.got_ref = bf16[8,2,256,256]{3,2,1,0:T(8,128)(2,1)S(1)} async-done(((bf16[8,2,256,256]{3,2,1,0:T(8,128)(2,1)}), bf16[8,2,256,256]{3,2,1,0:T(8,128)(2,1)S(1)}, u32[]{:S(2)}, u32[]{:S(2)}) %all-to-all-start) | async-done | bytes 2097184 | tf_op jit(solution)/shard_map/all_to_all | solution.py:343
  59.1 1.4 %copy-done = bf16[8,2,256,256]{3,2,1,0:T(8,128)(2,1)} copy-done((bf16[8,2,256,256]{3,2,1,0:T(8,128)(2,1)}, bf16[8,2,256,256]{3,2,1,0:T(8,128)(2,1)S(1)}, u32[]{:S(2)}) %copy-start) | copy-done | bytes 2097176
  60.5 27.2 %shard_map.48 = (f32[6,4,256]{2,1,0:T(4,128)}, f32[6,4,256]{2,1,0:T(4,128)}, f32[6,4,256]{2,1,0:T(4,128)}, f32[6,4,256]{2,1,0:T(4,128)}, bf16[32,4,256]{2,1,0:T(4,128)(2,1)}) custom-call(s32[7]{0:T(128)} %pad_add_fusion.1.place_ref, f32[6,16,256]{2,1,0:T(8,128)} %get-tuple-element.19.first_ref, bf16[6,48,512]{2,1,0:T(8,128)(2,1)} %get-tuple-element.20.rhs_ref, ...), custom_call_target="tpu_custom_call" | custom-call | tf_op jit(solution)/shard_map/pallas_call | solution.py:385
  87.6 3.7 %all-to-all-start.1 = ((bf16[32,4,256]{2,1,0:T(4,128)(2,1)}), bf16[32,4,256]{2,1,0:T(4,128)(2,1)S(1)}, u32[]{:S(2)}, u32[]{:S(2)}) async-start(bf16[32,4,256]{2,1,0:T(4,128)(2,1)} %get-tuple-element.22), calls=%async_computation.1 | async-start | bytes 131072 | tf_op jit(solution)/shard_map/all_to_all | solution.py:401
  91.6 1.7 %collective-permute-start.4 = (f32[6,4,256]{2,1,0:T(4,128)}, f32[6,4,256]{2,1,0:T(4,128)S(1)}, u32[]{:S(2)}, u32[]{:S(2)}) collective-permute-start(f32[6,4,256]{2,1,0:T(4,128)} %get-tuple-element.25), channel_id=1, source_target_pairs={{0,2},{1,3},{2,0},{3,1},{4,6},{5,7},{6,4},{7,5},{8,10},{9,11},{10,... | collective-permute-start | bytes 73736 | tf_op jit(solution)/shard_map/ppermute | solution.py:341
  93.3 1.3 %collective-permute-start.5 = (f32[6,4,256]{2,1,0:T(4,128)}, f32[6,4,256]{2,1,0:T(4,128)S(1)}, u32[]{:S(2)}, u32[]{:S(2)}) collective-permute-start(f32[6,4,256]{2,1,0:T(4,128)} %get-tuple-element.26), channel_id=1, source_target_pairs={{0,3},{1,0},{2,1},{3,2},{4,7},{5,4},{6,5},{7,6},{8,11},{9,8},{10,9... | collective-permute-start | bytes 73736 | tf_op jit(solution)/shard_map/ppermute | solution.py:341
  94.6 0.6 pad_add_fusion.place_ref
  95.2 0.4 collective-permute-done.4.refs_2_
  95.7 0.7 collective-permute-done.5.refs_3_
  96.3 2.4 %all-to-all-done.1.low_ref = bf16[32,4,256]{2,1,0:T(4,128)(2,1)S(1)} async-done(((bf16[32,4,256]{2,1,0:T(4,128)(2,1)}), bf16[32,4,256]{2,1,0:T(4,128)(2,1)S(1)}, u32[]{:S(2)}, u32[]{:S(2)}) %all-to-all-start.1) | async-done | bytes 65568 | tf_op jit(solution)/shard_map/all_to_all | solution.py:401
  98.7 0.6 copy-done.1
  99.3 1.6 %shard_map.49 = bf16[4,6144]{1,0:T(4,128)(2,1)} custom-call(s32[25]{0:T(128)} %pad_add_fusion.place_ref, bf16[32,4,256]{2,1,0:T(4,128)(2,1)} %copy-done.1, f32[6,4,256]{2,1,0:T(4,128)} %get-tuple-element.23.refs_0_, f32[6,4,256]{2,1,0:T(4,128)} %copy-done.3, f32[6,4,256]{2,1,0:T(4,128)} %copy-done.4, f32[6,4,256]{2,1,0:T(4,128)} %copy-done.5), custom_call_target="tpu_custom_call" | custom-call | tf_op jit(solution)/shard_map/pallas_call | solution.py:403
  (23 shorter events, 0.6 us)
Async XLA Ops:
  0.0 1.4 %slice-start = ((bf16[6,5,256,256]{3,2,1,0:T(8,128)(2,1)}), bf16[6,2,256,256]{3,2,1,0:T(8,128)(2,1)S(1)}, s32[]{:S(2)}) async-start(bf16[6,5,256,256]{3,2,1,0:T(8,128)(2,1)} %tiles_ref.1), calls=%async_computation.2 | async-start | bytes 3145728 | tf_op jit(solution)/shard_map/slice | solution.py:343
  3.5 7.4 %copy-start.6 = (s32[192]{0:T(256)S(1)}, s32[192]{0:T(256)}, u32[]{:S(2)}) copy-start(s32[192]{0:T(256)} %param.6) | copy-start | bytes 2308
  3.5 55.7 %all-to-all-start = ((bf16[8,2,256,256]{3,2,1,0:T(8,128)(2,1)}), bf16[8,2,256,256]{3,2,1,0:T(8,128)(2,1)S(1)}, u32[]{:S(2)}, u32[]{:S(2)}) async-start(bf16[8,2,256,256]{3,2,1,0:T(8,128)(2,1)} %gather_fusion), calls=%async_computation | async-start | bytes 4194304 | tf_op jit(solution)/shard_map/all_to_all | solution.py:343
  11.5 25.2 %copy-start.2 = (bf16[4,6144]{1,0:T(4,128)(2,1)S(1)}, bf16[4,6144]{1,0:T(4,128)(2,1)}, u32[]{:S(2)}) copy-start(bf16[4,6144]{1,0:T(4,128)(2,1)} %param.7) | copy-start | bytes 147460
  36.7 3.9 %collective-permute-start.2 = (bf16[4,1536]{1,0:T(4,128)(2,1)S(1)}, bf16[4,1536]{1,0:T(4,128)(2,1)S(1)}, u32[]{:S(2)}, u32[]{:S(2)}) collective-permute-start(bf16[4,1536]{1,0:T(4,128)(2,1)S(1)} %get-tuple-element.28), channel_id=1, source_target_pairs={{0,1},{1,2},{2,3},{3,0},{4,5},{5,6},{6,7},{7,4},{8,9},{9,10},{10,1... | collective-permute-start | bytes 36872 | tf_op jit(solution)/shard_map/ppermute | solution.py:341
  36.7 3.8 %collective-permute-start.1 = (bf16[4,1536]{1,0:T(4,128)(2,1)S(1)}, bf16[4,1536]{1,0:T(4,128)(2,1)S(1)}, u32[]{:S(2)}, u32[]{:S(2)}) collective-permute-start(bf16[4,1536]{1,0:T(4,128)(2,1)S(1)} %get-tuple-element.29), channel_id=1, source_target_pairs={{0,2},{1,3},{2,0},{3,1},{4,6},{5,7},{6,4},{7,5},{8,10},{9,11},{10,... | collective-permute-start | bytes 36872 | tf_op jit(solution)/shard_map/ppermute | solution.py:341
  38.5 2.8 %collective-permute-start = (bf16[4,1536]{1,0:T(4,128)(2,1)S(1)}, bf16[4,1536]{1,0:T(4,128)(2,1)S(1)}, u32[]{:S(2)}, u32[]{:S(2)}) collective-permute-start(bf16[4,1536]{1,0:T(4,128)(2,1)S(1)} %get-tuple-element.30), channel_id=1, source_target_pairs={{0,3},{1,0},{2,1},{3,2},{4,7},{5,4},{6,5},{7,6},{8,11},{9,8},{10,9... | collective-permute-start | bytes 36872 | tf_op jit(solution)/shard_map/ppermute | solution.py:341
  59.1 1.4 %copy-start = (bf16[8,2,256,256]{3,2,1,0:T(8,128)(2,1)}, bf16[8,2,256,256]{3,2,1,0:T(8,128)(2,1)S(1)}, u32[]{:S(2)}) copy-start(bf16[8,2,256,256]{3,2,1,0:T(8,128)(2,1)S(1)} %all-to-all-done.got_ref) | copy-start | bytes 6291460
  87.6 11.1 %all-to-all-start.1 = ((bf16[32,4,256]{2,1,0:T(4,128)(2,1)}), bf16[32,4,256]{2,1,0:T(4,128)(2,1)S(1)}, u32[]{:S(2)}, u32[]{:S(2)}) async-start(bf16[32,4,256]{2,1,0:T(4,128)(2,1)} %get-tuple-element.22), calls=%async_computation.1 | async-start | bytes 131072 | tf_op jit(solution)/shard_map/all_to_all | solution.py:401
  91.3 3.9 %collective-permute-start.3 = (f32[6,4,256]{2,1,0:T(4,128)}, f32[6,4,256]{2,1,0:T(4,128)S(1)}, u32[]{:S(2)}, u32[]{:S(2)}) collective-permute-start(f32[6,4,256]{2,1,0:T(4,128)} %get-tuple-element.24), channel_id=1, source_target_pairs={{0,1},{1,2},{2,3},{3,0},{4,5},{5,6},{6,7},{7,4},{8,9},{9,10},{10,1... | collective-permute-start | bytes 73736 | tf_op jit(solution)/shard_map/ppermute | solution.py:341
  91.6 4.0 %collective-permute-start.4 = (f32[6,4,256]{2,1,0:T(4,128)}, f32[6,4,256]{2,1,0:T(4,128)S(1)}, u32[]{:S(2)}, u32[]{:S(2)}) collective-permute-start(f32[6,4,256]{2,1,0:T(4,128)} %get-tuple-element.25), channel_id=1, source_target_pairs={{0,2},{1,3},{2,0},{3,1},{4,6},{5,7},{6,4},{7,5},{8,10},{9,11},{10,... | collective-permute-start | bytes 73736 | tf_op jit(solution)/shard_map/ppermute | solution.py:341
  93.3 3.1 %collective-permute-start.5 = (f32[6,4,256]{2,1,0:T(4,128)}, f32[6,4,256]{2,1,0:T(4,128)S(1)}, u32[]{:S(2)}, u32[]{:S(2)}) collective-permute-start(f32[6,4,256]{2,1,0:T(4,128)} %get-tuple-element.26), channel_id=1, source_target_pairs={{0,3},{1,0},{2,1},{3,2},{4,7},{5,4},{6,5},{7,6},{8,11},{9,8},{10,9... | collective-permute-start | bytes 73736 | tf_op jit(solution)/shard_map/ppermute | solution.py:341
  95.2 3.5 %copy-start.3 = (f32[6,4,256]{2,1,0:T(4,128)}, f32[6,4,256]{2,1,0:T(4,128)S(1)}, u32[]{:S(2)}) copy-start(f32[6,4,256]{2,1,0:T(4,128)S(1)} %collective-permute-done.3.refs_1_) | copy-start | bytes 73732
  95.6 3.1 %copy-start.4 = (f32[6,4,256]{2,1,0:T(4,128)}, f32[6,4,256]{2,1,0:T(4,128)S(1)}, u32[]{:S(2)}) copy-start(f32[6,4,256]{2,1,0:T(4,128)S(1)} %collective-permute-done.4.refs_2_) | copy-start | bytes 73732
  96.3 2.4 %copy-start.5 = (f32[6,4,256]{2,1,0:T(4,128)}, f32[6,4,256]{2,1,0:T(4,128)S(1)}, u32[]{:S(2)}) copy-start(f32[6,4,256]{2,1,0:T(4,128)S(1)} %collective-permute-done.5.refs_3_) | copy-start | bytes 73732
  98.7 0.6 copy-start.1

commit v14 on v13

--- a/solution.py
+++ b/solution.py
@@ -6,7 +6,7 @@
 from jax.experimental.pallas import tpu as pltpu
 from jax.sharding import PartitionSpec as P
 
-STEP = 32
+STEP = 64
 NT = (((1,), (1,)), ((), ()))
 NN = (((1,), (0,)), ((), ()))
 TN = (((0,), (0,)), ((), ()))

time: 101 us -> 102 us (level)
  transfers between devices with their start and end apart: 8 -> 8, of which waited for: 5 -> 6; matrix products, arithmetic and copies ran while one was open for 3% -> 2% of each run, Pallas kernels for 31% -> 31%
where the time goes in v14:
time: 102 us; the launch traced here: 101 us
  Pallas kernels  60.2 us (59%)
  starting transfers between devices  17.4 us (17%)
  waiting for transfers between devices  15.5 us (15%)
  local copies, waits for them, and re-layouts  5.01 us (5%)
  other arithmetic  2.95 us (3%)
    pallas_call x1, Pallas kernels, on_device(): pl.pallas_call(functools.partial(pair_kernel, lanes), out_shape=[piece] *...  27.4 us
    pallas_call x1, Pallas kernels, on_device(): pl.pallas_call(own_kernel, out_shape=(jax.ShapeDtypeStruct((systems, 2, w...  25.2 us
    all_to_all x1, waiting for transfers between devices, on_device(): lax.all_to_all(tiles[:, :2][slot_of], 'panel', split_axis=0, concat_axis=...  11.3 us
    all_to_all x1, starting transfers between devices, on_device(): lax.all_to_all(tiles[:, :2][slot_of], 'panel', split_axis=0, concat_axis=...  7.41 us
    ppermute x6, starting transfers between devices, shift(): lax.ppermute(value, 'rhs', [(i, (i + by) % lanes) for i in range(lanes)])  6.32 us
    pallas_call x1, Pallas kernels, on_device(): pl.pallas_call(ready_kernel, out_shape=(rows, jax.ShapeDtypeStruct((syste...  6.04 us
    all_to_all x1, starting transfers between devices, on_device(): lax.all_to_all(low, ('panel', 'rhs'), split_axis=0, concat_axis=0, tiled=...  3.67 us
    all_to_all x1, waiting for transfers between devices, on_device(): lax.all_to_all(low, ('panel', 'rhs'), split_axis=0, concat_axis=0, tiled=...  2.36 us
  transfers between devices with their start and end apart: 8, of which 6 were waited for; matrix products, arithmetic and copies ran while one was open for 2% of the time, Pallas kernels for 31%

profile of v14, /device:TPU:0, one launch (start us, length us, event | category | flops | bytes accessed | tf_op | source)
XLA Modules:
  0.0 101.1 jit_solution(10452498536673530959)
XLA Ops:
  0.0 0.9 bitcast_select_fusion
  1.1 0.3 slice-done
  1.4 2.0 %gather_fusion = bf16[8,2,256,256]{3,2,1,0:T(8,128)(2,1)} fusion(bf16[6,2,256,256]{3,2,1,0:T(8,128)(2,1)S(1)} %slice-done, s32[1024]{0:T(1024)S(1)} %pad_clamp_fusion), kind=kCustom, calls=%fused_computation | custom fusion | bytes 4194336 | tf_op jit(solution)/shard_map/gather | solution.py:343
  3.5 7.4 %all-to-all-start = ((bf16[8,2,256,256]{3,2,1,0:T(8,128)(2,1)}), bf16[8,2,256,256]{3,2,1,0:T(8,128)(2,1)S(1)}, u32[]{:S(2)}, u32[]{:S(2)}) async-start(bf16[8,2,256,256]{3,2,1,0:T(8,128)(2,1)} %gather_fusion), calls=%async_computation | async-start | bytes 4194304 | tf_op jit(solution)/shard_map/all_to_all | solution.py:343
  10.9 0.6 dynamic_slice.23.counts_ref
  11.5 25.2 %shard_map.46 = (bf16[6,2,256,256]{3,2,1,0:T(8,128)(2,1)}, bf16[6,256,1536]{2,1,0:T(8,128)(2,1)}) custom-call(s32[6]{0:T(128)} %dynamic_slice.23.counts_ref, bf16[6,5,256,256]{3,2,1,0:T(8,128)(2,1)} %tiles_ref.1), custom_call_target="tpu_custom_call" | custom-call | flops 40000000000 | bytes 8000000 | tf_op jit(solution)/shard_map/pallas_call | solution.py:349
  36.8 1.7 %collective-permute-start.1 = (bf16[4,1536]{1,0:T(4,128)(2,1)S(1)}, bf16[4,1536]{1,0:T(4,128)(2,1)S(1)}, u32[]{:S(2)}, u32[]{:S(2)}) collective-permute-start(bf16[4,1536]{1,0:T(4,128)(2,1)S(1)} %get-tuple-element.29), channel_id=1, source_target_pairs={{0,2},{1,3},{2,0},{3,1},{4,6},{5,7},{6,4},{7,5},{8,10},{9,11},{10,... | collective-permute-start | bytes 36872 | tf_op jit(solution)/shard_map/ppermute | solution.py:341
  38.4 1.3 %collective-permute-start = (bf16[4,1536]{1,0:T(4,128)(2,1)S(1)}, bf16[4,1536]{1,0:T(4,128)(2,1)S(1)}, u32[]{:S(2)}, u32[]{:S(2)}) collective-permute-start(bf16[4,1536]{1,0:T(4,128)(2,1)S(1)} %get-tuple-element.30), channel_id=1, source_target_pairs={{0,3},{1,0},{2,1},{3,2},{4,7},{5,4},{6,5},{7,6},{8,11},{9,8},{10,9... | collective-permute-start | bytes 36872 | tf_op jit(solution)/shard_map/ppermute | solution.py:341
  39.7 0.7 pad_add_fusion.1.place_ref
  40.5 0.6 collective-permute-done
  41.1 0.7 pad_maximum_fusion.x_ref
  41.8 6.0 %shard_map.47 = (f32[6,16,256]{2,1,0:T(8,128)}, bf16[6,48,512]{2,1,0:T(8,128)(2,1)}) custom-call(bf16[16,1536]{1,0:T(8,128)(2,1)} %pad_maximum_fusion.x_ref, bf16[6,256,1536]{2,1,0:T(8,128)(2,1)} %get-tuple-element.18.z_any), custom_call_target="tpu_custom_call" | custom-call | flops 5000000000 | bytes 8000000 | tf_op jit(solution)/shard_map/pallas_call | solution.py:371
  47.8 11.3 %all-to-all-done.got_ref = bf16[8,2,256,256]{3,2,1,0:T(8,128)(2,1)S(1)} async-done(((bf16[8,2,256,256]{3,2,1,0:T(8,128)(2,1)}), bf16[8,2,256,256]{3,2,1,0:T(8,128)(2,1)S(1)}, u32[]{:S(2)}, u32[]{:S(2)}) %all-to-all-start) | async-done | bytes 2097184 | tf_op jit(solution)/shard_map/all_to_all | solution.py:343
  59.1 1.4 %copy-done = bf16[8,2,256,256]{3,2,1,0:T(8,128)(2,1)} copy-done((bf16[8,2,256,256]{3,2,1,0:T(8,128)(2,1)}, bf16[8,2,256,256]{3,2,1,0:T(8,128)(2,1)S(1)}, u32[]{:S(2)}) %copy-start) | copy-done | bytes 2097176
  60.5 27.4 %shard_map.48 = (f32[6,4,256]{2,1,0:T(4,128)}, f32[6,4,256]{2,1,0:T(4,128)}, f32[6,4,256]{2,1,0:T(4,128)}, f32[6,4,256]{2,1,0:T(4,128)}, bf16[32,4,256]{2,1,0:T(4,128)(2,1)}) custom-call(s32[7]{0:T(128)} %pad_add_fusion.1.place_ref, f32[6,16,256]{2,1,0:T(8,128)} %get-tuple-element.19.first_ref, bf16[6,48,512]{2,1,0:T(8,128)(2,1)} %get-tuple-element.20.rhs_ref, ...), custom_call_target="tpu_custom_call" | custom-call | tf_op jit(solution)/shard_map/pallas_call | solution.py:385
  87.9 3.7 %all-to-all-start.1 = ((bf16[32,4,256]{2,1,0:T(4,128)(2,1)}), bf16[32,4,256]{2,1,0:T(4,128)(2,1)S(1)}, u32[]{:S(2)}, u32[]{:S(2)}) async-start(bf16[32,4,256]{2,1,0:T(4,128)(2,1)} %get-tuple-element.22), calls=%async_computation.1 | async-start | bytes 131072 | tf_op jit(solution)/shard_map/all_to_all | solution.py:401
  91.9 1.7 %collective-permute-start.4 = (f32[6,4,256]{2,1,0:T(4,128)}, f32[6,4,256]{2,1,0:T(4,128)S(1)}, u32[]{:S(2)}, u32[]{:S(2)}) collective-permute-start(f32[6,4,256]{2,1,0:T(4,128)} %get-tuple-element.25), channel_id=1, source_target_pairs={{0,2},{1,3},{2,0},{3,1},{4,6},{5,7},{6,4},{7,5},{8,10},{9,11},{10,... | collective-permute-start | bytes 73736 | tf_op jit(solution)/shard_map/ppermute | solution.py:341
  93.5 1.3 %collective-permute-start.5 = (f32[6,4,256]{2,1,0:T(4,128)}, f32[6,4,256]{2,1,0:T(4,128)S(1)}, u32[]{:S(2)}, u32[]{:S(2)}) collective-permute-start(f32[6,4,256]{2,1,0:T(4,128)} %get-tuple-element.26), channel_id=1, source_target_pairs={{0,3},{1,0},{2,1},{3,2},{4,7},{5,4},{6,5},{7,6},{8,11},{9,8},{10,9... | collective-permute-start | bytes 73736 | tf_op jit(solution)/shard_map/ppermute | solution.py:341
  94.9 0.6 pad_add_fusion.place_ref
  95.5 0.4 collective-permute-done.4.refs_2_
  95.9 0.7 collective-permute-done.5.refs_3_
  96.6 2.4 %all-to-all-done.1.low_ref = bf16[32,4,256]{2,1,0:T(4,128)(2,1)S(1)} async-done(((bf16[32,4,256]{2,1,0:T(4,128)(2,1)}), bf16[32,4,256]{2,1,0:T(4,128)(2,1)S(1)}, u32[]{:S(2)}, u32[]{:S(2)}) %all-to-all-start.1) | async-done | bytes 65568 | tf_op jit(solution)/shard_map/all_to_all | solution.py:401
  99.0 0.6 copy-done.1
  99.6 1.6 %shard_map.49 = bf16[4,6144]{1,0:T(4,128)(2,1)} custom-call(s32[25]{0:T(128)} %pad_add_fusion.place_ref, bf16[32,4,256]{2,1,0:T(4,128)(2,1)} %copy-done.1, f32[6,4,256]{2,1,0:T(4,128)} %get-tuple-element.23.refs_0_, f32[6,4,256]{2,1,0:T(4,128)} %copy-done.3, f32[6,4,256]{2,1,0:T(4,128)} %copy-done.4, f32[6,4,256]{2,1,0:T(4,128)} %copy-done.5), custom_call_target="tpu_custom_call" | custom-call | tf_op jit(solution)/shard_map/pallas_call | solution.py:403
  (23 shorter events, 0.8 us)
Async XLA Ops:
  0.0 1.4 %slice-start = ((bf16[6,5,256,256]{3,2,1,0:T(8,128)(2,1)}), bf16[6,2,256,256]{3,2,1,0:T(8,128)(2,1)S(1)}, s32[]{:S(2)}) async-start(bf16[6,5,256,256]{3,2,1,0:T(8,128)(2,1)} %tiles_ref.1), calls=%async_computation.2 | async-start | bytes 3145728 | tf_op jit(solution)/shard_map/slice | solution.py:343
  3.5 7.4 %copy-start.6 = (s32[192]{0:T(256)S(1)}, s32[192]{0:T(256)}, u32[]{:S(2)}) copy-start(s32[192]{0:T(256)} %param.6) | copy-start | bytes 2308
  3.5 55.7 %all-to-all-start = ((bf16[8,2,256,256]{3,2,1,0:T(8,128)(2,1)}), bf16[8,2,256,256]{3,2,1,0:T(8,128)(2,1)S(1)}, u32[]{:S(2)}, u32[]{:S(2)}) async-start(bf16[8,2,256,256]{3,2,1,0:T(8,128)(2,1)} %gather_fusion), calls=%async_computation | async-start | bytes 4194304 | tf_op jit(solution)/shard_map/all_to_all | solution.py:343
  11.5 25.2 %copy-start.2 = (bf16[4,6144]{1,0:T(4,128)(2,1)S(1)}, bf16[4,6144]{1,0:T(4,128)(2,1)}, u32[]{:S(2)}) copy-start(bf16[4,6144]{1,0:T(4,128)(2,1)} %param.7) | copy-start | bytes 147460
  36.7 3.7 %collective-permute-start.2 = (bf16[4,1536]{1,0:T(4,128)(2,1)S(1)}, bf16[4,1536]{1,0:T(4,128)(2,1)S(1)}, u32[]{:S(2)}, u32[]{:S(2)}) collective-permute-start(bf16[4,1536]{1,0:T(4,128)(2,1)S(1)} %get-tuple-element.28), channel_id=1, source_target_pairs={{0,1},{1,2},{2,3},{3,0},{4,5},{5,6},{6,7},{7,4},{8,9},{9,10},{10,1... | collective-permute-start | bytes 36872 | tf_op jit(solution)/shard_map/ppermute | solution.py:341
  36.8 3.8 %collective-permute-start.1 = (bf16[4,1536]{1,0:T(4,128)(2,1)S(1)}, bf16[4,1536]{1,0:T(4,128)(2,1)S(1)}, u32[]{:S(2)}, u32[]{:S(2)}) collective-permute-start(bf16[4,1536]{1,0:T(4,128)(2,1)S(1)} %get-tuple-element.29), channel_id=1, source_target_pairs={{0,2},{1,3},{2,0},{3,1},{4,6},{5,7},{6,4},{7,5},{8,10},{9,11},{10,... | collective-permute-start | bytes 36872 | tf_op jit(solution)/shard_map/ppermute | solution.py:341
  38.4 2.7 %collective-permute-start = (bf16[4,1536]{1,0:T(4,128)(2,1)S(1)}, bf16[4,1536]{1,0:T(4,128)(2,1)S(1)}, u32[]{:S(2)}, u32[]{:S(2)}) collective-permute-start(bf16[4,1536]{1,0:T(4,128)(2,1)S(1)} %get-tuple-element.30), channel_id=1, source_target_pairs={{0,3},{1,0},{2,1},{3,2},{4,7},{5,4},{6,5},{7,6},{8,11},{9,8},{10,9... | collective-permute-start | bytes 36872 | tf_op jit(solution)/shard_map/ppermute | solution.py:341
  59.1 1.4 %copy-start = (bf16[8,2,256,256]{3,2,1,0:T(8,128)(2,1)}, bf16[8,2,256,256]{3,2,1,0:T(8,128)(2,1)S(1)}, u32[]{:S(2)}) copy-start(bf16[8,2,256,256]{3,2,1,0:T(8,128)(2,1)S(1)} %all-to-all-done.got_ref) | copy-start | bytes 6291460
  87.9 11.1 %all-to-all-start.1 = ((bf16[32,4,256]{2,1,0:T(4,128)(2,1)}), bf16[32,4,256]{2,1,0:T(4,128)(2,1)S(1)}, u32[]{:S(2)}, u32[]{:S(2)}) async-start(bf16[32,4,256]{2,1,0:T(4,128)(2,1)} %get-tuple-element.22), calls=%async_computation.1 | async-start | bytes 131072 | tf_op jit(solution)/shard_map/all_to_all | solution.py:401
  91.6 3.9 %collective-permute-start.3 = (f32[6,4,256]{2,1,0:T(4,128)}, f32[6,4,256]{2,1,0:T(4,128)S(1)}, u32[]{:S(2)}, u32[]{:S(2)}) collective-permute-start(f32[6,4,256]{2,1,0:T(4,128)} %get-tuple-element.24), channel_id=1, source_target_pairs={{0,1},{1,2},{2,3},{3,0},{4,5},{5,6},{6,7},{7,4},{8,9},{9,10},{10,1... | collective-permute-start | bytes 73736 | tf_op jit(solution)/shard_map/ppermute | solution.py:341
  91.9 4.0 %collective-permute-start.4 = (f32[6,4,256]{2,1,0:T(4,128)}, f32[6,4,256]{2,1,0:T(4,128)S(1)}, u32[]{:S(2)}, u32[]{:S(2)}) collective-permute-start(f32[6,4,256]{2,1,0:T(4,128)} %get-tuple-element.25), channel_id=1, source_target_pairs={{0,2},{1,3},{2,0},{3,1},{4,6},{5,7},{6,4},{7,5},{8,10},{9,11},{10,... | collective-permute-start | bytes 73736 | tf_op jit(solution)/shard_map/ppermute | solution.py:341
  93.5 3.1 %collective-permute-start.5 = (f32[6,4,256]{2,1,0:T(4,128)}, f32[6,4,256]{2,1,0:T(4,128)S(1)}, u32[]{:S(2)}, u32[]{:S(2)}) collective-permute-start(f32[6,4,256]{2,1,0:T(4,128)} %get-tuple-element.26), channel_id=1, source_target_pairs={{0,3},{1,0},{2,1},{3,2},{4,7},{5,4},{6,5},{7,6},{8,11},{9,8},{10,9... | collective-permute-start | bytes 73736 | tf_op jit(solution)/shard_map/ppermute | solution.py:341
  95.5 3.5 %copy-start.3 = (f32[6,4,256]{2,1,0:T(4,128)}, f32[6,4,256]{2,1,0:T(4,128)S(1)}, u32[]{:S(2)}) copy-start(f32[6,4,256]{2,1,0:T(4,128)S(1)} %collective-permute-done.3.refs_1_) | copy-start | bytes 73732
  95.9 3.1 %copy-start.4 = (f32[6,4,256]{2,1,0:T(4,128)}, f32[6,4,256]{2,1,0:T(4,128)S(1)}, u32[]{:S(2)}) copy-start(f32[6,4,256]{2,1,0:T(4,128)S(1)} %collective-permute-done.4.refs_2_) | copy-start | bytes 73732
  96.6 2.4 %copy-start.5 = (f32[6,4,256]{2,1,0:T(4,128)}, f32[6,4,256]{2,1,0:T(4,128)S(1)}, u32[]{:S(2)}) copy-start(f32[6,4,256]{2,1,0:T(4,128)S(1)} %collective-permute-done.5.refs_3_) | copy-start | bytes 73732
  98.9 0.6 copy-start.1

commit v15 on v13

--- a/solution.py
+++ b/solution.py
@@ -7,6 +7,7 @@
 from jax.sharding import PartitionSpec as P
 
 STEP = 32
+ROUND = 8
 NT = (((1,), (1,)), ((), ()))
 NN = (((1,), (0,)), ((), ()))
 TN = (((0,), (0,)), ((), ()))
@@ -84,45 +85,45 @@
 
     def pivots(packs, pieces):
         placed = 0
-        for first in range(0, STEP, 4):
+        for first in range(0, STEP, ROUND):
             top, start = first // 8, first % 8
             tall = range(top, groups)
-            own = (place >= first) & (place < first + 4)
+            own = (place >= first) & (place < first + ROUND)
             one = jnp.where(place - 8 * top == sub, 1.0, 0.0)
             each = range(len(packs))
             if start == 0:
                 inverses = [None for _ in each]
             u = [
-                [{g: jnp.take_along_axis(x[g], lane - place + (first + q), axis=1) for g in tall} for q in range(4)]
+                [{g: jnp.take_along_axis(x[g], lane - place + (first + q), axis=1) for g in tall} for q in range(ROUND)]
                 for x in packs
             ]
-            a = [{(i, j): spread(u[s][j][top][start + i:start + i + 1, :]) for j in range(4) for i in range(j + 1)} for s in each]
+            a = [{(i, j): spread(u[s][j][top][start + i:start + i + 1, :]) for j in range(ROUND) for i in range(j + 1)} for s in each]
             for x in packs:
                 for g in tall:
                     x[g] = jnp.where(own, one if g == top else 0.0, x[g])
-            y = [[spread(x[top][start + q:start + q + 1, :]) for q in range(4)] for x in packs]
+            y = [[spread(x[top][start + q:start + q + 1, :]) for q in range(ROUND)] for x in packs]
             low = [{} for _ in each]
-            inv = [[None] * 4 for _ in each]
-            for p in (0, 2):
+            inv = [[None] * ROUND for _ in each]
+            for p in range(0, ROUND, 2):
                 n = p + 1
                 delta = [a[s][p, p] * a[s][n, n] - a[s][p, n] * a[s][p, n] for s in each]
                 for s in each:
                     inv[s][p] = pl.reciprocal(a[s][p, p], approx=True)
                     inv[s][n] = pl.reciprocal(delta[s], approx=True) * a[s][p, p]
-                for j in range(n, 4):
+                for j in range(n, ROUND):
                     for s in each:
                         low[s][j, p] = a[s][p, j] * inv[s][p]
-                for j in range(n + 1, 4):
+                for j in range(n + 1, ROUND):
                     for s in each:
                         a[s][n, j] = a[s][n, j] - low[s][n, p] * a[s][p, j]
-                for j in range(n + 1, 4):
+                for j in range(n + 1, ROUND):
                     for s in each:
                         low[s][j, n] = a[s][n, j] * inv[s][n]
-                for i in range(n + 1, 4):
-                    for j in range(i, 4):
+                for i in range(n + 1, ROUND):
+                    for j in range(i, ROUND):
                         for s in each:
                             a[s][i, j] = (a[s][i, j] - low[s][i, p] * a[s][p, j]) - low[s][i, n] * a[s][n, j]
-            for q in range(4):
+            for q in range(ROUND):
                 at = start + q
                 for s in each:
                     for k in range(q):
@@ -138,7 +139,7 @@
                 while placed * STEP < (first + q + 1) * len(pieces):
                     pieces[placed]()
                     placed += 1
-            if start + 4 == 8:
+            if start + ROUND == 8:
                 for s, x in enumerate(packs):
                     x[top] = x[top] * (inverses[s] * lax.rsqrt(inverses[s]))
 

time: 101 us -> 98.9 us (0.979)
  Pallas kernels: 59.9 us -> 53.9 us
  waiting for transfers between devices: 15.3 us -> 19.2 us
    all_to_all x1, waiting for transfers between devices: 11.1 us -> 15 us  [on_device(): lax.all_to_all(tiles[:, :2][slot_of], 'panel', split_axis=0, concat_axis=...]
    pallas_call x1, Pallas kernels: 25.2 us -> 21.5 us  [on_device(): pl.pallas_call(own_kernel, out_shape=(jax.ShapeDtypeStruct((systems, 2, w...]
    pallas_call x1, Pallas kernels: 27.2 us -> 24.8 us  [on_device(): pl.pallas_call(functools.partial(pair_kernel, lanes), out_shape=[piece] *...]
  transfers between devices with their start and end apart: 8 -> 8, of which waited for: 5 -> 5; matrix products, arithmetic and copies ran while one was open for 3% -> 3% of each run, Pallas kernels for 31% -> 28%
where the time goes in v15:
time: 98.9 us; the launch traced here: 98.5 us
  Pallas kernels  53.9 us (54%)
  waiting for transfers between devices  19.2 us (19%)
  starting transfers between devices  17.4 us (18%)
  local copies, waits for them, and re-layouts  5.01 us (5%)
  other arithmetic  2.95 us (3%)
    pallas_call x1, Pallas kernels, on_device(): pl.pallas_call(functools.partial(pair_kernel, lanes), out_shape=[piece] *...  24.8 us
    pallas_call x1, Pallas kernels, on_device(): pl.pallas_call(own_kernel, out_shape=(jax.ShapeDtypeStruct((systems, 2, w...  21.5 us
    all_to_all x1, waiting for transfers between devices, on_device(): lax.all_to_all(tiles[:, :2][slot_of], 'panel', split_axis=0, concat_axis=...  15 us
    all_to_all x1, starting transfers between devices, on_device(): lax.all_to_all(tiles[:, :2][slot_of], 'panel', split_axis=0, concat_axis=...  7.41 us
    ppermute x6, starting transfers between devices, shift(): lax.ppermute(value, 'rhs', [(i, (i + by) % lanes) for i in range(lanes)])  6.31 us
    pallas_call x1, Pallas kernels, on_device(): pl.pallas_call(ready_kernel, out_shape=(rows, jax.ShapeDtypeStruct((syste...  6.04 us
    all_to_all x1, starting transfers between devices, on_device(): lax.all_to_all(low, ('panel', 'rhs'), split_axis=0, concat_axis=0, tiled=...  3.66 us
    all_to_all x1, waiting for transfers between devices, on_device(): lax.all_to_all(low, ('panel', 'rhs'), split_axis=0, concat_axis=0, tiled=...  2.36 us
  transfers between devices with their start and end apart: 8, of which 5 were waited for; matrix products, arithmetic and copies ran while one was open for 3% of the time, Pallas kernels for 28%

profile of v15, /device:TPU:0, one launch (start us, length us, event | category | flops | bytes accessed | tf_op | source)
XLA Modules:
  0.0 98.5 jit_solution(6857701054305081355)
XLA Ops:
  0.0 0.9 bitcast_select_fusion
  1.4 2.0 %gather_fusion = bf16[8,2,256,256]{3,2,1,0:T(8,128)(2,1)} fusion(bf16[6,2,256,256]{3,2,1,0:T(8,128)(2,1)S(1)} %slice-done, s32[1024]{0:T(1024)S(1)} %pad_clamp_fusion), kind=kCustom, calls=%fused_computation | custom fusion | bytes 4194336 | tf_op jit(solution)/shard_map/gather | solution.py:344
  3.5 7.4 %all-to-all-start = ((bf16[8,2,256,256]{3,2,1,0:T(8,128)(2,1)}), bf16[8,2,256,256]{3,2,1,0:T(8,128)(2,1)S(1)}, u32[]{:S(2)}, u32[]{:S(2)}) async-start(bf16[8,2,256,256]{3,2,1,0:T(8,128)(2,1)} %gather_fusion), calls=%async_computation | async-start | bytes 4194304 | tf_op jit(solution)/shard_map/all_to_all | solution.py:344
  10.9 0.6 dynamic_slice.23.counts_ref
  11.5 21.5 %shard_map.46 = (bf16[6,2,256,256]{3,2,1,0:T(8,128)(2,1)}, bf16[6,256,1536]{2,1,0:T(8,128)(2,1)}) custom-call(s32[6]{0:T(128)} %dynamic_slice.23.counts_ref, bf16[6,5,256,256]{3,2,1,0:T(8,128)(2,1)} %tiles_ref.1), custom_call_target="tpu_custom_call" | custom-call | flops 40000000000 | bytes 8000000 | tf_op jit(solution)/shard_map/pallas_call | solution.py:350
  33.0 0.6 collective-permute-start.2
  33.7 1.0 %collective-permute-start.1 = (bf16[4,1536]{1,0:T(4,128)(2,1)S(1)}, bf16[4,1536]{1,0:T(4,128)(2,1)S(1)}, u32[]{:S(2)}, u32[]{:S(2)}) collective-permute-start(bf16[4,1536]{1,0:T(4,128)(2,1)S(1)} %get-tuple-element.29), channel_id=1, source_target_pairs={{0,2},{1,3},{2,0},{3,1},{4,6},{5,7},{6,4},{7,5},{8,10},{9,11},{10,... | collective-permute-start | bytes 36872 | tf_op jit(solution)/shard_map/ppermute | solution.py:342
  34.7 1.4 %collective-permute-start = (bf16[4,1536]{1,0:T(4,128)(2,1)S(1)}, bf16[4,1536]{1,0:T(4,128)(2,1)S(1)}, u32[]{:S(2)}, u32[]{:S(2)}) collective-permute-start(bf16[4,1536]{1,0:T(4,128)(2,1)S(1)} %get-tuple-element.30), channel_id=1, source_target_pairs={{0,3},{1,0},{2,1},{3,2},{4,7},{5,4},{6,5},{7,6},{8,11},{9,8},{10,9... | collective-permute-start | bytes 36872 | tf_op jit(solution)/shard_map/ppermute | solution.py:342
  36.0 0.7 pad_add_fusion.1.place_ref
  36.7 0.7 collective-permute-done.1
  37.4 0.7 pad_maximum_fusion.x_ref
  38.1 6.0 %shard_map.47 = (f32[6,16,256]{2,1,0:T(8,128)}, bf16[6,48,512]{2,1,0:T(8,128)(2,1)}) custom-call(bf16[16,1536]{1,0:T(8,128)(2,1)} %pad_maximum_fusion.x_ref, bf16[6,256,1536]{2,1,0:T(8,128)(2,1)} %get-tuple-element.18.z_any), custom_call_target="tpu_custom_call" | custom-call | flops 5000000000 | bytes 8000000 | tf_op jit(solution)/shard_map/pallas_call | solution.py:372
  44.1 15.0 %all-to-all-done.got_ref = bf16[8,2,256,256]{3,2,1,0:T(8,128)(2,1)S(1)} async-done(((bf16[8,2,256,256]{3,2,1,0:T(8,128)(2,1)}), bf16[8,2,256,256]{3,2,1,0:T(8,128)(2,1)S(1)}, u32[]{:S(2)}, u32[]{:S(2)}) %all-to-all-start) | async-done | bytes 2097184 | tf_op jit(solution)/shard_map/all_to_all | solution.py:344
  59.1 1.4 %copy-done = bf16[8,2,256,256]{3,2,1,0:T(8,128)(2,1)} copy-done((bf16[8,2,256,256]{3,2,1,0:T(8,128)(2,1)}, bf16[8,2,256,256]{3,2,1,0:T(8,128)(2,1)S(1)}, u32[]{:S(2)}) %copy-start) | copy-done | bytes 2097176
  60.5 24.8 %shard_map.48 = (f32[6,4,256]{2,1,0:T(4,128)}, f32[6,4,256]{2,1,0:T(4,128)}, f32[6,4,256]{2,1,0:T(4,128)}, f32[6,4,256]{2,1,0:T(4,128)}, bf16[32,4,256]{2,1,0:T(4,128)(2,1)}) custom-call(s32[7]{0:T(128)} %pad_add_fusion.1.place_ref, f32[6,16,256]{2,1,0:T(8,128)} %get-tuple-element.19.first_ref, bf16[6,48,512]{2,1,0:T(8,128)(2,1)} %get-tuple-element.20.rhs_ref, ...), custom_call_target="tpu_custom_call" | custom-call | tf_op jit(solution)/shard_map/pallas_call | solution.py:386
  85.3 3.7 %all-to-all-start.1 = ((bf16[32,4,256]{2,1,0:T(4,128)(2,1)}), bf16[32,4,256]{2,1,0:T(4,128)(2,1)S(1)}, u32[]{:S(2)}, u32[]{:S(2)}) async-start(bf16[32,4,256]{2,1,0:T(4,128)(2,1)} %get-tuple-element.22), calls=%async_computation.1 | async-start | bytes 131072 | tf_op jit(solution)/shard_map/all_to_all | solution.py:402
  89.2 1.7 %collective-permute-start.4 = (f32[6,4,256]{2,1,0:T(4,128)}, f32[6,4,256]{2,1,0:T(4,128)S(1)}, u32[]{:S(2)}, u32[]{:S(2)}) collective-permute-start(f32[6,4,256]{2,1,0:T(4,128)} %get-tuple-element.25), channel_id=1, source_target_pairs={{0,2},{1,3},{2,0},{3,1},{4,6},{5,7},{6,4},{7,5},{8,10},{9,11},{10,... | collective-permute-start | bytes 73736 | tf_op jit(solution)/shard_map/ppermute | solution.py:342
  90.9 1.3 %collective-permute-start.5 = (f32[6,4,256]{2,1,0:T(4,128)}, f32[6,4,256]{2,1,0:T(4,128)S(1)}, u32[]{:S(2)}, u32[]{:S(2)}) collective-permute-start(f32[6,4,256]{2,1,0:T(4,128)} %get-tuple-element.26), channel_id=1, source_target_pairs={{0,3},{1,0},{2,1},{3,2},{4,7},{5,4},{6,5},{7,6},{8,11},{9,8},{10,9... | collective-permute-start | bytes 73736 | tf_op jit(solution)/shard_map/ppermute | solution.py:342
  92.2 0.6 pad_add_fusion.place_ref
  92.9 0.4 collective-permute-done.4.refs_2_
  93.3 0.7 collective-permute-done.5.refs_3_
  94.0 2.4 %all-to-all-done.1.low_ref = bf16[32,4,256]{2,1,0:T(4,128)(2,1)S(1)} async-done(((bf16[32,4,256]{2,1,0:T(4,128)(2,1)}), bf16[32,4,256]{2,1,0:T(4,128)(2,1)S(1)}, u32[]{:S(2)}, u32[]{:S(2)}) %all-to-all-start.1) | async-done | bytes 65568 | tf_op jit(solution)/shard_map/all_to_all | solution.py:402
  96.4 0.6 copy-done.1
  97.0 1.6 %shard_map.49 = bf16[4,6144]{1,0:T(4,128)(2,1)} custom-call(s32[25]{0:T(128)} %pad_add_fusion.place_ref, bf16[32,4,256]{2,1,0:T(4,128)(2,1)} %copy-done.1, f32[6,4,256]{2,1,0:T(4,128)} %get-tuple-element.23.refs_0_, f32[6,4,256]{2,1,0:T(4,128)} %copy-done.3, f32[6,4,256]{2,1,0:T(4,128)} %copy-done.4, f32[6,4,256]{2,1,0:T(4,128)} %copy-done.5), custom_call_target="tpu_custom_call" | custom-call | tf_op jit(solution)/shard_map/pallas_call | solution.py:404
  (23 shorter events, 0.9 us)
Async XLA Ops:
  0.0 1.4 %slice-start = ((bf16[6,5,256,256]{3,2,1,0:T(8,128)(2,1)}), bf16[6,2,256,256]{3,2,1,0:T(8,128)(2,1)S(1)}, s32[]{:S(2)}) async-start(bf16[6,5,256,256]{3,2,1,0:T(8,128)(2,1)} %tiles_ref.1), calls=%async_computation.2 | async-start | bytes 3145728 | tf_op jit(solution)/shard_map/slice | solution.py:344
  3.5 7.4 %copy-start.6 = (s32[192]{0:T(256)S(1)}, s32[192]{0:T(256)}, u32[]{:S(2)}) copy-start(s32[192]{0:T(256)} %param.6) | copy-start | bytes 2308
  3.5 55.7 %all-to-all-start = ((bf16[8,2,256,256]{3,2,1,0:T(8,128)(2,1)}), bf16[8,2,256,256]{3,2,1,0:T(8,128)(2,1)S(1)}, u32[]{:S(2)}, u32[]{:S(2)}) async-start(bf16[8,2,256,256]{3,2,1,0:T(8,128)(2,1)} %gather_fusion), calls=%async_computation | async-start | bytes 4194304 | tf_op jit(solution)/shard_map/all_to_all | solution.py:344
  11.5 21.5 %copy-start.2 = (bf16[4,6144]{1,0:T(4,128)(2,1)S(1)}, bf16[4,6144]{1,0:T(4,128)(2,1)}, u32[]{:S(2)}) copy-start(bf16[4,6144]{1,0:T(4,128)(2,1)} %param.7) | copy-start | bytes 147460
  33.0 3.7 %collective-permute-start.2 = (bf16[4,1536]{1,0:T(4,128)(2,1)S(1)}, bf16[4,1536]{1,0:T(4,128)(2,1)S(1)}, u32[]{:S(2)}, u32[]{:S(2)}) collective-permute-start(bf16[4,1536]{1,0:T(4,128)(2,1)S(1)} %get-tuple-element.28), channel_id=1, source_target_pairs={{0,1},{1,2},{2,3},{3,0},{4,5},{5,6},{6,7},{7,4},{8,9},{9,10},{10,1... | collective-permute-start | bytes 36872 | tf_op jit(solution)/shard_map/ppermute | solution.py:342
  33.7 3.8 %collective-permute-start.1 = (bf16[4,1536]{1,0:T(4,128)(2,1)S(1)}, bf16[4,1536]{1,0:T(4,128)(2,1)S(1)}, u32[]{:S(2)}, u32[]{:S(2)}) collective-permute-start(bf16[4,1536]{1,0:T(4,128)(2,1)S(1)} %get-tuple-element.29), channel_id=1, source_target_pairs={{0,2},{1,3},{2,0},{3,1},{4,6},{5,7},{6,4},{7,5},{8,10},{9,11},{10,... | collective-permute-start | bytes 36872 | tf_op jit(solution)/shard_map/ppermute | solution.py:342
  34.7 2.8 %collective-permute-start = (bf16[4,1536]{1,0:T(4,128)(2,1)S(1)}, bf16[4,1536]{1,0:T(4,128)(2,1)S(1)}, u32[]{:S(2)}, u32[]{:S(2)}) collective-permute-start(bf16[4,1536]{1,0:T(4,128)(2,1)S(1)} %get-tuple-element.30), channel_id=1, source_target_pairs={{0,3},{1,0},{2,1},{3,2},{4,7},{5,4},{6,5},{7,6},{8,11},{9,8},{10,9... | collective-permute-start | bytes 36872 | tf_op jit(solution)/shard_map/ppermute | solution.py:342
  59.1 1.4 %copy-start = (bf16[8,2,256,256]{3,2,1,0:T(8,128)(2,1)}, bf16[8,2,256,256]{3,2,1,0:T(8,128)(2,1)S(1)}, u32[]{:S(2)}) copy-start(bf16[8,2,256,256]{3,2,1,0:T(8,128)(2,1)S(1)} %all-to-all-done.got_ref) | copy-start | bytes 6291460
  85.3 11.1 %all-to-all-start.1 = ((bf16[32,4,256]{2,1,0:T(4,128)(2,1)}), bf16[32,4,256]{2,1,0:T(4,128)(2,1)S(1)}, u32[]{:S(2)}, u32[]{:S(2)}) async-start(bf16[32,4,256]{2,1,0:T(4,128)(2,1)} %get-tuple-element.22), calls=%async_computation.1 | async-start | bytes 131072 | tf_op jit(solution)/shard_map/all_to_all | solution.py:402
  88.9 3.9 %collective-permute-start.3 = (f32[6,4,256]{2,1,0:T(4,128)}, f32[6,4,256]{2,1,0:T(4,128)S(1)}, u32[]{:S(2)}, u32[]{:S(2)}) collective-permute-start(f32[6,4,256]{2,1,0:T(4,128)} %get-tuple-element.24), channel_id=1, source_target_pairs={{0,1},{1,2},{2,3},{3,0},{4,5},{5,6},{6,7},{7,4},{8,9},{9,10},{10,1... | collective-permute-start | bytes 73736 | tf_op jit(solution)/shard_map/ppermute | solution.py:342
  89.2 4.0 %collective-permute-start.4 = (f32[6,4,256]{2,1,0:T(4,128)}, f32[6,4,256]{2,1,0:T(4,128)S(1)}, u32[]{:S(2)}, u32[]{:S(2)}) collective-permute-start(f32[6,4,256]{2,1,0:T(4,128)} %get-tuple-element.25), channel_id=1, source_target_pairs={{0,2},{1,3},{2,0},{3,1},{4,6},{5,7},{6,4},{7,5},{8,10},{9,11},{10,... | collective-permute-start | bytes 73736 | tf_op jit(solution)/shard_map/ppermute | solution.py:342
  90.9 3.1 %collective-permute-start.5 = (f32[6,4,256]{2,1,0:T(4,128)}, f32[6,4,256]{2,1,0:T(4,128)S(1)}, u32[]{:S(2)}, u32[]{:S(2)}) collective-permute-start(f32[6,4,256]{2,1,0:T(4,128)} %get-tuple-element.26), channel_id=1, source_target_pairs={{0,3},{1,0},{2,1},{3,2},{4,7},{5,4},{6,5},{7,6},{8,11},{9,8},{10,9... | collective-permute-start | bytes 73736 | tf_op jit(solution)/shard_map/ppermute | solution.py:342
  92.9 3.5 %copy-start.3 = (f32[6,4,256]{2,1,0:T(4,128)}, f32[6,4,256]{2,1,0:T(4,128)S(1)}, u32[]{:S(2)}) copy-start(f32[6,4,256]{2,1,0:T(4,128)S(1)} %collective-permute-done.3.refs_1_) | copy-start | bytes 73732
  93.3 3.1 %copy-start.4 = (f32[6,4,256]{2,1,0:T(4,128)}, f32[6,4,256]{2,1,0:T(4,128)S(1)}, u32[]{:S(2)}) copy-start(f32[6,4,256]{2,1,0:T(4,128)S(1)} %collective-permute-done.4.refs_2_) | copy-start | bytes 73732
  94.0 2.4 %copy-start.5 = (f32[6,4,256]{2,1,0:T(4,128)}, f32[6,4,256]{2,1,0:T(4,128)S(1)}, u32[]{:S(2)}) copy-start(f32[6,4,256]{2,1,0:T(4,128)S(1)} %collective-permute-done.5.refs_3_) | copy-start | bytes 73732
  96.3 0.6 copy-start.1

commit v16 on v10

--- a/solution.py
+++ b/solution.py
@@ -7,6 +7,7 @@
 from jax.sharding import PartitionSpec as P
 
 STEP = 32
+ROUND = 8
 NT = (((1,), (1,)), ((), ()))
 NN = (((1,), (0,)), ((), ()))
 TN = (((0,), (0,)), ((), ()))
@@ -84,45 +85,45 @@
 
     def pivots(packs, pieces):
         placed = 0
-        for first in range(0, STEP, 4):
+        for first in range(0, STEP, ROUND):
             top, start = first // 8, first % 8
             tall = range(top, groups)
-            own = (place >= first) & (place < first + 4)
+            own = (place >= first) & (place < first + ROUND)
             one = jnp.where(place - 8 * top == sub, 1.0, 0.0)
             each = range(len(packs))
             if start == 0:
                 inverses = [None for _ in each]
             u = [
-                [{g: jnp.take_along_axis(x[g], lane - place + (first + q), axis=1) for g in tall} for q in range(4)]
+                [{g: jnp.take_along_axis(x[g], lane - place + (first + q), axis=1) for g in tall} for q in range(ROUND)]
                 for x in packs
             ]
-            a = [{(i, j): spread(u[s][j][top][start + i:start + i + 1, :]) for j in range(4) for i in range(j + 1)} for s in each]
+            a = [{(i, j): spread(u[s][j][top][start + i:start + i + 1, :]) for j in range(ROUND) for i in range(j + 1)} for s in each]
             for x in packs:
                 for g in tall:
                     x[g] = jnp.where(own, one if g == top else 0.0, x[g])
-            y = [[spread(x[top][start + q:start + q + 1, :]) for q in range(4)] for x in packs]
+            y = [[spread(x[top][start + q:start + q + 1, :]) for q in range(ROUND)] for x in packs]
             low = [{} for _ in each]
-            inv = [[None] * 4 for _ in each]
-            for p in (0, 2):
+            inv = [[None] * ROUND for _ in each]
+            for p in range(0, ROUND, 2):
                 n = p + 1
                 delta = [a[s][p, p] * a[s][n, n] - a[s][p, n] * a[s][p, n] for s in each]
                 for s in each:
                     inv[s][p] = pl.reciprocal(a[s][p, p], approx=True)
                     inv[s][n] = pl.reciprocal(delta[s], approx=True) * a[s][p, p]
-                for j in range(n, 4):
+                for j in range(n, ROUND):
                     for s in each:
                         low[s][j, p] = a[s][p, j] * inv[s][p]
-                for j in range(n + 1, 4):
+                for j in range(n + 1, ROUND):
                     for s in each:
                         a[s][n, j] = a[s][n, j] - low[s][n, p] * a[s][p, j]
-                for j in range(n + 1, 4):
+                for j in range(n + 1, ROUND):
                     for s in each:
                         low[s][j, n] = a[s][n, j] * inv[s][n]
-                for i in range(n + 1, 4):
-                    for j in range(i, 4):
+                for i in range(n + 1, ROUND):
+                    for j in range(i, ROUND):
                         for s in each:
                             a[s][i, j] = (a[s][i, j] - low[s][i, p] * a[s][p, j]) - low[s][i, n] * a[s][n, j]
-            for q in range(4):
+            for q in range(ROUND):
                 at = start + q
                 for s in each:
                     for k in range(q):
@@ -138,7 +139,7 @@
                 while placed * STEP < (first + q + 1) * len(pieces):
                     pieces[placed]()
                     placed += 1
-            if start + 4 == 8:
+            if start + ROUND == 8:
                 for s, x in enumerate(packs):
                     x[top] = x[top] * (inverses[s] * lax.rsqrt(inverses[s]))
 
@@ -391,14 +392,15 @@
     pairs = shards - 1
     every = tuple(range(1, shards))
     late = (1, shards - 1)
-    early = tuple(e for e in every if e not in late)
+    early = tuple(sorted((e for e in every if e not in late), key=lambda e: abs(2 * e - shards)))
+    most = pltpu.CompilerParams(vmem_limit_bytes=60 * 1024 * 1024)
     pieces = pl.pallas_call(
         pick_kernel,
         out_shape=[jax.ShapeDtypeStruct((2, width, width), jnp.bfloat16)] * pairs,
         in_specs=[smem, anywhere],
         out_specs=[vmem] * pairs,
         scratch_shapes=[pltpu.SemaphoreType.DMA((pairs,))],
-        compiler_params=params,
+        compiler_params=most,
     )(slots((my_panel + hops) % shards), tiles)
     received = {e: shift(pieces[e - 1], "panel", e) for e in early}
 

time: 100 us -> 101 us (1.010)
  starting transfers between devices: 25.1 us -> 33.1 us
  Pallas kernels: 57.4 us -> 52.3 us
  local copies, waits for them, and re-layouts: 6.78 us -> 4.68 us
    all_to_all x1, starting transfers between devices: 2.81 us -> 9.1 us  [on_device(): lax.all_to_all(low, ('panel', 'rhs'), split_axis=0, concat_axis=0, tiled=...]
    pallas_call x1, Pallas kernels: 22.8 us -> 18.4 us  [on_device(): pl.pallas_call(own_kernel, out_shape=(jax.ShapeDtypeStruct((systems, 2, w...]
    pallas_call x1, Pallas kernels: 22.6 us -> 20.2 us  [on_device(): pl.pallas_call(functools.partial(pair_kernel, lanes, every, late), out_sh...]
    unnamed x18 -> x20, local copies, waits for them, and re-layouts: 6.61 us -> 4.51 us
    pallas_call x1, Pallas kernels: 1.84 us -> 3.56 us  [on_device(): pl.pallas_call(pick_kernel, out_shape=[jax.ShapeDtypeStruct((2, width, wi...]
    ppermute x10, starting transfers between devices: 19.1 us -> 20.4 us  [shift(): lax.ppermute(value, axis, [(i, (i + by) % size) for i in range(size)])]
  transfers between devices with their start and end apart: 12 -> 12, of which waited for: 5 -> 5; matrix products, arithmetic and copies ran while one was open for 1% -> 1% of each run, Pallas kernels for 31% -> 27%
where the time goes in v16:
time: 101 us
  Pallas kernels  52.3 us (52%)
  starting transfers between devices  33.1 us (33%)
  waiting for transfers between devices  8.69 us (9%)
  local copies, waits for them, and re-layouts  4.68 us (5%)
  other arithmetic  2.28 us (2%)
    ppermute x10, starting transfers between devices, shift(): lax.ppermute(value, axis, [(i, (i + by) % size) for i in range(size)])  20.4 us
    pallas_call x1, Pallas kernels, on_device(): pl.pallas_call(functools.partial(pair_kernel, lanes, every, late), out_sh...  20.2 us
    pallas_call x1, Pallas kernels, on_device(): pl.pallas_call(own_kernel, out_shape=(jax.ShapeDtypeStruct((systems, 2, w...  18.4 us
    all_to_all x1, starting transfers between devices, on_device(): lax.all_to_all(low, ('panel', 'rhs'), split_axis=0, concat_axis=0, tiled=...  9.1 us
    pallas_call x1, Pallas kernels, on_device(): pl.pallas_call(functools.partial(link_kernel, early), out_shape=(jax.Shap...  8.58 us
    unnamed x20, local copies, waits for them, and re-layouts  4.51 us
    all_to_all x1, waiting for transfers between devices, on_device(): x = lax.all_to_all(inputs, 'rhs', split_axis=1, concat_axis=0, tiled=True)  3.96 us
    all_to_all x1, starting transfers between devices, on_device(): x = lax.all_to_all(inputs, 'rhs', split_axis=1, concat_axis=0, tiled=True)  3.63 us
  transfers between devices with their start and end apart: 12, of which 5 were waited for; matrix products, arithmetic and copies ran while one was open for 1% of the time, Pallas kernels for 27%

profile of v16, /device:TPU:0, one launch (start us, length us, event | category | flops | bytes accessed | tf_op | source)
XLA Modules:
  0.0 101.3 jit_solution(2183591079233109142)
XLA Ops:
  0.0 0.8 bitcast_select_fusion
  0.9 0.7 select_reduce_fusion
  1.6 3.6 %shard_map.47 = (bf16[2,256,256]{2,1,0:T(8,128)(2,1)}, bf16[2,256,256]{2,1,0:T(8,128)(2,1)}, bf16[2,256,256]{2,1,0:T(8,128)(2,1)}, bf16[2,256,256]{2,1,0:T(8,128...) custom-call(s32[7]{0:T(128)} %get-tuple-element.57.slot_ref, ...), custom_call_target="tpu_custom_call" | custom-call | tf_op jit(solution)/shard_map/pallas_call | solution.py:397
  5.2 4.1 %collective-permute-start = (bf16[2,256,256]{2,1,0:T(8,128)(2,1)}, bf16[2,256,256]{2,1,0:T(8,128)(2,1)S(1)}, u32[]{:S(2)}, u32[]{:S(2)}) collective-permute-start(bf16[2,256,256]{2,1,0:T(8,128)(2,1)} %get-tuple-element.37), channel_id=1, source_target_pairs={{0,16},{4,20},{8,24},{12,28},{16,0},{20,4},{24,8},{28,12},{1,17},{... | collective-permute-start | bytes 786440 | tf_op jit(solution)/shard_map/ppermute | solution.py:386
  9.3 2.5 %collective-permute-start.1 = (bf16[2,256,256]{2,1,0:T(8,128)(2,1)}, bf16[2,256,256]{2,1,0:T(8,128)(2,1)S(1)}, u32[]{:S(2)}, u32[]{:S(2)}) collective-permute-start(bf16[2,256,256]{2,1,0:T(8,128)(2,1)} %get-tuple-element.38), channel_id=1, source_target_pairs={{0,12},{4,16},{8,20},{12,24},{16,28},{20,0},{24,4},{28,8},{1,13},{... | collective-permute-start | bytes 786440 | tf_op jit(solution)/shard_map/ppermute | solution.py:386
  11.8 1.3 %collective-permute-start.2 = (bf16[2,256,256]{2,1,0:T(8,128)(2,1)}, bf16[2,256,256]{2,1,0:T(8,128)(2,1)S(1)}, u32[]{:S(2)}, u32[]{:S(2)}) collective-permute-start(bf16[2,256,256]{2,1,0:T(8,128)(2,1)} %get-tuple-element.39), channel_id=1, source_target_pairs={{0,20},{4,24},{8,28},{12,0},{16,4},{20,8},{24,12},{28,16},{1,21},{... | collective-permute-start | bytes 786440 | tf_op jit(solution)/shard_map/ppermute | solution.py:386
  13.1 1.6 %collective-permute-start.3 = (bf16[2,256,256]{2,1,0:T(8,128)(2,1)}, bf16[2,256,256]{2,1,0:T(8,128)(2,1)S(1)}, u32[]{:S(2)}, u32[]{:S(2)}) collective-permute-start(bf16[2,256,256]{2,1,0:T(8,128)(2,1)} %get-tuple-element.40), channel_id=1, source_target_pairs={{0,8},{4,12},{8,16},{12,20},{16,24},{20,28},{24,0},{28,4},{1,9},{5... | collective-permute-start | bytes 786440 | tf_op jit(solution)/shard_map/ppermute | solution.py:386
  14.6 2.3 %collective-permute-start.4 = (bf16[2,256,256]{2,1,0:T(8,128)(2,1)}, bf16[2,256,256]{2,1,0:T(8,128)(2,1)S(1)}, u32[]{:S(2)}, u32[]{:S(2)}) collective-permute-start(bf16[2,256,256]{2,1,0:T(8,128)(2,1)} %get-tuple-element.41), channel_id=1, source_target_pairs={{0,24},{4,28},{8,0},{12,4},{16,8},{20,12},{24,16},{28,20},{1,25},{... | collective-permute-start | bytes 786440 | tf_op jit(solution)/shard_map/ppermute | solution.py:386
  17.0 2.1 %copy-done = bf16[6,5,256,256]{3,2,1,0:T(8,128)(2,1)S(1)} copy-done((bf16[6,5,256,256]{3,2,1,0:T(8,128)(2,1)S(1)}, bf16[6,5,256,256]{3,2,1,0:T(8,128)(2,1)}, u32[]{:S(2)}) %copy-start) | copy-done | bytes 3932184
  19.1 18.4 %shard_map.46 = (bf16[6,2,256,256]{3,2,1,0:T(8,128)(2,1)S(1)}, bf16[6,3,256,512]{3,2,1,0:T(8,128)(2,1)}) custom-call(s32[6]{0:T(128)S(1)} %dynamic_slice.14.counts_ref, bf16[6,5,256,256]{3,2,1,0:T(8,128)(2,1)S(1)} %copy-done), custom_call_target="tpu_custom_call" | custom-call | flops 30000001024 | bytes 8000000 | tf_op jit(solution)/shard_map/pallas_call | solution.py:407
  37.5 3.6 %all-to-all-start = ((bf16[4,4,1536]{2,0,1:T(4,128)(2,1)}), bf16[4,4,1536]{2,0,1:T(4,128)(2,1)S(1)}, u32[]{:S(2)}, u32[]{:S(2)}) async-start(bf16[4,4,1536]{2,0,1:T(4,128)(2,1)} %bitcast.3), calls=%async_computation | async-start | bytes 98304 | tf_op jit(solution)/shard_map/all_to_all | solution.py:421
  41.2 4.0 %all-to-all-done = bf16[4,4,1536]{2,0,1:T(4,128)(2,1)S(1)} async-done(((bf16[4,4,1536]{2,0,1:T(4,128)(2,1)}), bf16[4,4,1536]{2,0,1:T(4,128)(2,1)S(1)}, u32[]{:S(2)}, u32[]{:S(2)}) %all-to-all-start) | async-done | bytes 49184 | tf_op jit(solution)/shard_map/all_to_all | solution.py:421
  45.3 5.4 %collective-permute-start.5 = (bf16[2,256,256]{2,1,0:T(8,128)(2,1)S(1)}, bf16[2,256,256]{2,1,0:T(8,128)(2,1)S(1)}, u32[]{:S(2)}, u32[]{:S(2)}) collective-permute-start(bf16[2,256,256]{2,1,0:T(8,128)(2,1)S(1)} %copy-done.8), channel_id=1, source_target_pairs={{0,4},{4,8},{8,12},{12,16},{16,20},{20,24},{24,28},{28,0},{1,5},{5... | collective-permute-start | bytes 786440 | tf_op jit(solution)/shard_map/ppermute | solution.py:386
  50.7 8.6 %shard_map.48 = (bf16[6,2,256,256]{3,2,1,0:T(8,128)(2,1)S(1)}, f32[6,256,256]{2,1,0:T(8,128)S(1)}) custom-call(s32[7]{0:T(128)S(1)} %get-tuple-element.58.slot_ref, bf16[6,3,256,512]{3,2,1,0:T(8,128)(2,1)} %get-tuple-element.42.z_any, bf16[2,256,256]{2,1,0:T(8,128)(2,1)S(1)} %collective-permute-done.refs_0_.refs_3_, ...), custom_call_target="tpu_custom_call" | custom-call | flops 12000000000 | bytes 8000000 | tf_op jit(solution)/shard_map/pallas_call | solution.py:429
  59.3 1.2 %copy-done.1 = f32[6,256,256]{2,1,0:T(8,128)} copy-done((f32[6,256,256]{2,1,0:T(8,128)}, f32[6,256,256]{2,1,0:T(8,128)S(1)}, u32[]{:S(2)}) %copy-start.1) | copy-done | bytes 1572888
  60.5 1.3 %collective-permute-done.5.refs_0_ = bf16[2,256,256]{2,1,0:T(8,128)(2,1)S(1)} collective-permute-done((bf16[2,256,256]{2,1,0:T(8,128)(2,1)S(1)}, bf16[2,256,256]{2,1,0:T(8,128)(2,1)S(1)}, u32[]{:S(2)}, u32[]{:S(2)}) %collective-permute-start.5) | collective-permute-done | bytes 262176 | tf_op jit(solution)/shard_map/ppermute | solution.py:386
  61.7 20.2 %shard_map.49 = (f32[6,4,256]{2,1,0:T(4,128)S(1)}, f32[6,4,256]{2,1,0:T(4,128)S(1)}, f32[6,4,256]{2,1,0:T(4,128)S(1)}, f32[6,4,256]{2,1,0:T(4,128)S(1)}, bf16[32,4,256]{2,1,0:T(4,128)(2,1)}) custom-call(s32[7]{0:T(128)S(1)} %pad_add_fusion.1.place_ref, s32[7]{0:T(128)S(1)} %get-tuple-element.58.slot_ref, bf16[16,1536]{1,0:T(8,128)(2,1)S(1)} %fusion.x_ref, ...), custom_call_target="tpu_custom_call" | custom-call | tf_op jit(solution)/shard_map/pallas_call | solution.py:449
  82.5 9.1 %all-to-all-start.1 = ((bf16[32,4,256]{2,1,0:T(4,128)(2,1)}), bf16[32,4,256]{2,1,0:T(4,128)(2,1)S(1)}, u32[]{:S(2)}, u32[]{:S(2)}) async-start(bf16[32,4,256]{2,1,0:T(4,128)(2,1)} %get-tuple-element.52), calls=%async_computation.1 | async-start | bytes 131072 | tf_op jit(solution)/shard_map/all_to_all | solution.py:471
  91.9 1.7 %collective-permute-start.8 = (f32[6,4,256]{2,1,0:T(4,128)S(1)}, f32[6,4,256]{2,1,0:T(4,128)S(1)}, u32[]{:S(2)}, u32[]{:S(2)}) collective-permute-start(f32[6,4,256]{2,1,0:T(4,128)S(1)} %get-tuple-element.55), channel_id=1, source_target_pairs={{0,2},{1,3},{2,0},{3,1},{4,6},{5,7},{6,4},{7,5},{8,10},{9,11},{10,... | collective-permute-start | bytes 73736 | tf_op jit(solution)/shard_map/ppermute | solution.py:386
  93.6 1.3 %collective-permute-start.9 = (f32[6,4,256]{2,1,0:T(4,128)S(1)}, f32[6,4,256]{2,1,0:T(4,128)S(1)}, u32[]{:S(2)}, u32[]{:S(2)}) collective-permute-start(f32[6,4,256]{2,1,0:T(4,128)S(1)} %get-tuple-element.56), channel_id=1, source_target_pairs={{0,3},{1,0},{2,1},{3,2},{4,7},{5,4},{6,5},{7,6},{8,11},{9,8},{10,9... | collective-permute-start | bytes 73736 | tf_op jit(solution)/shard_map/ppermute | solution.py:386
  94.9 0.6 pad_add_fusion.place_ref
  95.8 0.6 collective-permute-done.9.refs_3_
  96.5 2.6 %all-to-all-done.1.low_ref = bf16[32,4,256]{2,1,0:T(4,128)(2,1)S(1)} async-done(((bf16[32,4,256]{2,1,0:T(4,128)(2,1)}), bf16[32,4,256]{2,1,0:T(4,128)(2,1)S(1)}, u32[]{:S(2)}, u32[]{:S(2)}) %all-to-all-start.1) | async-done | bytes 65568 | tf_op jit(solution)/shard_map/all_to_all | solution.py:471
  99.7 1.6 %shard_map.50 = bf16[4,6144]{1,0:T(4,128)(2,1)} custom-call(s32[25]{0:T(128)} %pad_add_fusion.place_ref, bf16[32,4,256]{2,1,0:T(4,128)(2,1)} %copy-done.3, f32[6,4,256]{2,1,0:T(4,128)} %copy-done.2, f32[6,4,256]{2,1,0:T(4,128)} %copy-done.4, f32[6,4,256]{2,1,0:T(4,128)} %copy-done.5, f32[6,4,256]{2,1,0:T(4,128)} %copy-done.6), custom_call_target="tpu_custom_call" | custom-call | tf_op jit(solution)/shard_map/pallas_call | solution.py:473
  (34 shorter events, 2.1 us)
Async XLA Ops:
  1.6 15.3 %copy-start.9 = (s32[192]{0:T(256)S(1)}, s32[192]{0:T(256)}, u32[]{:S(2)}) copy-start(s32[192]{0:T(256)} %param.6) | copy-start | bytes 2308
  5.2 40.1 %collective-permute-start = (bf16[2,256,256]{2,1,0:T(8,128)(2,1)}, bf16[2,256,256]{2,1,0:T(8,128)(2,1)S(1)}, u32[]{:S(2)}, u32[]{:S(2)}) collective-permute-start(bf16[2,256,256]{2,1,0:T(8,128)(2,1)} %get-tuple-element.37), channel_id=1, source_target_pairs={{0,16},{4,20},{8,24},{12,28},{16,0},{20,4},{24,8},{28,12},{1,17},{... | collective-permute-start | bytes 786440 | tf_op jit(solution)/shard_map/ppermute | solution.py:386
  9.3 36.0 %collective-permute-start.1 = (bf16[2,256,256]{2,1,0:T(8,128)(2,1)}, bf16[2,256,256]{2,1,0:T(8,128)(2,1)S(1)}, u32[]{:S(2)}, u32[]{:S(2)}) collective-permute-start(bf16[2,256,256]{2,1,0:T(8,128)(2,1)} %get-tuple-element.38), channel_id=1, source_target_pairs={{0,12},{4,16},{8,20},{12,24},{16,28},{20,0},{24,4},{28,8},{1,13},{... | collective-permute-start | bytes 786440 | tf_op jit(solution)/shard_map/ppermute | solution.py:386
  11.8 33.5 %collective-permute-start.2 = (bf16[2,256,256]{2,1,0:T(8,128)(2,1)}, bf16[2,256,256]{2,1,0:T(8,128)(2,1)S(1)}, u32[]{:S(2)}, u32[]{:S(2)}) collective-permute-start(bf16[2,256,256]{2,1,0:T(8,128)(2,1)} %get-tuple-element.39), channel_id=1, source_target_pairs={{0,20},{4,24},{8,28},{12,0},{16,4},{20,8},{24,12},{28,16},{1,21},{... | collective-permute-start | bytes 786440 | tf_op jit(solution)/shard_map/ppermute | solution.py:386
  13.1 32.2 %collective-permute-start.3 = (bf16[2,256,256]{2,1,0:T(8,128)(2,1)}, bf16[2,256,256]{2,1,0:T(8,128)(2,1)S(1)}, u32[]{:S(2)}, u32[]{:S(2)}) collective-permute-start(bf16[2,256,256]{2,1,0:T(8,128)(2,1)} %get-tuple-element.40), channel_id=1, source_target_pairs={{0,8},{4,12},{8,16},{12,20},{16,24},{20,28},{24,0},{28,4},{1,9},{5... | collective-permute-start | bytes 786440 | tf_op jit(solution)/shard_map/ppermute | solution.py:386
  14.6 30.7 %collective-permute-start.4 = (bf16[2,256,256]{2,1,0:T(8,128)(2,1)}, bf16[2,256,256]{2,1,0:T(8,128)(2,1)S(1)}, u32[]{:S(2)}, u32[]{:S(2)}) collective-permute-start(bf16[2,256,256]{2,1,0:T(8,128)(2,1)} %get-tuple-element.41), channel_id=1, source_target_pairs={{0,24},{4,28},{8,0},{12,4},{16,8},{20,12},{24,16},{28,20},{1,25},{... | collective-permute-start | bytes 786440 | tf_op jit(solution)/shard_map/ppermute | solution.py:386
  17.0 2.1 %copy-start = (bf16[6,5,256,256]{3,2,1,0:T(8,128)(2,1)S(1)}, bf16[6,5,256,256]{3,2,1,0:T(8,128)(2,1)}, u32[]{:S(2)}) copy-start(bf16[6,5,256,256]{3,2,1,0:T(8,128)(2,1)} %tiles_ref.3) | copy-start | bytes 11796484
  19.1 26.2 %copy-start.8 = (bf16[2,256,256]{2,1,0:T(8,128)(2,1)S(1)}, bf16[2,256,256]{2,1,0:T(8,128)(2,1)}, u32[]{:S(2)}) copy-start(bf16[2,256,256]{2,1,0:T(8,128)(2,1)} %get-tuple-element.50) | copy-start | bytes 786436
  19.1 31.6 %copy-start.7 = (bf16[2,256,256]{2,1,0:T(8,128)(2,1)S(1)}, bf16[2,256,256]{2,1,0:T(8,128)(2,1)}, u32[]{:S(2)}) copy-start(bf16[2,256,256]{2,1,0:T(8,128)(2,1)} %get-tuple-element.51) | copy-start | bytes 786436
  37.5 7.7 %all-to-all-start = ((bf16[4,4,1536]{2,0,1:T(4,128)(2,1)}), bf16[4,4,1536]{2,0,1:T(4,128)(2,1)S(1)}, u32[]{:S(2)}, u32[]{:S(2)}) async-start(bf16[4,4,1536]{2,0,1:T(4,128)(2,1)} %bitcast.3), calls=%async_computation | async-start | bytes 98304 | tf_op jit(solution)/shard_map/all_to_all | solution.py:421
  45.3 16.4 %collective-permute-start.5 = (bf16[2,256,256]{2,1,0:T(8,128)(2,1)S(1)}, bf16[2,256,256]{2,1,0:T(8,128)(2,1)S(1)}, u32[]{:S(2)}, u32[]{:S(2)}) collective-permute-start(bf16[2,256,256]{2,1,0:T(8,128)(2,1)S(1)} %copy-done.8), channel_id=1, source_target_pairs={{0,4},{4,8},{8,12},{12,16},{16,20},{20,24},{24,28},{28,0},{1,5},{5... | collective-permute-start | bytes 786440 | tf_op jit(solution)/shard_map/ppermute | solution.py:386
  50.7 11.0 %collective-permute-start.6 = (bf16[2,256,256]{2,1,0:T(8,128)(2,1)S(1)}, bf16[2,256,256]{2,1,0:T(8,128)(2,1)S(1)}, u32[]{:S(2)}, u32[]{:S(2)}) collective-permute-start(bf16[2,256,256]{2,1,0:T(8,128)(2,1)S(1)} %copy-done.7), channel_id=1, source_target_pairs={{0,28},{4,0},{8,4},{12,8},{16,12},{20,16},{24,20},{28,24},{1,29},{... | collective-permute-start | bytes 786440 | tf_op jit(solution)/shard_map/ppermute | solution.py:386
  59.3 1.2 %copy-start.1 = (f32[6,256,256]{2,1,0:T(8,128)}, f32[6,256,256]{2,1,0:T(8,128)S(1)}, u32[]{:S(2)}) copy-start(f32[6,256,256]{2,1,0:T(8,128)S(1)} %get-tuple-element.49.t_any) | copy-start | bytes 4718596
  81.9 0.6 copy-start.2
  82.5 16.5 %all-to-all-start.1 = ((bf16[32,4,256]{2,1,0:T(4,128)(2,1)}), bf16[32,4,256]{2,1,0:T(4,128)(2,1)S(1)}, u32[]{:S(2)}, u32[]{:S(2)}) async-start(bf16[32,4,256]{2,1,0:T(4,128)(2,1)} %get-tuple-element.52), calls=%async_computation.1 | async-start | bytes 131072 | tf_op jit(solution)/shard_map/all_to_all | solution.py:471
  91.6 4.0 %collective-permute-start.7 = (f32[6,4,256]{2,1,0:T(4,128)S(1)}, f32[6,4,256]{2,1,0:T(4,128)S(1)}, u32[]{:S(2)}, u32[]{:S(2)}) collective-permute-start(f32[6,4,256]{2,1,0:T(4,128)S(1)} %get-tuple-element.54), channel_id=1, source_target_pairs={{0,1},{1,2},{2,3},{3,0},{4,5},{5,6},{6,7},{7,4},{8,9},{9,10},{10,1... | collective-permute-start | bytes 73736 | tf_op jit(solution)/shard_map/ppermute | solution.py:386
  91.9 3.9 %collective-permute-start.8 = (f32[6,4,256]{2,1,0:T(4,128)S(1)}, f32[6,4,256]{2,1,0:T(4,128)S(1)}, u32[]{:S(2)}, u32[]{:S(2)}) collective-permute-start(f32[6,4,256]{2,1,0:T(4,128)S(1)} %get-tuple-element.55), channel_id=1, source_target_pairs={{0,2},{1,3},{2,0},{3,1},{4,6},{5,7},{6,4},{7,5},{8,10},{9,11},{10,... | collective-permute-start | bytes 73736 | tf_op jit(solution)/shard_map/ppermute | solution.py:386
  93.6 2.9 %collective-permute-start.9 = (f32[6,4,256]{2,1,0:T(4,128)S(1)}, f32[6,4,256]{2,1,0:T(4,128)S(1)}, u32[]{:S(2)}, u32[]{:S(2)}) collective-permute-start(f32[6,4,256]{2,1,0:T(4,128)S(1)} %get-tuple-element.56), channel_id=1, source_target_pairs={{0,3},{1,0},{2,1},{3,2},{4,7},{5,4},{6,5},{7,6},{8,11},{9,8},{10,9... | collective-permute-start | bytes 73736 | tf_op jit(solution)/shard_map/ppermute | solution.py:386
  95.6 3.5 %copy-start.4 = (f32[6,4,256]{2,1,0:T(4,128)}, f32[6,4,256]{2,1,0:T(4,128)S(1)}, u32[]{:S(2)}) copy-start(f32[6,4,256]{2,1,0:T(4,128)S(1)} %collective-permute-done.7.refs_1_) | copy-start | bytes 73732
  95.8 3.2 %copy-start.5 = (f32[6,4,256]{2,1,0:T(4,128)}, f32[6,4,256]{2,1,0:T(4,128)S(1)}, u32[]{:S(2)}) copy-start(f32[6,4,256]{2,1,0:T(4,128)S(1)} %collective-permute-done.8.refs_2_) | copy-start | bytes 73732
  96.5 2.6 %copy-start.6 = (f32[6,4,256]{2,1,0:T(4,128)}, f32[6,4,256]{2,1,0:T(4,128)S(1)}, u32[]{:S(2)}) copy-start(f32[6,4,256]{2,1,0:T(4,128)S(1)} %collective-permute-done.9.refs_3_) | copy-start | bytes 73732
  99.0 0.6 copy-start.3

commit v17 on v16

--- a/solution.py
+++ b/solution.py
@@ -392,7 +392,7 @@
     pairs = shards - 1
     every = tuple(range(1, shards))
     late = (1, shards - 1)
-    early = tuple(sorted((e for e in every if e not in late), key=lambda e: abs(2 * e - shards)))
+    early = tuple(e for e in every if e not in late)
     most = pltpu.CompilerParams(vmem_limit_bytes=60 * 1024 * 1024)
     pieces = pl.pallas_call(
         pick_kernel,
@@ -417,14 +417,13 @@
         cost_estimate=pl.CostEstimate(flops=30 * 10**9, bytes_accessed=8 * 10**6, transcendentals=0),
     )(own_cnt, tiles)
 
-    inputs, w = lax.optimization_barrier((inputs, w))
+    come = [received[e] for e in early[:2]]
+    held, z, come, inputs = lax.optimization_barrier(([pieces[e - 1] for e in late], z, come, inputs))
+    received.update(zip(early, come))
+    received.update({e: shift(piece, "panel", e) for e, piece in zip(late, held)})
     x = lax.all_to_all(inputs, "rhs", split_axis=1, concat_axis=0, tiled=True)
     x = lax.dynamic_slice_in_dim(jnp.concatenate([x, x], axis=0), my_lane * nrhs_dev, lanes * nrhs_dev, 0)
 
-    come = [received[e] for e in early]
-    held, z, come = lax.optimization_barrier(([pieces[e - 1] for e in late], z, come))
-    received.update(zip(early, come))
-    received.update({e: shift(piece, "panel", e) for e, piece in zip(late, held)})
     from_slot = slots((my_panel - hops) % shards)
     v, t = pl.pallas_call(
         functools.partial(link_kernel, early),

time: 101 us -> 109 us (1.079)
  local copies, waits for them, and re-layouts: 4.68 us -> 15.2 us
  waiting for transfers between devices: 8.69 us -> 3.57 us
  starting transfers between devices: 33.1 us -> 35.4 us
    unnamed x20 -> x40, local copies, waits for them, and re-layouts: 4.51 us -> 15 us
    all_to_all x1, starting transfers between devices: 9.1 us -> 13.2 us  [on_device(): lax.all_to_all(low, ('panel', 'rhs'), split_axis=0, concat_axis=0, tiled=...]
    all_to_all x1, waiting for transfers between devices: 3.96 us -> 0.01 us  [on_device(): x = lax.all_to_all(inputs, 'rhs', split_axis=1, concat_axis=0, tiled=True)]
    ppermute x10, starting transfers between devices: 20.4 us -> 18.9 us  [shift(): lax.ppermute(value, axis, [(i, (i + by) % size) for i in range(size)])]
    ppermute x10, waiting for transfers between devices: 2.14 us -> 0.98 us  [shift(): lax.ppermute(value, axis, [(i, (i + by) % size) for i in range(size)])]
  transfers between devices with their start and end apart: 12 -> 12, of which waited for: 5 -> 3; matrix products, arithmetic and copies ran while one was open for 1% -> 1% of each run, Pallas kernels for 27% -> 25%
where the time goes in v17:
time: 109 us; the launch traced here: 110 us
  Pallas kernels  53.1 us (49%)
  starting transfers between devices  35.4 us (32%)
  local copies, waits for them, and re-layouts  15.2 us (14%)
  waiting for transfers between devices  3.57 us (3%)
  other arithmetic  2.2 us (2%)
    pallas_call x1, Pallas kernels, on_device(): pl.pallas_call(functools.partial(pair_kernel, lanes, every, late), out_sh...  20.3 us
    pallas_call x1, Pallas kernels, on_device(): pl.pallas_call(own_kernel, out_shape=(jax.ShapeDtypeStruct((systems, 2, w...  19.1 us
    ppermute x10, starting transfers between devices, shift(): lax.ppermute(value, axis, [(i, (i + by) % size) for i in range(size)])  18.9 us
    unnamed x40, local copies, waits for them, and re-layouts  15 us
    all_to_all x1, starting transfers between devices, on_device(): lax.all_to_all(low, ('panel', 'rhs'), split_axis=0, concat_axis=0, tiled=...  13.2 us
    pallas_call x1, Pallas kernels, on_device(): pl.pallas_call(functools.partial(link_kernel, early), out_shape=(jax.Shap...  8.58 us
    pallas_call x1, Pallas kernels, on_device(): pl.pallas_call(pick_kernel, out_shape=[jax.ShapeDtypeStruct((2, width, wi...  3.61 us
    all_to_all x1, starting transfers between devices, on_device(): x = lax.all_to_all(inputs, 'rhs', split_axis=1, concat_axis=0, tiled=True)  3.27 us
  transfers between devices with their start and end apart: 12, of which 3 were waited for; matrix products, arithmetic and copies ran while one was open for 1% of the time, Pallas kernels for 25%

profile of v17, /device:TPU:0, one launch (start us, length us, event | category | flops | bytes accessed | tf_op | source)
XLA Modules:
  0.0 109.5 jit_solution(7574695992255008450)
XLA Ops:
  1.6 3.6 %shard_map.46 = (bf16[2,256,256]{2,1,0:T(8,128)(2,1)}, bf16[2,256,256]{2,1,0:T(8,128)(2,1)}, bf16[2,256,256]{2,1,0:T(8,128)(2,1)}, bf16[2,256,256]{2,1,0:T(8,128...) custom-call(s32[7]{0:T(128)} %get-tuple-element.49.slot_ref, ...), custom_call_target="tpu_custom_call" | custom-call | tf_op jit(solution)/shard_map/pallas_call | solution.py:397
  5.2 3.1 %collective-permute-start = (bf16[2,256,256]{2,1,0:T(8,128)(2,1)}, bf16[2,256,256]{2,1,0:T(8,128)(2,1)S(1)}, u32[]{:S(2)}, u32[]{:S(2)}) collective-permute-start(bf16[2,256,256]{2,1,0:T(8,128)(2,1)} %get-tuple-element.30), channel_id=1, source_target_pairs={{0,8},{4,12},{8,16},{12,20},{16,24},{20,28},{24,0},{28,4},{1,9},{5... | collective-permute-start | bytes 786440 | tf_op jit(solution)/shard_map/ppermute | solution.py:386
  8.3 2.5 %collective-permute-start.1 = (bf16[2,256,256]{2,1,0:T(8,128)(2,1)}, bf16[2,256,256]{2,1,0:T(8,128)(2,1)S(1)}, u32[]{:S(2)}, u32[]{:S(2)}) collective-permute-start(bf16[2,256,256]{2,1,0:T(8,128)(2,1)} %get-tuple-element.31), channel_id=1, source_target_pairs={{0,12},{4,16},{8,20},{12,24},{16,28},{20,0},{24,4},{28,8},{1,13},{... | collective-permute-start | bytes 786440 | tf_op jit(solution)/shard_map/ppermute | solution.py:386
  10.8 1.2 %collective-permute-start.2 = (bf16[2,256,256]{2,1,0:T(8,128)(2,1)}, bf16[2,256,256]{2,1,0:T(8,128)(2,1)S(1)}, u32[]{:S(2)}, u32[]{:S(2)}) collective-permute-start(bf16[2,256,256]{2,1,0:T(8,128)(2,1)} %get-tuple-element.37), channel_id=1, source_target_pairs={{0,16},{4,20},{8,24},{12,28},{16,0},{20,4},{24,8},{28,12},{1,17},{... | collective-permute-start | bytes 786440 | tf_op jit(solution)/shard_map/ppermute | solution.py:386
  12.1 2.6 %collective-permute-start.3 = (bf16[2,256,256]{2,1,0:T(8,128)(2,1)}, bf16[2,256,256]{2,1,0:T(8,128)(2,1)S(1)}, u32[]{:S(2)}, u32[]{:S(2)}) collective-permute-start(bf16[2,256,256]{2,1,0:T(8,128)(2,1)} %get-tuple-element.38), channel_id=1, source_target_pairs={{0,20},{4,24},{8,28},{12,0},{16,4},{20,8},{24,12},{28,16},{1,21},{... | collective-permute-start | bytes 786440 | tf_op jit(solution)/shard_map/ppermute | solution.py:386
  14.7 1.4 %collective-permute-start.4 = (bf16[2,256,256]{2,1,0:T(8,128)(2,1)}, bf16[2,256,256]{2,1,0:T(8,128)(2,1)S(1)}, u32[]{:S(2)}, u32[]{:S(2)}) collective-permute-start(bf16[2,256,256]{2,1,0:T(8,128)(2,1)} %get-tuple-element.39), channel_id=1, source_target_pairs={{0,24},{4,28},{8,0},{12,4},{16,8},{20,12},{24,16},{28,20},{1,25},{... | collective-permute-start | bytes 786440 | tf_op jit(solution)/shard_map/ppermute | solution.py:386
  16.1 2.1 %copy-done = bf16[6,5,256,256]{3,2,1,0:T(8,128)(2,1)S(1)} copy-done((bf16[6,5,256,256]{3,2,1,0:T(8,128)(2,1)S(1)}, bf16[6,5,256,256]{3,2,1,0:T(8,128)(2,1)}, u32[]{:S(2)}) %copy-start) | copy-done | bytes 3932184
  18.2 19.1 %shard_map.47 = (bf16[6,2,256,256]{3,2,1,0:T(8,128)(2,1)S(1)}, bf16[6,3,256,512]{3,2,1,0:T(8,128)(2,1)}) custom-call(s32[6]{0:T(128)S(1)} %dynamic_slice.14.counts_ref, bf16[6,5,256,256]{3,2,1,0:T(8,128)(2,1)S(1)} %copy-done), custom_call_target="tpu_custom_call" | custom-call | flops 30000001024 | bytes 8000000 | tf_op jit(solution)/shard_map/pallas_call | solution.py:407
  38.1 3.3 %all-to-all-start = ((bf16[4,4,1536]{2,0,1:T(4,128)(2,1)}), bf16[4,4,1536]{2,0,1:T(4,128)(2,1)S(1)}, u32[]{:S(2)}, u32[]{:S(2)}) async-start(bf16[4,4,1536]{2,0,1:T(4,128)(2,1)} %bitcast.3), calls=%async_computation | async-start | bytes 98304 | tf_op jit(solution)/shard_map/all_to_all | solution.py:424
  41.4 4.7 %collective-permute-start.6 = (bf16[2,256,256]{2,1,0:T(8,128)(2,1)}, bf16[2,256,256]{2,1,0:T(8,128)(2,1)}, u32[]{:S(2)}, u32[]{:S(2)}) collective-permute-start(bf16[2,256,256]{2,1,0:T(8,128)(2,1)} %get-tuple-element.43), channel_id=1, source_target_pairs={{0,28},{4,0},{8,4},{12,8},{16,12},{20,16},{24,20},{28,24},{1,29},{... | collective-permute-start | bytes 786440 | tf_op jit(solution)/shard_map/ppermute | solution.py:386
  48.3 0.9 copy-done.3
  49.3 0.9 copy-done.6
  50.2 0.9 copy-done.9
  51.2 0.9 copy-done.12
  52.1 8.6 %shard_map.48 = (bf16[6,2,256,256]{3,2,1,0:T(8,128)(2,1)S(1)}, f32[6,256,256]{2,1,0:T(8,128)S(1)}) custom-call(s32[7]{0:T(128)S(1)} %get-tuple-element.50.slot_ref, bf16[6,3,256,512]{3,2,1,0:T(8,128)(2,1)} %get-tuple-element.34.z_any, bf16[2,256,256]{2,1,0:T(8,128)(2,1)S(1)} %collective-permute-done.refs_0_.refs_1_, bf16[2,256,256]{2,1,0:T(8,128)(2,1)S(1)} %copy-done.3, ...), custom_call_target="tpu_custom_call" | custom-call | flops 12000000000 | bytes 8000000 | tf_op jit(solution)/shard_map/pallas_call | solution.py:428
  60.7 1.2 %copy-done.1 = f32[6,256,256]{2,1,0:T(8,128)} copy-done((f32[6,256,256]{2,1,0:T(8,128)}, f32[6,256,256]{2,1,0:T(8,128)S(1)}, u32[]{:S(2)}) %copy-start.1) | copy-done | bytes 1572888
  63.0 0.9 copy-done.7
  64.0 0.9 copy-done.10
  65.9 20.3 %shard_map.49 = (f32[6,4,256]{2,1,0:T(4,128)S(1)}, f32[6,4,256]{2,1,0:T(4,128)S(1)}, f32[6,4,256]{2,1,0:T(4,128)S(1)}, f32[6,4,256]{2,1,0:T(4,128)S(1)}, bf16[32,4,256]{2,1,0:T(4,128)(2,1)}) custom-call(s32[7]{0:T(128)S(1)} %pad_add_fusion.1.place_ref, s32[7]{0:T(128)S(1)} %get-tuple-element.50.slot_ref, bf16[16,1536]{1,0:T(8,128)(2,1)S(1)} %fusion.x_ref, ...), custom_call_target="tpu_custom_call" | custom-call | tf_op jit(solution)/shard_map/pallas_call | solution.py:448
  86.7 13.2 %all-to-all-start.1 = ((bf16[32,4,256]{2,1,0:T(4,128)(2,1)}), bf16[32,4,256]{2,1,0:T(4,128)(2,1)S(1)}, u32[]{:S(2)}, u32[]{:S(2)}) async-start(bf16[32,4,256]{2,1,0:T(4,128)(2,1)} %get-tuple-element.44), calls=%async_computation.1 | async-start | bytes 131072 | tf_op jit(solution)/shard_map/all_to_all | solution.py:470
  100.2 1.7 %collective-permute-start.8 = (f32[6,4,256]{2,1,0:T(4,128)S(1)}, f32[6,4,256]{2,1,0:T(4,128)S(1)}, u32[]{:S(2)}, u32[]{:S(2)}) collective-permute-start(f32[6,4,256]{2,1,0:T(4,128)S(1)} %get-tuple-element.47), channel_id=1, source_target_pairs={{0,2},{1,3},{2,0},{3,1},{4,6},{5,7},{6,4},{7,5},{8,10},{9,11},{10,... | collective-permute-start | bytes 73736 | tf_op jit(solution)/shard_map/ppermute | solution.py:386
  101.9 1.3 %collective-permute-start.9 = (f32[6,4,256]{2,1,0:T(4,128)S(1)}, f32[6,4,256]{2,1,0:T(4,128)S(1)}, u32[]{:S(2)}, u32[]{:S(2)}) collective-permute-start(f32[6,4,256]{2,1,0:T(4,128)S(1)} %get-tuple-element.48), channel_id=1, source_target_pairs={{0,3},{1,0},{2,1},{3,2},{4,7},{5,4},{6,5},{7,6},{8,11},{9,8},{10,9... | collective-permute-start | bytes 73736 | tf_op jit(solution)/shard_map/ppermute | solution.py:386
  104.7 2.6 %all-to-all-done.1.low_ref = bf16[32,4,256]{2,1,0:T(4,128)(2,1)S(1)} async-done(((bf16[32,4,256]{2,1,0:T(4,128)(2,1)}), bf16[32,4,256]{2,1,0:T(4,128)(2,1)S(1)}, u32[]{:S(2)}, u32[]{:S(2)}) %all-to-all-start.1) | async-done | bytes 65568 | tf_op jit(solution)/shard_map/all_to_all | solution.py:470
  107.9 1.6 %shard_map.50 = bf16[4,6144]{1,0:T(4,128)(2,1)} custom-call(s32[25]{0:T(128)} %pad_add_fusion.place_ref, bf16[32,4,256]{2,1,0:T(4,128)(2,1)} %copy-done.15, f32[6,4,256]{2,1,0:T(4,128)} %copy-done.14, f32[6,4,256]{2,1,0:T(4,128)} %copy-done.16, f32[6,4,256]{2,1,0:T(4,128)} %copy-done.17, f32[6,4,256]{2,1,0:T(4,128)} %copy-done.18), custom_call_target="tpu_custom_call" | custom-call | tf_op jit(solution)/shard_map/pallas_call | solution.py:472
  (54 shorter events, 9.7 us)
Async XLA Ops:
  1.6 14.5 %copy-start.19 = (s32[192]{0:T(256)S(1)}, s32[192]{0:T(256)}, u32[]{:S(2)}) copy-start(s32[192]{0:T(256)} %param.6) | copy-start | bytes 2308
  5.2 32.2 %collective-permute-start = (bf16[2,256,256]{2,1,0:T(8,128)(2,1)}, bf16[2,256,256]{2,1,0:T(8,128)(2,1)S(1)}, u32[]{:S(2)}, u32[]{:S(2)}) collective-permute-start(bf16[2,256,256]{2,1,0:T(8,128)(2,1)} %get-tuple-element.30), channel_id=1, source_target_pairs={{0,8},{4,12},{8,16},{12,20},{16,24},{20,28},{24,0},{28,4},{1,9},{5... | collective-permute-start | bytes 786440 | tf_op jit(solution)/shard_map/ppermute | solution.py:386
  8.3 29.1 %collective-permute-start.1 = (bf16[2,256,256]{2,1,0:T(8,128)(2,1)}, bf16[2,256,256]{2,1,0:T(8,128)(2,1)S(1)}, u32[]{:S(2)}, u32[]{:S(2)}) collective-permute-start(bf16[2,256,256]{2,1,0:T(8,128)(2,1)} %get-tuple-element.31), channel_id=1, source_target_pairs={{0,12},{4,16},{8,20},{12,24},{16,28},{20,0},{24,4},{28,8},{1,13},{... | collective-permute-start | bytes 786440 | tf_op jit(solution)/shard_map/ppermute | solution.py:386
  10.8 35.3 %collective-permute-start.2 = (bf16[2,256,256]{2,1,0:T(8,128)(2,1)}, bf16[2,256,256]{2,1,0:T(8,128)(2,1)S(1)}, u32[]{:S(2)}, u32[]{:S(2)}) collective-permute-start(bf16[2,256,256]{2,1,0:T(8,128)(2,1)} %get-tuple-element.37), channel_id=1, source_target_pairs={{0,16},{4,20},{8,24},{12,28},{16,0},{20,4},{24,8},{28,12},{1,17},{... | collective-permute-start | bytes 786440 | tf_op jit(solution)/shard_map/ppermute | solution.py:386
  12.1 34.8 %collective-permute-start.3 = (bf16[2,256,256]{2,1,0:T(8,128)(2,1)}, bf16[2,256,256]{2,1,0:T(8,128)(2,1)S(1)}, u32[]{:S(2)}, u32[]{:S(2)}) collective-permute-start(bf16[2,256,256]{2,1,0:T(8,128)(2,1)} %get-tuple-element.38), channel_id=1, source_target_pairs={{0,20},{4,24},{8,28},{12,0},{16,4},{20,8},{24,12},{28,16},{1,21},{... | collective-permute-start | bytes 786440 | tf_op jit(solution)/shard_map/ppermute | solution.py:386
  14.7 32.9 %collective-permute-start.4 = (bf16[2,256,256]{2,1,0:T(8,128)(2,1)}, bf16[2,256,256]{2,1,0:T(8,128)(2,1)S(1)}, u32[]{:S(2)}, u32[]{:S(2)}) collective-permute-start(bf16[2,256,256]{2,1,0:T(8,128)(2,1)} %get-tuple-element.39), channel_id=1, source_target_pairs={{0,24},{4,28},{8,0},{12,4},{16,8},{20,12},{24,16},{28,20},{1,25},{... | collective-permute-start | bytes 786440 | tf_op jit(solution)/shard_map/ppermute | solution.py:386
  16.1 2.1 %copy-start = (bf16[6,5,256,256]{3,2,1,0:T(8,128)(2,1)S(1)}, bf16[6,5,256,256]{3,2,1,0:T(8,128)(2,1)}, u32[]{:S(2)}) copy-start(bf16[6,5,256,256]{3,2,1,0:T(8,128)(2,1)} %tiles_ref.3) | copy-start | bytes 11796484
  38.1 23.8 %all-to-all-start = ((bf16[4,4,1536]{2,0,1:T(4,128)(2,1)}), bf16[4,4,1536]{2,0,1:T(4,128)(2,1)S(1)}, u32[]{:S(2)}, u32[]{:S(2)}) async-start(bf16[4,4,1536]{2,0,1:T(4,128)(2,1)} %bitcast.3), calls=%async_computation | async-start | bytes 98304 | tf_op jit(solution)/shard_map/all_to_all | solution.py:424
  41.4 20.7 %collective-permute-start.5 = (bf16[2,256,256]{2,1,0:T(8,128)(2,1)}, bf16[2,256,256]{2,1,0:T(8,128)(2,1)}, u32[]{:S(2)}, u32[]{:S(2)}) collective-permute-start(bf16[2,256,256]{2,1,0:T(8,128)(2,1)} %get-tuple-element.42), channel_id=1, source_target_pairs={{0,4},{4,8},{8,12},{12,16},{16,20},{20,24},{24,28},{28,0},{1,5},{5... | collective-permute-start | bytes 786440 | tf_op jit(solution)/shard_map/ppermute | solution.py:386
  41.4 20.6 %collective-permute-start.6 = (bf16[2,256,256]{2,1,0:T(8,128)(2,1)}, bf16[2,256,256]{2,1,0:T(8,128)(2,1)}, u32[]{:S(2)}, u32[]{:S(2)}) collective-permute-start(bf16[2,256,256]{2,1,0:T(8,128)(2,1)} %get-tuple-element.43), channel_id=1, source_target_pairs={{0,28},{4,0},{8,4},{12,8},{16,12},{20,16},{24,20},{28,24},{1,29},{... | collective-permute-start | bytes 786440 | tf_op jit(solution)/shard_map/ppermute | solution.py:386
  48.3 0.9 copy-start.3
  49.3 0.9 copy-start.6
  50.2 0.9 copy-start.9
  51.2 0.9 copy-start.12
  60.7 1.2 %copy-start.1 = (f32[6,256,256]{2,1,0:T(8,128)}, f32[6,256,256]{2,1,0:T(8,128)S(1)}, u32[]{:S(2)}) copy-start(f32[6,256,256]{2,1,0:T(8,128)S(1)} %get-tuple-element.41.t_any) | copy-start | bytes 4718596
  62.1 1.0 copy-start.4
  63.0 0.9 copy-start.7
  86.7 20.6 %all-to-all-start.1 = ((bf16[32,4,256]{2,1,0:T(4,128)(2,1)}), bf16[32,4,256]{2,1,0:T(4,128)(2,1)S(1)}, u32[]{:S(2)}, u32[]{:S(2)}) async-start(bf16[32,4,256]{2,1,0:T(4,128)(2,1)} %get-tuple-element.44), calls=%async_computation.1 | async-start | bytes 131072 | tf_op jit(solution)/shard_map/all_to_all | solution.py:470
  99.9 3.9 %collective-permute-start.7 = (f32[6,4,256]{2,1,0:T(4,128)S(1)}, f32[6,4,256]{2,1,0:T(4,128)S(1)}, u32[]{:S(2)}, u32[]{:S(2)}) collective-permute-start(f32[6,4,256]{2,1,0:T(4,128)S(1)} %get-tuple-element.46), channel_id=1, source_target_pairs={{0,1},{1,2},{2,3},{3,0},{4,5},{5,6},{6,7},{7,4},{8,9},{9,10},{10,1... | collective-permute-start | bytes 73736 | tf_op jit(solution)/shard_map/ppermute | solution.py:386
  100.2 3.9 %collective-permute-start.8 = (f32[6,4,256]{2,1,0:T(4,128)S(1)}, f32[6,4,256]{2,1,0:T(4,128)S(1)}, u32[]{:S(2)}, u32[]{:S(2)}) collective-permute-start(f32[6,4,256]{2,1,0:T(4,128)S(1)} %get-tuple-element.47), channel_id=1, source_target_pairs={{0,2},{1,3},{2,0},{3,1},{4,6},{5,7},{6,4},{7,5},{8,10},{9,11},{10,... | collective-permute-start | bytes 73736 | tf_op jit(solution)/shard_map/ppermute | solution.py:386
  101.9 2.9 %collective-permute-start.9 = (f32[6,4,256]{2,1,0:T(4,128)S(1)}, f32[6,4,256]{2,1,0:T(4,128)S(1)}, u32[]{:S(2)}, u32[]{:S(2)}) collective-permute-start(f32[6,4,256]{2,1,0:T(4,128)S(1)} %get-tuple-element.48), channel_id=1, source_target_pairs={{0,3},{1,0},{2,1},{3,2},{4,7},{5,4},{6,5},{7,6},{8,11},{9,8},{10,9... | collective-permute-start | bytes 73736 | tf_op jit(solution)/shard_map/ppermute | solution.py:386
  103.8 3.6 %copy-start.16 = (f32[6,4,256]{2,1,0:T(4,128)}, f32[6,4,256]{2,1,0:T(4,128)S(1)}, u32[]{:S(2)}) copy-start(f32[6,4,256]{2,1,0:T(4,128)S(1)} %collective-permute-done.7.refs_1_) | copy-start | bytes 73732
  104.1 3.2 %copy-start.17 = (f32[6,4,256]{2,1,0:T(4,128)}, f32[6,4,256]{2,1,0:T(4,128)S(1)}, u32[]{:S(2)}) copy-start(f32[6,4,256]{2,1,0:T(4,128)S(1)} %collective-permute-done.8.refs_2_) | copy-start | bytes 73732
  104.7 2.6 %copy-start.18 = (f32[6,4,256]{2,1,0:T(4,128)}, f32[6,4,256]{2,1,0:T(4,128)S(1)}, u32[]{:S(2)}) copy-start(f32[6,4,256]{2,1,0:T(4,128)S(1)} %collective-permute-done.9.refs_3_) | copy-start | bytes 73732
  (8 other events, 6.0 us)

commit v18 on v16

--- a/solution.py
+++ b/solution.py
@@ -392,7 +392,7 @@
     pairs = shards - 1
     every = tuple(range(1, shards))
     late = (1, shards - 1)
-    early = tuple(sorted((e for e in every if e not in late), key=lambda e: abs(2 * e - shards)))
+    early = tuple(e for e in every if e not in late)
     most = pltpu.CompilerParams(vmem_limit_bytes=60 * 1024 * 1024)
     pieces = pl.pallas_call(
         pick_kernel,

time: 101 us -> 98.1 us (0.971)
  starting transfers between devices: 33.1 us -> 29.2 us
    all_to_all x1, starting transfers between devices: 9.1 us -> 3.09 us  [on_device(): lax.all_to_all(low, ('panel', 'rhs'), split_axis=0, concat_axis=0, tiled=...]
    ppermute x10, starting transfers between devices: 20.4 us -> 22.8 us  [shift(): lax.ppermute(value, axis, [(i, (i + by) % size) for i in range(size)])]
  transfers between devices with their start and end apart: 12 -> 12, of which waited for: 5 -> 5; matrix products, arithmetic and copies ran while one was open for 1% -> 1% of each run, Pallas kernels for 27% -> 28%
where the time goes in v18:
time: 98.1 us; the launch traced here: 97.7 us
  Pallas kernels  53 us (54%)
  starting transfers between devices  29.2 us (30%)
  waiting for transfers between devices  8.37 us (9%)
  local copies, waits for them, and re-layouts  4.68 us (5%)
  other arithmetic  2.28 us (2%)
    ppermute x10, starting transfers between devices, shift(): lax.ppermute(value, axis, [(i, (i + by) % size) for i in range(size)])  22.8 us
    pallas_call x1, Pallas kernels, on_device(): pl.pallas_call(functools.partial(pair_kernel, lanes, every, late), out_sh...  20.2 us
    pallas_call x1, Pallas kernels, on_device(): pl.pallas_call(own_kernel, out_shape=(jax.ShapeDtypeStruct((systems, 2, w...  19.1 us
    pallas_call x1, Pallas kernels, on_device(): pl.pallas_call(functools.partial(link_kernel, early), out_shape=(jax.Shap...  8.59 us
    unnamed x20, local copies, waits for them, and re-layouts  4.51 us
    all_to_all x1, waiting for transfers between devices, on_device(): x = lax.all_to_all(inputs, 'rhs', split_axis=1, concat_axis=0, tiled=True)  3.92 us
    pallas_call x1, Pallas kernels, on_device(): pl.pallas_call(pick_kernel, out_shape=[jax.ShapeDtypeStruct((2, width, wi...  3.56 us
    all_to_all x1, starting transfers between devices, on_device(): x = lax.all_to_all(inputs, 'rhs', split_axis=1, concat_axis=0, tiled=True)  3.27 us
  transfers between devices with their start and end apart: 12, of which 5 were waited for; matrix products, arithmetic and copies ran while one was open for 1% of the time, Pallas kernels for 28%

profile of v18, /device:TPU:0, one launch (start us, length us, event | category | flops | bytes accessed | tf_op | source)
XLA Modules:
  0.0 97.7 jit_solution(5842888495572816575)
XLA Ops:
  0.0 0.8 bitcast_select_fusion
  0.9 0.7 select_reduce_fusion
  1.6 3.6 %shard_map.47 = (bf16[2,256,256]{2,1,0:T(8,128)(2,1)}, bf16[2,256,256]{2,1,0:T(8,128)(2,1)}, bf16[2,256,256]{2,1,0:T(8,128)(2,1)}, bf16[2,256,256]{2,1,0:T(8,128...) custom-call(s32[7]{0:T(128)} %get-tuple-element.57.slot_ref, ...), custom_call_target="tpu_custom_call" | custom-call | tf_op jit(solution)/shard_map/pallas_call | solution.py:397
  5.2 3.1 %collective-permute-start = (bf16[2,256,256]{2,1,0:T(8,128)(2,1)}, bf16[2,256,256]{2,1,0:T(8,128)(2,1)S(1)}, u32[]{:S(2)}, u32[]{:S(2)}) collective-permute-start(bf16[2,256,256]{2,1,0:T(8,128)(2,1)} %get-tuple-element.37), channel_id=1, source_target_pairs={{0,8},{4,12},{8,16},{12,20},{16,24},{20,28},{24,0},{28,4},{1,9},{5... | collective-permute-start | bytes 786440 | tf_op jit(solution)/shard_map/ppermute | solution.py:386
  8.2 2.6 %collective-permute-start.1 = (bf16[2,256,256]{2,1,0:T(8,128)(2,1)}, bf16[2,256,256]{2,1,0:T(8,128)(2,1)S(1)}, u32[]{:S(2)}, u32[]{:S(2)}) collective-permute-start(bf16[2,256,256]{2,1,0:T(8,128)(2,1)} %get-tuple-element.38), channel_id=1, source_target_pairs={{0,12},{4,16},{8,20},{12,24},{16,28},{20,0},{24,4},{28,8},{1,13},{... | collective-permute-start | bytes 786440 | tf_op jit(solution)/shard_map/ppermute | solution.py:386
  10.8 1.2 %collective-permute-start.2 = (bf16[2,256,256]{2,1,0:T(8,128)(2,1)}, bf16[2,256,256]{2,1,0:T(8,128)(2,1)S(1)}, u32[]{:S(2)}, u32[]{:S(2)}) collective-permute-start(bf16[2,256,256]{2,1,0:T(8,128)(2,1)} %get-tuple-element.39), channel_id=1, source_target_pairs={{0,16},{4,20},{8,24},{12,28},{16,0},{20,4},{24,8},{28,12},{1,17},{... | collective-permute-start | bytes 786440 | tf_op jit(solution)/shard_map/ppermute | solution.py:386
  12.0 2.6 %collective-permute-start.3 = (bf16[2,256,256]{2,1,0:T(8,128)(2,1)}, bf16[2,256,256]{2,1,0:T(8,128)(2,1)S(1)}, u32[]{:S(2)}, u32[]{:S(2)}) collective-permute-start(bf16[2,256,256]{2,1,0:T(8,128)(2,1)} %get-tuple-element.40), channel_id=1, source_target_pairs={{0,20},{4,24},{8,28},{12,0},{16,4},{20,8},{24,12},{28,16},{1,21},{... | collective-permute-start | bytes 786440 | tf_op jit(solution)/shard_map/ppermute | solution.py:386
  14.6 1.4 %collective-permute-start.4 = (bf16[2,256,256]{2,1,0:T(8,128)(2,1)}, bf16[2,256,256]{2,1,0:T(8,128)(2,1)S(1)}, u32[]{:S(2)}, u32[]{:S(2)}) collective-permute-start(bf16[2,256,256]{2,1,0:T(8,128)(2,1)} %get-tuple-element.41), channel_id=1, source_target_pairs={{0,24},{4,28},{8,0},{12,4},{16,8},{20,12},{24,16},{28,20},{1,25},{... | collective-permute-start | bytes 786440 | tf_op jit(solution)/shard_map/ppermute | solution.py:386
  16.1 2.1 %copy-done = bf16[6,5,256,256]{3,2,1,0:T(8,128)(2,1)S(1)} copy-done((bf16[6,5,256,256]{3,2,1,0:T(8,128)(2,1)S(1)}, bf16[6,5,256,256]{3,2,1,0:T(8,128)(2,1)}, u32[]{:S(2)}) %copy-start) | copy-done | bytes 3932184
  18.2 19.1 %shard_map.46 = (bf16[6,2,256,256]{3,2,1,0:T(8,128)(2,1)S(1)}, bf16[6,3,256,512]{3,2,1,0:T(8,128)(2,1)}) custom-call(s32[6]{0:T(128)S(1)} %dynamic_slice.14.counts_ref, bf16[6,5,256,256]{3,2,1,0:T(8,128)(2,1)S(1)} %copy-done), custom_call_target="tpu_custom_call" | custom-call | flops 30000001024 | bytes 8000000 | tf_op jit(solution)/shard_map/pallas_call | solution.py:407
  37.2 3.3 %all-to-all-start = ((bf16[4,4,1536]{2,0,1:T(4,128)(2,1)}), bf16[4,4,1536]{2,0,1:T(4,128)(2,1)S(1)}, u32[]{:S(2)}, u32[]{:S(2)}) async-start(bf16[4,4,1536]{2,0,1:T(4,128)(2,1)} %bitcast.3), calls=%async_computation | async-start | bytes 98304 | tf_op jit(solution)/shard_map/all_to_all | solution.py:421
  40.6 3.9 %all-to-all-done = bf16[4,4,1536]{2,0,1:T(4,128)(2,1)S(1)} async-done(((bf16[4,4,1536]{2,0,1:T(4,128)(2,1)}), bf16[4,4,1536]{2,0,1:T(4,128)(2,1)S(1)}, u32[]{:S(2)}, u32[]{:S(2)}) %all-to-all-start) | async-done | bytes 49184 | tf_op jit(solution)/shard_map/all_to_all | solution.py:421
  44.7 1.8 %collective-permute-start.5 = (bf16[2,256,256]{2,1,0:T(8,128)(2,1)S(1)}, bf16[2,256,256]{2,1,0:T(8,128)(2,1)S(1)}, u32[]{:S(2)}, u32[]{:S(2)}) collective-permute-start(bf16[2,256,256]{2,1,0:T(8,128)(2,1)S(1)} %copy-done.8), channel_id=1, source_target_pairs={{0,4},{4,8},{8,12},{12,16},{16,20},{20,24},{24,28},{28,0},{1,5},{5... | collective-permute-start | bytes 786440 | tf_op jit(solution)/shard_map/ppermute | solution.py:386
  46.5 6.9 %collective-permute-start.6 = (bf16[2,256,256]{2,1,0:T(8,128)(2,1)S(1)}, bf16[2,256,256]{2,1,0:T(8,128)(2,1)S(1)}, u32[]{:S(2)}, u32[]{:S(2)}) collective-permute-start(bf16[2,256,256]{2,1,0:T(8,128)(2,1)S(1)} %copy-done.7), channel_id=1, source_target_pairs={{0,28},{4,0},{8,4},{12,8},{16,12},{20,16},{24,20},{28,24},{1,29},{... | collective-permute-start | bytes 786440 | tf_op jit(solution)/shard_map/ppermute | solution.py:386
  53.4 8.6 %shard_map.48 = (bf16[6,2,256,256]{3,2,1,0:T(8,128)(2,1)S(1)}, f32[6,256,256]{2,1,0:T(8,128)S(1)}) custom-call(s32[7]{0:T(128)S(1)} %get-tuple-element.58.slot_ref, bf16[6,3,256,512]{3,2,1,0:T(8,128)(2,1)} %get-tuple-element.42.z_any, bf16[2,256,256]{2,1,0:T(8,128)(2,1)S(1)} %collective-permute-done.refs_0_.refs_1_, ...), custom_call_target="tpu_custom_call" | custom-call | flops 12000000000 | bytes 8000000 | tf_op jit(solution)/shard_map/pallas_call | solution.py:429
  62.0 1.2 %copy-done.1 = f32[6,256,256]{2,1,0:T(8,128)} copy-done((f32[6,256,256]{2,1,0:T(8,128)}, f32[6,256,256]{2,1,0:T(8,128)S(1)}, u32[]{:S(2)}) %copy-start.1) | copy-done | bytes 1572888
  63.2 1.0 %collective-permute-done.6.refs_6_ = bf16[2,256,256]{2,1,0:T(8,128)(2,1)S(1)} collective-permute-done((bf16[2,256,256]{2,1,0:T(8,128)(2,1)S(1)}, bf16[2,256,256]{2,1,0:T(8,128)(2,1)S(1)}, u32[]{:S(2)}, u32[]{:S(2)}) %collective-permute-start.6) | collective-permute-done | bytes 262176 | tf_op jit(solution)/shard_map/ppermute | solution.py:386
  64.1 20.2 %shard_map.49 = (f32[6,4,256]{2,1,0:T(4,128)S(1)}, f32[6,4,256]{2,1,0:T(4,128)S(1)}, f32[6,4,256]{2,1,0:T(4,128)S(1)}, f32[6,4,256]{2,1,0:T(4,128)S(1)}, bf16[32,4,256]{2,1,0:T(4,128)(2,1)}) custom-call(s32[7]{0:T(128)S(1)} %pad_add_fusion.1.place_ref, s32[7]{0:T(128)S(1)} %get-tuple-element.58.slot_ref, bf16[16,1536]{1,0:T(8,128)(2,1)S(1)} %fusion.x_ref, ...), custom_call_target="tpu_custom_call" | custom-call | tf_op jit(solution)/shard_map/pallas_call | solution.py:449
  84.9 3.1 %all-to-all-start.1 = ((bf16[32,4,256]{2,1,0:T(4,128)(2,1)}), bf16[32,4,256]{2,1,0:T(4,128)(2,1)S(1)}, u32[]{:S(2)}, u32[]{:S(2)}) async-start(bf16[32,4,256]{2,1,0:T(4,128)(2,1)} %get-tuple-element.52), calls=%async_computation.1 | async-start | bytes 131072 | tf_op jit(solution)/shard_map/all_to_all | solution.py:471
  88.3 1.7 %collective-permute-start.8 = (f32[6,4,256]{2,1,0:T(4,128)S(1)}, f32[6,4,256]{2,1,0:T(4,128)S(1)}, u32[]{:S(2)}, u32[]{:S(2)}) collective-permute-start(f32[6,4,256]{2,1,0:T(4,128)S(1)} %get-tuple-element.55), channel_id=1, source_target_pairs={{0,2},{1,3},{2,0},{3,1},{4,6},{5,7},{6,4},{7,5},{8,10},{9,11},{10,... | collective-permute-start | bytes 73736 | tf_op jit(solution)/shard_map/ppermute | solution.py:386
  90.0 1.3 %collective-permute-start.9 = (f32[6,4,256]{2,1,0:T(4,128)S(1)}, f32[6,4,256]{2,1,0:T(4,128)S(1)}, u32[]{:S(2)}, u32[]{:S(2)}) collective-permute-start(f32[6,4,256]{2,1,0:T(4,128)S(1)} %get-tuple-element.56), channel_id=1, source_target_pairs={{0,3},{1,0},{2,1},{3,2},{4,7},{5,4},{6,5},{7,6},{8,11},{9,8},{10,9... | collective-permute-start | bytes 73736 | tf_op jit(solution)/shard_map/ppermute | solution.py:386
  91.3 0.6 pad_add_fusion.place_ref
  92.9 2.6 %all-to-all-done.1.low_ref = bf16[32,4,256]{2,1,0:T(4,128)(2,1)S(1)} async-done(((bf16[32,4,256]{2,1,0:T(4,128)(2,1)}), bf16[32,4,256]{2,1,0:T(4,128)(2,1)S(1)}, u32[]{:S(2)}, u32[]{:S(2)}) %all-to-all-start.1) | async-done | bytes 65568 | tf_op jit(solution)/shard_map/all_to_all | solution.py:471
  96.1 1.6 %shard_map.50 = bf16[4,6144]{1,0:T(4,128)(2,1)} custom-call(s32[25]{0:T(128)} %pad_add_fusion.place_ref, bf16[32,4,256]{2,1,0:T(4,128)(2,1)} %copy-done.3, f32[6,4,256]{2,1,0:T(4,128)} %copy-done.2, f32[6,4,256]{2,1,0:T(4,128)} %copy-done.4, f32[6,4,256]{2,1,0:T(4,128)} %copy-done.5, f32[6,4,256]{2,1,0:T(4,128)} %copy-done.6), custom_call_target="tpu_custom_call" | custom-call | tf_op jit(solution)/shard_map/pallas_call | solution.py:473
  (34 shorter events, 2.7 us)
Async XLA Ops:
  1.6 14.4 %copy-start.9 = (s32[192]{0:T(256)S(1)}, s32[192]{0:T(256)}, u32[]{:S(2)}) copy-start(s32[192]{0:T(256)} %param.6) | copy-start | bytes 2308
  5.2 39.5 %collective-permute-start = (bf16[2,256,256]{2,1,0:T(8,128)(2,1)}, bf16[2,256,256]{2,1,0:T(8,128)(2,1)S(1)}, u32[]{:S(2)}, u32[]{:S(2)}) collective-permute-start(bf16[2,256,256]{2,1,0:T(8,128)(2,1)} %get-tuple-element.37), channel_id=1, source_target_pairs={{0,8},{4,12},{8,16},{12,20},{16,24},{20,28},{24,0},{28,4},{1,9},{5... | collective-permute-start | bytes 786440 | tf_op jit(solution)/shard_map/ppermute | solution.py:386
  8.2 36.4 %collective-permute-start.1 = (bf16[2,256,256]{2,1,0:T(8,128)(2,1)}, bf16[2,256,256]{2,1,0:T(8,128)(2,1)S(1)}, u32[]{:S(2)}, u32[]{:S(2)}) collective-permute-start(bf16[2,256,256]{2,1,0:T(8,128)(2,1)} %get-tuple-element.38), channel_id=1, source_target_pairs={{0,12},{4,16},{8,20},{12,24},{16,28},{20,0},{24,4},{28,8},{1,13},{... | collective-permute-start | bytes 786440 | tf_op jit(solution)/shard_map/ppermute | solution.py:386
  10.8 33.8 %collective-permute-start.2 = (bf16[2,256,256]{2,1,0:T(8,128)(2,1)}, bf16[2,256,256]{2,1,0:T(8,128)(2,1)S(1)}, u32[]{:S(2)}, u32[]{:S(2)}) collective-permute-start(bf16[2,256,256]{2,1,0:T(8,128)(2,1)} %get-tuple-element.39), channel_id=1, source_target_pairs={{0,16},{4,20},{8,24},{12,28},{16,0},{20,4},{24,8},{28,12},{1,17},{... | collective-permute-start | bytes 786440 | tf_op jit(solution)/shard_map/ppermute | solution.py:386
  12.0 32.6 %collective-permute-start.3 = (bf16[2,256,256]{2,1,0:T(8,128)(2,1)}, bf16[2,256,256]{2,1,0:T(8,128)(2,1)S(1)}, u32[]{:S(2)}, u32[]{:S(2)}) collective-permute-start(bf16[2,256,256]{2,1,0:T(8,128)(2,1)} %get-tuple-element.40), channel_id=1, source_target_pairs={{0,20},{4,24},{8,28},{12,0},{16,4},{20,8},{24,12},{28,16},{1,21},{... | collective-permute-start | bytes 786440 | tf_op jit(solution)/shard_map/ppermute | solution.py:386
  14.6 30.0 %collective-permute-start.4 = (bf16[2,256,256]{2,1,0:T(8,128)(2,1)}, bf16[2,256,256]{2,1,0:T(8,128)(2,1)S(1)}, u32[]{:S(2)}, u32[]{:S(2)}) collective-permute-start(bf16[2,256,256]{2,1,0:T(8,128)(2,1)} %get-tuple-element.41), channel_id=1, source_target_pairs={{0,24},{4,28},{8,0},{12,4},{16,8},{20,12},{24,16},{28,20},{1,25},{... | collective-permute-start | bytes 786440 | tf_op jit(solution)/shard_map/ppermute | solution.py:386
  16.1 2.1 %copy-start = (bf16[6,5,256,256]{3,2,1,0:T(8,128)(2,1)S(1)}, bf16[6,5,256,256]{3,2,1,0:T(8,128)(2,1)}, u32[]{:S(2)}) copy-start(bf16[6,5,256,256]{3,2,1,0:T(8,128)(2,1)} %tiles_ref.3) | copy-start | bytes 11796484
  18.2 26.5 %copy-start.8 = (bf16[2,256,256]{2,1,0:T(8,128)(2,1)S(1)}, bf16[2,256,256]{2,1,0:T(8,128)(2,1)}, u32[]{:S(2)}) copy-start(bf16[2,256,256]{2,1,0:T(8,128)(2,1)} %get-tuple-element.50) | copy-start | bytes 786436
  18.2 28.3 %copy-start.7 = (bf16[2,256,256]{2,1,0:T(8,128)(2,1)S(1)}, bf16[2,256,256]{2,1,0:T(8,128)(2,1)}, u32[]{:S(2)}) copy-start(bf16[2,256,256]{2,1,0:T(8,128)(2,1)} %get-tuple-element.51) | copy-start | bytes 786436
  37.2 7.3 %all-to-all-start = ((bf16[4,4,1536]{2,0,1:T(4,128)(2,1)}), bf16[4,4,1536]{2,0,1:T(4,128)(2,1)S(1)}, u32[]{:S(2)}, u32[]{:S(2)}) async-start(bf16[4,4,1536]{2,0,1:T(4,128)(2,1)} %bitcast.3), calls=%async_computation | async-start | bytes 98304 | tf_op jit(solution)/shard_map/all_to_all | solution.py:421
  44.7 18.5 %collective-permute-start.5 = (bf16[2,256,256]{2,1,0:T(8,128)(2,1)S(1)}, bf16[2,256,256]{2,1,0:T(8,128)(2,1)S(1)}, u32[]{:S(2)}, u32[]{:S(2)}) collective-permute-start(bf16[2,256,256]{2,1,0:T(8,128)(2,1)S(1)} %copy-done.8), channel_id=1, source_target_pairs={{0,4},{4,8},{8,12},{12,16},{16,20},{20,24},{24,28},{28,0},{1,5},{5... | collective-permute-start | bytes 786440 | tf_op jit(solution)/shard_map/ppermute | solution.py:386
  46.5 17.7 %collective-permute-start.6 = (bf16[2,256,256]{2,1,0:T(8,128)(2,1)S(1)}, bf16[2,256,256]{2,1,0:T(8,128)(2,1)S(1)}, u32[]{:S(2)}, u32[]{:S(2)}) collective-permute-start(bf16[2,256,256]{2,1,0:T(8,128)(2,1)S(1)} %copy-done.7), channel_id=1, source_target_pairs={{0,28},{4,0},{8,4},{12,8},{16,12},{20,16},{24,20},{28,24},{1,29},{... | collective-permute-start | bytes 786440 | tf_op jit(solution)/shard_map/ppermute | solution.py:386
  62.0 1.2 %copy-start.1 = (f32[6,256,256]{2,1,0:T(8,128)}, f32[6,256,256]{2,1,0:T(8,128)S(1)}, u32[]{:S(2)}) copy-start(f32[6,256,256]{2,1,0:T(8,128)S(1)} %get-tuple-element.49.t_any) | copy-start | bytes 4718596
  84.3 0.6 copy-start.2
  84.9 10.5 %all-to-all-start.1 = ((bf16[32,4,256]{2,1,0:T(4,128)(2,1)}), bf16[32,4,256]{2,1,0:T(4,128)(2,1)S(1)}, u32[]{:S(2)}, u32[]{:S(2)}) async-start(bf16[32,4,256]{2,1,0:T(4,128)(2,1)} %get-tuple-element.52), calls=%async_computation.1 | async-start | bytes 131072 | tf_op jit(solution)/shard_map/all_to_all | solution.py:471
  88.0 4.0 %collective-permute-start.7 = (f32[6,4,256]{2,1,0:T(4,128)S(1)}, f32[6,4,256]{2,1,0:T(4,128)S(1)}, u32[]{:S(2)}, u32[]{:S(2)}) collective-permute-start(f32[6,4,256]{2,1,0:T(4,128)S(1)} %get-tuple-element.54), channel_id=1, source_target_pairs={{0,1},{1,2},{2,3},{3,0},{4,5},{5,6},{6,7},{7,4},{8,9},{9,10},{10,1... | collective-permute-start | bytes 73736 | tf_op jit(solution)/shard_map/ppermute | solution.py:386
  88.3 3.9 %collective-permute-start.8 = (f32[6,4,256]{2,1,0:T(4,128)S(1)}, f32[6,4,256]{2,1,0:T(4,128)S(1)}, u32[]{:S(2)}, u32[]{:S(2)}) collective-permute-start(f32[6,4,256]{2,1,0:T(4,128)S(1)} %get-tuple-element.55), channel_id=1, source_target_pairs={{0,2},{1,3},{2,0},{3,1},{4,6},{5,7},{6,4},{7,5},{8,10},{9,11},{10,... | collective-permute-start | bytes 73736 | tf_op jit(solution)/shard_map/ppermute | solution.py:386
  90.0 2.9 %collective-permute-start.9 = (f32[6,4,256]{2,1,0:T(4,128)S(1)}, f32[6,4,256]{2,1,0:T(4,128)S(1)}, u32[]{:S(2)}, u32[]{:S(2)}) collective-permute-start(f32[6,4,256]{2,1,0:T(4,128)S(1)} %get-tuple-element.56), channel_id=1, source_target_pairs={{0,3},{1,0},{2,1},{3,2},{4,7},{5,4},{6,5},{7,6},{8,11},{9,8},{10,9... | collective-permute-start | bytes 73736 | tf_op jit(solution)/shard_map/ppermute | solution.py:386
  92.0 3.5 %copy-start.4 = (f32[6,4,256]{2,1,0:T(4,128)}, f32[6,4,256]{2,1,0:T(4,128)S(1)}, u32[]{:S(2)}) copy-start(f32[6,4,256]{2,1,0:T(4,128)S(1)} %collective-permute-done.7.refs_1_) | copy-start | bytes 73732
  92.2 3.2 %copy-start.5 = (f32[6,4,256]{2,1,0:T(4,128)}, f32[6,4,256]{2,1,0:T(4,128)S(1)}, u32[]{:S(2)}) copy-start(f32[6,4,256]{2,1,0:T(4,128)S(1)} %collective-permute-done.8.refs_2_) | copy-start | bytes 73732
  92.9 2.6 %copy-start.6 = (f32[6,4,256]{2,1,0:T(4,128)}, f32[6,4,256]{2,1,0:T(4,128)S(1)}, u32[]{:S(2)}) copy-start(f32[6,4,256]{2,1,0:T(4,128)S(1)} %collective-permute-done.9.refs_3_) | copy-start | bytes 73732
  95.5 0.6 copy-start.3

commit v19 on v18

--- a/solution.py
+++ b/solution.py
@@ -280,9 +280,9 @@
     return v, dot(near_t, near, NN) - dot6(v, v, NT)
 
 
-def link_kernel(shifts, slot_ref, z_any, *refs):
+def link_kernel(shifts, slot_ref, x_ref, z_any, *refs):
     got_refs, refs = refs[:len(shifts)], refs[len(shifts):]
-    v_ref, t_ref, z_ref, near_ref, z_sems, sems = refs
+    v_ref, t_ref, first_ref, z_ref, near_ref, z_sems, sems = refs
     systems, _, width, _ = z_ref.shape
     for s in range(systems):
         near_ref[s] = jnp.zeros(near_ref.shape[1:], near_ref.dtype)
@@ -294,14 +294,16 @@
         copy.wait()
     for s in range(systems):
         z_copies[s].wait()
+        x = x_ref[:, s * width:(s + 1) * width]
+        first_ref[s] = dot(x, z_ref[s, 0, :, width:], NT) + dot(x, z_ref[s, 1, :, width:], NT)
         v, t_ref[s] = schur(near_ref[s].reshape(2 * width, width), [z_ref[s, i] for i in range(3)])
         v_ref[s, 0] = v[0]
         v_ref[s, 1] = v[1]
 
 
-def pair_kernel(lanes, shifts, late, place_ref, slot_ref, x_ref, w_any, z_any, v_any, t_any, *refs):
+def pair_kernel(lanes, shifts, late, place_ref, slot_ref, x_ref, first_ref, w_any, z_any, v_any, t_any, *refs):
     got_refs, up_refs, refs = refs[:len(shifts)], refs[len(shifts):len(shifts) + lanes], refs[len(shifts) + lanes:]
-    low_ref, near_ref, w_ref, z_ref, zj_ref, v_ref, t_ref, r_ref, first_ref, near_sems, sems, *scratch = refs
+    low_ref, near_ref, w_ref, z_ref, v_ref, t_ref, r_ref, near_sems, sems, *scratch = refs
     _, _, width, _ = z_ref.shape
     systems = first_ref.shape[0]
     count = x_ref.shape[0] // lanes
@@ -312,26 +314,27 @@
     ] + [
         pltpu.make_async_copy(t_any, t_ref.at[0:systems], sems.at[2]),
         pltpu.make_async_copy(v_any, v_ref.at[0:systems], sems.at[3]),
-        pltpu.make_async_copy(z_any.at[:, 0:2, :, width:], zj_ref, sems.at[4]),
     ]
-    w_copy = pltpu.make_async_copy(w_any, w_ref, sems.at[5])
+    w_copy = pltpu.make_async_copy(w_any, w_ref, sems.at[4])
     for copy in copies + [w_copy]:
         copy.start()
     low_ref[...] = jnp.zeros(low_ref.shape, low_ref.dtype)
-    for copy in near_copies + copies[:-1]:
+    for copy in near_copies + copies[:-2]:
+        copy.wait()
+    formed = []
+    for i, slot in enumerate(late_slots):
+        near = near_ref[jnp.maximum(slot, 0)].reshape(2 * width, width)
+        formed.append(schur(near, [z_ref[i, p] for p in range(3)]))
+    for s in range(systems):
+        r_ref[s] = dot(x_ref[:, s * width:(s + 1) * width], near_ref[s, 1], NN)
+    for copy in copies[-2:]:
         copy.wait()
     for i, slot in enumerate(late_slots):
         at = jnp.where(slot >= 0, slot, systems + i)
-        near = near_ref[jnp.maximum(slot, 0)].reshape(2 * width, width)
-        v, t_ref[at] = schur(near, [z_ref[i, p] for p in range(3)])
+        v, t_ref[at] = formed[i]
         v_ref[at, 0] = v[0]
         v_ref[at, 1] = v[1]
-    copies[-1].wait()
     roots = []
-    for s in range(systems):
-        x = x_ref[:, s * width:(s + 1) * width]
-        first_ref[s] = dot(x, zj_ref[s, 0], NT) + dot(x, zj_ref[s, 1], NT)
-        r_ref[s] = dot(x, near_ref[s, 1], NN)
     for s in range(systems):
         r_ref[s] = r_ref[s] - apply(first_ref[s], (v_ref[s, 0], v_ref[s, 1]), NT)
         t_ref[s], root = scaled(t_ref[s])
@@ -426,14 +429,15 @@
     received.update(zip(early, come))
     received.update({e: shift(piece, "panel", e) for e, piece in zip(late, held)})
     from_slot = slots((my_panel - hops) % shards)
-    v, t = pl.pallas_call(
+    v, t, first = pl.pallas_call(
         functools.partial(link_kernel, early),
         out_shape=(
             jax.ShapeDtypeStruct((systems, 2, width, width), jnp.bfloat16),
             jax.ShapeDtypeStruct((systems, width, width), jnp.float32),
+            jax.ShapeDtypeStruct((systems, lanes * nrhs_dev, width), jnp.float32),
         ),
-        in_specs=[smem] + [anywhere] * (1 + len(early)),
-        out_specs=(vmem, vmem),
+        in_specs=[smem, vmem] + [anywhere] * (1 + len(early)),
+        out_specs=(vmem, vmem, vmem),
         scratch_shapes=[
             pltpu.VMEM((systems, 3, width, 2 * width), jnp.bfloat16),
             pltpu.VMEM((systems + len(early), 2, width, width), jnp.bfloat16),
@@ -442,30 +446,28 @@
         ],
         compiler_params=params,
         cost_estimate=pl.CostEstimate(flops=12 * 10**9, bytes_accessed=8 * 10**6, transcendentals=0),
-    )(from_slot, z, *[received[e] for e in early])
+    )(from_slot, x, z, *[received[e] for e in early])
 
     nrhs = lanes * nrhs_dev
     piece = jax.ShapeDtypeStruct((systems, nrhs_dev, width), jnp.float32)
     *up, low = pl.pallas_call(
         functools.partial(pair_kernel, lanes, every, late),
         out_shape=[piece] * lanes + [jax.ShapeDtypeStruct((shards * lanes, nrhs_dev, width), jnp.bfloat16)],
-        in_specs=[smem, smem, vmem] + [anywhere] * (4 + pairs),
+        in_specs=[smem, smem, vmem, vmem] + [anywhere] * (4 + pairs),
         out_specs=[vmem] * (lanes + 1),
         scratch_shapes=[
             pltpu.VMEM((systems + pairs, 2, width, width), jnp.bfloat16),
             pltpu.VMEM((systems, 2, width, width), jnp.bfloat16),
             pltpu.VMEM((len(late), 3, width, 2 * width), jnp.bfloat16),
-            pltpu.VMEM((systems, 2, width, width), jnp.bfloat16),
             pltpu.VMEM((systems + len(late), 2, width, width), jnp.bfloat16),
             pltpu.VMEM((systems + len(late), width, width), jnp.float32),
             pltpu.VMEM((systems, nrhs, width), jnp.float32),
-            pltpu.VMEM((systems, nrhs, width), jnp.float32),
             pltpu.SemaphoreType.DMA((pairs,)),
-            pltpu.SemaphoreType.DMA((6,)),
+            pltpu.SemaphoreType.DMA((5,)),
         ] + factor_scratch(systems, width),
         compiler_params=params,
     )(
-        jnp.concatenate([mate_panel, lane_word]), from_slot, x, w, z, v, t,
+        jnp.concatenate([mate_panel, lane_word]), from_slot, x, first, w, z, v, t,
         *[received[e] for e in every],
     )
     low = lax.all_to_all(low, ("panel", "rhs"), split_axis=0, concat_axis=0, tiled=True)

time: 98.1 us -> 97 us (0.989)
    pallas_call x1, Pallas kernels: 20.2 us -> 19.1 us  [on_device(): pl.pallas_call(functools.partial(pair_kernel, lanes, every, late), out_sh...]
  transfers between devices with their start and end apart: 12 -> 12, of which waited for: 5 -> 5; matrix products, arithmetic and copies ran while one was open for 1% -> 1% of each run, Pallas kernels for 28% -> 30%
where the time goes in v19:
time: 97 us; the launch traced here: 96.6 us
  Pallas kernels  53.6 us (55%)
  starting transfers between devices  28.3 us (29%)
  waiting for transfers between devices  7.6 us (8%)
  local copies, waits for them, and re-layouts  4.68 us (5%)
  other arithmetic  2.28 us (2%)
    ppermute x10, starting transfers between devices, shift(): lax.ppermute(value, axis, [(i, (i + by) % size) for i in range(size)])  22 us
    pallas_call x1, Pallas kernels, on_device(): pl.pallas_call(own_kernel, out_shape=(jax.ShapeDtypeStruct((systems, 2, w...  19.9 us
    pallas_call x1, Pallas kernels, on_device(): pl.pallas_call(functools.partial(pair_kernel, lanes, every, late), out_sh...  19.1 us
    pallas_call x1, Pallas kernels, on_device(): pl.pallas_call(functools.partial(link_kernel, early), out_shape=(jax.Shap...  9.39 us
    unnamed x20, local copies, waits for them, and re-layouts  4.51 us
    all_to_all x1, waiting for transfers between devices, on_device(): x = lax.all_to_all(inputs, 'rhs', split_axis=1, concat_axis=0, tiled=True)  3.92 us
    pallas_call x1, Pallas kernels, on_device(): pl.pallas_call(pick_kernel, out_shape=[jax.ShapeDtypeStruct((2, width, wi...  3.56 us
    all_to_all x1, starting transfers between devices, on_device(): x = lax.all_to_all(inputs, 'rhs', split_axis=1, concat_axis=0, tiled=True)  3.27 us
  transfers between devices with their start and end apart: 12, of which 5 were waited for; matrix products, arithmetic and copies ran while one was open for 1% of the time, Pallas kernels for 30%

profile of v19, /device:TPU:0, one launch (start us, length us, event | category | flops | bytes accessed | tf_op | source)
XLA Modules:
  0.0 96.6 jit_solution(5361702710686121734)
XLA Ops:
  0.0 0.8 bitcast_select_fusion
  0.9 0.7 select_reduce_fusion
  1.6 3.6 %shard_map.47 = (bf16[2,256,256]{2,1,0:T(8,128)(2,1)}, bf16[2,256,256]{2,1,0:T(8,128)(2,1)}, bf16[2,256,256]{2,1,0:T(8,128)(2,1)}, bf16[2,256,256]{2,1,0:T(8,128...) custom-call(s32[7]{0:T(128)} %get-tuple-element.59.slot_ref, ...), custom_call_target="tpu_custom_call" | custom-call | tf_op jit(solution)/shard_map/pallas_call | solution.py:400
  5.2 3.1 %collective-permute-start = (bf16[2,256,256]{2,1,0:T(8,128)(2,1)}, bf16[2,256,256]{2,1,0:T(8,128)(2,1)S(1)}, u32[]{:S(2)}, u32[]{:S(2)}) collective-permute-start(bf16[2,256,256]{2,1,0:T(8,128)(2,1)} %get-tuple-element.37), channel_id=1, source_target_pairs={{0,8},{4,12},{8,16},{12,20},{16,24},{20,28},{24,0},{28,4},{1,9},{5... | collective-permute-start | bytes 786440 | tf_op jit(solution)/shard_map/ppermute | solution.py:389
  8.2 2.5 %collective-permute-start.1 = (bf16[2,256,256]{2,1,0:T(8,128)(2,1)}, bf16[2,256,256]{2,1,0:T(8,128)(2,1)S(1)}, u32[]{:S(2)}, u32[]{:S(2)}) collective-permute-start(bf16[2,256,256]{2,1,0:T(8,128)(2,1)} %get-tuple-element.38), channel_id=1, source_target_pairs={{0,12},{4,16},{8,20},{12,24},{16,28},{20,0},{24,4},{28,8},{1,13},{... | collective-permute-start | bytes 786440 | tf_op jit(solution)/shard_map/ppermute | solution.py:389
  10.8 1.2 %collective-permute-start.2 = (bf16[2,256,256]{2,1,0:T(8,128)(2,1)}, bf16[2,256,256]{2,1,0:T(8,128)(2,1)S(1)}, u32[]{:S(2)}, u32[]{:S(2)}) collective-permute-start(bf16[2,256,256]{2,1,0:T(8,128)(2,1)} %get-tuple-element.39), channel_id=1, source_target_pairs={{0,16},{4,20},{8,24},{12,28},{16,0},{20,4},{24,8},{28,12},{1,17},{... | collective-permute-start | bytes 786440 | tf_op jit(solution)/shard_map/ppermute | solution.py:389
  12.0 2.6 %collective-permute-start.3 = (bf16[2,256,256]{2,1,0:T(8,128)(2,1)}, bf16[2,256,256]{2,1,0:T(8,128)(2,1)S(1)}, u32[]{:S(2)}, u32[]{:S(2)}) collective-permute-start(bf16[2,256,256]{2,1,0:T(8,128)(2,1)} %get-tuple-element.40), channel_id=1, source_target_pairs={{0,20},{4,24},{8,28},{12,0},{16,4},{20,8},{24,12},{28,16},{1,21},{... | collective-permute-start | bytes 786440 | tf_op jit(solution)/shard_map/ppermute | solution.py:389
  14.6 1.4 %collective-permute-start.4 = (bf16[2,256,256]{2,1,0:T(8,128)(2,1)}, bf16[2,256,256]{2,1,0:T(8,128)(2,1)S(1)}, u32[]{:S(2)}, u32[]{:S(2)}) collective-permute-start(bf16[2,256,256]{2,1,0:T(8,128)(2,1)} %get-tuple-element.41), channel_id=1, source_target_pairs={{0,24},{4,28},{8,0},{12,4},{16,8},{20,12},{24,16},{28,20},{1,25},{... | collective-permute-start | bytes 786440 | tf_op jit(solution)/shard_map/ppermute | solution.py:389
  16.1 2.1 %copy-done = bf16[6,5,256,256]{3,2,1,0:T(8,128)(2,1)S(1)} copy-done((bf16[6,5,256,256]{3,2,1,0:T(8,128)(2,1)S(1)}, bf16[6,5,256,256]{3,2,1,0:T(8,128)(2,1)}, u32[]{:S(2)}) %copy-start) | copy-done | bytes 3932184
  18.2 19.9 %shard_map.46 = (bf16[6,2,256,256]{3,2,1,0:T(8,128)(2,1)S(1)}, bf16[6,3,256,512]{3,2,1,0:T(8,128)(2,1)}) custom-call(s32[6]{0:T(128)S(1)} %dynamic_slice.14.counts_ref, bf16[6,5,256,256]{3,2,1,0:T(8,128)(2,1)S(1)} %copy-done), custom_call_target="tpu_custom_call" | custom-call | flops 30000001024 | bytes 8000000 | tf_op jit(solution)/shard_map/pallas_call | solution.py:410
  38.1 3.3 %all-to-all-start = ((bf16[4,4,1536]{2,0,1:T(4,128)(2,1)}), bf16[4,4,1536]{2,0,1:T(4,128)(2,1)S(1)}, u32[]{:S(2)}, u32[]{:S(2)}) async-start(bf16[4,4,1536]{2,0,1:T(4,128)(2,1)} %bitcast.3), calls=%async_computation | async-start | bytes 98304 | tf_op jit(solution)/shard_map/all_to_all | solution.py:424
  41.5 3.9 %all-to-all-done = bf16[4,4,1536]{2,0,1:T(4,128)(2,1)S(1)} async-done(((bf16[4,4,1536]{2,0,1:T(4,128)(2,1)}), bf16[4,4,1536]{2,0,1:T(4,128)(2,1)S(1)}, u32[]{:S(2)}, u32[]{:S(2)}) %all-to-all-start) | async-done | bytes 49184 | tf_op jit(solution)/shard_map/all_to_all | solution.py:424
  45.6 1.5 %collective-permute-start.5 = (bf16[2,256,256]{2,1,0:T(8,128)(2,1)S(1)}, bf16[2,256,256]{2,1,0:T(8,128)(2,1)S(1)}, u32[]{:S(2)}, u32[]{:S(2)}) collective-permute-start(bf16[2,256,256]{2,1,0:T(8,128)(2,1)S(1)} %copy-done.8), channel_id=1, source_target_pairs={{0,4},{4,8},{8,12},{12,16},{16,20},{20,24},{24,28},{28,0},{1,5},{5... | collective-permute-start | bytes 786440 | tf_op jit(solution)/shard_map/ppermute | solution.py:389
  47.1 6.3 %collective-permute-start.6 = (bf16[2,256,256]{2,1,0:T(8,128)(2,1)S(1)}, bf16[2,256,256]{2,1,0:T(8,128)(2,1)S(1)}, u32[]{:S(2)}, u32[]{:S(2)}) collective-permute-start(bf16[2,256,256]{2,1,0:T(8,128)(2,1)S(1)} %copy-done.7), channel_id=1, source_target_pairs={{0,28},{4,0},{8,4},{12,8},{16,12},{20,16},{24,20},{28,24},{1,29},{... | collective-permute-start | bytes 786440 | tf_op jit(solution)/shard_map/ppermute | solution.py:389
  53.4 9.4 %shard_map.48 = (bf16[6,2,256,256]{3,2,1,0:T(8,128)(2,1)S(1)}, f32[6,256,256]{2,1,0:T(8,128)S(1)}, f32[6,16,256]{2,1,0:T(8,128)S(1)}) custom-call(s32[7]{0:T(128)S(1)} %get-tuple-element.60.slot_ref, bf16[16,1536]{1,0:T(8,128)(2,1)S(1)} %fusion.x_ref, bf16[6,3,256,512]{3,2,1,0:T(8,128)(2,1)} %get-tuple-element.42.z_any, ...), custom_call_target="tpu_custom_call" | custom-call | flops 12000000000 | bytes 8000000 | tf_op jit(solution)/shard_map/pallas_call | solution.py:432
  62.8 1.2 %copy-done.1 = f32[6,256,256]{2,1,0:T(8,128)} copy-done((f32[6,256,256]{2,1,0:T(8,128)}, f32[6,256,256]{2,1,0:T(8,128)S(1)}, u32[]{:S(2)}) %copy-start.1) | copy-done | bytes 1572888
  64.2 19.1 %shard_map.49 = (f32[6,4,256]{2,1,0:T(4,128)S(1)}, f32[6,4,256]{2,1,0:T(4,128)S(1)}, f32[6,4,256]{2,1,0:T(4,128)S(1)}, f32[6,4,256]{2,1,0:T(4,128)S(1)}, bf16[32,4,256]{2,1,0:T(4,128)(2,1)}) custom-call(s32[7]{0:T(128)S(1)} %pad_add_fusion.1.place_ref, s32[7]{0:T(128)S(1)} %get-tuple-element.60.slot_ref, bf16[16,1536]{1,0:T(8,128)(2,1)S(1)} %fusion.x_ref, ...), custom_call_target="tpu_custom_call" | custom-call | tf_op jit(solution)/shard_map/pallas_call | solution.py:453
  83.9 3.0 %all-to-all-start.1 = ((bf16[32,4,256]{2,1,0:T(4,128)(2,1)}), bf16[32,4,256]{2,1,0:T(4,128)(2,1)S(1)}, u32[]{:S(2)}, u32[]{:S(2)}) async-start(bf16[32,4,256]{2,1,0:T(4,128)(2,1)} %get-tuple-element.54), calls=%async_computation.1 | async-start | bytes 131072 | tf_op jit(solution)/shard_map/all_to_all | solution.py:473
  87.3 1.7 %collective-permute-start.8 = (f32[6,4,256]{2,1,0:T(4,128)S(1)}, f32[6,4,256]{2,1,0:T(4,128)S(1)}, u32[]{:S(2)}, u32[]{:S(2)}) collective-permute-start(f32[6,4,256]{2,1,0:T(4,128)S(1)} %get-tuple-element.57), channel_id=1, source_target_pairs={{0,2},{1,3},{2,0},{3,1},{4,6},{5,7},{6,4},{7,5},{8,10},{9,11},{10,... | collective-permute-start | bytes 73736 | tf_op jit(solution)/shard_map/ppermute | solution.py:389
  88.9 1.3 %collective-permute-start.9 = (f32[6,4,256]{2,1,0:T(4,128)S(1)}, f32[6,4,256]{2,1,0:T(4,128)S(1)}, u32[]{:S(2)}, u32[]{:S(2)}) collective-permute-start(f32[6,4,256]{2,1,0:T(4,128)S(1)} %get-tuple-element.58), channel_id=1, source_target_pairs={{0,3},{1,0},{2,1},{3,2},{4,7},{5,4},{6,5},{7,6},{8,11},{9,8},{10,9... | collective-permute-start | bytes 73736 | tf_op jit(solution)/shard_map/ppermute | solution.py:389
  90.3 0.6 pad_add_fusion.place_ref
  91.1 0.6 collective-permute-done.9.refs_3_
  91.8 2.6 %all-to-all-done.1.low_ref = bf16[32,4,256]{2,1,0:T(4,128)(2,1)S(1)} async-done(((bf16[32,4,256]{2,1,0:T(4,128)(2,1)}), bf16[32,4,256]{2,1,0:T(4,128)(2,1)S(1)}, u32[]{:S(2)}, u32[]{:S(2)}) %all-to-all-start.1) | async-done | bytes 65568 | tf_op jit(solution)/shard_map/all_to_all | solution.py:473
  95.0 1.6 %shard_map.50 = bf16[4,6144]{1,0:T(4,128)(2,1)} custom-call(s32[25]{0:T(128)} %pad_add_fusion.place_ref, bf16[32,4,256]{2,1,0:T(4,128)(2,1)} %copy-done.3, f32[6,4,256]{2,1,0:T(4,128)} %copy-done.2, f32[6,4,256]{2,1,0:T(4,128)} %copy-done.4, f32[6,4,256]{2,1,0:T(4,128)} %copy-done.5, f32[6,4,256]{2,1,0:T(4,128)} %copy-done.6), custom_call_target="tpu_custom_call" | custom-call | tf_op jit(solution)/shard_map/pallas_call | solution.py:475
  (34 shorter events, 2.3 us)
Async XLA Ops:
  1.6 14.4 %copy-start.9 = (s32[192]{0:T(256)S(1)}, s32[192]{0:T(256)}, u32[]{:S(2)}) copy-start(s32[192]{0:T(256)} %param.6) | copy-start | bytes 2308
  5.2 40.3 %collective-permute-start = (bf16[2,256,256]{2,1,0:T(8,128)(2,1)}, bf16[2,256,256]{2,1,0:T(8,128)(2,1)S(1)}, u32[]{:S(2)}, u32[]{:S(2)}) collective-permute-start(bf16[2,256,256]{2,1,0:T(8,128)(2,1)} %get-tuple-element.37), channel_id=1, source_target_pairs={{0,8},{4,12},{8,16},{12,20},{16,24},{20,28},{24,0},{28,4},{1,9},{5... | collective-permute-start | bytes 786440 | tf_op jit(solution)/shard_map/ppermute | solution.py:389
  8.2 37.3 %collective-permute-start.1 = (bf16[2,256,256]{2,1,0:T(8,128)(2,1)}, bf16[2,256,256]{2,1,0:T(8,128)(2,1)S(1)}, u32[]{:S(2)}, u32[]{:S(2)}) collective-permute-start(bf16[2,256,256]{2,1,0:T(8,128)(2,1)} %get-tuple-element.38), channel_id=1, source_target_pairs={{0,12},{4,16},{8,20},{12,24},{16,28},{20,0},{24,4},{28,8},{1,13},{... | collective-permute-start | bytes 786440 | tf_op jit(solution)/shard_map/ppermute | solution.py:389
  10.8 34.8 %collective-permute-start.2 = (bf16[2,256,256]{2,1,0:T(8,128)(2,1)}, bf16[2,256,256]{2,1,0:T(8,128)(2,1)S(1)}, u32[]{:S(2)}, u32[]{:S(2)}) collective-permute-start(bf16[2,256,256]{2,1,0:T(8,128)(2,1)} %get-tuple-element.39), channel_id=1, source_target_pairs={{0,16},{4,20},{8,24},{12,28},{16,0},{20,4},{24,8},{28,12},{1,17},{... | collective-permute-start | bytes 786440 | tf_op jit(solution)/shard_map/ppermute | solution.py:389
  12.0 33.5 %collective-permute-start.3 = (bf16[2,256,256]{2,1,0:T(8,128)(2,1)}, bf16[2,256,256]{2,1,0:T(8,128)(2,1)S(1)}, u32[]{:S(2)}, u32[]{:S(2)}) collective-permute-start(bf16[2,256,256]{2,1,0:T(8,128)(2,1)} %get-tuple-element.40), channel_id=1, source_target_pairs={{0,20},{4,24},{8,28},{12,0},{16,4},{20,8},{24,12},{28,16},{1,21},{... | collective-permute-start | bytes 786440 | tf_op jit(solution)/shard_map/ppermute | solution.py:389
  14.6 30.9 %collective-permute-start.4 = (bf16[2,256,256]{2,1,0:T(8,128)(2,1)}, bf16[2,256,256]{2,1,0:T(8,128)(2,1)S(1)}, u32[]{:S(2)}, u32[]{:S(2)}) collective-permute-start(bf16[2,256,256]{2,1,0:T(8,128)(2,1)} %get-tuple-element.41), channel_id=1, source_target_pairs={{0,24},{4,28},{8,0},{12,4},{16,8},{20,12},{24,16},{28,20},{1,25},{... | collective-permute-start | bytes 786440 | tf_op jit(solution)/shard_map/ppermute | solution.py:389
  16.1 2.1 %copy-start = (bf16[6,5,256,256]{3,2,1,0:T(8,128)(2,1)S(1)}, bf16[6,5,256,256]{3,2,1,0:T(8,128)(2,1)}, u32[]{:S(2)}) copy-start(bf16[6,5,256,256]{3,2,1,0:T(8,128)(2,1)} %tiles_ref.3) | copy-start | bytes 11796484
  18.2 27.3 %copy-start.8 = (bf16[2,256,256]{2,1,0:T(8,128)(2,1)S(1)}, bf16[2,256,256]{2,1,0:T(8,128)(2,1)}, u32[]{:S(2)}) copy-start(bf16[2,256,256]{2,1,0:T(8,128)(2,1)} %get-tuple-element.52) | copy-start | bytes 786436
  18.2 28.9 %copy-start.7 = (bf16[2,256,256]{2,1,0:T(8,128)(2,1)S(1)}, bf16[2,256,256]{2,1,0:T(8,128)(2,1)}, u32[]{:S(2)}) copy-start(bf16[2,256,256]{2,1,0:T(8,128)(2,1)} %get-tuple-element.53) | copy-start | bytes 786436
  38.1 7.3 %all-to-all-start = ((bf16[4,4,1536]{2,0,1:T(4,128)(2,1)}), bf16[4,4,1536]{2,0,1:T(4,128)(2,1)S(1)}, u32[]{:S(2)}, u32[]{:S(2)}) async-start(bf16[4,4,1536]{2,0,1:T(4,128)(2,1)} %bitcast.3), calls=%async_computation | async-start | bytes 98304 | tf_op jit(solution)/shard_map/all_to_all | solution.py:424
  45.6 18.4 %collective-permute-start.5 = (bf16[2,256,256]{2,1,0:T(8,128)(2,1)S(1)}, bf16[2,256,256]{2,1,0:T(8,128)(2,1)S(1)}, u32[]{:S(2)}, u32[]{:S(2)}) collective-permute-start(bf16[2,256,256]{2,1,0:T(8,128)(2,1)S(1)} %copy-done.8), channel_id=1, source_target_pairs={{0,4},{4,8},{8,12},{12,16},{16,20},{20,24},{24,28},{28,0},{1,5},{5... | collective-permute-start | bytes 786440 | tf_op jit(solution)/shard_map/ppermute | solution.py:389
  47.1 17.1 %collective-permute-start.6 = (bf16[2,256,256]{2,1,0:T(8,128)(2,1)S(1)}, bf16[2,256,256]{2,1,0:T(8,128)(2,1)S(1)}, u32[]{:S(2)}, u32[]{:S(2)}) collective-permute-start(bf16[2,256,256]{2,1,0:T(8,128)(2,1)S(1)} %copy-done.7), channel_id=1, source_target_pairs={{0,28},{4,0},{8,4},{12,8},{16,12},{20,16},{24,20},{28,24},{1,29},{... | collective-permute-start | bytes 786440 | tf_op jit(solution)/shard_map/ppermute | solution.py:389
  62.8 1.2 %copy-start.1 = (f32[6,256,256]{2,1,0:T(8,128)}, f32[6,256,256]{2,1,0:T(8,128)S(1)}, u32[]{:S(2)}) copy-start(f32[6,256,256]{2,1,0:T(8,128)S(1)} %get-tuple-element.51.t_any) | copy-start | bytes 4718596
  83.3 0.6 copy-start.2
  83.9 10.5 %all-to-all-start.1 = ((bf16[32,4,256]{2,1,0:T(4,128)(2,1)}), bf16[32,4,256]{2,1,0:T(4,128)(2,1)S(1)}, u32[]{:S(2)}, u32[]{:S(2)}) async-start(bf16[32,4,256]{2,1,0:T(4,128)(2,1)} %get-tuple-element.54), calls=%async_computation.1 | async-start | bytes 131072 | tf_op jit(solution)/shard_map/all_to_all | solution.py:473
  87.0 4.0 %collective-permute-start.7 = (f32[6,4,256]{2,1,0:T(4,128)S(1)}, f32[6,4,256]{2,1,0:T(4,128)S(1)}, u32[]{:S(2)}, u32[]{:S(2)}) collective-permute-start(f32[6,4,256]{2,1,0:T(4,128)S(1)} %get-tuple-element.56), channel_id=1, source_target_pairs={{0,1},{1,2},{2,3},{3,0},{4,5},{5,6},{6,7},{7,4},{8,9},{9,10},{10,1... | collective-permute-start | bytes 73736 | tf_op jit(solution)/shard_map/ppermute | solution.py:389
  87.3 3.9 %collective-permute-start.8 = (f32[6,4,256]{2,1,0:T(4,128)S(1)}, f32[6,4,256]{2,1,0:T(4,128)S(1)}, u32[]{:S(2)}, u32[]{:S(2)}) collective-permute-start(f32[6,4,256]{2,1,0:T(4,128)S(1)} %get-tuple-element.57), channel_id=1, source_target_pairs={{0,2},{1,3},{2,0},{3,1},{4,6},{5,7},{6,4},{7,5},{8,10},{9,11},{10,... | collective-permute-start | bytes 73736 | tf_op jit(solution)/shard_map/ppermute | solution.py:389
  88.9 2.9 %collective-permute-start.9 = (f32[6,4,256]{2,1,0:T(4,128)S(1)}, f32[6,4,256]{2,1,0:T(4,128)S(1)}, u32[]{:S(2)}, u32[]{:S(2)}) collective-permute-start(f32[6,4,256]{2,1,0:T(4,128)S(1)} %get-tuple-element.58), channel_id=1, source_target_pairs={{0,3},{1,0},{2,1},{3,2},{4,7},{5,4},{6,5},{7,6},{8,11},{9,8},{10,9... | collective-permute-start | bytes 73736 | tf_op jit(solution)/shard_map/ppermute | solution.py:389
  90.9 3.5 %copy-start.4 = (f32[6,4,256]{2,1,0:T(4,128)}, f32[6,4,256]{2,1,0:T(4,128)S(1)}, u32[]{:S(2)}) copy-start(f32[6,4,256]{2,1,0:T(4,128)S(1)} %collective-permute-done.7.refs_1_) | copy-start | bytes 73732
  91.1 3.2 %copy-start.5 = (f32[6,4,256]{2,1,0:T(4,128)}, f32[6,4,256]{2,1,0:T(4,128)S(1)}, u32[]{:S(2)}) copy-start(f32[6,4,256]{2,1,0:T(4,128)S(1)} %collective-permute-done.8.refs_2_) | copy-start | bytes 73732
  91.8 2.6 %copy-start.6 = (f32[6,4,256]{2,1,0:T(4,128)}, f32[6,4,256]{2,1,0:T(4,128)S(1)}, u32[]{:S(2)}) copy-start(f32[6,4,256]{2,1,0:T(4,128)S(1)} %collective-permute-done.9.refs_3_) | copy-start | bytes 73732
  94.4 0.6 copy-start.3

commit v20 on v19

--- a/solution.py
+++ b/solution.py
@@ -6,7 +6,7 @@
 from jax.experimental.pallas import tpu as pltpu
 from jax.sharding import PartitionSpec as P
 
-STEP = 32
+STEP = 64
 ROUND = 8
 NT = (((1,), (1,)), ((), ()))
 NN = (((1,), (0,)), ((), ()))

time: 97 us -> 99.3 us (1.024)
  Pallas kernels: 53.6 us -> 58.6 us
  starting transfers between devices: 28.3 us -> 25.4 us
    pallas_call x1, Pallas kernels: 19.9 us -> 22.7 us  [on_device(): pl.pallas_call(own_kernel, out_shape=(jax.ShapeDtypeStruct((systems, 2, w...]
    ppermute x10, starting transfers between devices: 22 us -> 19.2 us  [shift(): lax.ppermute(value, axis, [(i, (i + by) % size) for i in range(size)])]
    pallas_call x1, Pallas kernels: 19.1 us -> 21.4 us  [on_device(): pl.pallas_call(functools.partial(pair_kernel, lanes, every, late), out_sh...]
  transfers between devices with their start and end apart: 12 -> 12, of which waited for: 5 -> 5; matrix products, arithmetic and copies ran while one was open for 1% -> 1% of each run, Pallas kernels for 30% -> 32%
where the time goes in v20:
time: 99.3 us; the launch traced here: 98.9 us
  Pallas kernels  58.6 us (59%)
  starting transfers between devices  25.4 us (26%)
  waiting for transfers between devices  7.79 us (8%)
  local copies, waits for them, and re-layouts  4.68 us (5%)
  other arithmetic  2.28 us (2%)
    pallas_call x1, Pallas kernels, on_device(): pl.pallas_call(own_kernel, out_shape=(jax.ShapeDtypeStruct((systems, 2, w...  22.7 us
    pallas_call x1, Pallas kernels, on_device(): pl.pallas_call(functools.partial(pair_kernel, lanes, every, late), out_sh...  21.4 us
    ppermute x10, starting transfers between devices, shift(): lax.ppermute(value, axis, [(i, (i + by) % size) for i in range(size)])  19.2 us
    pallas_call x1, Pallas kernels, on_device(): pl.pallas_call(functools.partial(link_kernel, early), out_shape=(jax.Shap...  9.39 us
    unnamed x20, local copies, waits for them, and re-layouts  4.51 us
    all_to_all x1, waiting for transfers between devices, on_device(): x = lax.all_to_all(inputs, 'rhs', split_axis=1, concat_axis=0, tiled=True)  3.92 us
    pallas_call x1, Pallas kernels, on_device(): pl.pallas_call(pick_kernel, out_shape=[jax.ShapeDtypeStruct((2, width, wi...  3.56 us
    all_to_all x1, starting transfers between devices, on_device(): x = lax.all_to_all(inputs, 'rhs', split_axis=1, concat_axis=0, tiled=True)  3.27 us
  transfers between devices with their start and end apart: 12, of which 5 were waited for; matrix products, arithmetic and copies ran while one was open for 1% of the time, Pallas kernels for 32%

profile of v20, /device:TPU:0, one launch (start us, length us, event | category | flops | bytes accessed | tf_op | source)
XLA Modules:
  0.0 98.9 jit_solution(9808489368868741392)
XLA Ops:
  0.0 0.8 bitcast_select_fusion
  0.9 0.7 select_reduce_fusion
  1.6 3.6 %shard_map.47 = (bf16[2,256,256]{2,1,0:T(8,128)(2,1)}, bf16[2,256,256]{2,1,0:T(8,128)(2,1)}, bf16[2,256,256]{2,1,0:T(8,128)(2,1)}, bf16[2,256,256]{2,1,0:T(8,128...) custom-call(s32[7]{0:T(128)} %get-tuple-element.59.slot_ref, ...), custom_call_target="tpu_custom_call" | custom-call | tf_op jit(solution)/shard_map/pallas_call | solution.py:400
  5.2 3.1 %collective-permute-start = (bf16[2,256,256]{2,1,0:T(8,128)(2,1)}, bf16[2,256,256]{2,1,0:T(8,128)(2,1)S(1)}, u32[]{:S(2)}, u32[]{:S(2)}) collective-permute-start(bf16[2,256,256]{2,1,0:T(8,128)(2,1)} %get-tuple-element.37), channel_id=1, source_target_pairs={{0,8},{4,12},{8,16},{12,20},{16,24},{20,28},{24,0},{28,4},{1,9},{5... | collective-permute-start | bytes 786440 | tf_op jit(solution)/shard_map/ppermute | solution.py:389
  8.2 2.5 %collective-permute-start.1 = (bf16[2,256,256]{2,1,0:T(8,128)(2,1)}, bf16[2,256,256]{2,1,0:T(8,128)(2,1)S(1)}, u32[]{:S(2)}, u32[]{:S(2)}) collective-permute-start(bf16[2,256,256]{2,1,0:T(8,128)(2,1)} %get-tuple-element.38), channel_id=1, source_target_pairs={{0,12},{4,16},{8,20},{12,24},{16,28},{20,0},{24,4},{28,8},{1,13},{... | collective-permute-start | bytes 786440 | tf_op jit(solution)/shard_map/ppermute | solution.py:389
  10.8 1.2 %collective-permute-start.2 = (bf16[2,256,256]{2,1,0:T(8,128)(2,1)}, bf16[2,256,256]{2,1,0:T(8,128)(2,1)S(1)}, u32[]{:S(2)}, u32[]{:S(2)}) collective-permute-start(bf16[2,256,256]{2,1,0:T(8,128)(2,1)} %get-tuple-element.39), channel_id=1, source_target_pairs={{0,16},{4,20},{8,24},{12,28},{16,0},{20,4},{24,8},{28,12},{1,17},{... | collective-permute-start | bytes 786440 | tf_op jit(solution)/shard_map/ppermute | solution.py:389
  12.0 2.6 %collective-permute-start.3 = (bf16[2,256,256]{2,1,0:T(8,128)(2,1)}, bf16[2,256,256]{2,1,0:T(8,128)(2,1)S(1)}, u32[]{:S(2)}, u32[]{:S(2)}) collective-permute-start(bf16[2,256,256]{2,1,0:T(8,128)(2,1)} %get-tuple-element.40), channel_id=1, source_target_pairs={{0,20},{4,24},{8,28},{12,0},{16,4},{20,8},{24,12},{28,16},{1,21},{... | collective-permute-start | bytes 786440 | tf_op jit(solution)/shard_map/ppermute | solution.py:389
  14.6 1.4 %collective-permute-start.4 = (bf16[2,256,256]{2,1,0:T(8,128)(2,1)}, bf16[2,256,256]{2,1,0:T(8,128)(2,1)S(1)}, u32[]{:S(2)}, u32[]{:S(2)}) collective-permute-start(bf16[2,256,256]{2,1,0:T(8,128)(2,1)} %get-tuple-element.41), channel_id=1, source_target_pairs={{0,24},{4,28},{8,0},{12,4},{16,8},{20,12},{24,16},{28,20},{1,25},{... | collective-permute-start | bytes 786440 | tf_op jit(solution)/shard_map/ppermute | solution.py:389
  16.1 2.1 %copy-done = bf16[6,5,256,256]{3,2,1,0:T(8,128)(2,1)S(1)} copy-done((bf16[6,5,256,256]{3,2,1,0:T(8,128)(2,1)S(1)}, bf16[6,5,256,256]{3,2,1,0:T(8,128)(2,1)}, u32[]{:S(2)}) %copy-start) | copy-done | bytes 3932184
  18.2 22.7 %shard_map.46 = (bf16[6,2,256,256]{3,2,1,0:T(8,128)(2,1)S(1)}, bf16[6,3,256,512]{3,2,1,0:T(8,128)(2,1)}) custom-call(s32[6]{0:T(128)S(1)} %dynamic_slice.14.counts_ref, bf16[6,5,256,256]{3,2,1,0:T(8,128)(2,1)S(1)} %copy-done), custom_call_target="tpu_custom_call" | custom-call | flops 30000001024 | bytes 8000000 | tf_op jit(solution)/shard_map/pallas_call | solution.py:410
  40.8 3.3 %all-to-all-start = ((bf16[4,4,1536]{2,0,1:T(4,128)(2,1)}), bf16[4,4,1536]{2,0,1:T(4,128)(2,1)S(1)}, u32[]{:S(2)}, u32[]{:S(2)}) async-start(bf16[4,4,1536]{2,0,1:T(4,128)(2,1)} %bitcast.3), calls=%async_computation | async-start | bytes 98304 | tf_op jit(solution)/shard_map/all_to_all | solution.py:424
  44.2 3.9 %all-to-all-done = bf16[4,4,1536]{2,0,1:T(4,128)(2,1)S(1)} async-done(((bf16[4,4,1536]{2,0,1:T(4,128)(2,1)}), bf16[4,4,1536]{2,0,1:T(4,128)(2,1)S(1)}, u32[]{:S(2)}, u32[]{:S(2)}) %all-to-all-start) | async-done | bytes 49184 | tf_op jit(solution)/shard_map/all_to_all | solution.py:424
  48.3 2.2 %collective-permute-start.5 = (bf16[2,256,256]{2,1,0:T(8,128)(2,1)S(1)}, bf16[2,256,256]{2,1,0:T(8,128)(2,1)S(1)}, u32[]{:S(2)}, u32[]{:S(2)}) collective-permute-start(bf16[2,256,256]{2,1,0:T(8,128)(2,1)S(1)} %copy-done.8), channel_id=1, source_target_pairs={{0,4},{4,8},{8,12},{12,16},{16,20},{20,24},{24,28},{28,0},{1,5},{5... | collective-permute-start | bytes 786440 | tf_op jit(solution)/shard_map/ppermute | solution.py:389
  50.5 2.9 %collective-permute-start.6 = (bf16[2,256,256]{2,1,0:T(8,128)(2,1)S(1)}, bf16[2,256,256]{2,1,0:T(8,128)(2,1)S(1)}, u32[]{:S(2)}, u32[]{:S(2)}) collective-permute-start(bf16[2,256,256]{2,1,0:T(8,128)(2,1)S(1)} %copy-done.7), channel_id=1, source_target_pairs={{0,28},{4,0},{8,4},{12,8},{16,12},{20,16},{24,20},{28,24},{1,29},{... | collective-permute-start | bytes 786440 | tf_op jit(solution)/shard_map/ppermute | solution.py:389
  53.4 9.4 %shard_map.48 = (bf16[6,2,256,256]{3,2,1,0:T(8,128)(2,1)S(1)}, f32[6,256,256]{2,1,0:T(8,128)S(1)}, f32[6,16,256]{2,1,0:T(8,128)S(1)}) custom-call(s32[7]{0:T(128)S(1)} %get-tuple-element.60.slot_ref, bf16[16,1536]{1,0:T(8,128)(2,1)S(1)} %fusion.x_ref, bf16[6,3,256,512]{3,2,1,0:T(8,128)(2,1)} %get-tuple-element.42.z_any, ...), custom_call_target="tpu_custom_call" | custom-call | flops 12000000000 | bytes 8000000 | tf_op jit(solution)/shard_map/pallas_call | solution.py:432
  62.8 1.2 %copy-done.1 = f32[6,256,256]{2,1,0:T(8,128)} copy-done((f32[6,256,256]{2,1,0:T(8,128)}, f32[6,256,256]{2,1,0:T(8,128)S(1)}, u32[]{:S(2)}) %copy-start.1) | copy-done | bytes 1572888
  64.4 21.4 %shard_map.49 = (f32[6,4,256]{2,1,0:T(4,128)S(1)}, f32[6,4,256]{2,1,0:T(4,128)S(1)}, f32[6,4,256]{2,1,0:T(4,128)S(1)}, f32[6,4,256]{2,1,0:T(4,128)S(1)}, bf16[32,4,256]{2,1,0:T(4,128)(2,1)}) custom-call(s32[7]{0:T(128)S(1)} %pad_add_fusion.1.place_ref, s32[7]{0:T(128)S(1)} %get-tuple-element.60.slot_ref, bf16[16,1536]{1,0:T(8,128)(2,1)S(1)} %fusion.x_ref, ...), custom_call_target="tpu_custom_call" | custom-call | tf_op jit(solution)/shard_map/pallas_call | solution.py:453
  86.4 2.9 %all-to-all-start.1 = ((bf16[32,4,256]{2,1,0:T(4,128)(2,1)}), bf16[32,4,256]{2,1,0:T(4,128)(2,1)S(1)}, u32[]{:S(2)}, u32[]{:S(2)}) async-start(bf16[32,4,256]{2,1,0:T(4,128)(2,1)} %get-tuple-element.54), calls=%async_computation.1 | async-start | bytes 131072 | tf_op jit(solution)/shard_map/all_to_all | solution.py:473
  89.6 1.7 %collective-permute-start.8 = (f32[6,4,256]{2,1,0:T(4,128)S(1)}, f32[6,4,256]{2,1,0:T(4,128)S(1)}, u32[]{:S(2)}, u32[]{:S(2)}) collective-permute-start(f32[6,4,256]{2,1,0:T(4,128)S(1)} %get-tuple-element.57), channel_id=1, source_target_pairs={{0,2},{1,3},{2,0},{3,1},{4,6},{5,7},{6,4},{7,5},{8,10},{9,11},{10,... | collective-permute-start | bytes 73736 | tf_op jit(solution)/shard_map/ppermute | solution.py:389
  91.3 1.3 %collective-permute-start.9 = (f32[6,4,256]{2,1,0:T(4,128)S(1)}, f32[6,4,256]{2,1,0:T(4,128)S(1)}, u32[]{:S(2)}, u32[]{:S(2)}) collective-permute-start(f32[6,4,256]{2,1,0:T(4,128)S(1)} %get-tuple-element.58), channel_id=1, source_target_pairs={{0,3},{1,0},{2,1},{3,2},{4,7},{5,4},{6,5},{7,6},{8,11},{9,8},{10,9... | collective-permute-start | bytes 73736 | tf_op jit(solution)/shard_map/ppermute | solution.py:389
  92.6 0.6 pad_add_fusion.place_ref
  93.5 0.6 collective-permute-done.9.refs_3_
  94.1 2.6 %all-to-all-done.1.low_ref = bf16[32,4,256]{2,1,0:T(4,128)(2,1)S(1)} async-done(((bf16[32,4,256]{2,1,0:T(4,128)(2,1)}), bf16[32,4,256]{2,1,0:T(4,128)(2,1)S(1)}, u32[]{:S(2)}, u32[]{:S(2)}) %all-to-all-start.1) | async-done | bytes 65568 | tf_op jit(solution)/shard_map/all_to_all | solution.py:473
  97.4 1.6 %shard_map.50 = bf16[4,6144]{1,0:T(4,128)(2,1)} custom-call(s32[25]{0:T(128)} %pad_add_fusion.place_ref, bf16[32,4,256]{2,1,0:T(4,128)(2,1)} %copy-done.3, f32[6,4,256]{2,1,0:T(4,128)} %copy-done.2, f32[6,4,256]{2,1,0:T(4,128)} %copy-done.4, f32[6,4,256]{2,1,0:T(4,128)} %copy-done.5, f32[6,4,256]{2,1,0:T(4,128)} %copy-done.6), custom_call_target="tpu_custom_call" | custom-call | tf_op jit(solution)/shard_map/pallas_call | solution.py:475
  (34 shorter events, 2.5 us)
Async XLA Ops:
  1.6 14.4 %copy-start.9 = (s32[192]{0:T(256)S(1)}, s32[192]{0:T(256)}, u32[]{:S(2)}) copy-start(s32[192]{0:T(256)} %param.6) | copy-start | bytes 2308
  5.2 43.1 %collective-permute-start = (bf16[2,256,256]{2,1,0:T(8,128)(2,1)}, bf16[2,256,256]{2,1,0:T(8,128)(2,1)S(1)}, u32[]{:S(2)}, u32[]{:S(2)}) collective-permute-start(bf16[2,256,256]{2,1,0:T(8,128)(2,1)} %get-tuple-element.37), channel_id=1, source_target_pairs={{0,8},{4,12},{8,16},{12,20},{16,24},{20,28},{24,0},{28,4},{1,9},{5... | collective-permute-start | bytes 786440 | tf_op jit(solution)/shard_map/ppermute | solution.py:389
  8.2 40.0 %collective-permute-start.1 = (bf16[2,256,256]{2,1,0:T(8,128)(2,1)}, bf16[2,256,256]{2,1,0:T(8,128)(2,1)S(1)}, u32[]{:S(2)}, u32[]{:S(2)}) collective-permute-start(bf16[2,256,256]{2,1,0:T(8,128)(2,1)} %get-tuple-element.38), channel_id=1, source_target_pairs={{0,12},{4,16},{8,20},{12,24},{16,28},{20,0},{24,4},{28,8},{1,13},{... | collective-permute-start | bytes 786440 | tf_op jit(solution)/shard_map/ppermute | solution.py:389
  10.8 37.5 %collective-permute-start.2 = (bf16[2,256,256]{2,1,0:T(8,128)(2,1)}, bf16[2,256,256]{2,1,0:T(8,128)(2,1)S(1)}, u32[]{:S(2)}, u32[]{:S(2)}) collective-permute-start(bf16[2,256,256]{2,1,0:T(8,128)(2,1)} %get-tuple-element.39), channel_id=1, source_target_pairs={{0,16},{4,20},{8,24},{12,28},{16,0},{20,4},{24,8},{28,12},{1,17},{... | collective-permute-start | bytes 786440 | tf_op jit(solution)/shard_map/ppermute | solution.py:389
  12.0 36.2 %collective-permute-start.3 = (bf16[2,256,256]{2,1,0:T(8,128)(2,1)}, bf16[2,256,256]{2,1,0:T(8,128)(2,1)S(1)}, u32[]{:S(2)}, u32[]{:S(2)}) collective-permute-start(bf16[2,256,256]{2,1,0:T(8,128)(2,1)} %get-tuple-element.40), channel_id=1, source_target_pairs={{0,20},{4,24},{8,28},{12,0},{16,4},{20,8},{24,12},{28,16},{1,21},{... | collective-permute-start | bytes 786440 | tf_op jit(solution)/shard_map/ppermute | solution.py:389
  14.6 33.6 %collective-permute-start.4 = (bf16[2,256,256]{2,1,0:T(8,128)(2,1)}, bf16[2,256,256]{2,1,0:T(8,128)(2,1)S(1)}, u32[]{:S(2)}, u32[]{:S(2)}) collective-permute-start(bf16[2,256,256]{2,1,0:T(8,128)(2,1)} %get-tuple-element.41), channel_id=1, source_target_pairs={{0,24},{4,28},{8,0},{12,4},{16,8},{20,12},{24,16},{28,20},{1,25},{... | collective-permute-start | bytes 786440 | tf_op jit(solution)/shard_map/ppermute | solution.py:389
  16.1 2.1 %copy-start = (bf16[6,5,256,256]{3,2,1,0:T(8,128)(2,1)S(1)}, bf16[6,5,256,256]{3,2,1,0:T(8,128)(2,1)}, u32[]{:S(2)}) copy-start(bf16[6,5,256,256]{3,2,1,0:T(8,128)(2,1)} %tiles_ref.3) | copy-start | bytes 11796484
  18.2 30.1 %copy-start.8 = (bf16[2,256,256]{2,1,0:T(8,128)(2,1)S(1)}, bf16[2,256,256]{2,1,0:T(8,128)(2,1)}, u32[]{:S(2)}) copy-start(bf16[2,256,256]{2,1,0:T(8,128)(2,1)} %get-tuple-element.52) | copy-start | bytes 786436
  18.2 32.3 %copy-start.7 = (bf16[2,256,256]{2,1,0:T(8,128)(2,1)S(1)}, bf16[2,256,256]{2,1,0:T(8,128)(2,1)}, u32[]{:S(2)}) copy-start(bf16[2,256,256]{2,1,0:T(8,128)(2,1)} %get-tuple-element.53) | copy-start | bytes 786436
  40.8 7.3 %all-to-all-start = ((bf16[4,4,1536]{2,0,1:T(4,128)(2,1)}), bf16[4,4,1536]{2,0,1:T(4,128)(2,1)S(1)}, u32[]{:S(2)}, u32[]{:S(2)}) async-start(bf16[4,4,1536]{2,0,1:T(4,128)(2,1)} %bitcast.3), calls=%async_computation | async-start | bytes 98304 | tf_op jit(solution)/shard_map/all_to_all | solution.py:424
  48.3 15.7 %collective-permute-start.5 = (bf16[2,256,256]{2,1,0:T(8,128)(2,1)S(1)}, bf16[2,256,256]{2,1,0:T(8,128)(2,1)S(1)}, u32[]{:S(2)}, u32[]{:S(2)}) collective-permute-start(bf16[2,256,256]{2,1,0:T(8,128)(2,1)S(1)} %copy-done.8), channel_id=1, source_target_pairs={{0,4},{4,8},{8,12},{12,16},{16,20},{20,24},{24,28},{28,0},{1,5},{5... | collective-permute-start | bytes 786440 | tf_op jit(solution)/shard_map/ppermute | solution.py:389
  50.5 13.9 %collective-permute-start.6 = (bf16[2,256,256]{2,1,0:T(8,128)(2,1)S(1)}, bf16[2,256,256]{2,1,0:T(8,128)(2,1)S(1)}, u32[]{:S(2)}, u32[]{:S(2)}) collective-permute-start(bf16[2,256,256]{2,1,0:T(8,128)(2,1)S(1)} %copy-done.7), channel_id=1, source_target_pairs={{0,28},{4,0},{8,4},{12,8},{16,12},{20,16},{24,20},{28,24},{1,29},{... | collective-permute-start | bytes 786440 | tf_op jit(solution)/shard_map/ppermute | solution.py:389
  62.8 1.2 %copy-start.1 = (f32[6,256,256]{2,1,0:T(8,128)}, f32[6,256,256]{2,1,0:T(8,128)S(1)}, u32[]{:S(2)}) copy-start(f32[6,256,256]{2,1,0:T(8,128)S(1)} %get-tuple-element.51.t_any) | copy-start | bytes 4718596
  85.8 0.6 copy-start.2
  86.4 10.3 %all-to-all-start.1 = ((bf16[32,4,256]{2,1,0:T(4,128)(2,1)}), bf16[32,4,256]{2,1,0:T(4,128)(2,1)S(1)}, u32[]{:S(2)}, u32[]{:S(2)}) async-start(bf16[32,4,256]{2,1,0:T(4,128)(2,1)} %get-tuple-element.54), calls=%async_computation.1 | async-start | bytes 131072 | tf_op jit(solution)/shard_map/all_to_all | solution.py:473
  89.3 4.0 %collective-permute-start.7 = (f32[6,4,256]{2,1,0:T(4,128)S(1)}, f32[6,4,256]{2,1,0:T(4,128)S(1)}, u32[]{:S(2)}, u32[]{:S(2)}) collective-permute-start(f32[6,4,256]{2,1,0:T(4,128)S(1)} %get-tuple-element.56), channel_id=1, source_target_pairs={{0,1},{1,2},{2,3},{3,0},{4,5},{5,6},{6,7},{7,4},{8,9},{9,10},{10,1... | collective-permute-start | bytes 73736 | tf_op jit(solution)/shard_map/ppermute | solution.py:389
  89.6 3.9 %collective-permute-start.8 = (f32[6,4,256]{2,1,0:T(4,128)S(1)}, f32[6,4,256]{2,1,0:T(4,128)S(1)}, u32[]{:S(2)}, u32[]{:S(2)}) collective-permute-start(f32[6,4,256]{2,1,0:T(4,128)S(1)} %get-tuple-element.57), channel_id=1, source_target_pairs={{0,2},{1,3},{2,0},{3,1},{4,6},{5,7},{6,4},{7,5},{8,10},{9,11},{10,... | collective-permute-start | bytes 73736 | tf_op jit(solution)/shard_map/ppermute | solution.py:389
  91.3 2.9 %collective-permute-start.9 = (f32[6,4,256]{2,1,0:T(4,128)S(1)}, f32[6,4,256]{2,1,0:T(4,128)S(1)}, u32[]{:S(2)}, u32[]{:S(2)}) collective-permute-start(f32[6,4,256]{2,1,0:T(4,128)S(1)} %get-tuple-element.58), channel_id=1, source_target_pairs={{0,3},{1,0},{2,1},{3,2},{4,7},{5,4},{6,5},{7,6},{8,11},{9,8},{10,9... | collective-permute-start | bytes 73736 | tf_op jit(solution)/shard_map/ppermute | solution.py:389
  93.3 3.5 %copy-start.4 = (f32[6,4,256]{2,1,0:T(4,128)}, f32[6,4,256]{2,1,0:T(4,128)S(1)}, u32[]{:S(2)}) copy-start(f32[6,4,256]{2,1,0:T(4,128)S(1)} %collective-permute-done.7.refs_1_) | copy-start | bytes 73732
  93.5 3.2 %copy-start.5 = (f32[6,4,256]{2,1,0:T(4,128)}, f32[6,4,256]{2,1,0:T(4,128)S(1)}, u32[]{:S(2)}) copy-start(f32[6,4,256]{2,1,0:T(4,128)S(1)} %collective-permute-done.8.refs_2_) | copy-start | bytes 73732
  94.1 2.6 %copy-start.6 = (f32[6,4,256]{2,1,0:T(4,128)}, f32[6,4,256]{2,1,0:T(4,128)S(1)}, u32[]{:S(2)}) copy-start(f32[6,4,256]{2,1,0:T(4,128)S(1)} %collective-permute-done.9.refs_3_) | copy-start | bytes 73732
  96.7 0.6 copy-start.3
